TPU v7x, 32 devices: a whole 2x2x4 slice. The times are simulated.
32 devices in a mesh: groups: 2 (over y), session: 16 (over z, x, core).
Axes of the slice: x: 2, y: 2, z: 4, core: 2. Of those that a mesh axis runs over, the one named last changes fastest.
Arguments:
- hidden: bfloat16 [2, 32, 8192], P(None, ('groups', 'session')), parts along dimension 1, may hold values from -6 to 6
- norm_gain: bfloat16 [8192], replicated, may hold values from 0.5 to 1.5
- query_weight: bfloat16 [8192, 8192], P(None, 'session'), may hold values from -0.0625 to 0.0625
- kv_weight: bfloat16 [8192, 2048], P(None, 'session'), may hold values from -0.25 to 0.25
- out_weight: bfloat16 [8192, 8192], P('session'), may hold values from -0.0625 to 0.0625
- key_factors: bfloat16 [32, 512, 160], P(('groups', 'session')), parts along dimension 0, may hold values from -6 to 6
- key_basis: bfloat16 [32, 160, 1024], P(('groups', 'session')), parts along dimension 0, may hold values from -0.5 to 0.5
- value_store: bfloat16 [1024, 16, 1024], P(('groups', 'session')), parts along dimension 0, may hold values from -6 to 6
- lengths: int32 [32], P(('groups', 'session')), parts along dimension 0, may hold values from 256 to 512, as said below
- block_slot: int32 [32, 32], P(('groups', 'session')), parts along dimension 0, may hold values from 0 to 511, as said below
- selection: int32 [2, 32, 16], P(None, ('groups', 'session')), parts along dimension 1, may hold values from 0 to 31, as said below
Outputs:
- attended: bfloat16 [2, 32, 8192], P(None, ('groups', 'session')), parts along dimension 1
There are 2 independent parts, one for each index of `groups`. A program takes and returns all parts, laid end to end along the dimension named above; an argument that names none is the same for every part. Nothing has to cross between parts.
Inputs may be any that keep to these rules, and one draw needn't show every extreme that they name: `block_slot`: pages 2m and 2m+1 of a session lie in slots of one store device (slot // 32), which holds no other page of that session; no slot is used twice. `selection`: 16 different page numbers for each step and session, all below ceil(lengths / 16) of that session; in every one of them some pair 2m, 2m+1 is picked whole. `lengths`: some session has exactly 512.
All inputs are finite; a program needn't handle non-finite values.
Results may differ from a plain program's by a relative error of at most 0.012.
Values may be sent and summed in bfloat16 or wider, within the bound.
No kernel may reach another device: no remote copies, remote signals or barrier semaphores. Data moves between devices by JAX's collectives and lax.ppermute only.
A program may use at most 128 MiB of HBM per device.

v0:
```python
import math

import jax
import jax.numpy as jnp
from jax import lax
from jax.sharding import PartitionSpec as P

HEADS = 64
KV_HEADS = 8
HEAD_DIM = 128
STEPS = 2


def rotate(vector, angle):
    half = vector.shape[-1] // 2
    cosine = jnp.cos(angle)
    sine = jnp.sin(angle)
    first = vector[..., :half]
    second = vector[..., half:]
    return jnp.concatenate(
        [first * cosine - second * sine, second * cosine + first * sine], axis=-1
    )


def angles(positions):
    half = HEAD_DIM // 2
    frequency = jnp.exp(
        -jnp.arange(half, dtype=jnp.float32) * (2.0 * math.log(500000.0) / HEAD_DIM)
    )
    return positions[..., None] * frequency


def local(
    hidden,
    norm_gain,
    query_weight,
    kv_weight,
    out_weight,
    key_factors,
    key_basis,
    value_store,
    lengths,
    block_slot,
    selection,
):
    devices = lax.axis_size("session")
    slots_dev = value_store.shape[0]
    block_len = value_store.shape[1]
    rank_dim = key_factors.shape[2]
    model_width = hidden.shape[2]
    group_size = HEADS // KV_HEADS
    score_scale = 1.0 / math.sqrt(HEAD_DIM)
    query_cols = query_weight.shape[1]
    joined_weight = jnp.concatenate([query_weight, kv_weight], axis=1)
    factors_all = key_factors[0].reshape(-1, block_len, rank_dim)
    fresh_keys = []
    fresh_values = []
    results = []
    for step_index in range(STEPS):
        inputs = hidden[step_index].astype(jnp.float32)
        normed = (
            inputs
            * lax.rsqrt(jnp.mean(inputs * inputs, axis=-1, keepdims=True) + 1e-05)
            * norm_gain.astype(jnp.float32)
        ).astype(jnp.bfloat16)
        projected = jnp.dot(
            lax.all_gather(normed, "session", axis=0, tiled=True),
            joined_weight,
            preferred_element_type=jnp.float32,
        ).astype(jnp.bfloat16)
        columns = lax.all_to_all(projected, "session", split_axis=0, concat_axis=0, tiled=True)
        query_heads = columns[:, :query_cols].reshape(HEADS, HEAD_DIM)
        key_value = columns[:, query_cols:].reshape(2, KV_HEADS, HEAD_DIM)
        position = (lengths[0] + step_index).astype(jnp.float32)
        turned_query = rotate(query_heads.astype(jnp.float32), angles(position)).astype(
            jnp.bfloat16
        )
        turned_new = rotate(key_value[0].astype(jnp.float32), angles(position)).astype(jnp.bfloat16)
        fresh_keys.append(turned_new)
        fresh_values.append(key_value[1])
        stacked_keys = jnp.stack(fresh_keys)
        stacked_values = jnp.stack(fresh_values)
        chosen = selection[step_index, 0]
        places = (
            chosen[:, None] * block_len + jnp.arange(block_len, dtype=jnp.int32)[None, :]
        ).reshape(-1)
        factors = factors_all[chosen].reshape(-1, rank_dim)
        product = jnp.dot(factors, key_basis[0], preferred_element_type=jnp.float32)
        cached_keys = rotate(
            product.reshape(-1, KV_HEADS, HEAD_DIM), angles(places.astype(jnp.float32))[:, None, :]
        ).astype(jnp.bfloat16)
        grouped = turned_query.reshape(KV_HEADS, group_size, HEAD_DIM)
        scores = (
            jnp.einsum("kgd,mkd->kgm", grouped, cached_keys, preferred_element_type=jnp.float32)
            * score_scale
        )
        scores = jnp.where(places[None, None, :] < lengths[0], scores, -1e30)
        recent = (
            jnp.einsum("kgd,nkd->kgn", grouped, stacked_keys, preferred_element_type=jnp.float32)
            * score_scale
        )
        largest = jnp.maximum(jnp.max(scores, axis=-1), jnp.max(recent, axis=-1))
        cache_exp = jnp.exp(scores - largest[..., None])
        recent_exp = jnp.exp(recent - largest[..., None])
        denominator = jnp.sum(cache_exp, axis=-1) + jnp.sum(recent_exp, axis=-1)
        weights_cache = (cache_exp / denominator[..., None]).astype(jnp.bfloat16)
        weights_recent = (recent_exp / denominator[..., None]).astype(jnp.bfloat16)
        page_rows = block_slot[0][chosen]
        holder = page_rows // slots_dev
        local_row = page_rows % slots_dev
        parity = chosen % 2
        matches = (holder[:, None, None] == jnp.arange(devices, dtype=jnp.int32)[None, :, None]) & (
            parity[:, None, None] == jnp.arange(2, dtype=jnp.int32)[None, None, :]
        )
        requests = jnp.sum(jnp.where(matches, local_row[:, None, None] + 1, 0), axis=0)
        stored_pages = value_store[
            jnp.maximum(
                lax.all_to_all(requests, "session", split_axis=0, concat_axis=0, tiled=True) - 1, 0
            )
        ]
        fetched = lax.all_to_all(stored_pages, "session", split_axis=0, concat_axis=0, tiled=True)
        values_used = fetched[holder, parity].reshape(-1, KV_HEADS, HEAD_DIM)
        cache_part = jnp.einsum(
            "kgm,mkd->kgd", weights_cache, values_used, preferred_element_type=jnp.float32
        )
        mixed_heads = cache_part + jnp.einsum(
            "kgn,nkd->kgd", weights_recent, stacked_values, preferred_element_type=jnp.float32
        )
        head_output = mixed_heads.reshape(devices, model_width // devices).astype(jnp.bfloat16)
        head_rows = lax.all_to_all(head_output, "session", split_axis=0, concat_axis=0, tiled=True)
        mixed_rows = lax.psum_scatter(
            jnp.dot(head_rows, out_weight, preferred_element_type=jnp.float32),
            "session",
            scatter_dimension=0,
            tiled=True,
        )
        results.append(mixed_rows.astype(jnp.bfloat16))
    return jnp.stack(results)


def solution(mesh):
    return jax.shard_map(
        local,
        mesh=mesh,
        in_specs=(
            P(None, ("groups", "session"), None),
            P(),
            P(None, "session"),
            P(None, "session"),
            P("session", None),
            P(("groups", "session"), None, None),
            P(("groups", "session"), None, None),
            P(("groups", "session"), None, None),
            P(("groups", "session")),
            P(("groups", "session"), None),
            P(None, ("groups", "session"), None),
        ),
        out_specs=P(None, ("groups", "session"), None),
        check_vma=False,
    )
```

profile of v0, /device:TPU:0, one launch (start us, length us, event | category | flops | bytes accessed | tf_op | source)
XLA Modules:
  0.0 289.1 jit_solution(9924861758556147660)
XLA Ops:
  4.2 7.4 %all-to-all-start.1 = ((s32[16,1,2]{2,1,0:T(1,128)}), s32[16,1,2]{2,1,0:T(1,128)S(1)}, u32[]{:S(2)}, u32[]{:S(2)}) async-start(s32[16,1,2]{2,1,0:T(1,128)} %copy.114), calls=%async_computation.1 | async-start | bytes 16384 | tf_op jit(solution)/shard_map/all_to_all | solution.py:118
  24.9 23.9 %all-gather = bf16[131072]{0:T(1024)(128)(2,1)} all-gather(bf16[8192]{0:T(1024)(128)(2,1)S(1)} %get-tuple-element.24), channel_id=2, replica_groups=mesh['groups'=2,'session'=16] {'session'}, dimensions={0}, use_global_device_ids=true | all-gather | bytes 278528 | tf_op jit(solution)/shard_map/all_gather | solution.py:67
  49.9 7.3 %constant_dynamic-update-slice_fusion.1 = bf16[8192,640]{1,0:T(8,128)(2,1)} fusion(bf16[8192,512]{1,0:T(8,128)(2,1)} %param.13), kind=kLoop, calls=%fused_computation.107 | loop fusion | bytes 16777216
  58.7 5.5 %fusion.4 = bf16[16,1,640]{2,0,1:T(8,128)(2,1)S(1)} fusion(bf16[16,8192]{1,0:T(8,128)(2,1)S(1)} %reshape.1021, bf16[8192,640]{1,0:T(8,128)(2,1)} %constant_dynamic-update-slice_fusion), kind=kOutput, calls=%fused_computation.18 | convolution fusion | flops 167782400 | bytes 10768384 | tf_op jit(solution)/shard_map/dot_general | solution.py:66
  70.9 19.8 %all-gather.1 = bf16[131072]{0:T(1024)(128)(2,1)} all-gather(bf16[8192]{0:T(1024)(128)(2,1)} %get-tuple-element.25), channel_id=3, replica_groups=mesh['groups'=2,'session'=16] {'session'}, dimensions={0}, use_global_device_ids=true | all-gather | bytes 278528 | tf_op jit(solution)/shard_map/all_gather | solution.py:67
  91.8 5.4 %fusion.5 = bf16[16,1,640]{2,0,1:T(8,128)(2,1)S(1)} fusion(bf16[16,8192]{1,0:T(8,128)(2,1)S(1)} %reshape.1022, bf16[8192,640]{1,0:T(8,128)(2,1)} %constant_dynamic-update-slice_fusion), kind=kOutput, calls=%fused_computation.19 | convolution fusion | flops 167782400 | bytes 10768384 | tf_op jit(solution)/shard_map/dot_general | solution.py:66
  101.4 3.5 %all-to-all-start.5 = ((s32[16,1,2]{2,1,0:T(1,128)}), s32[16,1,2]{2,1,0:T(1,128)S(1)}, u32[]{:S(2)}, u32[]{:S(2)}) async-start(s32[16,1,2]{2,1,0:T(1,128)} %copy.125), calls=%async_computation.5 | async-start | bytes 16384 | tf_op jit(solution)/shard_map/all_to_all | solution.py:118
  104.9 6.4 %all-to-all-done.5 = s32[16,1,2]{2,1,0:T(1,128)S(1)} async-done(((s32[16,1,2]{2,1,0:T(1,128)}), s32[16,1,2]{2,1,0:T(1,128)S(1)}, u32[]{:S(2)}, u32[]{:S(2)}) %all-to-all-start.5) | async-done | bytes 160 | tf_op jit(solution)/shard_map/all_to_all | solution.py:118
  111.3 3.4 %all-to-all-start = ((bf16[16,2,320]{2,1,0:T(2,128)(2,1)}), bf16[16,2,320]{2,1,0:T(2,128)(2,1)S(1)}, u32[]{:S(2)}, u32[]{:S(2)}) async-start(bf16[16,2,320]{2,1,0:T(2,128)(2,1)} %reshape.1047), calls=%async_computation | async-start | bytes 49152 | tf_op jit(solution)/shard_map/all_to_all | solution.py:71
  114.8 6.3 %all-to-all-done = bf16[16,2,320]{2,1,0:T(2,128)(2,1)S(1)} async-done(((bf16[16,2,320]{2,1,0:T(2,128)(2,1)}), bf16[16,2,320]{2,1,0:T(2,128)(2,1)S(1)}, u32[]{:S(2)}, u32[]{:S(2)}) %all-to-all-start) | async-done | bytes 20512 | tf_op jit(solution)/shard_map/all_to_all | solution.py:71
  121.2 3.5 %all-to-all-start.4 = ((bf16[16,2,320]{2,1,0:T(2,128)(2,1)}), bf16[16,2,320]{2,1,0:T(2,128)(2,1)S(1)}, u32[]{:S(2)}, u32[]{:S(2)}) async-start(bf16[16,2,320]{2,1,0:T(2,128)(2,1)} %reshape.1045), calls=%async_computation.4 | async-start | bytes 49152 | tf_op jit(solution)/shard_map/all_to_all | solution.py:71
  126.3 4.9 %all-to-all-done.4 = bf16[16,2,320]{2,1,0:T(2,128)(2,1)S(1)} async-done(((bf16[16,2,320]{2,1,0:T(2,128)(2,1)}), bf16[16,2,320]{2,1,0:T(2,128)(2,1)S(1)}, u32[]{:S(2)}, u32[]{:S(2)}) %all-to-all-start.4) | async-done | bytes 20512 | tf_op jit(solution)/shard_map/all_to_all | solution.py:71
  131.2 3.7 %all-to-all-start.2 = ((bf16[16,2,16,1024]{3,2,1,0:T(8,128)(2,1)}), bf16[16,2,16,1024]{3,2,1,0:T(8,128)(2,1)S(1)}, u32[]{:S(2)}, u32[]{:S(2)}) async-start(bf16[16,2,16,1024]{3,2,1,0:T(8,128)(2,1)} %bitcast.18), calls=%async_computation.2 | async-start | bytes 2097152 | tf_op jit(solution)/shard_map/all_to_all | solution.py:121
  138.2 1.8 subtract_convert_fusion
  143.9 1.9 fusion.89
  145.8 12.0 %all-to-all-done.2 = bf16[16,2,16,1024]{3,2,1,0:T(8,128)(2,1)S(1)} async-done(((bf16[16,2,16,1024]{3,2,1,0:T(8,128)(2,1)}), bf16[16,2,16,1024]{3,2,1,0:T(8,128)(2,1)S(1)}, u32[]{:S(2)}, u32[]{:S(2)}) %all-to-all-start.2) | async-done | bytes 1048608 | tf_op jit(solution)/shard_map/all_to_all | solution.py:121
  157.8 6.8 %all-to-all-start.6 = ((bf16[16,2,16,1024]{3,2,1,0:T(8,128)(2,1)}), bf16[16,2,16,1024]{3,2,1,0:T(8,128)(2,1)S(1)}, u32[]{:S(2)}, u32[]{:S(2)}) async-start(bf16[16,2,16,1024]{3,2,1,0:T(8,128)(2,1)} %bitcast.36), calls=%async_computation.6 | async-start | bytes 2097152 | tf_op jit(solution)/shard_map/all_to_all | solution.py:121
  179.7 7.8 %all-to-all-done.6 = bf16[16,2,16,1024]{3,2,1,0:T(8,128)(2,1)S(1)} async-done(((bf16[16,2,16,1024]{3,2,1,0:T(8,128)(2,1)}), bf16[16,2,16,1024]{3,2,1,0:T(8,128)(2,1)S(1)}, u32[]{:S(2)}, u32[]{:S(2)}) %all-to-all-start.6) | async-done | bytes 1048608 | tf_op jit(solution)/shard_map/all_to_all | solution.py:121
  187.5 6.9 %all-to-all-start.3 = ((bf16[16,2,256]{2,1,0:T(2,128)(2,1)}), bf16[16,2,256]{2,1,0:T(2,128)(2,1)S(1)}, u32[]{:S(2)}, u32[]{:S(2)}) async-start(bf16[16,2,256]{2,1,0:T(2,128)(2,1)} %reshape.1051), calls=%async_computation.3 | async-start | bytes 32768 | tf_op jit(solution)/shard_map/all_to_all | solution.py:130
  198.3 2.6 all-to-all-done.3
  200.9 3.7 %all-to-all-start.7 = ((bf16[16,2,256]{2,1,0:T(2,128)(2,1)}), bf16[16,2,256]{2,1,0:T(2,128)(2,1)S(1)}, u32[]{:S(2)}, u32[]{:S(2)}) async-start(bf16[16,2,256]{2,1,0:T(2,128)(2,1)} %reshape.1049), calls=%async_computation.7 | async-start | bytes 32768 | tf_op jit(solution)/shard_map/all_to_all | solution.py:130
  204.6 4.6 %fusion.38 = f32[16,8192]{1,0:T(8,128)S(1)} fusion(bf16[512,8192]{1,0:T(8,128)(2,1)} %param.15, bf16[16,1,512]{2,1,0:T(2,128)(2,1)S(1)} %reshape.1052), kind=kOutput, calls=%fused_computation.84 | convolution fusion | flops 134217728 | bytes 8929280 | tf_op jit(solution)/shard_map/dot_general | solution.py:132
  210.9 4.6 %fusion.35 = f32[16,8192]{1,0:T(8,128)S(1)} fusion(bf16[512,8192]{1,0:T(8,128)(2,1)} %param.15, bf16[16,1,512]{2,1,0:T(2,128)(2,1)S(1)} %reshape.1050), kind=kOutput, calls=%fused_computation.81 | convolution fusion | flops 134217728 | bytes 8929280 | tf_op jit(solution)/shard_map/dot_general | solution.py:132
  215.5 71.7 %all-reduce.4 = (bf16[16,8192]{1,0:T(8,128)(2,1)S(1)}, bf16[16,8192]{1,0:T(8,128)(2,1)S(1)}) all-reduce(f32[16,8192]{1,0:T(8,128)S(1)} %fusion.35, f32[16,8192]{1,0:T(8,128)S(1)} %fusion.38), channel_id=5, replica_groups=mesh['groups'=2,'session'=16] {'session'}, use_global_device_ids=true, to_apply=%region_11.12.clone | all-reduce | flops 262144 | bytes 1572864
  (141 shorter events, 61.4 us)
Async XLA Ops:
  0.0 124.7 %copy-start = (bf16[32,16,1024]{2,1,0:T(8,128)(2,1)S(1)}, bf16[32,16,1024]{2,1,0:T(8,128)(2,1)}, u32[]{:S(2)}) copy-start(bf16[32,16,1024]{2,1,0:T(8,128)(2,1)} %param.18) | copy-start | bytes 3145732
  0.0 57.2 %copy-start.1 = (bf16[8192,128]{1,0:T(8,128)(2,1)S(1)}, bf16[8192,128]{1,0:T(8,128)(2,1)}, u32[]{:S(2)}) copy-start(bf16[8192,128]{1,0:T(8,128)(2,1)} %param.14) | copy-start | bytes 6291460
  2.0 12.0 %copy-start.8 = (s32[1024]{0:T(1024)}, s32[1024]{0:T(1024)S(1)}, u32[]{:S(2)}) copy-start(s32[1024]{0:T(1024)S(1)} %pad_clamp_fusion.3) | copy-start | bytes 12292
  4.2 97.2 %all-to-all-start.1 = ((s32[16,1,2]{2,1,0:T(1,128)}), s32[16,1,2]{2,1,0:T(1,128)S(1)}, u32[]{:S(2)}, u32[]{:S(2)}) async-start(s32[16,1,2]{2,1,0:T(1,128)} %copy.114), calls=%async_computation.1 | async-start | bytes 16384 | tf_op jit(solution)/shard_map/all_to_all | solution.py:118
  58.7 8.6 %copy-start.10 = (s32[16]{0:T(128)S(1)}, s32[16]{0:T(128)}, u32[]{:S(2)}) copy-start(s32[16]{0:T(128)} %get-tuple-element.36) | copy-start | bytes 196
  58.7 8.6 %copy-start.11 = (s32[16]{0:T(128)S(1)}, s32[16]{0:T(128)}, u32[]{:S(2)}) copy-start(s32[16]{0:T(128)} %get-tuple-element.39) | copy-start | bytes 196
  58.7 9.3 %copy-start.15 = (s32[16]{0:T(128)S(1)}, s32[16]{0:T(128)}, u32[]{:S(2)}) copy-start(s32[16]{0:T(128)} %get-tuple-element.48) | copy-start | bytes 196
  58.7 9.9 %copy-start.16 = (s32[16]{0:T(128)S(1)}, s32[16]{0:T(128)}, u32[]{:S(2)}) copy-start(s32[16]{0:T(128)} %get-tuple-element.38) | copy-start | bytes 196
  58.7 10.4 %copy-start.2 = (bf16[1,160,1024]{2,1,0:T(8,128)(2,1)S(1)}, bf16[1,160,1024]{2,1,0:T(8,128)(2,1)}, u32[]{:S(2)}) copy-start(bf16[1,160,1024]{2,1,0:T(8,128)(2,1)} %param.17) | copy-start | bytes 983044
  69.5 27.8 %copy-start.12 = (f32[256]{0:T(256)S(1)}, f32[256]{0:T(256)}, u32[]{:S(2)}) copy-start(f32[256]{0:T(256)} %convert_element_type.169) | copy-start | bytes 3076
  69.5 27.8 %copy-start.13 = (f32[256]{0:T(256)S(1)}, f32[256]{0:T(256)}, u32[]{:S(2)}) copy-start(f32[256]{0:T(256)} %convert_element_type.184) | copy-start | bytes 3076
  69.5 27.8 %copy-start.14 = (f32[64]{0:T(128)S(1)}, f32[64]{0:T(128)}, u32[]{:S(2)}) copy-start(f32[64]{0:T(128)} %multiply_exponential_fusion) | copy-start | bytes 772
  91.8 7.5 %copy-start.6 = (pred[16,16]{1,0:T(8,128)(4,1)S(1)}, pred[16,16]{1,0:T(8,128)(4,1)}, u32[]{:S(2)}) copy-start(pred[16,16]{1,0:T(8,128)(4,1)} %iota_compare_fusion) | copy-start | bytes 772
  91.8 7.5 %copy-start.17 = (s32[16]{0:T(128)S(1)}, s32[16]{0:T(128)}, u32[]{:S(2)}) copy-start(s32[16]{0:T(128)} %get-tuple-element.49) | copy-start | bytes 196
  91.8 7.5 %copy-start.18 = (pred[16,2]{0,1:T(4,128)(4,1)S(1)}, pred[16,2]{0,1:T(4,128)(4,1)}, u32[]{:S(2)}) copy-start(pred[16,2]{0,1:T(4,128)(4,1)} %iota_compare_fusion.2) | copy-start | bytes 100
  101.4 9.9 %all-to-all-start.5 = ((s32[16,1,2]{2,1,0:T(1,128)}), s32[16,1,2]{2,1,0:T(1,128)S(1)}, u32[]{:S(2)}, u32[]{:S(2)}) async-start(s32[16,1,2]{2,1,0:T(1,128)} %copy.125), calls=%async_computation.5 | async-start | bytes 16384 | tf_op jit(solution)/shard_map/all_to_all | solution.py:118
  111.3 9.9 %all-to-all-start = ((bf16[16,2,320]{2,1,0:T(2,128)(2,1)}), bf16[16,2,320]{2,1,0:T(2,128)(2,1)S(1)}, u32[]{:S(2)}, u32[]{:S(2)}) async-start(bf16[16,2,320]{2,1,0:T(2,128)(2,1)} %reshape.1047), calls=%async_computation | async-start | bytes 49152 | tf_op jit(solution)/shard_map/all_to_all | solution.py:71
  121.2 10.0 %all-to-all-start.4 = ((bf16[16,2,320]{2,1,0:T(2,128)(2,1)}), bf16[16,2,320]{2,1,0:T(2,128)(2,1)S(1)}, u32[]{:S(2)}, u32[]{:S(2)}) async-start(bf16[16,2,320]{2,1,0:T(2,128)(2,1)} %reshape.1045), calls=%async_computation.4 | async-start | bytes 49152 | tf_op jit(solution)/shard_map/all_to_all | solution.py:71
  131.2 26.6 %all-to-all-start.2 = ((bf16[16,2,16,1024]{3,2,1,0:T(8,128)(2,1)}), bf16[16,2,16,1024]{3,2,1,0:T(8,128)(2,1)S(1)}, u32[]{:S(2)}, u32[]{:S(2)}) async-start(bf16[16,2,16,1024]{3,2,1,0:T(8,128)(2,1)} %bitcast.18), calls=%async_computation.2 | async-start | bytes 2097152 | tf_op jit(solution)/shard_map/all_to_all | solution.py:121
  143.9 13.9 %copy-start.5 = (bf16[8,8,64]{2,1,0:T(8,128)(2,1)}, bf16[8,8,64]{2,1,0:T(8,128)(2,1)S(1)}, u32[]{:S(2)}) copy-start(bf16[8,8,64]{2,1,0:T(8,128)(2,1)S(1)} %get-tuple-element.16) | copy-start | bytes 24580
  143.9 20.7 %copy-start.4 = (bf16[8,8,64]{2,1,0:T(8,128)(2,1)}, bf16[8,8,64]{2,1,0:T(8,128)(2,1)S(1)}, u32[]{:S(2)}) copy-start(bf16[8,8,64]{2,1,0:T(8,128)(2,1)S(1)} %get-tuple-element.15) | copy-start | bytes 24580
  157.8 29.8 %all-to-all-start.6 = ((bf16[16,2,16,1024]{3,2,1,0:T(8,128)(2,1)}), bf16[16,2,16,1024]{3,2,1,0:T(8,128)(2,1)S(1)}, u32[]{:S(2)}, u32[]{:S(2)}) async-start(bf16[16,2,16,1024]{3,2,1,0:T(8,128)(2,1)} %bitcast.36), calls=%async_computation.6 | async-start | bytes 2097152 | tf_op jit(solution)/shard_map/all_to_all | solution.py:121
  187.5 13.4 %all-to-all-start.3 = ((bf16[16,2,256]{2,1,0:T(2,128)(2,1)}), bf16[16,2,256]{2,1,0:T(2,128)(2,1)S(1)}, u32[]{:S(2)}, u32[]{:S(2)}) async-start(bf16[16,2,256]{2,1,0:T(2,128)(2,1)} %reshape.1051), calls=%async_computation.3 | async-start | bytes 32768 | tf_op jit(solution)/shard_map/all_to_all | solution.py:130
  200.9 10.0 %all-to-all-start.7 = ((bf16[16,2,256]{2,1,0:T(2,128)(2,1)}), bf16[16,2,256]{2,1,0:T(2,128)(2,1)S(1)}, u32[]{:S(2)}, u32[]{:S(2)}) async-start(bf16[16,2,256]{2,1,0:T(2,128)(2,1)} %reshape.1049), calls=%async_computation.7 | async-start | bytes 32768 | tf_op jit(solution)/shard_map/all_to_all | solution.py:130
  (3 other events, 4.0 us)
where the time goes:
time: 291 us; the launch traced here: 289 us
  blocking collectives  115 us (40%)
  waiting for transfers between devices  41.7 us (14%)
  starting transfers between devices  38.8 us (13%)
  local copies, waits for them, and re-layouts  38.5 us (13%)
  matrix products  29.1 us (10%)
  other arithmetic  23.2 us (8%)
    unnamed x1, blocking collectives  71.7 us
    all_gather x2, blocking collectives, local(): lax.all_gather(normed, 'session', axis=0, tiled=True)  43.7 us
    all_to_all x2, waiting for transfers between devices, local(): lax.all_to_all(stored_pages, 'session', split_axis=0, concat_axis=0, tile...  19.8 us
    unnamed x53, local copies, waits for them, and re-layouts  14.4 us
    all_to_all x2, waiting for transfers between devices, local(): lax.all_to_all(projected, 'session', split_axis=0, concat_axis=0, tiled=T...  11.2 us
    dot_general x2, matrix products, local(): jnp.dot(lax.all_gather(normed, 'session', axis=0, tiled=True), joined_wei...  10.9 us
    all_to_all x2, starting transfers between devices, local(): lax.all_to_all(requests, 'session', split_axis=0, concat_axis=0, tiled=True)  10.8 us
    all_to_all x2, starting transfers between devices, local(): lax.all_to_all(head_output, 'session', split_axis=0, concat_axis=0, tiled...  10.5 us
  transfers between devices with their start and end apart: 8, of which 7 were waited for; matrix products, arithmetic and copies ran while one was open for 27% of the time, Pallas kernels for 0%

commit v1 on v0

v1 whole, which is shorter than its diff:
```python
import functools
import math

import jax
import jax.numpy as jnp
from jax import lax
from jax.experimental import pallas as pl
from jax.experimental.pallas import tpu as pltpu
from jax.sharding import PartitionSpec as P

HEADS = 64
KV_HEADS = 8
HEAD_DIM = 128
STEPS = 2
GROUP = HEADS // KV_HEADS
LANES = 128
AXIS = "session"
VMEM = pltpu.VMEM
SMEM = pltpu.SMEM
F32 = jnp.float32
BF16 = jnp.bfloat16


def angles(positions):
    half = HEAD_DIM // 2
    frequency = jnp.exp(
        -jnp.arange(half, dtype=F32) * (2.0 * math.log(500000.0) / HEAD_DIM)
    )
    return positions[..., None] * frequency


def turn_tables(positions):
    angle = angles(positions)
    cosine, sine = jnp.cos(angle), jnp.sin(angle)
    return (
        jnp.concatenate([cosine, cosine], axis=-1),
        jnp.concatenate([-sine, sine], axis=-1),
    )


def whole(space=VMEM):
    return pl.BlockSpec(memory_space=space)


def keys_kernel(factors_ref, basis_ref, cos_ref, sin_ref, out_ref):
    product = jnp.dot(factors_ref[...], basis_ref[...], preferred_element_type=F32)
    cosine, sine = cos_ref[...], sin_ref[...]
    for head in range(KV_HEADS):
        lanes = slice(head * HEAD_DIM, (head + 1) * HEAD_DIM)
        part = product[:, lanes]
        turned = part * cosine + pltpu.roll(part, HEAD_DIM // 2, 1) * sine
        out_ref[:, lanes] = turned.astype(BF16)


def make_keys(factors, basis, cosine, sine):
    seq, rank = factors.shape
    width = basis.shape[1]
    rows = min(seq, 512)
    return pl.pallas_call(
        keys_kernel,
        grid=(seq // rows,),
        in_specs=[
            pl.BlockSpec((rows, rank), lambda i: (i, 0)),
            pl.BlockSpec((rank, width), lambda i: (0, 0)),
            pl.BlockSpec((rows, HEAD_DIM), lambda i: (i, 0)),
            pl.BlockSpec((rows, HEAD_DIM), lambda i: (i, 0)),
        ],
        out_specs=pl.BlockSpec((rows, width), lambda i: (i, 0)),
        out_shape=jax.ShapeDtypeStruct((seq, width), BF16),
        compiler_params=pltpu.CompilerParams(vmem_limit_bytes=32 * 2**20),
        cost_estimate=pl.CostEstimate(
            flops=2 * seq * rank * width, bytes_accessed=4 * seq * width, transcendentals=0
        ),
        name="turned_keys",
    )(factors, basis, cosine, sine)


def project_kernel(
    order, fast, me_ref, first_ref, second_ref, gain_ref, wq_ref, wk_ref, out_ref,
    x_scr, lhs_scr, wq_buf, wk_buf, out_scr, sems,
):
    depth, q_cols = wq_ref.shape
    k_cols = wk_ref.shape[1]
    chunks = wq_buf.shape[0]
    span = depth // chunks
    pieces = depth // LANES
    copies = []
    for i in range(chunks):
        rows = pl.ds(i * span, span)
        pair = (
            pltpu.make_async_copy(wq_ref.at[rows, :], wq_buf.at[i], sems.at[0, i]),
            pltpu.make_async_copy(wk_ref.at[rows, :], wk_buf.at[i], sems.at[1, i]),
        )
        for copy in pair:
            copy.start()
        copies.append(pair)
    half = first_ref.shape[0]
    x_scr[:half] = first_ref[...].astype(F32)
    x_scr[half:] = second_ref[...].astype(F32)
    count = 2 * half // pieces
    squares = jnp.zeros((count, LANES), F32)
    for c in range(pieces):
        part = x_scr[pl.ds(c, count, stride=pieces), :]
        squares = squares + part * part
    scale = lax.rsqrt(jnp.sum(squares, axis=1, keepdims=True) * (1.0 / depth) + 1e-05)
    for c in range(pieces):
        part = x_scr[pl.ds(c, count, stride=pieces), :]
        gain = gain_ref[pl.ds(c, 1), :].astype(F32)
        lhs_scr[:, c * LANES : (c + 1) * LANES] = (part * scale * gain).astype(BF16)
    q_sum = jnp.zeros((count, q_cols), F32)
    k_sum = jnp.zeros((count, k_cols), F32)
    for i in range(chunks):
        for copy in copies[i]:
            copy.wait()
        lhs = lhs_scr[:, i * span : (i + 1) * span]
        q_sum = q_sum + jnp.dot(lhs, wq_buf[i], preferred_element_type=F32)
        k_sum = k_sum + jnp.dot(lhs, wk_buf[i], preferred_element_type=F32)
    if not fast:
        out_ref[:, :q_cols] = q_sum.astype(BF16)
        out_ref[:, q_cols:] = k_sum.astype(BF16)
        return
    me = me_ref[0]
    per = q_cols // LANES
    out_scr[...] = jnp.zeros_like(out_scr)
    for j, other in enumerate(order):
        target = jnp.bitwise_xor(me, other)
        for step in range(STEPS):
            row = j * STEPS + step
            for c in range(per):
                out_scr[target, pl.ds(step * per + c, 1), :] = q_sum[
                    row : row + 1, c * LANES : (c + 1) * LANES
                ]
            out_scr[target, pl.ds(STEPS * per + step, 1), :] = k_sum[row : row + 1, :]
    out_ref[...] = out_scr[...].astype(BF16)


def project(me, first, second, gain, query_weight, kv_weight, order, fast):
    depth, q_cols = query_weight.shape
    k_cols = kv_weight.shape[1]
    pieces = depth // LANES
    rows = 2 * first.shape[0] // pieces
    devices = rows // STEPS
    chunks = 8
    span = depth // chunks
    shape = (devices, 16, LANES) if fast else (rows, q_cols + k_cols)
    return pl.pallas_call(
        functools.partial(project_kernel, order, fast),
        in_specs=[whole(SMEM), whole(), whole(), whole(), whole(pl.ANY), whole(pl.ANY)],
        out_specs=whole(),
        out_shape=jax.ShapeDtypeStruct(shape, BF16),
        scratch_shapes=[
            VMEM((rows * pieces, LANES), F32),
            VMEM((rows, depth), BF16),
            VMEM((chunks, span, q_cols), BF16),
            VMEM((chunks, span, k_cols), BF16),
            VMEM((devices, 16, LANES) if fast else (8, LANES), F32),
            pltpu.SemaphoreType.DMA((2, chunks)),
        ],
        compiler_params=pltpu.CompilerParams(vmem_limit_bytes=48 * 2**20),
        cost_estimate=pl.CostEstimate(
            flops=2 * rows * depth * (q_cols + k_cols),
            bytes_accessed=2 * depth * (q_cols + k_cols),
            transcendentals=0,
        ),
        name="norm_project",
    )(me, first, second, gain, query_weight, kv_weight)


def attend_kernel(
    holder_ref, columns_ref, keys_ref, bias_ref, cos_ref, sin_ref, pages_ref, out_ref, values_scr
):
    seq = keys_ref.shape[0]
    pairs, pair_rows = pages_ref.shape[0], pages_ref.shape[1]
    score_scale = 1.0 / math.sqrt(HEAD_DIM)
    half = HEAD_DIM // 2
    rows = 2 * GROUP
    for m in range(pairs):
        values_scr[m * pair_rows : (m + 1) * pair_rows, :] = pages_ref[holder_ref[m]]
    columns = columns_ref[...].astype(F32)
    count = columns.shape[0]
    query = columns[:, :8, :].reshape(count * 8, HEAD_DIM)
    fresh = columns[:, 8:, :]
    row_step = lax.rem(lax.broadcasted_iota(jnp.int32, (count * 8, 1), 0) // 4, STEPS)
    later = row_step == 1
    cosine = jnp.where(later, cos_ref[1:2, :], cos_ref[0:1, :])
    sine = jnp.where(later, sin_ref[1:2, :], sin_ref[0:1, :])
    turned = (query * cosine + pltpu.roll(query, half, 1) * sine).astype(BF16)
    turned_wide = turned.astype(F32)
    step_later = later[:rows]
    bias = jnp.where(step_later, bias_ref[1:2, :], bias_ref[0:1, :])
    new_keys = []
    for step in range(STEPS):
        part = fresh[:KV_HEADS, step, :]
        new = part * cos_ref[step : step + 1, :] + pltpu.roll(part, half, 1) * sin_ref[step : step + 1, :]
        new_keys.append(new.astype(BF16).astype(F32))
    for head in range(KV_HEADS):
        lanes = slice(head * HEAD_DIM, (head + 1) * HEAD_DIM)
        mine = slice(head * rows, (head + 1) * rows)
        scores = (
            lax.dot_general(
                turned[mine], keys_ref[:, lanes], (((1,), (1,)), ((), ())),
                preferred_element_type=F32,
            )
            * score_scale
            + bias
        )
        recent0 = (
            jnp.sum(turned_wide[mine] * new_keys[0][head : head + 1, :], axis=1, keepdims=True)
            * score_scale
        )
        recent1 = (
            jnp.sum(turned_wide[mine] * new_keys[1][head : head + 1, :], axis=1, keepdims=True)
            * score_scale
        )
        recent1 = jnp.where(step_later, recent1, -1e30)
        largest = jnp.maximum(
            jnp.max(scores, axis=1, keepdims=True), jnp.maximum(recent0, recent1)
        )
        cache_exp = jnp.exp(scores - largest)
        exp0 = jnp.exp(recent0 - largest)
        exp1 = jnp.exp(recent1 - largest)
        denominator = jnp.sum(cache_exp, axis=1, keepdims=True) + (exp0 + exp1)
        weights = (cache_exp / denominator).astype(BF16)
        weight0 = (exp0 / denominator).astype(BF16).astype(F32)
        weight1 = (exp1 / denominator).astype(BF16).astype(F32)
        mixed = jnp.dot(weights, values_scr[:, lanes], preferred_element_type=F32)
        mixed = mixed + weight0 * fresh[KV_HEADS + head, 0:1, :]
        mixed = mixed + weight1 * fresh[KV_HEADS + head, 1:2, :]
        out_ref[mine, :] = mixed.astype(BF16)


def attend(holder, columns, keys, bias, cosine, sine, pages):
    seq, width = keys.shape
    return pl.pallas_call(
        attend_kernel,
        in_specs=[whole(SMEM)] + [whole()] * 6,
        out_specs=whole(),
        out_shape=jax.ShapeDtypeStruct((STEPS * HEADS, HEAD_DIM), BF16),
        scratch_shapes=[VMEM((seq, width), BF16)],
        compiler_params=pltpu.CompilerParams(vmem_limit_bytes=48 * 2**20),
        cost_estimate=pl.CostEstimate(
            flops=4 * STEPS * HEADS * seq * HEAD_DIM,
            bytes_accessed=4 * seq * width,
            transcendentals=STEPS * HEADS * seq,
        ),
        name="attend",
    )(holder, columns, keys, bias, cosine, sine, pages)


def output_kernel(lhs_ref, weight_ref, out_ref, weight_buf, out_scr, sems):
    chunks, _, span = weight_buf.shape
    rows = lhs_ref.shape[0]
    pieces = chunks * span // LANES
    copies = []
    for i in range(chunks):
        copy = pltpu.make_async_copy(
            weight_ref.at[:, pl.ds(i * span, span)], weight_buf.at[i], sems.at[i]
        )
        copy.start()
        copies.append(copy)
    lhs = lhs_ref[...]
    for i in range(chunks):
        copies[i].wait()
        part = jnp.dot(lhs, weight_buf[i], preferred_element_type=F32)
        for c in range(span // LANES):
            out_scr[pl.ds(i * (span // LANES) + c, rows, stride=pieces), :] = part[
                :, c * LANES : (c + 1) * LANES
            ]
    out_ref[...] = out_scr[...].astype(BF16)


def output(lhs, weight):
    rows, depth = lhs.shape
    width = weight.shape[1]
    chunks = 8
    return pl.pallas_call(
        output_kernel,
        in_specs=[whole(), whole(pl.ANY)],
        out_specs=whole(),
        out_shape=jax.ShapeDtypeStruct((rows * width // LANES, LANES), BF16),
        scratch_shapes=[
            VMEM((chunks, depth, width // chunks), BF16),
            VMEM((rows * width // LANES, LANES), F32),
            pltpu.SemaphoreType.DMA((chunks,)),
        ],
        compiler_params=pltpu.CompilerParams(vmem_limit_bytes=48 * 2**20),
        cost_estimate=pl.CostEstimate(
            flops=2 * rows * depth * width, bytes_accessed=2 * depth * width, transcendentals=0
        ),
        name="output_project",
    )(lhs, weight)


def exchange(blocks):
    return lax.all_to_all(blocks, AXIS, split_axis=0, concat_axis=0, tiled=True)


def local(
    hidden,
    norm_gain,
    query_weight,
    kv_weight,
    out_weight,
    key_factors,
    key_basis,
    value_store,
    lengths,
    block_slot,
    selection,
):
    devices = lax.axis_size(AXIS)
    me = lax.axis_index(AXIS)
    slots_dev, block_len, width = value_store.shape
    seq = key_factors.shape[1]
    pages = block_slot.shape[1]
    model = hidden.shape[2]
    q_cols = query_weight.shape[1]
    k_cols = kv_weight.shape[1]
    fast = q_cols == 4 * HEAD_DIM and k_cols == HEAD_DIM
    pieces = model // LANES

    slots = block_slot[0].reshape(pages // 2, 2)
    holder = slots[:, 0] // slots_dev
    here = holder[None, :] == jnp.arange(devices, dtype=jnp.int32)[:, None]
    asked = jnp.sum(jnp.where(here[:, :, None], (slots % slots_dev)[None], 0), axis=1)
    asked_here = exchange(asked[:, None, :])
    sent_pages = value_store[asked_here.reshape(-1)]
    fetched = exchange(sent_pages.reshape(devices, 2 * block_len, width))

    block = hidden[:, 0].reshape(1, STEPS * pieces, LANES)
    order = [0]
    bit = devices // 2
    while bit:
        links = [(i, i ^ bit) for i in range(devices)]
        other = lax.ppermute(block, AXIS, links)
        order = order + [k ^ bit for k in order]
        bit //= 2
        if bit:
            block = jnp.concatenate([block, other], axis=0)
    columns = project(
        me.astype(jnp.int32).reshape(1),
        block.reshape(-1, LANES),
        other.reshape(-1, LANES),
        norm_gain.reshape(pieces, LANES),
        query_weight,
        kv_weight,
        tuple(order),
        fast,
    )
    if fast:
        columns = exchange(columns)
    else:
        places = jnp.bitwise_xor(me, jnp.array(order, dtype=jnp.int32))
        columns = exchange(columns.reshape(devices, STEPS, q_cols + k_cols)[places])
        query = columns[:, :, :q_cols].transpose(1, 0, 2).reshape(STEPS, HEADS // 4, 4, HEAD_DIM)
        query = query.transpose(1, 0, 2, 3).reshape(HEADS // 4, 8, HEAD_DIM)
        fresh = columns[:, :, q_cols:].transpose(1, 0, 2).reshape(STEPS, HEADS // 4, HEAD_DIM)
        fresh = jnp.pad(fresh.transpose(1, 0, 2), ((0, 0), (0, 8 - STEPS), (0, 0)))
        columns = jnp.concatenate([query, fresh], axis=1)

    cosine, sine = turn_tables(jnp.arange(seq, dtype=jnp.int32).astype(F32))
    keys = make_keys(key_factors[0], key_basis[0], cosine, sine)
    picked = jnp.any(
        selection[:, 0, :, None] == jnp.arange(pages, dtype=jnp.int32)[None, None, :], axis=1
    )
    usable = jnp.repeat(picked, block_len, axis=1) & (
        jnp.arange(seq, dtype=jnp.int32)[None, :] < lengths[0]
    )
    bias = jnp.where(usable, 0.0, -1e30).astype(F32)
    new_cos, new_sin = turn_tables(
        (lengths[0] + jnp.arange(STEPS, dtype=jnp.int32)).astype(F32)
    )
    heads = attend(holder, columns, keys, bias, new_cos, new_sin, fetched)

    if fast:
        rows = exchange(heads.reshape(devices, STEPS * 4, HEAD_DIM))
        lhs = rows.reshape(devices, STEPS, 4 * HEAD_DIM).reshape(devices * STEPS, 4 * HEAD_DIM)
    else:
        flat = heads.reshape(HEADS // 4, STEPS, 4 * HEAD_DIM).transpose(1, 0, 2)
        flat = flat.reshape(STEPS, devices, model // devices).transpose(1, 0, 2)
        lhs = exchange(flat).reshape(devices * STEPS, model // devices)
    partial = output(lhs, out_weight)
    arrived = exchange(partial.reshape(devices, STEPS * pieces, LANES))
    total = jnp.sum(arrived.astype(F32), axis=0).astype(BF16)
    return total.reshape(STEPS, 1, model)


def solution(mesh):
    return jax.shard_map(
        local,
        mesh=mesh,
        in_specs=(
            P(None, ("groups", "session"), None),
            P(),
            P(None, "session"),
            P(None, "session"),
            P("session", None),
            P(("groups", "session"), None, None),
            P(("groups", "session"), None, None),
            P(("groups", "session"), None, None),
            P(("groups", "session")),
            P(("groups", "session"), None),
            P(None, ("groups", "session"), None),
        ),
        out_specs=P(None, ("groups", "session"), None),
        check_vma=False,
    )
```

time: 291 us -> 114 us (0.39)
  blocking collectives: 115 us -> 30.3 us
  local copies, waits for them, and re-layouts: 38.5 us -> 8.36 us
  matrix products: 29.1 us -> 0 us
  other arithmetic: 23.2 us -> 3.67 us
  starting transfers between devices: 38.8 us -> 20.9 us
  Pallas kernels: 0 us -> 13 us
  waiting for transfers between devices: 41.7 us -> 36.2 us
    unnamed x1 -> x0, blocking collectives: 71.7 us -> none
    all_gather x2 -> x0, blocking collectives: 43.7 us -> none  [local(): lax.all_gather(normed, 'session', axis=0, tiled=True)]
    all_to_all x0 -> x2, blocking collectives: none -> 30.3 us  [exchange(): return lax.all_to_all(blocks, AXIS, split_axis=0, concat_axis=0, tiled=True)]
    dot_general x13 -> x0, matrix products: 29.1 us -> none  [the longest x2 10.9 us: local(): jnp.dot(lax.all_gather(normed, 'session', axis=0, tiled=True), joined_wei...]
    all_to_all x8 -> x3, starting transfers between devices: 38.8 us -> 13.4 us  [exchange(): return lax.all_to_all(blocks, AXIS, split_axis=0, concat_axis=0, tiled=True)]
    pallas_call x0 -> x4, Pallas kernels: none -> 13 us  [the longest x1 4.97 us: project(): pl.pallas_call(functools.partial(project_kernel, order, fast), in_specs=[...]
    all_to_all x8 -> x3, waiting for transfers between devices: 41.7 us -> 30.2 us  [exchange(): return lax.all_to_all(blocks, AXIS, split_axis=0, concat_axis=0, tiled=True)]
    unnamed x53 -> x17, local copies, waits for them, and re-layouts: 14.4 us -> 3.98 us
  transfers between devices with their start and end apart: 8 -> 7, of which waited for: 7 -> 6; matrix products, arithmetic and copies ran while one was open for 27% -> 6% of each run, Pallas kernels for 0% -> 1%
where the time goes in v1:
time: 114 us; the launch traced here: 113 us
  waiting for transfers between devices  36.2 us (32%)
  blocking collectives  30.3 us (27%)
  starting transfers between devices  20.9 us (18%)
  Pallas kernels  13 us (11%)
  local copies, waits for them, and re-layouts  8.36 us (7%)
  other arithmetic  3.67 us (3%)
    all_to_all x2, blocking collectives, exchange(): return lax.all_to_all(blocks, AXIS, split_axis=0, concat_axis=0, tiled=True)  30.3 us
    all_to_all x3, waiting for transfers between devices, exchange(): return lax.all_to_all(blocks, AXIS, split_axis=0, concat_axis=0, tiled=True)  30.2 us
    all_to_all x3, starting transfers between devices, exchange(): return lax.all_to_all(blocks, AXIS, split_axis=0, concat_axis=0, tiled=True)  13.4 us
    ppermute x4, starting transfers between devices, local(): other = lax.ppermute(block, AXIS, links)  7.56 us
    ppermute x4, waiting for transfers between devices, local(): other = lax.ppermute(block, AXIS, links)  6.06 us
    pallas_call x1, Pallas kernels, project(): pl.pallas_call(functools.partial(project_kernel, order, fast), in_specs=[...  4.97 us
    unnamed x17, local copies, waits for them, and re-layouts  3.98 us
    pallas_call x1, Pallas kernels, output(): pl.pallas_call(output_kernel, in_specs=[whole(), whole(pl.ANY)], out_spec...  3.95 us
  transfers between devices with their start and end apart: 7, of which 6 were waited for; matrix products, arithmetic and copies ran while one was open for 6% of the time, Pallas kernels for 1%

profile of v1, /device:TPU:0, one launch (start us, length us, event | category | flops | bytes accessed | tf_op | source)
XLA Modules:
  0.0 113.4 jit_solution(2032244761502270615)
XLA Ops:
  0.0 0.9 reshape_squeeze.7
  0.9 4.1 %collective-permute-start = (bf16[1,128,128]{2,1,0:T(8,128)(2,1)S(1)}, bf16[1,128,128]{2,1,0:T(8,128)(2,1)S(1)}, u32[]{:S(2)}, u32[]{:S(2)}) collective-permute-start(bf16[1,128,128]{2,1,0:T(8,128)(2,1)S(1)} %reshape_squeeze.7), channel_id=1, source_target_pairs={{0,8},{1,9},{2,10},{3,11},{4,12},{5,13},{6,14},{7,15},{8,0},{9,1},... | collective-permute-start | bytes 98312 | tf_op jit(solution)/shard_map/ppermute | solution.py:335
  5.5 1.3 %reduce.9 = s32[32]{0:T(128)S(1)} reduce(s32[1,32]{1,0:T(1,128)} %param.20, s32[]{:T(128)} %broadcast.118), dimensions={0}, to_apply=%param.20.reduce_sub_computation.3 | reduce | bytes 260 | tf_op args[9]
  7.3 1.6 %collective-permute-start.1 = (bf16[2,128,128]{2,1,0:T(8,128)(2,1)S(1)}, bf16[2,128,128]{2,1,0:T(8,128)(2,1)S(1)}, u32[]{:S(2)}, u32[]{:S(2)}) collective-permute-start(bf16[2,128,128]{2,1,0:T(8,128)(2,1)S(1)} %pad_maximum_fusion.3), channel_id=1, source_target_pairs={{0,4},{1,5},{2,6},{3,7},{4,0},{5,1},{6,2},{7,3},{8,12},{9,13},{10,... | collective-permute-start | bytes 196616 | tf_op jit(solution)/shard_map/ppermute | solution.py:335
  8.9 2.7 %collective-permute-done.1 = bf16[2,128,128]{2,1,0:T(8,128)(2,1)S(1)} collective-permute-done((bf16[2,128,128]{2,1,0:T(8,128)(2,1)S(1)}, bf16[2,128,128]{2,1,0:T(8,128)(2,1)S(1)}, u32[]{:S(2)}, u32[]{:S(2)}) %collective-permute-start.1) | collective-permute-done | bytes 65568 | tf_op jit(solution)/shard_map/ppermute | solution.py:335
  11.6 1.8 %collective-permute-start.2 = (bf16[4,128,128]{2,1,0:T(8,128)(2,1)S(1)}, bf16[4,128,128]{2,1,0:T(8,128)(2,1)S(1)}, u32[]{:S(2)}, u32[]{:S(2)}) collective-permute-start(bf16[4,128,128]{2,1,0:T(8,128)(2,1)S(1)} %pad_maximum_fusion.2), channel_id=1, source_target_pairs={{0,2},{1,3},{2,0},{3,1},{4,6},{5,7},{6,4},{7,5},{8,10},{9,11},{10,... | collective-permute-start | bytes 393224 | tf_op jit(solution)/shard_map/ppermute | solution.py:335
  13.4 3.2 %collective-permute-done.2 = bf16[4,128,128]{2,1,0:T(8,128)(2,1)S(1)} collective-permute-done((bf16[4,128,128]{2,1,0:T(8,128)(2,1)S(1)}, bf16[4,128,128]{2,1,0:T(8,128)(2,1)S(1)}, u32[]{:S(2)}, u32[]{:S(2)}) %collective-permute-start.2) | collective-permute-done | bytes 131104 | tf_op jit(solution)/shard_map/ppermute | solution.py:335
  17.6 6.2 %all-to-all-start.1 = ((s32[16,1,2]{2,1,0:T(1,128)}), s32[16,1,2]{2,1,0:T(1,128)S(1)}, u32[]{:S(2)}, u32[]{:S(2)}) async-start(s32[16,1,2]{2,1,0:T(1,128)} %copy.20), calls=%async_computation.1 | async-start | bytes 16384 | tf_op jit(solution)/shard_map/all_to_all | solution.py:295
  23.8 6.3 %all-to-all-done.1 = s32[16,1,2]{2,1,0:T(1,128)S(1)} async-done(((s32[16,1,2]{2,1,0:T(1,128)}), s32[16,1,2]{2,1,0:T(1,128)S(1)}, u32[]{:S(2)}, u32[]{:S(2)}) %all-to-all-start.1) | async-done | bytes 160 | tf_op jit(solution)/shard_map/all_to_all | solution.py:295
  30.9 1.6 %copy-done.1 = bf16[8192,128]{1,0:T(8,128)(2,1)S(1)} copy-done((bf16[8192,128]{1,0:T(8,128)(2,1)S(1)}, bf16[8192,128]{1,0:T(8,128)(2,1)}, u32[]{:S(2)}) %copy-start.1) | copy-done | bytes 2097176
  32.5 0.7 copy-done.3
  33.2 5.0 %norm_project.1 = bf16[16,16,128]{2,1,0:T(8,128)(2,1)} custom-call(s32[1]{0:T(128)} %bitcast.me_ref, bf16[1024,128]{1,0:T(8,128)(2,1)S(1)} %bitcast.20, bf16[1024,128]{1,0:T(8,128)(2,1)S(1)} %bitcast.22, bf16[64,128]{1,0:T(8,128)(2,1)S(1)} %bitcast.24, bf16[8192,512]{1,0:T(8,128)(2,1)} %wq_ref.1, bf16[8192,128]{1,0:T(8,128)(2,1)S(1)} %copy-done.1), custom_call_target="tpu_custom_call" | custom-call | flops 335544320 | bytes 10485760 | tf_op jit(solution)/shard_map/norm_project/pallas_call | solution.py:146
  38.1 3.5 %all-to-all-start = ((bf16[16,16,128]{2,1,0:T(8,128)(2,1)}), bf16[16,16,128]{2,1,0:T(8,128)(2,1)S(1)}, u32[]{:S(2)}, u32[]{:S(2)}) async-start(bf16[16,16,128]{2,1,0:T(8,128)(2,1)} %norm_project.1), calls=%async_computation | async-start | bytes 131072 | tf_op jit(solution)/shard_map/all_to_all | solution.py:295
  41.7 1.6 %gather_fusion = bf16[32,16,1024]{2,1,0:T(8,128)(2,1)} fusion(bf16[32,16,1024]{2,1,0:T(8,128)(2,1)S(1)} %copy-done, s32[1024]{0:T(1024)S(1)} %pad_clamp_fusion), kind=kCustom, calls=%fused_computation | custom fusion | bytes 2097280 | tf_op jit(solution)/shard_map/gather | solution.py:327
  43.3 5.2 %all-to-all-done.columns_ref = bf16[16,16,128]{2,1,0:T(8,128)(2,1)S(1)} async-done(((bf16[16,16,128]{2,1,0:T(8,128)(2,1)}), bf16[16,16,128]{2,1,0:T(8,128)(2,1)S(1)}, u32[]{:S(2)}, u32[]{:S(2)}) %all-to-all-start) | async-done | bytes 65568 | tf_op jit(solution)/shard_map/all_to_all | solution.py:295
  48.5 3.7 %all-to-all-start.2 = ((bf16[16,32,1024]{2,1,0:T(8,128)(2,1)}), bf16[16,32,1024]{2,1,0:T(8,128)(2,1)S(1)}, u32[]{:S(2)}, u32[]{:S(2)}) async-start(bf16[16,32,1024]{2,1,0:T(8,128)(2,1)} %bitcast.10), calls=%async_computation.2 | async-start | bytes 2097152 | tf_op jit(solution)/shard_map/all_to_all | solution.py:295
  53.3 1.0 fusion
  54.5 1.0 copy-done.2
  55.5 0.8 turned_keys.1.keys_ref
  56.5 18.6 %all-to-all-done.2.pages_ref = bf16[16,32,1024]{2,1,0:T(8,128)(2,1)S(1)} async-done(((bf16[16,32,1024]{2,1,0:T(8,128)(2,1)}), bf16[16,32,1024]{2,1,0:T(8,128)(2,1)S(1)}, u32[]{:S(2)}, u32[]{:S(2)}) %all-to-all-start.2) | async-done | bytes 1048608 | tf_op jit(solution)/shard_map/all_to_all | solution.py:295
  75.1 3.3 %attend.1 = bf16[128,128]{1,0:T(8,128)(2,1)S(1)} custom-call(s32[16]{0:T(128)S(1)} %and_select_fusion.1.holder_ref, bf16[16,16,128]{2,1,0:T(8,128)(2,1)S(1)} %all-to-all-done.columns_ref, bf16[512,1024]{1,0:T(8,128)(2,1)S(1)} %turned_keys.1.keys_ref, f32[2,512]{1,0:T(2,128)S(1)} %and_select_fusion.bias_ref, f32[2,128]{1,0:T(2,128)S(1)} %get-tuple-element.13.cos_ref, ...), custom_call_target="tpu_custom_call" | custom-call | flops 33554432 | bytes 2097152 | tf_op jit(solution)/shard_map/attend/pallas_call | solution.py:234
  78.4 13.2 %all_to_all.25 = bf16[16,8,128]{2,1,0:T(8,128)(2,1)S(1)} all-to-all(bf16[16,8,128]{2,1,0:T(8,128)(2,1)S(1)} %bitcast.23), channel_id=1, replica_groups=mesh['groups'=2,'session'=16] {'session'}, dimensions={0} | all-to-all | bytes 65536 | tf_op jit(solution)/shard_map/all_to_all | solution.py:295
  91.7 3.9 %output_project.1 = bf16[2048,128]{1,0:T(8,128)(2,1)S(1)} custom-call(bf16[32,512]{1,0:T(8,128)(2,1)S(1)} %reshape_reshape.3.lhs_ref, bf16[512,8192]{1,0:T(8,128)(2,1)} %weight_ref.1), custom_call_target="tpu_custom_call" | custom-call | flops 268435456 | bytes 8388608 | tf_op jit(solution)/shard_map/output_project/pallas_call | solution.py:276
  95.6 17.1 %all_to_all.26 = bf16[16,128,128]{2,1,0:T(8,128)(2,1)S(1)} all-to-all(bf16[16,128,128]{2,1,0:T(8,128)(2,1)S(1)} %bitcast.18), channel_id=1, replica_groups=mesh['groups'=2,'session'=16] {'session'}, dimensions={0} | all-to-all | bytes 1048576 | tf_op jit(solution)/shard_map/all_to_all | solution.py:295
  (46 shorter events, 4.2 us)
Async XLA Ops:
  0.0 41.7 %copy-start = (bf16[32,16,1024]{2,1,0:T(8,128)(2,1)S(1)}, bf16[32,16,1024]{2,1,0:T(8,128)(2,1)}, u32[]{:S(2)}) copy-start(bf16[32,16,1024]{2,1,0:T(8,128)(2,1)} %param.18) | copy-start | bytes 3145732
  0.0 52.2 %copy-start.4 = (bf16[1,512,160]{1,2,0:T(8,128)(2,1)S(1)}, bf16[1,512,160]{1,2,0:T(8,128)(2,1)}, u32[]{:S(2)}) copy-start(bf16[1,512,160]{1,2,0:T(8,128)(2,1)} %param.16) | copy-start | bytes 491524
  0.9 6.3 %collective-permute-start = (bf16[1,128,128]{2,1,0:T(8,128)(2,1)S(1)}, bf16[1,128,128]{2,1,0:T(8,128)(2,1)S(1)}, u32[]{:S(2)}, u32[]{:S(2)}) collective-permute-start(bf16[1,128,128]{2,1,0:T(8,128)(2,1)S(1)} %reshape_squeeze.7), channel_id=1, source_target_pairs={{0,8},{1,9},{2,10},{3,11},{4,12},{5,13},{6,14},{7,15},{8,0},{9,1},... | collective-permute-start | bytes 98312 | tf_op jit(solution)/shard_map/ppermute | solution.py:335
  7.3 45.7 %copy-start.5 = (s32[2,1,16]{2,1,0:T(1,128)S(1)}, s32[2,1,16]{2,1,0:T(1,128)}, u32[]{:S(2)}) copy-start(s32[2,1,16]{2,1,0:T(1,128)} %param.21) | copy-start | bytes 388
  7.3 4.3 %collective-permute-start.1 = (bf16[2,128,128]{2,1,0:T(8,128)(2,1)S(1)}, bf16[2,128,128]{2,1,0:T(8,128)(2,1)S(1)}, u32[]{:S(2)}, u32[]{:S(2)}) collective-permute-start(bf16[2,128,128]{2,1,0:T(8,128)(2,1)S(1)} %pad_maximum_fusion.3), channel_id=1, source_target_pairs={{0,4},{1,5},{2,6},{3,7},{4,0},{5,1},{6,2},{7,3},{8,12},{9,13},{10,... | collective-permute-start | bytes 196616 | tf_op jit(solution)/shard_map/ppermute | solution.py:335
  11.6 5.0 %collective-permute-start.2 = (bf16[4,128,128]{2,1,0:T(8,128)(2,1)S(1)}, bf16[4,128,128]{2,1,0:T(8,128)(2,1)S(1)}, u32[]{:S(2)}, u32[]{:S(2)}) collective-permute-start(bf16[4,128,128]{2,1,0:T(8,128)(2,1)S(1)} %pad_maximum_fusion.2), channel_id=1, source_target_pairs={{0,2},{1,3},{2,0},{3,1},{4,6},{5,7},{6,4},{7,5},{8,10},{9,11},{10,... | collective-permute-start | bytes 393224 | tf_op jit(solution)/shard_map/ppermute | solution.py:335
  16.7 14.2 %collective-permute-start.3 = (bf16[8,128,128]{2,1,0:T(8,128)(2,1)S(1)}, bf16[8,128,128]{2,1,0:T(8,128)(2,1)S(1)}, u32[]{:S(2)}, u32[]{:S(2)}) collective-permute-start(bf16[8,128,128]{2,1,0:T(8,128)(2,1)S(1)} %constant_dynamic-update-slice_fusion), channel_id=1, source_target_pairs={{0,1},{1,0},{2,3},{3,2},{4,5},{5,4},{6,7},{7,6},{8,9},{9,8},{10,11... | collective-permute-start | bytes 786440 | tf_op jit(solution)/shard_map/ppermute | solution.py:335
  17.6 12.6 %all-to-all-start.1 = ((s32[16,1,2]{2,1,0:T(1,128)}), s32[16,1,2]{2,1,0:T(1,128)S(1)}, u32[]{:S(2)}, u32[]{:S(2)}) async-start(s32[16,1,2]{2,1,0:T(1,128)} %copy.20), calls=%async_computation.1 | async-start | bytes 16384 | tf_op jit(solution)/shard_map/all_to_all | solution.py:295
  30.9 1.6 %copy-start.1 = (bf16[8192,128]{1,0:T(8,128)(2,1)S(1)}, bf16[8192,128]{1,0:T(8,128)(2,1)}, u32[]{:S(2)}) copy-start(bf16[8192,128]{1,0:T(8,128)(2,1)} %wk_ref.1) | copy-start | bytes 6291460
  32.5 0.7 copy-start.3
  38.1 10.4 %all-to-all-start = ((bf16[16,16,128]{2,1,0:T(8,128)(2,1)}), bf16[16,16,128]{2,1,0:T(8,128)(2,1)S(1)}, u32[]{:S(2)}, u32[]{:S(2)}) async-start(bf16[16,16,128]{2,1,0:T(8,128)(2,1)} %norm_project.1), calls=%async_computation | async-start | bytes 131072 | tf_op jit(solution)/shard_map/all_to_all | solution.py:295
  48.5 26.6 %all-to-all-start.2 = ((bf16[16,32,1024]{2,1,0:T(8,128)(2,1)}), bf16[16,32,1024]{2,1,0:T(8,128)(2,1)S(1)}, u32[]{:S(2)}, u32[]{:S(2)}) async-start(bf16[16,32,1024]{2,1,0:T(8,128)(2,1)} %bitcast.10), calls=%async_computation.2 | async-start | bytes 2097152 | tf_op jit(solution)/shard_map/all_to_all | solution.py:295
  54.5 1.0 copy-start.2

commit v2 on v1

--- a/solution.py
+++ b/solution.py
@@ -40,6 +40,63 @@
 
 def whole(space=VMEM):
     return pl.BlockSpec(memory_space=space)
+
+
+def ask_kernel(slots_dev, slots_ref, asked_ref, holder_ref):
+    for m in range(holder_ref.shape[0]):
+        slot = slots_ref[0, 2 * m]
+        holder = lax.div(slot, slots_dev)
+        holder_ref[m] = holder
+        asked_ref[holder, 0, 0] = slot - holder * slots_dev
+        asked_ref[holder, 0, 1] = slots_ref[0, 2 * m + 1] - holder * slots_dev
+
+
+def ask(block_slot, devices, slots_dev):
+    return pl.pallas_call(
+        functools.partial(ask_kernel, slots_dev),
+        in_specs=[whole(SMEM)],
+        out_specs=(whole(SMEM), whole(SMEM)),
+        out_shape=(
+            jax.ShapeDtypeStruct((devices, 1, 2), jnp.int32),
+            jax.ShapeDtypeStruct((block_slot.shape[1] // 2,), jnp.int32),
+        ),
+        name="ask_pages",
+    )(block_slot)
+
+
+def pick_kernel(asked_ref, store_ref, out_ref, sem):
+    count = asked_ref.shape[0]
+    block_len = store_ref.shape[1]
+
+    def copies(i):
+        return [
+            pltpu.make_async_copy(
+                store_ref.at[asked_ref[i, 0, k]],
+                out_ref.at[i, pl.ds(k * block_len, block_len), :],
+                sem.at[i, k],
+            )
+            for k in range(2)
+        ]
+
+    for i in range(count):
+        for copy in copies(i):
+            copy.start()
+    for i in range(count):
+        for copy in copies(i):
+            copy.wait()
+
+
+def pick_pages(asked, store):
+    count = asked.shape[0]
+    _, block_len, width = store.shape
+    return pl.pallas_call(
+        pick_kernel,
+        in_specs=[whole(SMEM), whole(pl.ANY)],
+        out_specs=whole(pl.ANY),
+        out_shape=jax.ShapeDtypeStruct((count, 2 * block_len, width), store.dtype),
+        scratch_shapes=[pltpu.SemaphoreType.DMA((count, 2))],
+        name="pick_pages",
+    )(asked, store)
 
 
 def keys_kernel(factors_ref, basis_ref, cos_ref, sin_ref, out_ref):
@@ -76,9 +133,10 @@
 
 
 def project_kernel(
-    order, fast, me_ref, first_ref, second_ref, gain_ref, wq_ref, wk_ref, out_ref,
-    x_scr, lhs_scr, wq_buf, wk_buf, out_scr, sems,
+    order, fast, first_ref, second_ref, gain_ref, wq_ref, wk_ref, *rest
 ):
+    out_refs = rest[: 2 if fast else 1]
+    x_scr, lhs_scr, wq_buf, wk_buf, out_scr, sems = rest[len(out_refs) :]
     depth, q_cols = wq_ref.shape
     k_cols = wk_ref.shape[1]
     chunks = wq_buf.shape[0]
@@ -116,25 +174,28 @@
         q_sum = q_sum + jnp.dot(lhs, wq_buf[i], preferred_element_type=F32)
         k_sum = k_sum + jnp.dot(lhs, wk_buf[i], preferred_element_type=F32)
     if not fast:
-        out_ref[:, :q_cols] = q_sum.astype(BF16)
-        out_ref[:, q_cols:] = k_sum.astype(BF16)
+        out_refs[0][:, :q_cols] = q_sum.astype(BF16)
+        out_refs[0][:, q_cols:] = k_sum.astype(BF16)
         return
-    me = me_ref[0]
     per = q_cols // LANES
     out_scr[...] = jnp.zeros_like(out_scr)
-    for j, other in enumerate(order):
-        target = jnp.bitwise_xor(me, other)
+    for j, place in enumerate(order):
         for step in range(STEPS):
             row = j * STEPS + step
             for c in range(per):
-                out_scr[target, pl.ds(step * per + c, 1), :] = q_sum[
+                out_scr[place, step * per + c : step * per + c + 1, :] = q_sum[
                     row : row + 1, c * LANES : (c + 1) * LANES
                 ]
-            out_scr[target, pl.ds(STEPS * per + step, 1), :] = k_sum[row : row + 1, :]
-    out_ref[...] = out_scr[...].astype(BF16)
-
-
-def project(me, first, second, gain, query_weight, kv_weight, order, fast):
+            out_scr[place, STEPS * per + step : STEPS * per + step + 1, :] = k_sum[
+                row : row + 1, :
+            ]
+    near_ref, far_ref = out_refs
+    half = near_ref.shape[0]
+    near_ref[...] = out_scr[:half].astype(BF16)
+    far_ref[...] = out_scr[half:].astype(BF16)
+
+
+def project(first, second, gain, query_weight, kv_weight, order, fast):
     depth, q_cols = query_weight.shape
     k_cols = kv_weight.shape[1]
     pieces = depth // LANES
@@ -142,12 +203,17 @@
     devices = rows // STEPS
     chunks = 8
     span = depth // chunks
-    shape = (devices, 16, LANES) if fast else (rows, q_cols + k_cols)
+    if fast:
+        shape = (jax.ShapeDtypeStruct((devices // 2, 16, LANES), BF16),) * 2
+        out_specs = (whole(), whole())
+    else:
+        shape = jax.ShapeDtypeStruct((rows, q_cols + k_cols), BF16)
+        out_specs = whole()
     return pl.pallas_call(
         functools.partial(project_kernel, order, fast),
-        in_specs=[whole(SMEM), whole(), whole(), whole(), whole(pl.ANY), whole(pl.ANY)],
-        out_specs=whole(),
-        out_shape=jax.ShapeDtypeStruct(shape, BF16),
+        in_specs=[whole(), whole(), whole(), whole(pl.ANY), whole(pl.ANY)],
+        out_specs=out_specs,
+        out_shape=shape,
         scratch_shapes=[
             VMEM((rows * pieces, LANES), F32),
             VMEM((rows, depth), BF16),
@@ -163,12 +229,16 @@
             transcendentals=0,
         ),
         name="norm_project",
-    )(me, first, second, gain, query_weight, kv_weight)
+    )(first, second, gain, query_weight, kv_weight)
 
 
 def attend_kernel(
-    holder_ref, columns_ref, keys_ref, bias_ref, cos_ref, sin_ref, pages_ref, out_ref, values_scr
+    places, holder_ref, where_ref, keys_ref, bias_ref, cos_ref, sin_ref, pages_ref, *rest
 ):
+    pieces = rest[:-3]
+    out_ref, values_scr, columns_scr = rest[-3:]
+    for r, (piece, row) in enumerate(places):
+        columns_scr[where_ref[r]] = pieces[piece][row, 0].astype(F32)
     seq = keys_ref.shape[0]
     pairs, pair_rows = pages_ref.shape[0], pages_ref.shape[1]
     score_scale = 1.0 / math.sqrt(HEAD_DIM)
@@ -176,7 +246,7 @@
     rows = 2 * GROUP
     for m in range(pairs):
         values_scr[m * pair_rows : (m + 1) * pair_rows, :] = pages_ref[holder_ref[m]]
-    columns = columns_ref[...].astype(F32)
+    columns = columns_scr[...]
     count = columns.shape[0]
     query = columns[:, :8, :].reshape(count * 8, HEAD_DIM)
     fresh = columns[:, 8:, :]
@@ -229,14 +299,14 @@
         out_ref[mine, :] = mixed.astype(BF16)
 
 
-def attend(holder, columns, keys, bias, cosine, sine, pages):
+def attend(holder, where, keys, bias, cosine, sine, pages, places, pieces):
     seq, width = keys.shape
     return pl.pallas_call(
-        attend_kernel,
-        in_specs=[whole(SMEM)] + [whole()] * 6,
+        functools.partial(attend_kernel, places),
+        in_specs=[whole(SMEM)] * 2 + [whole()] * (5 + len(pieces)),
         out_specs=whole(),
         out_shape=jax.ShapeDtypeStruct((STEPS * HEADS, HEAD_DIM), BF16),
-        scratch_shapes=[VMEM((seq, width), BF16)],
+        scratch_shapes=[VMEM((seq, width), BF16), VMEM((len(places), 16, LANES), F32)],
         compiler_params=pltpu.CompilerParams(vmem_limit_bytes=48 * 2**20),
         cost_estimate=pl.CostEstimate(
             flops=4 * STEPS * HEADS * seq * HEAD_DIM,
@@ -244,7 +314,7 @@
             transcendentals=STEPS * HEADS * seq,
         ),
         name="attend",
-    )(holder, columns, keys, bias, cosine, sine, pages)
+    )(holder, where, keys, bias, cosine, sine, pages, *pieces)
 
 
 def output_kernel(lhs_ref, weight_ref, out_ref, weight_buf, out_scr, sems):
@@ -289,6 +359,10 @@
         ),
         name="output_project",
     )(lhs, weight)
+
+
+def swap(block, bit, devices):
+    return lax.ppermute(block, AXIS, [(i, i ^ bit) for i in range(devices)])
 
 
 def exchange(blocks):
@@ -319,44 +393,61 @@
     fast = q_cols == 4 * HEAD_DIM and k_cols == HEAD_DIM
     pieces = model // LANES
 
-    slots = block_slot[0].reshape(pages // 2, 2)
-    holder = slots[:, 0] // slots_dev
-    here = holder[None, :] == jnp.arange(devices, dtype=jnp.int32)[:, None]
-    asked = jnp.sum(jnp.where(here[:, :, None], (slots % slots_dev)[None], 0), axis=1)
-    asked_here = exchange(asked[:, None, :])
-    sent_pages = value_store[asked_here.reshape(-1)]
-    fetched = exchange(sent_pages.reshape(devices, 2 * block_len, width))
+    asked, holder = ask(block_slot, devices, slots_dev)
+    sent_pages = pick_pages(exchange(asked), value_store)
+    fetched = exchange(sent_pages)
 
     block = hidden[:, 0].reshape(1, STEPS * pieces, LANES)
     order = [0]
     bit = devices // 2
     while bit:
-        links = [(i, i ^ bit) for i in range(devices)]
-        other = lax.ppermute(block, AXIS, links)
+        if bit == 2:
+            block, sent_pages = lax.optimization_barrier((block, sent_pages))
+        other = swap(block, bit, devices)
         order = order + [k ^ bit for k in order]
         bit //= 2
         if bit:
             block = jnp.concatenate([block, other], axis=0)
-    columns = project(
-        me.astype(jnp.int32).reshape(1),
+    if fast:
+        bits = devices.bit_length() - 1
+        turn = [int(format(k, "b").zfill(bits)[::-1], 2) for k in order]
+    else:
+        turn = order
+    projected = project(
         block.reshape(-1, LANES),
         other.reshape(-1, LANES),
         norm_gain.reshape(pieces, LANES),
         query_weight,
         kv_weight,
-        tuple(order),
+        tuple(turn),
         fast,
     )
     if fast:
-        columns = exchange(columns)
+        near, far = projected
+        sent, kept, arrived = far[None], [near[None]], [near[None]]
+        places = [(0, 0)]
+        bit = 1
+        while bit < devices:
+            if bit > 1:
+                middle = kept[0].shape[1] // 2
+                sent = jnp.concatenate([part[:, middle:] for part in kept], axis=0)
+                kept = [part[:, :middle] for part in kept]
+            part = swap(sent, bit, devices)
+            places += [(len(arrived), row) for row in range(part.shape[0])]
+            arrived.append(part)
+            kept.append(part)
+            bit *= 2
+        where = jnp.bitwise_xor(me, jnp.arange(devices, dtype=jnp.int32))
     else:
-        places = jnp.bitwise_xor(me, jnp.array(order, dtype=jnp.int32))
-        columns = exchange(columns.reshape(devices, STEPS, q_cols + k_cols)[places])
+        targets = jnp.bitwise_xor(me, jnp.array(order, dtype=jnp.int32))
+        columns = exchange(projected.reshape(devices, STEPS, q_cols + k_cols)[targets])
         query = columns[:, :, :q_cols].transpose(1, 0, 2).reshape(STEPS, HEADS // 4, 4, HEAD_DIM)
         query = query.transpose(1, 0, 2, 3).reshape(HEADS // 4, 8, HEAD_DIM)
         fresh = columns[:, :, q_cols:].transpose(1, 0, 2).reshape(STEPS, HEADS // 4, HEAD_DIM)
         fresh = jnp.pad(fresh.transpose(1, 0, 2), ((0, 0), (0, 8 - STEPS), (0, 0)))
-        columns = jnp.concatenate([query, fresh], axis=1)
+        arrived = [jnp.concatenate([query, fresh], axis=1)[:, None]]
+        places = [(0, row) for row in range(HEADS // 4)]
+        where = jnp.arange(HEADS // 4, dtype=jnp.int32)
 
     cosine, sine = turn_tables(jnp.arange(seq, dtype=jnp.int32).astype(F32))
     keys = make_keys(key_factors[0], key_basis[0], cosine, sine)
@@ -370,7 +461,9 @@
     new_cos, new_sin = turn_tables(
         (lengths[0] + jnp.arange(STEPS, dtype=jnp.int32)).astype(F32)
     )
-    heads = attend(holder, columns, keys, bias, new_cos, new_sin, fetched)
+    heads = attend(
+        holder, where, keys, bias, new_cos, new_sin, fetched, tuple(places), arrived
+    )
 
     if fast:
         rows = exchange(heads.reshape(devices, STEPS * 4, HEAD_DIM))

time: 114 us -> 140 us (1.23)
  Pallas kernels: 13 us -> 47.7 us
  waiting for transfers between devices: 36.2 us -> 30.2 us
  starting transfers between devices: 20.9 us -> 26.1 us
  local copies, waits for them, and re-layouts: 8.36 us -> 4.73 us
  blocking collectives: 30.3 us -> 27.5 us
    pallas_call x1 -> x3, Pallas kernels: 3.29 us -> 38.7 us  [the longest x1 33.9 us: pick_pages(): pl.pallas_call(pick_kernel, in_specs=[whole(SMEM), whole(pl.ANY)], out_sp...]
    all_to_all x3 -> x2, waiting for transfers between devices: 30.2 us -> 1.03 us  [exchange(): return lax.all_to_all(blocks, AXIS, split_axis=0, concat_axis=0, tiled=True)]
    ppermute x4 -> x8, waiting for transfers between devices: 6.06 us -> 29.1 us  [swap(): return lax.ppermute(block, AXIS, [(i, i ^ bit) for i in range(devices)])]
    ppermute x4 -> x8, starting transfers between devices: 7.56 us -> 15 us  [swap(): return lax.ppermute(block, AXIS, [(i, i ^ bit) for i in range(devices)])]
    all_to_all x2, blocking collectives: 30.3 us -> 27.5 us  [exchange(): return lax.all_to_all(blocks, AXIS, split_axis=0, concat_axis=0, tiled=True)]
    all_to_all x3 -> x2, starting transfers between devices: 13.4 us -> 11.2 us  [exchange(): return lax.all_to_all(blocks, AXIS, split_axis=0, concat_axis=0, tiled=True)]
    gather x1 -> x0, local copies, waits for them, and re-layouts: 1.59 us -> none  [local(): sent_pages = value_store[asked_here.reshape(-1)]]
    unnamed x17 -> x14, local copies, waits for them, and re-layouts: 3.98 us -> 3.06 us
  transfers between devices with their start and end apart: 7 -> 10, of which waited for: 6 -> 8; matrix products, arithmetic and copies ran while one was open for 6% -> 2% of each run, Pallas kernels for 1% -> 28%
where the time goes in v2:
time: 140 us; the launch traced here: 139 us
  Pallas kernels  47.7 us (34%)
  waiting for transfers between devices  30.2 us (22%)
  blocking collectives  27.5 us (20%)
  starting transfers between devices  26.1 us (19%)
  local copies, waits for them, and re-layouts  4.73 us (3%)
  other arithmetic  2.31 us (2%)
    pallas_call x1, Pallas kernels, pick_pages(): pl.pallas_call(pick_kernel, in_specs=[whole(SMEM), whole(pl.ANY)], out_sp...  33.9 us
    ppermute x8, waiting for transfers between devices, swap(): return lax.ppermute(block, AXIS, [(i, i ^ bit) for i in range(devices)])  29.1 us
    all_to_all x2, blocking collectives, exchange(): return lax.all_to_all(blocks, AXIS, split_axis=0, concat_axis=0, tiled=True)  27.5 us
    ppermute x8, starting transfers between devices, swap(): return lax.ppermute(block, AXIS, [(i, i ^ bit) for i in range(devices)])  15 us
    all_to_all x2, starting transfers between devices, exchange(): return lax.all_to_all(blocks, AXIS, split_axis=0, concat_axis=0, tiled=True)  11.2 us
    pallas_call x1, Pallas kernels, project(): pl.pallas_call(functools.partial(project_kernel, order, fast), in_specs=[...  4.32 us
    pallas_call x1, Pallas kernels, output(): pl.pallas_call(output_kernel, in_specs=[whole(), whole(pl.ANY)], out_spec...  3.95 us
    pallas_call x1, Pallas kernels, attend(): pl.pallas_call(functools.partial(attend_kernel, places), in_specs=[whole(...  3.33 us
  transfers between devices with their start and end apart: 10, of which 8 were waited for; matrix products, arithmetic and copies ran while one was open for 2% of the time, Pallas kernels for 28%

profile of v2, /device:TPU:0, one launch (start us, length us, event | category | flops | bytes accessed | tf_op | source)
XLA Modules:
  0.0 139.4 jit_solution(9841649080856586264)
XLA Ops:
  0.0 1.4 ask_pages.1
  1.4 7.4 %all-to-all-start = ((s32[16,1,2]{2,1,0:T(1,128)}), s32[16,1,2]{2,1,0:T(1,128)S(1)}, u32[]{:S(2)}, u32[]{:S(2)}) async-start(s32[16,1,2]{2,1,0:T(1,128)} %get-tuple-element.11), calls=%async_computation | async-start | bytes 16384 | tf_op jit(solution)/shard_map/all_to_all | solution.py:369
  9.6 2.9 %collective-permute-start = (bf16[1,128,128]{2,1,0:T(8,128)(2,1)S(1)}, bf16[1,128,128]{2,1,0:T(8,128)(2,1)S(1)}, u32[]{:S(2)}, u32[]{:S(2)}) collective-permute-start(bf16[1,128,128]{2,1,0:T(8,128)(2,1)S(1)} %reshape_squeeze.3), channel_id=1, source_target_pairs={{0,8},{1,9},{2,10},{3,11},{4,12},{5,13},{6,14},{7,15},{8,0},{9,1},... | collective-permute-start | bytes 98312 | tf_op jit(solution)/shard_map/ppermute | solution.py:365
  14.1 1.0 all-to-all-done.asked_ref
  15.7 33.9 %pick_pages.1 = bf16[16,32,1024]{2,1,0:T(8,128)(2,1)} custom-call(s32[16,1,2]{2,1,0:T(1,128)} %copy-done.5, bf16[32,16,1024]{2,1,0:T(8,128)(2,1)} %store_ref.1), custom_call_target="tpu_custom_call" | custom-call | tf_op jit(solution)/shard_map/pick_pages/pallas_call | solution.py:92
  49.7 3.8 %all-to-all-start.1 = ((bf16[16,32,1024]{2,1,0:T(8,128)(2,1)}), bf16[16,32,1024]{2,1,0:T(8,128)(2,1)S(1)}, u32[]{:S(2)}, u32[]{:S(2)}) async-start(bf16[16,32,1024]{2,1,0:T(8,128)(2,1)} %pick_pages.1), calls=%async_computation.1 | async-start | bytes 2097152 | tf_op jit(solution)/shard_map/all_to_all | solution.py:369
  53.5 1.9 %collective-permute-start.1 = (bf16[2,128,128]{2,1,0:T(8,128)(2,1)S(1)}, bf16[2,128,128]{2,1,0:T(8,128)(2,1)S(1)}, u32[]{:S(2)}, u32[]{:S(2)}) collective-permute-start(bf16[2,128,128]{2,1,0:T(8,128)(2,1)S(1)} %pad_maximum_fusion.3), channel_id=1, source_target_pairs={{0,4},{1,5},{2,6},{3,7},{4,0},{5,1},{6,2},{7,3},{8,12},{9,13},{10,... | collective-permute-start | bytes 196616 | tf_op jit(solution)/shard_map/ppermute | solution.py:365
  55.4 17.4 %collective-permute-done.1 = bf16[2,128,128]{2,1,0:T(8,128)(2,1)S(1)} collective-permute-done((bf16[2,128,128]{2,1,0:T(8,128)(2,1)S(1)}, bf16[2,128,128]{2,1,0:T(8,128)(2,1)S(1)}, u32[]{:S(2)}, u32[]{:S(2)}) %collective-permute-start.1) | collective-permute-done | bytes 65568 | tf_op jit(solution)/shard_map/ppermute | solution.py:365
  72.8 1.7 %collective-permute-start.2 = (bf16[4,128,128]{2,1,0:T(8,128)(2,1)S(1)}, bf16[4,128,128]{2,1,0:T(8,128)(2,1)S(1)}, u32[]{:S(2)}, u32[]{:S(2)}) collective-permute-start(bf16[4,128,128]{2,1,0:T(8,128)(2,1)S(1)} %pad_maximum_fusion.2), channel_id=1, source_target_pairs={{0,2},{1,3},{2,0},{3,1},{4,6},{5,7},{6,4},{7,5},{8,10},{9,11},{10,... | collective-permute-start | bytes 393224 | tf_op jit(solution)/shard_map/ppermute | solution.py:365
  74.5 5.0 %collective-permute-done.2 = bf16[4,128,128]{2,1,0:T(8,128)(2,1)S(1)} collective-permute-done((bf16[4,128,128]{2,1,0:T(8,128)(2,1)S(1)}, bf16[4,128,128]{2,1,0:T(8,128)(2,1)S(1)}, u32[]{:S(2)}, u32[]{:S(2)}) %collective-permute-start.2) | collective-permute-done | bytes 131104 | tf_op jit(solution)/shard_map/ppermute | solution.py:365
  79.6 1.0 fusion
  81.1 1.6 %copy-done = bf16[8192,128]{1,0:T(8,128)(2,1)S(1)} copy-done((bf16[8192,128]{1,0:T(8,128)(2,1)S(1)}, bf16[8192,128]{1,0:T(8,128)(2,1)}, u32[]{:S(2)}) %copy-start) | copy-done | bytes 2097176
  83.4 4.3 %norm_project.1 = (bf16[8,16,128]{2,1,0:T(8,128)(2,1)S(1)}, bf16[8,16,128]{2,1,0:T(8,128)(2,1)S(1)}) custom-call(bf16[1024,128]{1,0:T(8,128)(2,1)S(1)} %bitcast.17, bf16[1024,128]{1,0:T(8,128)(2,1)S(1)} %bitcast.19, bf16[64,128]{1,0:T(8,128)(2,1)S(1)} %bitcast.25, bf16[8192,512]{1,0:T(8,128)(2,1)} %wq_ref.1, bf16[8192,128]{1,0:T(8,128)(2,1)S(1)} %copy-done), custom_call_target="tpu_custom_call" | custom-call | flops 335544320 | bytes 10485760 | tf_op jit(solution)/shard_map/norm_project/pallas_call | solution.py:212
  88.1 1.0 collective-permute-done.4.rest_1_
  89.0 1.5 %collective-permute-start.5 = (bf16[2,4,16,128]{3,2,1,0:T(8,128)(2,1)S(1)}, bf16[2,4,16,128]{3,2,1,0:T(8,128)(2,1)S(1)}, u32[]{:S(2)}, u32[]{:S(2)}) collective-permute-start(bf16[2,4,16,128]{3,2,1,0:T(8,128)(2,1)S(1)} %pad_maximum_fusion.4), channel_id=1, source_target_pairs={{0,2},{1,3},{2,0},{3,1},{4,6},{5,7},{6,4},{7,5},{8,10},{9,11},{10,... | collective-permute-start | bytes 98312 | tf_op jit(solution)/shard_map/ppermute | solution.py:365
  90.8 2.3 %collective-permute-done.5.rest_2_ = bf16[2,4,16,128]{3,2,1,0:T(8,128)(2,1)S(1)} collective-permute-done((bf16[2,4,16,128]{3,2,1,0:T(8,128)(2,1)S(1)}, bf16[2,4,16,128]{3,2,1,0:T(8,128)(2,1)S(1)}, u32[]{:S(2)}, u32[]{:S(2)}) %collective-permute-start.5) | collective-permute-done | bytes 32800 | tf_op jit(solution)/shard_map/ppermute | solution.py:365
  93.0 2.5 %collective-permute-start.6 = (bf16[4,2,16,128]{3,2,1,0:T(8,128)(2,1)S(1)}, bf16[4,2,16,128]{3,2,1,0:T(8,128)(2,1)S(1)}, u32[]{:S(2)}, u32[]{:S(2)}) collective-permute-start(bf16[4,2,16,128]{3,2,1,0:T(8,128)(2,1)S(1)} %pad_maximum_fusion.5), channel_id=1, source_target_pairs={{0,4},{1,5},{2,6},{3,7},{4,0},{5,1},{6,2},{7,3},{8,12},{9,13},{10,... | collective-permute-start | bytes 98312 | tf_op jit(solution)/shard_map/ppermute | solution.py:365
  95.7 1.8 %collective-permute-done.6.rest_3_ = bf16[4,2,16,128]{3,2,1,0:T(8,128)(2,1)S(1)} collective-permute-done((bf16[4,2,16,128]{3,2,1,0:T(8,128)(2,1)S(1)}, bf16[4,2,16,128]{3,2,1,0:T(8,128)(2,1)S(1)}, u32[]{:S(2)}, u32[]{:S(2)}) %collective-permute-start.6) | collective-permute-done | bytes 32800 | tf_op jit(solution)/shard_map/ppermute | solution.py:365
  97.5 4.2 %collective-permute-start.7 = (bf16[8,1,16,128]{3,2,1,0:T(8,128)(2,1)S(1)}, bf16[8,1,16,128]{3,2,1,0:T(8,128)(2,1)S(1)}, u32[]{:S(2)}, u32[]{:S(2)}) collective-permute-start(bf16[8,1,16,128]{3,2,1,0:T(8,128)(2,1)S(1)} %pad_maximum_fusion.6), channel_id=1, source_target_pairs={{0,8},{1,9},{2,10},{3,11},{4,12},{5,13},{6,14},{7,15},{8,0},{9,1},... | collective-permute-start | bytes 98312 | tf_op jit(solution)/shard_map/ppermute | solution.py:365
  102.7 1.3 collective-permute-done.7.rest_4_
  103.9 3.3 %attend.1 = bf16[128,128]{1,0:T(8,128)(2,1)S(1)} custom-call(s32[16]{0:T(128)S(1)} %copy-done.3, s32[16]{0:T(128)S(1)} %iota_xor_fusion.where_ref, bf16[512,1024]{1,0:T(8,128)(2,1)S(1)} %turned_keys.1.keys_ref, f32[2,512]{1,0:T(2,128)S(1)} %and_select_fusion.bias_ref, f32[2,128]{1,0:T(2,128)S(1)} %get-tuple-element.23.cos_ref, ...), custom_call_target="tpu_custom_call" | custom-call | flops 33554432 | bytes 2097152 | tf_op jit(solution)/shard_map/attend/pallas_call | solution.py:304
  107.3 10.4 %all_to_all.20 = bf16[16,8,128]{2,1,0:T(8,128)(2,1)S(1)} all-to-all(bf16[16,8,128]{2,1,0:T(8,128)(2,1)S(1)} %bitcast.20), channel_id=1, replica_groups=mesh['groups'=2,'session'=16] {'session'}, dimensions={0} | all-to-all | bytes 65536 | tf_op jit(solution)/shard_map/all_to_all | solution.py:369
  117.7 3.9 %output_project.1 = bf16[2048,128]{1,0:T(8,128)(2,1)S(1)} custom-call(bf16[32,512]{1,0:T(8,128)(2,1)S(1)} %reshape_reshape.3.lhs_ref, bf16[512,8192]{1,0:T(8,128)(2,1)} %weight_ref.1), custom_call_target="tpu_custom_call" | custom-call | flops 268435456 | bytes 8388608 | tf_op jit(solution)/shard_map/output_project/pallas_call | solution.py:346
  121.6 17.1 %all_to_all.21 = bf16[16,128,128]{2,1,0:T(8,128)(2,1)S(1)} all-to-all(bf16[16,128,128]{2,1,0:T(8,128)(2,1)S(1)} %bitcast.15), channel_id=1, replica_groups=mesh['groups'=2,'session'=16] {'session'}, dimensions={0} | all-to-all | bytes 1048576 | tf_op jit(solution)/shard_map/all_to_all | solution.py:369
  (50 shorter events, 6.1 us)
Async XLA Ops:
  1.4 13.7 %all-to-all-start = ((s32[16,1,2]{2,1,0:T(1,128)}), s32[16,1,2]{2,1,0:T(1,128)S(1)}, u32[]{:S(2)}, u32[]{:S(2)}) async-start(s32[16,1,2]{2,1,0:T(1,128)} %get-tuple-element.11), calls=%async_computation | async-start | bytes 16384 | tf_op jit(solution)/shard_map/all_to_all | solution.py:369
  9.6 43.9 %collective-permute-start = (bf16[1,128,128]{2,1,0:T(8,128)(2,1)S(1)}, bf16[1,128,128]{2,1,0:T(8,128)(2,1)S(1)}, u32[]{:S(2)}, u32[]{:S(2)}) collective-permute-start(bf16[1,128,128]{2,1,0:T(8,128)(2,1)S(1)} %reshape_squeeze.3), channel_id=1, source_target_pairs={{0,8},{1,9},{2,10},{3,11},{4,12},{5,13},{6,14},{7,15},{8,0},{9,1},... | collective-permute-start | bytes 98312 | tf_op jit(solution)/shard_map/ppermute | solution.py:365
  15.1 0.6 copy-start.5
  49.7 52.0 %copy-start.4 = (bf16[1,512,160]{1,2,0:T(8,128)(2,1)S(1)}, bf16[1,512,160]{1,2,0:T(8,128)(2,1)}, u32[]{:S(2)}) copy-start(bf16[1,512,160]{1,2,0:T(8,128)(2,1)} %param.16) | copy-start | bytes 491524
  49.7 52.2 %copy-start.1 = (bf16[1,160,1024]{2,1,0:T(8,128)(2,1)S(1)}, bf16[1,160,1024]{2,1,0:T(8,128)(2,1)}, u32[]{:S(2)}) copy-start(bf16[1,160,1024]{2,1,0:T(8,128)(2,1)} %param.17) | copy-start | bytes 983044
  49.7 54.3 %all-to-all-start.1 = ((bf16[16,32,1024]{2,1,0:T(8,128)(2,1)}), bf16[16,32,1024]{2,1,0:T(8,128)(2,1)S(1)}, u32[]{:S(2)}, u32[]{:S(2)}) async-start(bf16[16,32,1024]{2,1,0:T(8,128)(2,1)} %pick_pages.1), calls=%async_computation.1 | async-start | bytes 2097152 | tf_op jit(solution)/shard_map/all_to_all | solution.py:369
  53.5 19.3 %collective-permute-start.1 = (bf16[2,128,128]{2,1,0:T(8,128)(2,1)S(1)}, bf16[2,128,128]{2,1,0:T(8,128)(2,1)S(1)}, u32[]{:S(2)}, u32[]{:S(2)}) collective-permute-start(bf16[2,128,128]{2,1,0:T(8,128)(2,1)S(1)} %pad_maximum_fusion.3), channel_id=1, source_target_pairs={{0,4},{1,5},{2,6},{3,7},{4,0},{5,1},{6,2},{7,3},{8,12},{9,13},{10,... | collective-permute-start | bytes 196616 | tf_op jit(solution)/shard_map/ppermute | solution.py:365
  72.8 31.2 %copy-start.3 = (s32[16]{0:T(128)S(1)}, s32[16]{0:T(128)}, u32[]{:S(2)}) copy-start(s32[16]{0:T(128)} %get-tuple-element.10.holder_ref) | copy-start | bytes 196
  72.8 6.7 %collective-permute-start.2 = (bf16[4,128,128]{2,1,0:T(8,128)(2,1)S(1)}, bf16[4,128,128]{2,1,0:T(8,128)(2,1)S(1)}, u32[]{:S(2)}, u32[]{:S(2)}) collective-permute-start(bf16[4,128,128]{2,1,0:T(8,128)(2,1)S(1)} %pad_maximum_fusion.2), channel_id=1, source_target_pairs={{0,2},{1,3},{2,0},{3,1},{4,6},{5,7},{6,4},{7,5},{8,10},{9,11},{10,... | collective-permute-start | bytes 393224 | tf_op jit(solution)/shard_map/ppermute | solution.py:365
  79.5 1.6 %collective-permute-start.3 = (bf16[8,128,128]{2,1,0:T(8,128)(2,1)S(1)}, bf16[8,128,128]{2,1,0:T(8,128)(2,1)S(1)}, u32[]{:S(2)}, u32[]{:S(2)}) collective-permute-start(bf16[8,128,128]{2,1,0:T(8,128)(2,1)S(1)} %constant_dynamic-update-slice_fusion), channel_id=1, source_target_pairs={{0,1},{1,0},{2,3},{3,2},{4,5},{5,4},{6,7},{7,6},{8,9},{9,8},{10,11... | collective-permute-start | bytes 786440 | tf_op jit(solution)/shard_map/ppermute | solution.py:365
  81.1 1.6 %copy-start = (bf16[8192,128]{1,0:T(8,128)(2,1)S(1)}, bf16[8192,128]{1,0:T(8,128)(2,1)}, u32[]{:S(2)}) copy-start(bf16[8192,128]{1,0:T(8,128)(2,1)} %wk_ref.1) | copy-start | bytes 6291460
  82.7 0.7 copy-start.2
  87.8 1.3 collective-permute-start.4
  89.0 4.0 %collective-permute-start.5 = (bf16[2,4,16,128]{3,2,1,0:T(8,128)(2,1)S(1)}, bf16[2,4,16,128]{3,2,1,0:T(8,128)(2,1)S(1)}, u32[]{:S(2)}, u32[]{:S(2)}) collective-permute-start(bf16[2,4,16,128]{3,2,1,0:T(8,128)(2,1)S(1)} %pad_maximum_fusion.4), channel_id=1, source_target_pairs={{0,2},{1,3},{2,0},{3,1},{4,6},{5,7},{6,4},{7,5},{8,10},{9,11},{10,... | collective-permute-start | bytes 98312 | tf_op jit(solution)/shard_map/ppermute | solution.py:365
  93.0 4.4 %collective-permute-start.6 = (bf16[4,2,16,128]{3,2,1,0:T(8,128)(2,1)S(1)}, bf16[4,2,16,128]{3,2,1,0:T(8,128)(2,1)S(1)}, u32[]{:S(2)}, u32[]{:S(2)}) collective-permute-start(bf16[4,2,16,128]{3,2,1,0:T(8,128)(2,1)S(1)} %pad_maximum_fusion.5), channel_id=1, source_target_pairs={{0,4},{1,5},{2,6},{3,7},{4,0},{5,1},{6,2},{7,3},{8,12},{9,13},{10,... | collective-permute-start | bytes 98312 | tf_op jit(solution)/shard_map/ppermute | solution.py:365
  97.5 6.5 %collective-permute-start.7 = (bf16[8,1,16,128]{3,2,1,0:T(8,128)(2,1)S(1)}, bf16[8,1,16,128]{3,2,1,0:T(8,128)(2,1)S(1)}, u32[]{:S(2)}, u32[]{:S(2)}) collective-permute-start(bf16[8,1,16,128]{3,2,1,0:T(8,128)(2,1)S(1)} %pad_maximum_fusion.6), channel_id=1, source_target_pairs={{0,8},{1,9},{2,10},{3,11},{4,12},{5,13},{6,14},{7,15},{8,0},{9,1},... | collective-permute-start | bytes 98312 | tf_op jit(solution)/shard_map/ppermute | solution.py:365

commit v3 on v2

--- a/solution.py
+++ b/solution.py
@@ -64,26 +64,11 @@
     )(block_slot)
 
 
-def pick_kernel(asked_ref, store_ref, out_ref, sem):
-    count = asked_ref.shape[0]
+def pick_kernel(asked_ref, store_ref, out_ref):
     block_len = store_ref.shape[1]
-
-    def copies(i):
-        return [
-            pltpu.make_async_copy(
-                store_ref.at[asked_ref[i, 0, k]],
-                out_ref.at[i, pl.ds(k * block_len, block_len), :],
-                sem.at[i, k],
-            )
-            for k in range(2)
-        ]
-
-    for i in range(count):
-        for copy in copies(i):
-            copy.start()
-    for i in range(count):
-        for copy in copies(i):
-            copy.wait()
+    for i in range(asked_ref.shape[0]):
+        for k in range(2):
+            out_ref[i, k * block_len : (k + 1) * block_len, :] = store_ref[asked_ref[i, 0, k]]
 
 
 def pick_pages(asked, store):
@@ -91,10 +76,10 @@
     _, block_len, width = store.shape
     return pl.pallas_call(
         pick_kernel,
-        in_specs=[whole(SMEM), whole(pl.ANY)],
-        out_specs=whole(pl.ANY),
+        in_specs=[whole(SMEM), whole()],
+        out_specs=whole(),
         out_shape=jax.ShapeDtypeStruct((count, 2 * block_len, width), store.dtype),
-        scratch_shapes=[pltpu.SemaphoreType.DMA((count, 2))],
+        compiler_params=pltpu.CompilerParams(vmem_limit_bytes=32 * 2**20),
         name="pick_pages",
     )(asked, store)
 
@@ -394,14 +379,16 @@
     pieces = model // LANES
 
     asked, holder = ask(block_slot, devices, slots_dev)
-    sent_pages = pick_pages(exchange(asked), value_store)
-    fetched = exchange(sent_pages)
+    asked_here = exchange(asked)
 
     block = hidden[:, 0].reshape(1, STEPS * pieces, LANES)
     order = [0]
     bit = devices // 2
     while bit:
         if bit == 2:
+            block, asked_here = lax.optimization_barrier((block, asked_here))
+            sent_pages = pick_pages(asked_here, value_store)
+            fetched = exchange(sent_pages)
             block, sent_pages = lax.optimization_barrier((block, sent_pages))
         other = swap(block, bit, devices)
         order = order + [k ^ bit for k in order]

time: 140 us -> 102 us (0.73)
  Pallas kernels: 47.7 us -> 15.5 us
  waiting for transfers between devices: 30.2 us -> 24.3 us
  starting transfers between devices: 26.1 us -> 23.9 us
  blocking collectives: 27.5 us -> 29.1 us
    pallas_call x1, Pallas kernels: 33.9 us -> 1.72 us  [pick_pages(): pl.pallas_call(pick_kernel, in_specs=[whole(SMEM), whole()], out_specs=wh...]
    ppermute x8, starting transfers between devices: 15 us -> 10.1 us  [swap(): return lax.ppermute(block, AXIS, [(i, i ^ bit) for i in range(devices)])]
    ppermute x8, waiting for transfers between devices: 29.1 us -> 24.3 us  [swap(): return lax.ppermute(block, AXIS, [(i, i ^ bit) for i in range(devices)])]
    all_to_all x2, starting transfers between devices: 11.2 us -> 13.8 us  [exchange(): return lax.all_to_all(blocks, AXIS, split_axis=0, concat_axis=0, tiled=True)]
    all_to_all x2, blocking collectives: 27.5 us -> 29.1 us  [exchange(): return lax.all_to_all(blocks, AXIS, split_axis=0, concat_axis=0, tiled=True)]
  transfers between devices with their start and end apart: 10 -> 10, of which waited for: 8 -> 8; matrix products, arithmetic and copies ran while one was open for 2% -> 3% of each run, Pallas kernels for 28% -> 5%
where the time goes in v3:
time: 102 us; the launch traced here: 101 us
  blocking collectives  29.1 us (29%)
  waiting for transfers between devices  24.3 us (24%)
  starting transfers between devices  23.9 us (23%)
  Pallas kernels  15.5 us (15%)
  local copies, waits for them, and re-layouts  5.35 us (5%)
  other arithmetic  2.31 us (2%)
    all_to_all x2, blocking collectives, exchange(): return lax.all_to_all(blocks, AXIS, split_axis=0, concat_axis=0, tiled=True)  29.1 us
    ppermute x8, waiting for transfers between devices, swap(): return lax.ppermute(block, AXIS, [(i, i ^ bit) for i in range(devices)])  24.3 us
    all_to_all x2, starting transfers between devices, exchange(): return lax.all_to_all(blocks, AXIS, split_axis=0, concat_axis=0, tiled=True)  13.8 us
    ppermute x8, starting transfers between devices, swap(): return lax.ppermute(block, AXIS, [(i, i ^ bit) for i in range(devices)])  10.1 us
    pallas_call x1, Pallas kernels, project(): pl.pallas_call(functools.partial(project_kernel, order, fast), in_specs=[...  4.32 us
    pallas_call x1, Pallas kernels, output(): pl.pallas_call(output_kernel, in_specs=[whole(), whole(pl.ANY)], out_spec...  3.95 us
    unnamed x14, local copies, waits for them, and re-layouts  3.68 us
    pallas_call x1, Pallas kernels, attend(): pl.pallas_call(functools.partial(attend_kernel, places), in_specs=[whole(...  3.33 us
  transfers between devices with their start and end apart: 10, of which 8 were waited for; matrix products, arithmetic and copies ran while one was open for 3% of the time, Pallas kernels for 5%

profile of v3, /device:TPU:0, one launch (start us, length us, event | category | flops | bytes accessed | tf_op | source)
XLA Modules:
  0.0 101.2 jit_solution(18201022141893648878)
XLA Ops:
  0.0 1.4 %ask_pages.1 = (s32[16,1,2]{2,1,0:T(1,128)}, s32[16]{0:T(128)}) custom-call(s32[1,32]{1,0:T(1,128)} %slots_ref.1), custom_call_target="tpu_custom_call" | custom-call | tf_op jit(solution)/shard_map/ask_pages/pallas_call | solution.py:55
  1.4 7.4 %all-to-all-start = ((s32[16,1,2]{2,1,0:T(1,128)}), s32[16,1,2]{2,1,0:T(1,128)S(1)}, u32[]{:S(2)}, u32[]{:S(2)}) async-start(s32[16,1,2]{2,1,0:T(1,128)} %get-tuple-element.13), calls=%async_computation | async-start | bytes 16384 | tf_op jit(solution)/shard_map/all_to_all | solution.py:354
  8.8 0.8 reshape_squeeze.3
  9.6 2.9 %collective-permute-start = (bf16[1,128,128]{2,1,0:T(8,128)(2,1)S(1)}, bf16[1,128,128]{2,1,0:T(8,128)(2,1)S(1)}, u32[]{:S(2)}, u32[]{:S(2)}) collective-permute-start(bf16[1,128,128]{2,1,0:T(8,128)(2,1)S(1)} %reshape_squeeze.3), channel_id=1, source_target_pairs={{0,8},{1,9},{2,10},{3,11},{4,12},{5,13},{6,14},{7,15},{8,0},{9,1},... | collective-permute-start | bytes 98312 | tf_op jit(solution)/shard_map/ppermute | solution.py:350
  14.5 1.9 %collective-permute-start.1 = (bf16[2,128,128]{2,1,0:T(8,128)(2,1)S(1)}, bf16[2,128,128]{2,1,0:T(8,128)(2,1)S(1)}, u32[]{:S(2)}, u32[]{:S(2)}) collective-permute-start(bf16[2,128,128]{2,1,0:T(8,128)(2,1)S(1)} %pad_maximum_fusion.3), channel_id=1, source_target_pairs={{0,4},{1,5},{2,6},{3,7},{4,0},{5,1},{6,2},{7,3},{8,12},{9,13},{10,... | collective-permute-start | bytes 196616 | tf_op jit(solution)/shard_map/ppermute | solution.py:350
  16.4 2.4 %collective-permute-done.1 = bf16[2,128,128]{2,1,0:T(8,128)(2,1)S(1)} collective-permute-done((bf16[2,128,128]{2,1,0:T(8,128)(2,1)S(1)}, bf16[2,128,128]{2,1,0:T(8,128)(2,1)S(1)}, u32[]{:S(2)}, u32[]{:S(2)}) %collective-permute-start.1) | collective-permute-done | bytes 65568 | tf_op jit(solution)/shard_map/ppermute | solution.py:350
  18.9 1.2 %copy-done.1 = bf16[32,16,1024]{2,1,0:T(8,128)(2,1)S(1)} copy-done((bf16[32,16,1024]{2,1,0:T(8,128)(2,1)S(1)}, bf16[32,16,1024]{2,1,0:T(8,128)(2,1)}, u32[]{:S(2)}) %copy-start.1) | copy-done | bytes 1048600
  20.1 1.7 %pick_pages.1 = bf16[16,32,1024]{2,1,0:T(8,128)(2,1)} custom-call(s32[16,1,2]{2,1,0:T(1,128)S(1)} %all-to-all-done.asked_ref, bf16[32,16,1024]{2,1,0:T(8,128)(2,1)S(1)} %copy-done.1), custom_call_target="tpu_custom_call" | custom-call | tf_op jit(solution)/shard_map/pick_pages/pallas_call | solution.py:77
  21.8 6.4 %all-to-all-start.1 = ((bf16[16,32,1024]{2,1,0:T(8,128)(2,1)}), bf16[16,32,1024]{2,1,0:T(8,128)(2,1)S(1)}, u32[]{:S(2)}, u32[]{:S(2)}) async-start(bf16[16,32,1024]{2,1,0:T(8,128)(2,1)} %pick_pages.1), calls=%async_computation.1 | async-start | bytes 2097152 | tf_op jit(solution)/shard_map/all_to_all | solution.py:354
  28.3 2.0 %collective-permute-start.2 = (bf16[4,128,128]{2,1,0:T(8,128)(2,1)S(1)}, bf16[4,128,128]{2,1,0:T(8,128)(2,1)S(1)}, u32[]{:S(2)}, u32[]{:S(2)}) collective-permute-start(bf16[4,128,128]{2,1,0:T(8,128)(2,1)S(1)} %pad_maximum_fusion.2), channel_id=1, source_target_pairs={{0,2},{1,3},{2,0},{3,1},{4,6},{5,7},{6,4},{7,5},{8,10},{9,11},{10,... | collective-permute-start | bytes 393224 | tf_op jit(solution)/shard_map/ppermute | solution.py:350
  30.3 11.4 %collective-permute-done.2 = bf16[4,128,128]{2,1,0:T(8,128)(2,1)S(1)} collective-permute-done((bf16[4,128,128]{2,1,0:T(8,128)(2,1)S(1)}, bf16[4,128,128]{2,1,0:T(8,128)(2,1)S(1)}, u32[]{:S(2)}, u32[]{:S(2)}) %collective-permute-start.2) | collective-permute-done | bytes 131104 | tf_op jit(solution)/shard_map/ppermute | solution.py:350
  41.8 1.0 fusion
  43.3 1.6 %copy-done = bf16[8192,128]{1,0:T(8,128)(2,1)S(1)} copy-done((bf16[8192,128]{1,0:T(8,128)(2,1)S(1)}, bf16[8192,128]{1,0:T(8,128)(2,1)}, u32[]{:S(2)}) %copy-start) | copy-done | bytes 2097176
  45.6 4.3 %norm_project.1 = (bf16[8,16,128]{2,1,0:T(8,128)(2,1)S(1)}, bf16[8,16,128]{2,1,0:T(8,128)(2,1)S(1)}) custom-call(bf16[1024,128]{1,0:T(8,128)(2,1)S(1)} %bitcast.17, bf16[1024,128]{1,0:T(8,128)(2,1)S(1)} %bitcast.19, bf16[64,128]{1,0:T(8,128)(2,1)S(1)} %bitcast.25, bf16[8192,512]{1,0:T(8,128)(2,1)} %wq_ref.1, bf16[8192,128]{1,0:T(8,128)(2,1)S(1)} %copy-done), custom_call_target="tpu_custom_call" | custom-call | flops 335544320 | bytes 10485760 | tf_op jit(solution)/shard_map/norm_project/pallas_call | solution.py:197
  50.3 0.9 collective-permute-done.4.rest_1_
  51.5 3.7 %collective-permute-done.5.rest_2_ = bf16[2,4,16,128]{3,2,1,0:T(8,128)(2,1)S(1)} collective-permute-done((bf16[2,4,16,128]{3,2,1,0:T(8,128)(2,1)S(1)}, bf16[2,4,16,128]{3,2,1,0:T(8,128)(2,1)S(1)}, u32[]{:S(2)}, u32[]{:S(2)}) %collective-permute-start.5) | collective-permute-done | bytes 32800 | tf_op jit(solution)/shard_map/ppermute | solution.py:350
  55.4 3.8 %collective-permute-done.6.rest_3_ = bf16[4,2,16,128]{3,2,1,0:T(8,128)(2,1)S(1)} collective-permute-done((bf16[4,2,16,128]{3,2,1,0:T(8,128)(2,1)S(1)}, bf16[4,2,16,128]{3,2,1,0:T(8,128)(2,1)S(1)}, u32[]{:S(2)}, u32[]{:S(2)}) %collective-permute-start.6) | collective-permute-done | bytes 32800 | tf_op jit(solution)/shard_map/ppermute | solution.py:350
  59.2 2.8 %collective-permute-start.7 = (bf16[8,1,16,128]{3,2,1,0:T(8,128)(2,1)S(1)}, bf16[8,1,16,128]{3,2,1,0:T(8,128)(2,1)S(1)}, u32[]{:S(2)}, u32[]{:S(2)}) collective-permute-start(bf16[8,1,16,128]{3,2,1,0:T(8,128)(2,1)S(1)} %pad_maximum_fusion.6), channel_id=1, source_target_pairs={{0,8},{1,9},{2,10},{3,11},{4,12},{5,13},{6,14},{7,15},{8,0},{9,1},... | collective-permute-start | bytes 98312 | tf_op jit(solution)/shard_map/ppermute | solution.py:350
  62.2 0.8 turned_keys.1.keys_ref
  63.0 1.1 %collective-permute-done.7.rest_4_ = bf16[8,1,16,128]{3,2,1,0:T(8,128)(2,1)S(1)} collective-permute-done((bf16[8,1,16,128]{3,2,1,0:T(8,128)(2,1)S(1)}, bf16[8,1,16,128]{3,2,1,0:T(8,128)(2,1)S(1)}, u32[]{:S(2)}, u32[]{:S(2)}) %collective-permute-start.7) | collective-permute-done | bytes 32800 | tf_op jit(solution)/shard_map/ppermute | solution.py:350
  64.1 3.3 %attend.1 = bf16[128,128]{1,0:T(8,128)(2,1)S(1)} custom-call(s32[16]{0:T(128)S(1)} %copy-done.4, s32[16]{0:T(128)S(1)} %iota_xor_fusion.where_ref, bf16[512,1024]{1,0:T(8,128)(2,1)S(1)} %turned_keys.1.keys_ref, f32[2,512]{1,0:T(2,128)S(1)} %and_select_fusion.bias_ref, f32[2,128]{1,0:T(2,128)S(1)} %get-tuple-element.27.cos_ref, ...), custom_call_target="tpu_custom_call" | custom-call | flops 33554432 | bytes 2097152 | tf_op jit(solution)/shard_map/attend/pallas_call | solution.py:289
  67.4 12.0 %all_to_all.20 = bf16[16,8,128]{2,1,0:T(8,128)(2,1)S(1)} all-to-all(bf16[16,8,128]{2,1,0:T(8,128)(2,1)S(1)} %bitcast.20), channel_id=1, replica_groups=mesh['groups'=2,'session'=16] {'session'}, dimensions={0} | all-to-all | bytes 65536 | tf_op jit(solution)/shard_map/all_to_all | solution.py:354
  79.5 3.9 %output_project.1 = bf16[2048,128]{1,0:T(8,128)(2,1)S(1)} custom-call(bf16[32,512]{1,0:T(8,128)(2,1)S(1)} %reshape_reshape.3.lhs_ref, bf16[512,8192]{1,0:T(8,128)(2,1)} %weight_ref.1), custom_call_target="tpu_custom_call" | custom-call | flops 268435456 | bytes 8388608 | tf_op jit(solution)/shard_map/output_project/pallas_call | solution.py:331
  83.4 17.1 %all_to_all.21 = bf16[16,128,128]{2,1,0:T(8,128)(2,1)S(1)} all-to-all(bf16[16,128,128]{2,1,0:T(8,128)(2,1)S(1)} %bitcast.15), channel_id=1, replica_groups=mesh['groups'=2,'session'=16] {'session'}, dimensions={0} | all-to-all | bytes 1048576 | tf_op jit(solution)/shard_map/all_to_all | solution.py:354
  (50 shorter events, 4.4 us)
Async XLA Ops:
  1.4 17.5 %all-to-all-start = ((s32[16,1,2]{2,1,0:T(1,128)}), s32[16,1,2]{2,1,0:T(1,128)S(1)}, u32[]{:S(2)}, u32[]{:S(2)}) async-start(s32[16,1,2]{2,1,0:T(1,128)} %get-tuple-element.13), calls=%async_computation | async-start | bytes 16384 | tf_op jit(solution)/shard_map/all_to_all | solution.py:354
  9.6 4.9 %collective-permute-start = (bf16[1,128,128]{2,1,0:T(8,128)(2,1)S(1)}, bf16[1,128,128]{2,1,0:T(8,128)(2,1)S(1)}, u32[]{:S(2)}, u32[]{:S(2)}) collective-permute-start(bf16[1,128,128]{2,1,0:T(8,128)(2,1)S(1)} %reshape_squeeze.3), channel_id=1, source_target_pairs={{0,8},{1,9},{2,10},{3,11},{4,12},{5,13},{6,14},{7,15},{8,0},{9,1},... | collective-permute-start | bytes 98312 | tf_op jit(solution)/shard_map/ppermute | solution.py:350
  14.5 4.3 %collective-permute-start.1 = (bf16[2,128,128]{2,1,0:T(8,128)(2,1)S(1)}, bf16[2,128,128]{2,1,0:T(8,128)(2,1)S(1)}, u32[]{:S(2)}, u32[]{:S(2)}) collective-permute-start(bf16[2,128,128]{2,1,0:T(8,128)(2,1)S(1)} %pad_maximum_fusion.3), channel_id=1, source_target_pairs={{0,4},{1,5},{2,6},{3,7},{4,0},{5,1},{6,2},{7,3},{8,12},{9,13},{10,... | collective-permute-start | bytes 196616 | tf_op jit(solution)/shard_map/ppermute | solution.py:350
  18.9 1.2 %copy-start.1 = (bf16[32,16,1024]{2,1,0:T(8,128)(2,1)S(1)}, bf16[32,16,1024]{2,1,0:T(8,128)(2,1)}, u32[]{:S(2)}) copy-start(bf16[32,16,1024]{2,1,0:T(8,128)(2,1)} %store_ref.1) | copy-start | bytes 3145732
  21.8 40.2 %copy-start.5 = (bf16[1,512,160]{1,2,0:T(8,128)(2,1)S(1)}, bf16[1,512,160]{1,2,0:T(8,128)(2,1)}, u32[]{:S(2)}) copy-start(bf16[1,512,160]{1,2,0:T(8,128)(2,1)} %param.16) | copy-start | bytes 491524
  21.8 40.4 %copy-start.2 = (bf16[1,160,1024]{2,1,0:T(8,128)(2,1)S(1)}, bf16[1,160,1024]{2,1,0:T(8,128)(2,1)}, u32[]{:S(2)}) copy-start(bf16[1,160,1024]{2,1,0:T(8,128)(2,1)} %param.17) | copy-start | bytes 983044
  21.8 42.3 %all-to-all-start.1 = ((bf16[16,32,1024]{2,1,0:T(8,128)(2,1)}), bf16[16,32,1024]{2,1,0:T(8,128)(2,1)S(1)}, u32[]{:S(2)}, u32[]{:S(2)}) async-start(bf16[16,32,1024]{2,1,0:T(8,128)(2,1)} %pick_pages.1), calls=%async_computation.1 | async-start | bytes 2097152 | tf_op jit(solution)/shard_map/all_to_all | solution.py:354
  28.3 35.8 %copy-start.4 = (s32[16]{0:T(128)S(1)}, s32[16]{0:T(128)}, u32[]{:S(2)}) copy-start(s32[16]{0:T(128)} %get-tuple-element.12.holder_ref) | copy-start | bytes 196
  28.3 13.4 %collective-permute-start.2 = (bf16[4,128,128]{2,1,0:T(8,128)(2,1)S(1)}, bf16[4,128,128]{2,1,0:T(8,128)(2,1)S(1)}, u32[]{:S(2)}, u32[]{:S(2)}) collective-permute-start(bf16[4,128,128]{2,1,0:T(8,128)(2,1)S(1)} %pad_maximum_fusion.2), channel_id=1, source_target_pairs={{0,2},{1,3},{2,0},{3,1},{4,6},{5,7},{6,4},{7,5},{8,10},{9,11},{10,... | collective-permute-start | bytes 393224 | tf_op jit(solution)/shard_map/ppermute | solution.py:350
  41.7 1.6 %collective-permute-start.3 = (bf16[8,128,128]{2,1,0:T(8,128)(2,1)S(1)}, bf16[8,128,128]{2,1,0:T(8,128)(2,1)S(1)}, u32[]{:S(2)}, u32[]{:S(2)}) collective-permute-start(bf16[8,128,128]{2,1,0:T(8,128)(2,1)S(1)} %constant_dynamic-update-slice_fusion), channel_id=1, source_target_pairs={{0,1},{1,0},{2,3},{3,2},{4,5},{5,4},{6,7},{7,6},{8,9},{9,8},{10,11... | collective-permute-start | bytes 786440 | tf_op jit(solution)/shard_map/ppermute | solution.py:350
  43.3 1.6 %copy-start = (bf16[8192,128]{1,0:T(8,128)(2,1)S(1)}, bf16[8192,128]{1,0:T(8,128)(2,1)}, u32[]{:S(2)}) copy-start(bf16[8192,128]{1,0:T(8,128)(2,1)} %wk_ref.1) | copy-start | bytes 6291460
  44.9 0.7 copy-start.3
  49.9 1.3 %collective-permute-start.4 = (bf16[1,8,16,128]{3,2,1,0:T(8,128)(2,1)S(1)}, bf16[1,8,16,128]{3,2,1,0:T(8,128)(2,1)S(1)}, u32[]{:S(2)}, u32[]{:S(2)}) collective-permute-start(bf16[1,8,16,128]{3,2,1,0:T(8,128)(2,1)S(1)} %bitcast.26), channel_id=1, source_target_pairs={{0,1},{1,0},{2,3},{3,2},{4,5},{5,4},{6,7},{7,6},{8,9},{9,8},{10,11... | collective-permute-start | bytes 98312 | tf_op jit(solution)/shard_map/ppermute | solution.py:350
  51.2 4.0 %collective-permute-start.5 = (bf16[2,4,16,128]{3,2,1,0:T(8,128)(2,1)S(1)}, bf16[2,4,16,128]{3,2,1,0:T(8,128)(2,1)S(1)}, u32[]{:S(2)}, u32[]{:S(2)}) collective-permute-start(bf16[2,4,16,128]{3,2,1,0:T(8,128)(2,1)S(1)} %pad_maximum_fusion.4), channel_id=1, source_target_pairs={{0,2},{1,3},{2,0},{3,1},{4,6},{5,7},{6,4},{7,5},{8,10},{9,11},{10,... | collective-permute-start | bytes 98312 | tf_op jit(solution)/shard_map/ppermute | solution.py:350
  55.2 4.0 %collective-permute-start.6 = (bf16[4,2,16,128]{3,2,1,0:T(8,128)(2,1)S(1)}, bf16[4,2,16,128]{3,2,1,0:T(8,128)(2,1)S(1)}, u32[]{:S(2)}, u32[]{:S(2)}) collective-permute-start(bf16[4,2,16,128]{3,2,1,0:T(8,128)(2,1)S(1)} %pad_maximum_fusion.5), channel_id=1, source_target_pairs={{0,4},{1,5},{2,6},{3,7},{4,0},{5,1},{6,2},{7,3},{8,12},{9,13},{10,... | collective-permute-start | bytes 98312 | tf_op jit(solution)/shard_map/ppermute | solution.py:350
  59.2 4.9 %collective-permute-start.7 = (bf16[8,1,16,128]{3,2,1,0:T(8,128)(2,1)S(1)}, bf16[8,1,16,128]{3,2,1,0:T(8,128)(2,1)S(1)}, u32[]{:S(2)}, u32[]{:S(2)}) collective-permute-start(bf16[8,1,16,128]{3,2,1,0:T(8,128)(2,1)S(1)} %pad_maximum_fusion.6), channel_id=1, source_target_pairs={{0,8},{1,9},{2,10},{3,11},{4,12},{5,13},{6,14},{7,15},{8,0},{9,1},... | collective-permute-start | bytes 98312 | tf_op jit(solution)/shard_map/ppermute | solution.py:350

commit v4 on v3

--- a/solution.py
+++ b/solution.py
@@ -14,6 +14,7 @@
 STEPS = 2
 GROUP = HEADS // KV_HEADS
 LANES = 128
+EXTRA = 16
 AXIS = "session"
 VMEM = pltpu.VMEM
 SMEM = pltpu.SMEM
@@ -42,46 +43,80 @@
     return pl.BlockSpec(memory_space=space)
 
 
-def ask_kernel(slots_dev, slots_ref, asked_ref, holder_ref):
+def prepare_kernel(slots_dev, hidden_ref, slots_ref, block_ref, holder_ref, wide_scr):
+    steps, model = hidden_ref.shape
+    pieces = model // LANES
+    wide = hidden_ref[...].astype(F32)
+    for step in range(steps):
+        for c in range(pieces):
+            row = step * pieces + c
+            wide_scr[row : row + 1, :] = wide[step : step + 1, c * LANES : (c + 1) * LANES]
+    lane = lax.broadcasted_iota(jnp.int32, (EXTRA, LANES), 1)
+    parity = lax.broadcasted_iota(jnp.int32, (EXTRA, LANES), 0)
+    table = jnp.zeros((EXTRA, LANES), jnp.int32)
     for m in range(holder_ref.shape[0]):
         slot = slots_ref[0, 2 * m]
         holder = lax.div(slot, slots_dev)
         holder_ref[m] = holder
-        asked_ref[holder, 0, 0] = slot - holder * slots_dev
-        asked_ref[holder, 0, 1] = slots_ref[0, 2 * m + 1] - holder * slots_dev
-
-
-def ask(block_slot, devices, slots_dev):
+        base = holder * slots_dev
+        pair = jnp.where(parity == 0, slot - base, slots_ref[0, 2 * m + 1] - base)
+        table = jnp.where(lane == holder, pair, table)
+    wide_scr[steps * pieces :, :] = table.astype(F32)
+    block_ref[0] = wide_scr[...].astype(BF16)
+
+
+def prepare(hidden, block_slot, slots_dev):
+    assert slots_dev <= 256
+    steps, model = hidden.shape
+    rows = steps * model // LANES + EXTRA
     return pl.pallas_call(
-        functools.partial(ask_kernel, slots_dev),
-        in_specs=[whole(SMEM)],
-        out_specs=(whole(SMEM), whole(SMEM)),
+        functools.partial(prepare_kernel, slots_dev),
+        in_specs=[whole(), whole(SMEM)],
+        out_specs=(whole(), whole(SMEM)),
         out_shape=(
-            jax.ShapeDtypeStruct((devices, 1, 2), jnp.int32),
+            jax.ShapeDtypeStruct((1, rows, LANES), BF16),
             jax.ShapeDtypeStruct((block_slot.shape[1] // 2,), jnp.int32),
         ),
-        name="ask_pages",
-    )(block_slot)
-
-
-def pick_kernel(asked_ref, store_ref, out_ref):
+        scratch_shapes=[VMEM((rows, LANES), F32)],
+        name="prepare",
+    )(hidden, block_slot)
+
+
+def pick_kernel(order, me_ref, first_ref, second_ref, store_ref, out_ref, table_scr, table_smem, sem):
     block_len = store_ref.shape[1]
-    for i in range(asked_ref.shape[0]):
+    half, rows, _ = first_ref.shape
+    for j in range(2 * half):
+        source = first_ref if j < half else second_ref
+        asked = source[j % half, rows - EXTRA :, :].astype(F32)
+        table_scr[j] = asked[:8].astype(jnp.int32)
+    copy = pltpu.make_async_copy(table_scr, table_smem, sem)
+    copy.start()
+    copy.wait()
+    me = me_ref[0]
+    for j in range(2 * half):
+        target = jnp.bitwise_xor(me, order[j])
         for k in range(2):
-            out_ref[i, k * block_len : (k + 1) * block_len, :] = store_ref[asked_ref[i, 0, k]]
-
-
-def pick_pages(asked, store):
-    count = asked.shape[0]
+            out_ref[target, k * block_len : (k + 1) * block_len, :] = store_ref[
+                table_smem[j, k, me]
+            ]
+
+
+def pick_pages(me, first, second, store, order):
+    count = 2 * first.shape[0]
     _, block_len, width = store.shape
     return pl.pallas_call(
-        pick_kernel,
-        in_specs=[whole(SMEM), whole()],
+        functools.partial(pick_kernel, order),
+        in_specs=[whole(SMEM), whole(), whole(), whole()],
         out_specs=whole(),
         out_shape=jax.ShapeDtypeStruct((count, 2 * block_len, width), store.dtype),
-        compiler_params=pltpu.CompilerParams(vmem_limit_bytes=32 * 2**20),
+        scratch_shapes=[
+            VMEM((count, 8, LANES), jnp.int32),
+            SMEM((count, 8, LANES), jnp.int32),
+            pltpu.SemaphoreType.DMA(()),
+        ],
+        compiler_params=pltpu.CompilerParams(vmem_limit_bytes=36 * 2**20),
         name="pick_pages",
-    )(asked, store)
+    )(me, first, second, store)
 
 
 def keys_kernel(factors_ref, basis_ref, cos_ref, sin_ref, out_ref):
@@ -138,9 +173,11 @@
             copy.start()
         copies.append(pair)
     half = first_ref.shape[0]
-    x_scr[:half] = first_ref[...].astype(F32)
-    x_scr[half:] = second_ref[...].astype(F32)
-    count = 2 * half // pieces
+    count = 2 * half * STEPS
+    rows = STEPS * pieces
+    for j in range(2 * half):
+        source = first_ref if j < half else second_ref
+        x_scr[j * rows : (j + 1) * rows] = source[j % half, :rows, :].astype(F32)
     squares = jnp.zeros((count, LANES), F32)
     for c in range(pieces):
         part = x_scr[pl.ds(c, count, stride=pieces), :]
@@ -184,8 +221,8 @@
     depth, q_cols = query_weight.shape
     k_cols = kv_weight.shape[1]
     pieces = depth // LANES
-    rows = 2 * first.shape[0] // pieces
-    devices = rows // STEPS
+    devices = 2 * first.shape[0]
+    rows = devices * STEPS
     chunks = 8
     span = depth // chunks
     if fast:
@@ -378,31 +415,27 @@
     fast = q_cols == 4 * HEAD_DIM and k_cols == HEAD_DIM
     pieces = model // LANES
 
-    asked, holder = ask(block_slot, devices, slots_dev)
-    asked_here = exchange(asked)
-
-    block = hidden[:, 0].reshape(1, STEPS * pieces, LANES)
+    block, holder = prepare(hidden[:, 0], block_slot, slots_dev)
     order = [0]
     bit = devices // 2
     while bit:
-        if bit == 2:
-            block, asked_here = lax.optimization_barrier((block, asked_here))
-            sent_pages = pick_pages(asked_here, value_store)
-            fetched = exchange(sent_pages)
-            block, sent_pages = lax.optimization_barrier((block, sent_pages))
         other = swap(block, bit, devices)
         order = order + [k ^ bit for k in order]
         bit //= 2
         if bit:
             block = jnp.concatenate([block, other], axis=0)
+    me_word = me.astype(jnp.int32).reshape(1)
+    sent_pages = pick_pages(me_word, block, other, value_store, tuple(order))
+    block, other, sent_pages = lax.optimization_barrier((block, other, sent_pages))
+    fetched = exchange(sent_pages)
     if fast:
         bits = devices.bit_length() - 1
         turn = [int(format(k, "b").zfill(bits)[::-1], 2) for k in order]
     else:
         turn = order
     projected = project(
-        block.reshape(-1, LANES),
-        other.reshape(-1, LANES),
+        block,
+        other,
         norm_gain.reshape(pieces, LANES),
         query_weight,
         kv_weight,

time: 102 us -> 95.1 us (0.932)
  waiting for transfers between devices: 24.3 us -> 19.1 us
  starting transfers between devices: 23.9 us -> 21.5 us
  blocking collectives: 29.1 us -> 27.2 us
  other arithmetic: 2.31 us -> 3.85 us
  Pallas kernels: 15.5 us -> 16.6 us
    all_to_all x2 -> x1, starting transfers between devices: 13.8 us -> 6.27 us  [exchange(): return lax.all_to_all(blocks, AXIS, split_axis=0, concat_axis=0, tiled=True)]
    ppermute x8, waiting for transfers between devices: 24.3 us -> 19.1 us  [swap(): return lax.ppermute(block, AXIS, [(i, i ^ bit) for i in range(devices)])]
    ppermute x8, starting transfers between devices: 10.1 us -> 15.2 us  [swap(): return lax.ppermute(block, AXIS, [(i, i ^ bit) for i in range(devices)])]
    all_to_all x2, blocking collectives: 29.1 us -> 27.2 us  [exchange(): return lax.all_to_all(blocks, AXIS, split_axis=0, concat_axis=0, tiled=True)]
    concatenate x2, other arithmetic: 0.02 us -> 1.56 us  [local(): block = jnp.concatenate([block, other], axis=0)]
    pallas_call x2, Pallas kernels: 3.11 us -> 4.24 us  [the longest x1 2.74 us: pick_pages(): pl.pallas_call(functools.partial(pick_kernel, order), in_specs=[whole(SME...]
    unnamed x14 -> x16, local copies, waits for them, and re-layouts: 3.68 us -> 4.47 us
  transfers between devices with their start and end apart: 10 -> 9, of which waited for: 8 -> 8; matrix products, arithmetic and copies ran while one was open for 3% -> 4% of each run, Pallas kernels for 5% -> 5%
where the time goes in v4:
time: 95.1 us; the launch traced here: 94.5 us
  blocking collectives  27.2 us (29%)
  starting transfers between devices  21.5 us (23%)
  waiting for transfers between devices  19.1 us (20%)
  Pallas kernels  16.6 us (17%)
  local copies, waits for them, and re-layouts  5.35 us (6%)
  other arithmetic  3.85 us (4%)
    all_to_all x2, blocking collectives, exchange(): return lax.all_to_all(blocks, AXIS, split_axis=0, concat_axis=0, tiled=True)  27.2 us
    ppermute x8, waiting for transfers between devices, swap(): return lax.ppermute(block, AXIS, [(i, i ^ bit) for i in range(devices)])  19.1 us
    ppermute x8, starting transfers between devices, swap(): return lax.ppermute(block, AXIS, [(i, i ^ bit) for i in range(devices)])  15.2 us
    all_to_all x1, starting transfers between devices, exchange(): return lax.all_to_all(blocks, AXIS, split_axis=0, concat_axis=0, tiled=True)  6.27 us
    unnamed x16, local copies, waits for them, and re-layouts  4.47 us
    pallas_call x1, Pallas kernels, project(): pl.pallas_call(functools.partial(project_kernel, order, fast), in_specs=[...  4.32 us
    pallas_call x1, Pallas kernels, output(): pl.pallas_call(output_kernel, in_specs=[whole(), whole(pl.ANY)], out_spec...  3.95 us
    pallas_call x1, Pallas kernels, attend(): pl.pallas_call(functools.partial(attend_kernel, places), in_specs=[whole(...  3.33 us
  transfers between devices with their start and end apart: 9, of which 8 were waited for; matrix products, arithmetic and copies ran while one was open for 4% of the time, Pallas kernels for 5%

profile of v4, /device:TPU:0, one launch (start us, length us, event | category | flops | bytes accessed | tf_op | source)
XLA Modules:
  0.0 94.5 jit_solution(3504413796222631491)
XLA Ops:
  0.0 1.5 %prepare.1 = (bf16[1,144,128]{2,1,0:T(8,128)(2,1)}, s32[16]{0:T(128)}) custom-call(bf16[2,8192]{1,0:T(2,128)(2,1)} %bitcast.23, s32[1,32]{1,0:T(1,128)} %slots_ref.1), custom_call_target="tpu_custom_call" | custom-call | tf_op jit(solution)/shard_map/prepare/pallas_call | solution.py:72
  1.5 4.1 %collective-permute-start = (bf16[1,144,128]{2,1,0:T(8,128)(2,1)}, bf16[1,144,128]{2,1,0:T(8,128)(2,1)S(1)}, u32[]{:S(2)}, u32[]{:S(2)}) collective-permute-start(bf16[1,144,128]{2,1,0:T(8,128)(2,1)} %get-tuple-element.13), channel_id=1, source_target_pairs={{0,8},{1,9},{2,10},{3,11},{4,12},{5,13},{6,14},{7,15},{8,0},{9,1},... | collective-permute-start | bytes 110600 | tf_op jit(solution)/shard_map/ppermute | solution.py:387
  5.6 2.5 %collective-permute-done = bf16[1,144,128]{2,1,0:T(8,128)(2,1)S(1)} collective-permute-done((bf16[1,144,128]{2,1,0:T(8,128)(2,1)}, bf16[1,144,128]{2,1,0:T(8,128)(2,1)S(1)}, u32[]{:S(2)}, u32[]{:S(2)}) %collective-permute-start) | collective-permute-done | bytes 36896 | tf_op jit(solution)/shard_map/ppermute | solution.py:387
  8.9 1.5 %collective-permute-start.1 = (bf16[2,144,128]{2,1,0:T(8,128)(2,1)S(1)}, bf16[2,144,128]{2,1,0:T(8,128)(2,1)S(1)}, u32[]{:S(2)}, u32[]{:S(2)}) collective-permute-start(bf16[2,144,128]{2,1,0:T(8,128)(2,1)S(1)} %pad_maximum_fusion.3), channel_id=1, source_target_pairs={{0,4},{1,5},{2,6},{3,7},{4,0},{5,1},{6,2},{7,3},{8,12},{9,13},{10,... | collective-permute-start | bytes 221192 | tf_op jit(solution)/shard_map/ppermute | solution.py:387
  11.2 2.1 %collective-permute-done.1 = bf16[2,144,128]{2,1,0:T(8,128)(2,1)S(1)} collective-permute-done((bf16[2,144,128]{2,1,0:T(8,128)(2,1)S(1)}, bf16[2,144,128]{2,1,0:T(8,128)(2,1)S(1)}, u32[]{:S(2)}, u32[]{:S(2)}) %collective-permute-start.1) | collective-permute-done | bytes 73760 | tf_op jit(solution)/shard_map/ppermute | solution.py:387
  14.1 1.8 %collective-permute-start.2 = (bf16[4,144,128]{2,1,0:T(8,128)(2,1)S(1)}, bf16[4,144,128]{2,1,0:T(8,128)(2,1)S(1)}, u32[]{:S(2)}, u32[]{:S(2)}) collective-permute-start(bf16[4,144,128]{2,1,0:T(8,128)(2,1)S(1)} %pad_maximum_fusion.2), channel_id=1, source_target_pairs={{0,2},{1,3},{2,0},{3,1},{4,6},{5,7},{6,4},{7,5},{8,10},{9,11},{10,... | collective-permute-start | bytes 442376 | tf_op jit(solution)/shard_map/ppermute | solution.py:387
  15.9 3.4 %collective-permute-done.2 = bf16[4,144,128]{2,1,0:T(8,128)(2,1)S(1)} collective-permute-done((bf16[4,144,128]{2,1,0:T(8,128)(2,1)S(1)}, bf16[4,144,128]{2,1,0:T(8,128)(2,1)S(1)}, u32[]{:S(2)}, u32[]{:S(2)}) %collective-permute-start.2) | collective-permute-done | bytes 147488 | tf_op jit(solution)/shard_map/ppermute | solution.py:387
  20.0 0.9 collective-permute-done.3.second_ref
  21.0 1.2 %copy-done.1 = bf16[32,16,1024]{2,1,0:T(8,128)(2,1)S(1)} copy-done((bf16[32,16,1024]{2,1,0:T(8,128)(2,1)S(1)}, bf16[32,16,1024]{2,1,0:T(8,128)(2,1)}, u32[]{:S(2)}) %copy-start.1) | copy-done | bytes 1048600
  22.2 2.7 %pick_pages.1 = bf16[16,32,1024]{2,1,0:T(8,128)(2,1)} custom-call(s32[1]{0:T(128)} %bitcast.5.me_ref, bf16[8,144,128]{2,1,0:T(8,128)(2,1)S(1)} %constant_dynamic-update-slice_fusion.first_ref, bf16[8,144,128]{2,1,0:T(8,128)(2,1)S(1)} %collective-permute-done.3.second_ref, bf16[32,16,1024]{2,1,0:T(8,128)(2,1)S(1)} %copy-done.1), custom_call_target="tpu_custom_call" | custom-call | tf_op jit(solution)/shard_map/pick_pages/pallas_call | solution.py:107
  25.0 6.3 %all-to-all-start = ((bf16[16,32,1024]{2,1,0:T(8,128)(2,1)}), bf16[16,32,1024]{2,1,0:T(8,128)(2,1)S(1)}, u32[]{:S(2)}, u32[]{:S(2)}) async-start(bf16[16,32,1024]{2,1,0:T(8,128)(2,1)} %pick_pages.1), calls=%async_computation | async-start | bytes 2097152 | tf_op jit(solution)/shard_map/all_to_all | solution.py:391
  32.3 1.0 %fusion = (f32[512,64]{1,0:T(8,128)S(1)}, f32[512,64]{1,0:T(8,128)S(1)}, f32[512,64]{1,0:T(8,128)S(1)}) fusion(f32[64]{0:T(128)S(1)} %multiply_exponential_fusion, f32[512]{0:T(512)S(1)} %iota_convert_fusion), kind=kLoop, calls=%fused_computation.5 | loop fusion | flops 65536 | bytes 395520 | tf_op jit(solution)/shard_map/neg | solution.py:38
  33.3 1.6 %copy-done = bf16[8192,128]{1,0:T(8,128)(2,1)S(1)} copy-done((bf16[8192,128]{1,0:T(8,128)(2,1)S(1)}, bf16[8192,128]{1,0:T(8,128)(2,1)}, u32[]{:S(2)}) %copy-start) | copy-done | bytes 2097176
  35.6 4.3 %norm_project.1 = (bf16[8,16,128]{2,1,0:T(8,128)(2,1)S(1)}, bf16[8,16,128]{2,1,0:T(8,128)(2,1)S(1)}) custom-call(bf16[8,144,128]{2,1,0:T(8,128)(2,1)S(1)} %constant_dynamic-update-slice_fusion.first_ref, bf16[8,144,128]{2,1,0:T(8,128)(2,1)S(1)} %collective-permute-done.3.second_ref, bf16[64,128]{1,0:T(8,128)(2,1)S(1)} %bitcast.21, bf16[8192,512]{1,0:T(8,128)(2,1)} %wq_ref.1, ...), custom_call_target="tpu_custom_call" | custom-call | flops 335544320 | bytes 10485760 | tf_op jit(solution)/shard_map/norm_project/pallas_call | solution.py:234
  41.2 1.9 %collective-permute-start.5 = (bf16[2,4,16,128]{3,2,1,0:T(8,128)(2,1)S(1)}, bf16[2,4,16,128]{3,2,1,0:T(8,128)(2,1)S(1)}, u32[]{:S(2)}, u32[]{:S(2)}) collective-permute-start(bf16[2,4,16,128]{3,2,1,0:T(8,128)(2,1)S(1)} %pad_maximum_fusion.4), channel_id=1, source_target_pairs={{0,2},{1,3},{2,0},{3,1},{4,6},{5,7},{6,4},{7,5},{8,10},{9,11},{10,... | collective-permute-start | bytes 98312 | tf_op jit(solution)/shard_map/ppermute | solution.py:387
  43.4 2.7 %collective-permute-done.5.rest_2_ = bf16[2,4,16,128]{3,2,1,0:T(8,128)(2,1)S(1)} collective-permute-done((bf16[2,4,16,128]{3,2,1,0:T(8,128)(2,1)S(1)}, bf16[2,4,16,128]{3,2,1,0:T(8,128)(2,1)S(1)}, u32[]{:S(2)}, u32[]{:S(2)}) %collective-permute-start.5) | collective-permute-done | bytes 32800 | tf_op jit(solution)/shard_map/ppermute | solution.py:387
  46.2 1.0 %collective-permute-start.6 = (bf16[4,2,16,128]{3,2,1,0:T(8,128)(2,1)S(1)}, bf16[4,2,16,128]{3,2,1,0:T(8,128)(2,1)S(1)}, u32[]{:S(2)}, u32[]{:S(2)}) collective-permute-start(bf16[4,2,16,128]{3,2,1,0:T(8,128)(2,1)S(1)} %pad_maximum_fusion.5), channel_id=1, source_target_pairs={{0,4},{1,5},{2,6},{3,7},{4,0},{5,1},{6,2},{7,3},{8,12},{9,13},{10,... | collective-permute-start | bytes 98312 | tf_op jit(solution)/shard_map/ppermute | solution.py:387
  47.3 2.9 %collective-permute-done.6.rest_3_ = bf16[4,2,16,128]{3,2,1,0:T(8,128)(2,1)S(1)} collective-permute-done((bf16[4,2,16,128]{3,2,1,0:T(8,128)(2,1)S(1)}, bf16[4,2,16,128]{3,2,1,0:T(8,128)(2,1)S(1)}, u32[]{:S(2)}, u32[]{:S(2)}) %collective-permute-start.6) | collective-permute-done | bytes 32800 | tf_op jit(solution)/shard_map/ppermute | solution.py:387
  50.2 4.3 %collective-permute-start.7 = (bf16[8,1,16,128]{3,2,1,0:T(8,128)(2,1)S(1)}, bf16[8,1,16,128]{3,2,1,0:T(8,128)(2,1)S(1)}, u32[]{:S(2)}, u32[]{:S(2)}) collective-permute-start(bf16[8,1,16,128]{3,2,1,0:T(8,128)(2,1)S(1)} %pad_maximum_fusion.6), channel_id=1, source_target_pairs={{0,8},{1,9},{2,10},{3,11},{4,12},{5,13},{6,14},{7,15},{8,0},{9,1},... | collective-permute-start | bytes 98312 | tf_op jit(solution)/shard_map/ppermute | solution.py:387
  55.4 3.8 %collective-permute-done.7.rest_4_ = bf16[8,1,16,128]{3,2,1,0:T(8,128)(2,1)S(1)} collective-permute-done((bf16[8,1,16,128]{3,2,1,0:T(8,128)(2,1)S(1)}, bf16[8,1,16,128]{3,2,1,0:T(8,128)(2,1)S(1)}, u32[]{:S(2)}, u32[]{:S(2)}) %collective-permute-start.7) | collective-permute-done | bytes 32800 | tf_op jit(solution)/shard_map/ppermute | solution.py:387
  59.2 3.3 %attend.1 = bf16[128,128]{1,0:T(8,128)(2,1)S(1)} custom-call(s32[16]{0:T(128)S(1)} %copy-done.4, s32[16]{0:T(128)S(1)} %iota_xor_fusion.where_ref, bf16[512,1024]{1,0:T(8,128)(2,1)S(1)} %turned_keys.1.keys_ref, f32[2,512]{1,0:T(2,128)S(1)} %and_select_fusion.bias_ref, f32[2,128]{1,0:T(2,128)S(1)} %get-tuple-element.27.cos_ref, ...), custom_call_target="tpu_custom_call" | custom-call | flops 33554432 | bytes 2097152 | tf_op jit(solution)/shard_map/attend/pallas_call | solution.py:326
  62.5 10.2 %all_to_all.15 = bf16[16,8,128]{2,1,0:T(8,128)(2,1)S(1)} all-to-all(bf16[16,8,128]{2,1,0:T(8,128)(2,1)S(1)} %bitcast.16), channel_id=1, replica_groups=mesh['groups'=2,'session'=16] {'session'}, dimensions={0} | all-to-all | bytes 65536 | tf_op jit(solution)/shard_map/all_to_all | solution.py:391
  72.7 3.9 %output_project.1 = bf16[2048,128]{1,0:T(8,128)(2,1)S(1)} custom-call(bf16[32,512]{1,0:T(8,128)(2,1)S(1)} %reshape_reshape.3.lhs_ref, bf16[512,8192]{1,0:T(8,128)(2,1)} %weight_ref.1), custom_call_target="tpu_custom_call" | custom-call | flops 268435456 | bytes 8388608 | tf_op jit(solution)/shard_map/output_project/pallas_call | solution.py:368
  76.7 17.1 %all_to_all.16 = bf16[16,128,128]{2,1,0:T(8,128)(2,1)S(1)} all-to-all(bf16[16,128,128]{2,1,0:T(8,128)(2,1)S(1)} %bitcast.13), channel_id=1, replica_groups=mesh['groups'=2,'session'=16] {'session'}, dimensions={0} | all-to-all | bytes 1048576 | tf_op jit(solution)/shard_map/all_to_all | solution.py:391
  (49 shorter events, 7.5 us)
Async XLA Ops:
  1.5 6.6 %collective-permute-start = (bf16[1,144,128]{2,1,0:T(8,128)(2,1)}, bf16[1,144,128]{2,1,0:T(8,128)(2,1)S(1)}, u32[]{:S(2)}, u32[]{:S(2)}) collective-permute-start(bf16[1,144,128]{2,1,0:T(8,128)(2,1)} %get-tuple-element.13), channel_id=1, source_target_pairs={{0,8},{1,9},{2,10},{3,11},{4,12},{5,13},{6,14},{7,15},{8,0},{9,1},... | collective-permute-start | bytes 110600 | tf_op jit(solution)/shard_map/ppermute | solution.py:387
  8.9 4.4 %collective-permute-start.1 = (bf16[2,144,128]{2,1,0:T(8,128)(2,1)S(1)}, bf16[2,144,128]{2,1,0:T(8,128)(2,1)S(1)}, u32[]{:S(2)}, u32[]{:S(2)}) collective-permute-start(bf16[2,144,128]{2,1,0:T(8,128)(2,1)S(1)} %pad_maximum_fusion.3), channel_id=1, source_target_pairs={{0,4},{1,5},{2,6},{3,7},{4,0},{5,1},{6,2},{7,3},{8,12},{9,13},{10,... | collective-permute-start | bytes 221192 | tf_op jit(solution)/shard_map/ppermute | solution.py:387
  14.1 5.2 %collective-permute-start.2 = (bf16[4,144,128]{2,1,0:T(8,128)(2,1)S(1)}, bf16[4,144,128]{2,1,0:T(8,128)(2,1)S(1)}, u32[]{:S(2)}, u32[]{:S(2)}) collective-permute-start(bf16[4,144,128]{2,1,0:T(8,128)(2,1)S(1)} %pad_maximum_fusion.2), channel_id=1, source_target_pairs={{0,2},{1,3},{2,0},{3,1},{4,6},{5,7},{6,4},{7,5},{8,10},{9,11},{10,... | collective-permute-start | bytes 442376 | tf_op jit(solution)/shard_map/ppermute | solution.py:387
  19.3 1.6 %collective-permute-start.3 = (bf16[8,144,128]{2,1,0:T(8,128)(2,1)S(1)}, bf16[8,144,128]{2,1,0:T(8,128)(2,1)S(1)}, u32[]{:S(2)}, u32[]{:S(2)}) collective-permute-start(bf16[8,144,128]{2,1,0:T(8,128)(2,1)S(1)} %constant_dynamic-update-slice_fusion.first_ref), channel_id=1, source_target_pairs={{0,1},{1,0},{2,3},{3,2},{4,5},{5,4},{6,7},{7,6},{8,9},{9,8},{10,11... | collective-permute-start | bytes 884744 | tf_op jit(solution)/shard_map/ppermute | solution.py:387
  21.0 1.2 %copy-start.1 = (bf16[32,16,1024]{2,1,0:T(8,128)(2,1)S(1)}, bf16[32,16,1024]{2,1,0:T(8,128)(2,1)}, u32[]{:S(2)}) copy-start(bf16[32,16,1024]{2,1,0:T(8,128)(2,1)} %store_ref.1) | copy-start | bytes 3145732
  24.9 29.6 %copy-start.5 = (bf16[1,512,160]{1,2,0:T(8,128)(2,1)S(1)}, bf16[1,512,160]{1,2,0:T(8,128)(2,1)}, u32[]{:S(2)}) copy-start(bf16[1,512,160]{1,2,0:T(8,128)(2,1)} %param.16) | copy-start | bytes 491524
  24.9 29.7 %copy-start.2 = (bf16[1,160,1024]{2,1,0:T(8,128)(2,1)S(1)}, bf16[1,160,1024]{2,1,0:T(8,128)(2,1)}, u32[]{:S(2)}) copy-start(bf16[1,160,1024]{2,1,0:T(8,128)(2,1)} %param.17) | copy-start | bytes 983044
  25.0 34.2 %all-to-all-start = ((bf16[16,32,1024]{2,1,0:T(8,128)(2,1)}), bf16[16,32,1024]{2,1,0:T(8,128)(2,1)S(1)}, u32[]{:S(2)}, u32[]{:S(2)}) async-start(bf16[16,32,1024]{2,1,0:T(8,128)(2,1)} %pick_pages.1), calls=%async_computation | async-start | bytes 2097152 | tf_op jit(solution)/shard_map/all_to_all | solution.py:391
  31.2 28.0 %copy-start.4 = (s32[16]{0:T(128)S(1)}, s32[16]{0:T(128)}, u32[]{:S(2)}) copy-start(s32[16]{0:T(128)} %get-tuple-element.12.holder_ref) | copy-start | bytes 196
  33.3 1.6 %copy-start = (bf16[8192,128]{1,0:T(8,128)(2,1)S(1)}, bf16[8192,128]{1,0:T(8,128)(2,1)}, u32[]{:S(2)}) copy-start(bf16[8192,128]{1,0:T(8,128)(2,1)} %wk_ref.1) | copy-start | bytes 6291460
  34.9 0.7 copy-start.3
  39.9 1.3 %collective-permute-start.4 = (bf16[1,8,16,128]{3,2,1,0:T(8,128)(2,1)S(1)}, bf16[1,8,16,128]{3,2,1,0:T(8,128)(2,1)S(1)}, u32[]{:S(2)}, u32[]{:S(2)}) collective-permute-start(bf16[1,8,16,128]{3,2,1,0:T(8,128)(2,1)S(1)} %bitcast.22), channel_id=1, source_target_pairs={{0,1},{1,0},{2,3},{3,2},{4,5},{5,4},{6,7},{7,6},{8,9},{9,8},{10,11... | collective-permute-start | bytes 98312 | tf_op jit(solution)/shard_map/ppermute | solution.py:387
  41.2 4.9 %collective-permute-start.5 = (bf16[2,4,16,128]{3,2,1,0:T(8,128)(2,1)S(1)}, bf16[2,4,16,128]{3,2,1,0:T(8,128)(2,1)S(1)}, u32[]{:S(2)}, u32[]{:S(2)}) collective-permute-start(bf16[2,4,16,128]{3,2,1,0:T(8,128)(2,1)S(1)} %pad_maximum_fusion.4), channel_id=1, source_target_pairs={{0,2},{1,3},{2,0},{3,1},{4,6},{5,7},{6,4},{7,5},{8,10},{9,11},{10,... | collective-permute-start | bytes 98312 | tf_op jit(solution)/shard_map/ppermute | solution.py:387
  46.2 4.0 %collective-permute-start.6 = (bf16[4,2,16,128]{3,2,1,0:T(8,128)(2,1)S(1)}, bf16[4,2,16,128]{3,2,1,0:T(8,128)(2,1)S(1)}, u32[]{:S(2)}, u32[]{:S(2)}) collective-permute-start(bf16[4,2,16,128]{3,2,1,0:T(8,128)(2,1)S(1)} %pad_maximum_fusion.5), channel_id=1, source_target_pairs={{0,4},{1,5},{2,6},{3,7},{4,0},{5,1},{6,2},{7,3},{8,12},{9,13},{10,... | collective-permute-start | bytes 98312 | tf_op jit(solution)/shard_map/ppermute | solution.py:387
  50.2 9.0 %collective-permute-start.7 = (bf16[8,1,16,128]{3,2,1,0:T(8,128)(2,1)S(1)}, bf16[8,1,16,128]{3,2,1,0:T(8,128)(2,1)S(1)}, u32[]{:S(2)}, u32[]{:S(2)}) collective-permute-start(bf16[8,1,16,128]{3,2,1,0:T(8,128)(2,1)S(1)} %pad_maximum_fusion.6), channel_id=1, source_target_pairs={{0,8},{1,9},{2,10},{3,11},{4,12},{5,13},{6,14},{7,15},{8,0},{9,1},... | collective-permute-start | bytes 98312 | tf_op jit(solution)/shard_map/ppermute | solution.py:387

commit v5 on v4

--- a/solution.py
+++ b/solution.py
@@ -15,6 +15,7 @@
 GROUP = HEADS // KV_HEADS
 LANES = 128
 EXTRA = 16
+PLANE = 4
 AXIS = "session"
 VMEM = pltpu.VMEM
 SMEM = pltpu.SMEM
@@ -43,7 +44,7 @@
     return pl.BlockSpec(memory_space=space)
 
 
-def prepare_kernel(slots_dev, hidden_ref, slots_ref, block_ref, holder_ref, wide_scr):
+def prepare_kernel(slots_dev, hidden_ref, slots_ref, block_ref, holder_ref, pair_ref, wide_scr):
     steps, model = hidden_ref.shape
     pieces = model // LANES
     wide = hidden_ref[...].astype(F32)
@@ -58,6 +59,7 @@
         slot = slots_ref[0, 2 * m]
         holder = lax.div(slot, slots_dev)
         holder_ref[m] = holder
+        pair_ref[holder] = m
         base = holder * slots_dev
         pair = jnp.where(parity == 0, slot - base, slots_ref[0, 2 * m + 1] - base)
         table = jnp.where(lane == holder, pair, table)
@@ -72,9 +74,10 @@
     return pl.pallas_call(
         functools.partial(prepare_kernel, slots_dev),
         in_specs=[whole(), whole(SMEM)],
-        out_specs=(whole(), whole(SMEM)),
+        out_specs=(whole(), whole(SMEM), whole(SMEM)),
         out_shape=(
             jax.ShapeDtypeStruct((1, rows, LANES), BF16),
+            jax.ShapeDtypeStruct((block_slot.shape[1] // 2,), jnp.int32),
             jax.ShapeDtypeStruct((block_slot.shape[1] // 2,), jnp.int32),
         ),
         scratch_shapes=[VMEM((rows, LANES), F32)],
@@ -119,8 +122,124 @@
     )(me, first, second, store)
 
 
-def keys_kernel(factors_ref, basis_ref, cos_ref, sin_ref, out_ref):
-    product = jnp.dot(factors_ref[...], basis_ref[...], preferred_element_type=F32)
+def split_kernel(x_ref, store_ref, keep_ref, send_ref):
+    slots, block_len, width = store_ref.shape
+    for x in range(2):
+
+        @pl.when(x_ref[0] == x)
+        def _():
+            for head in range(width // LANES):
+                target = keep_ref if head % 2 == x else send_ref
+                lanes = slice(head // 2 * LANES, (head // 2 + 1) * LANES)
+                part = store_ref[:, :, head * LANES : (head + 1) * LANES]
+                target[:, lanes] = part.reshape(slots * block_len, LANES)
+
+
+def split_values(x, store):
+    slots, block_len, width = store.shape
+    half = jax.ShapeDtypeStruct((slots * block_len, width // 2), store.dtype)
+    return pl.pallas_call(
+        split_kernel,
+        in_specs=[whole(SMEM), whole()],
+        out_specs=(whole(), whole()),
+        out_shape=(half, half),
+        compiler_params=pltpu.CompilerParams(vmem_limit_bytes=16 * 2**20),
+        name="split_values",
+    )(x, store)
+
+
+def rows_kernel(order, me_ref, first_ref, second_ref, out_ref, table_scr, table_smem, sem):
+    half, rows, _ = first_ref.shape
+    for j in range(2 * half):
+        source = first_ref if j < half else second_ref
+        asked = source[j % half, rows - EXTRA :, :].astype(F32)
+        table_scr[j] = asked[:8].astype(jnp.int32)
+    copy = pltpu.make_async_copy(table_scr, table_smem, sem)
+    copy.start()
+    copy.wait()
+    me = me_ref[0]
+    plane = jnp.bitwise_and(me, -PLANE)
+    for j in range(2 * half):
+        session = jnp.bitwise_xor(me, order[j])
+        for k in range(2):
+            for b in range(PLANE):
+                out_ref[session * (2 * PLANE) + k * PLANE + b] = table_smem[j, k, plane + b]
+
+
+def plane_rows(me, first, second, order):
+    count = 2 * first.shape[0]
+    return pl.pallas_call(
+        functools.partial(rows_kernel, order),
+        in_specs=[whole(SMEM), whole(), whole()],
+        out_specs=whole(SMEM),
+        out_shape=jax.ShapeDtypeStruct((count * 2 * PLANE,), jnp.int32),
+        scratch_shapes=[
+            VMEM((count, 8, LANES), jnp.int32),
+            SMEM((count, 8, LANES), jnp.int32),
+            pltpu.SemaphoreType.DMA(()),
+        ],
+        name="plane_rows",
+    )(me, first, second)
+
+
+def mix_kernel(me_ref, rows_ref, weights_ref, *rest):
+    stores, (out_ref, values_scr, sum_scr) = rest[:PLANE], rest[PLANE:]
+    me = me_ref[0]
+    low = jnp.bitwise_and(me, PLANE - 1)
+    z_me = lax.div(me, PLANE)
+    sessions = weights_ref.shape[0]
+    planes = out_ref.shape[0]
+    block_len = values_scr.shape[1] // (2 * PLANE)
+    for session in range(sessions):
+        for q, store in enumerate(stores):
+            device = jnp.bitwise_xor(low, q)
+            for k in range(2):
+                row = rows_ref[session * (2 * PLANE) + k * PLANE + device]
+                source = pl.ds(pl.multiple_of(row * block_len, block_len), block_len)
+                target = pl.ds(
+                    pl.multiple_of((device * 2 + k) * block_len, block_len), block_len
+                )
+                values_scr[session, target, :] = store[source, :]
+        block = weights_ref[session]
+        product = jnp.dot(
+            block[: planes * 8], values_scr[session], preferred_element_type=F32
+        )
+        mine = slice(session * 8, (session + 1) * 8)
+        for z in range(planes):
+            sum_scr[z, mine, :] = product[z * 8 : (z + 1) * 8, z * LANES : (z + 1) * LANES]
+        recent = block[planes * 8 :].astype(F32)
+        sum_scr[z_me, mine, :] += recent[:8]
+    out_ref[...] = sum_scr[...].astype(BF16)
+
+
+def mix(me, rows, weights, stores):
+    sessions = weights.shape[0]
+    planes = stores[0].shape[1] // LANES
+    shape = (planes, sessions * 8, LANES)
+    return pl.pallas_call(
+        mix_kernel,
+        in_specs=[whole(SMEM)] * 2 + [whole()] * (1 + PLANE),
+        out_specs=whole(),
+        out_shape=jax.ShapeDtypeStruct(shape, BF16),
+        scratch_shapes=[VMEM((sessions, LANES, planes * LANES), BF16), VMEM(shape, F32)],
+        compiler_params=pltpu.CompilerParams(vmem_limit_bytes=16 * 2**20),
+        cost_estimate=pl.CostEstimate(
+            flops=2 * sessions * 32 * LANES * planes * LANES,
+            bytes_accessed=4 * stores[0].size * PLANE,
+            transcendentals=0,
+        ),
+        name="mix_values",
+    )(me, rows, weights, *stores)
+
+
+def keys_kernel(pair_ref, factors_ref, basis_ref, cos_ref, sin_ref, out_ref, rows_scr):
+    span = factors_ref.shape[0] // pair_ref.shape[0]
+    count = rows_scr.shape[0] // span
+    base = pl.program_id(0) * count
+    for p in range(count):
+        source = pl.ds(pl.multiple_of(pair_ref[base + p] * span, span), span)
+        rows_scr[p * span : (p + 1) * span, :] = factors_ref[source, :]
+    product = jnp.dot(rows_scr[...], basis_ref[...], preferred_element_type=F32)
     cosine, sine = cos_ref[...], sin_ref[...]
     for head in range(KV_HEADS):
         lanes = slice(head * HEAD_DIM, (head + 1) * HEAD_DIM)
@@ -129,7 +248,7 @@
         out_ref[:, lanes] = turned.astype(BF16)
 
 
-def make_keys(factors, basis, cosine, sine):
+def make_keys(pair, factors, basis, cosine, sine):
     seq, rank = factors.shape
     width = basis.shape[1]
     rows = min(seq, 512)
@@ -137,26 +256,27 @@
         keys_kernel,
         grid=(seq // rows,),
         in_specs=[
-            pl.BlockSpec((rows, rank), lambda i: (i, 0)),
+            whole(SMEM),
+            pl.BlockSpec((seq, rank), lambda i: (0, 0)),
             pl.BlockSpec((rank, width), lambda i: (0, 0)),
             pl.BlockSpec((rows, HEAD_DIM), lambda i: (i, 0)),
             pl.BlockSpec((rows, HEAD_DIM), lambda i: (i, 0)),
         ],
         out_specs=pl.BlockSpec((rows, width), lambda i: (i, 0)),
         out_shape=jax.ShapeDtypeStruct((seq, width), BF16),
+        scratch_shapes=[VMEM((rows, rank), BF16)],
         compiler_params=pltpu.CompilerParams(vmem_limit_bytes=32 * 2**20),
         cost_estimate=pl.CostEstimate(
             flops=2 * seq * rank * width, bytes_accessed=4 * seq * width, transcendentals=0
         ),
         name="turned_keys",
-    )(factors, basis, cosine, sine)
+    )(pair, factors, basis, cosine, sine)
 
 
 def project_kernel(
-    order, fast, first_ref, second_ref, gain_ref, wq_ref, wk_ref, *rest
+    order, fast, me_ref, first_ref, second_ref, gain_ref, wq_ref, wk_ref, out_ref,
+    x_scr, lhs_scr, wq_buf, wk_buf, out_scr, sems,
 ):
-    out_refs = rest[: 2 if fast else 1]
-    x_scr, lhs_scr, wq_buf, wk_buf, out_scr, sems = rest[len(out_refs) :]
     depth, q_cols = wq_ref.shape
     k_cols = wk_ref.shape[1]
     chunks = wq_buf.shape[0]
@@ -196,12 +316,14 @@
         q_sum = q_sum + jnp.dot(lhs, wq_buf[i], preferred_element_type=F32)
         k_sum = k_sum + jnp.dot(lhs, wk_buf[i], preferred_element_type=F32)
     if not fast:
-        out_refs[0][:, :q_cols] = q_sum.astype(BF16)
-        out_refs[0][:, q_cols:] = k_sum.astype(BF16)
+        out_ref[:, :q_cols] = q_sum.astype(BF16)
+        out_ref[:, q_cols:] = k_sum.astype(BF16)
         return
+    me = me_ref[0]
     per = q_cols // LANES
     out_scr[...] = jnp.zeros_like(out_scr)
-    for j, place in enumerate(order):
+    for j, other in enumerate(order):
+        place = jnp.bitwise_xor(me, other)
         for step in range(STEPS):
             row = j * STEPS + step
             for c in range(per):
@@ -211,13 +333,10 @@
             out_scr[place, STEPS * per + step : STEPS * per + step + 1, :] = k_sum[
                 row : row + 1, :
             ]
-    near_ref, far_ref = out_refs
-    half = near_ref.shape[0]
-    near_ref[...] = out_scr[:half].astype(BF16)
-    far_ref[...] = out_scr[half:].astype(BF16)
-
-
-def project(first, second, gain, query_weight, kv_weight, order, fast):
+    out_ref[...] = out_scr[...].astype(BF16)
+
+
+def project(me, first, second, gain, query_weight, kv_weight, order, fast):
     depth, q_cols = query_weight.shape
     k_cols = kv_weight.shape[1]
     pieces = depth // LANES
@@ -225,17 +344,12 @@
     rows = devices * STEPS
     chunks = 8
     span = depth // chunks
-    if fast:
-        shape = (jax.ShapeDtypeStruct((devices // 2, 16, LANES), BF16),) * 2
-        out_specs = (whole(), whole())
-    else:
-        shape = jax.ShapeDtypeStruct((rows, q_cols + k_cols), BF16)
-        out_specs = whole()
+    shape = (devices, 16, LANES) if fast else (rows, q_cols + k_cols)
     return pl.pallas_call(
         functools.partial(project_kernel, order, fast),
-        in_specs=[whole(), whole(), whole(), whole(pl.ANY), whole(pl.ANY)],
-        out_specs=out_specs,
-        out_shape=shape,
+        in_specs=[whole(SMEM), whole(), whole(), whole(), whole(pl.ANY), whole(pl.ANY)],
+        out_specs=whole(),
+        out_shape=jax.ShapeDtypeStruct(shape, BF16),
         scratch_shapes=[
             VMEM((rows * pieces, LANES), F32),
             VMEM((rows, depth), BF16),
@@ -251,27 +365,21 @@
             transcendentals=0,
         ),
         name="norm_project",
-    )(first, second, gain, query_weight, kv_weight)
-
-
-def attend_kernel(
-    places, holder_ref, where_ref, keys_ref, bias_ref, cos_ref, sin_ref, pages_ref, *rest
-):
-    pieces = rest[:-3]
-    out_ref, values_scr, columns_scr = rest[-3:]
-    for r, (piece, row) in enumerate(places):
-        columns_scr[where_ref[r]] = pieces[piece][row, 0].astype(F32)
-    seq = keys_ref.shape[0]
-    pairs, pair_rows = pages_ref.shape[0], pages_ref.shape[1]
+    )(me, first, second, gain, query_weight, kv_weight)
+
+
+def attend_kernel(fast, columns_ref, keys_ref, bias_ref, cos_ref, sin_ref, *rest):
+    pages_ref, out_ref, out_scr = (None, *rest) if fast else rest
     score_scale = 1.0 / math.sqrt(HEAD_DIM)
     half = HEAD_DIM // 2
     rows = 2 * GROUP
-    for m in range(pairs):
-        values_scr[m * pair_rows : (m + 1) * pair_rows, :] = pages_ref[holder_ref[m]]
-    columns = columns_scr[...]
+    columns = columns_ref[...].astype(F32)
     count = columns.shape[0]
     query = columns[:, :8, :].reshape(count * 8, HEAD_DIM)
     fresh = columns[:, 8:, :]
+    if fast:
+        planes = count // PLANE
+        out_scr[...] = jnp.zeros_like(out_scr)
     row_step = lax.rem(lax.broadcasted_iota(jnp.int32, (count * 8, 1), 0) // 4, STEPS)
     later = row_step == 1
     cosine = jnp.where(later, cos_ref[1:2, :], cos_ref[0:1, :])
@@ -315,20 +423,43 @@
         weights = (cache_exp / denominator).astype(BF16)
         weight0 = (exp0 / denominator).astype(BF16).astype(F32)
         weight1 = (exp1 / denominator).astype(BF16).astype(F32)
-        mixed = jnp.dot(weights, values_scr[:, lanes], preferred_element_type=F32)
-        mixed = mixed + weight0 * fresh[KV_HEADS + head, 0:1, :]
-        mixed = mixed + weight1 * fresh[KV_HEADS + head, 1:2, :]
-        out_ref[mine, :] = mixed.astype(BF16)
-
-
-def attend(holder, where, keys, bias, cosine, sine, pages, places, pieces):
+        recent = weight0 * fresh[KV_HEADS + head, 0:1, :]
+        recent = recent + weight1 * fresh[KV_HEADS + head, 1:2, :]
+        if not fast:
+            values = pages_ref[:, :, lanes].reshape(keys_ref.shape[0], HEAD_DIM)
+            mixed = jnp.dot(weights, values, preferred_element_type=F32)
+            out_ref[mine, :] = (mixed + recent).astype(BF16)
+            continue
+        weights = weights.astype(F32)
+        z, x = divmod(head, 2)
+        for c in range(2):
+            part = slice(c * 8, (c + 1) * 8)
+            for plane in range(planes):
+                out_scr[plane * PLANE + 2 * x + c, z * 8 : (z + 1) * 8, :] = weights[
+                    part, plane * LANES : (plane + 1) * LANES
+                ]
+            out_scr[z * PLANE + 2 * x + c, planes * 8 : planes * 8 + 8, :] = recent[part]
+    if fast:
+        out_ref[...] = out_scr[...].astype(BF16)
+
+
+def attend(columns, keys, bias, cosine, sine, pages, fast):
     seq, width = keys.shape
-    return pl.pallas_call(
-        functools.partial(attend_kernel, places),
-        in_specs=[whole(SMEM)] * 2 + [whole()] * (5 + len(pieces)),
+    count = columns.shape[0]
+    if fast:
+        shape = (count, count // PLANE * 8 + 16, LANES)
+        scratch = [VMEM(shape, F32)]
+        operands = (columns, keys, bias, cosine, sine)
+    else:
+        shape = (STEPS * HEADS, HEAD_DIM)
+        scratch = [VMEM((8, LANES), F32)]
+        operands = (columns, keys, bias, cosine, sine, pages)
+    return pl.pallas_call(
+        functools.partial(attend_kernel, fast),
+        in_specs=[whole()] * len(operands),
         out_specs=whole(),
-        out_shape=jax.ShapeDtypeStruct((STEPS * HEADS, HEAD_DIM), BF16),
-        scratch_shapes=[VMEM((seq, width), BF16), VMEM((len(places), 16, LANES), F32)],
+        out_shape=jax.ShapeDtypeStruct(shape, BF16),
+        scratch_shapes=scratch,
         compiler_params=pltpu.CompilerParams(vmem_limit_bytes=48 * 2**20),
         cost_estimate=pl.CostEstimate(
             flops=4 * STEPS * HEADS * seq * HEAD_DIM,
@@ -336,12 +467,12 @@
             transcendentals=STEPS * HEADS * seq,
         ),
         name="attend",
-    )(holder, where, keys, bias, cosine, sine, pages, *pieces)
-
-
-def output_kernel(lhs_ref, weight_ref, out_ref, weight_buf, out_scr, sems):
+    )(*operands)
+
+
+def output_kernel(fast, lhs_ref, weight_ref, out_ref, weight_buf, out_scr, heads_scr, sems):
     chunks, _, span = weight_buf.shape
-    rows = lhs_ref.shape[0]
+    rows = out_ref.shape[0] * LANES // (chunks * span)
     pieces = chunks * span // LANES
     copies = []
     for i in range(chunks):
@@ -350,7 +481,17 @@
         )
         copy.start()
         copies.append(copy)
-    lhs = lhs_ref[...]
+    if fast:
+        per = heads_scr.shape[0] // rows
+        total = lhs_ref[0].astype(F32)
+        for z in range(1, lhs_ref.shape[0]):
+            total = total + lhs_ref[z].astype(F32)
+        heads_scr[...] = total
+        lhs = jnp.concatenate(
+            [heads_scr[pl.ds(g, rows, stride=per), :].astype(BF16) for g in range(per)], axis=1
+        )
+    else:
+        lhs = lhs_ref[...]
     for i in range(chunks):
         copies[i].wait()
         part = jnp.dot(lhs, weight_buf[i], preferred_element_type=F32)
@@ -361,18 +502,18 @@
     out_ref[...] = out_scr[...].astype(BF16)
 
 
-def output(lhs, weight):
-    rows, depth = lhs.shape
-    width = weight.shape[1]
+def output(lhs, weight, rows, fast):
+    depth, width = weight.shape
     chunks = 8
     return pl.pallas_call(
-        output_kernel,
+        functools.partial(output_kernel, fast),
         in_specs=[whole(), whole(pl.ANY)],
         out_specs=whole(),
         out_shape=jax.ShapeDtypeStruct((rows * width // LANES, LANES), BF16),
         scratch_shapes=[
             VMEM((chunks, depth, width // chunks), BF16),
             VMEM((rows * width // LANES, LANES), F32),
+            VMEM(lhs.shape[1:] if fast else (8, LANES), F32),
             pltpu.SemaphoreType.DMA((chunks,)),
         ],
         compiler_params=pltpu.CompilerParams(vmem_limit_bytes=48 * 2**20),
@@ -387,8 +528,10 @@
     return lax.ppermute(block, AXIS, [(i, i ^ bit) for i in range(devices)])
 
 
-def exchange(blocks):
-    return lax.all_to_all(blocks, AXIS, split_axis=0, concat_axis=0, tiled=True)
+def exchange(blocks, groups=None):
+    return lax.all_to_all(
+        blocks, AXIS, split_axis=0, concat_axis=0, tiled=True, axis_index_groups=groups
+    )
 
 
 def local(
@@ -415,7 +558,12 @@
     fast = q_cols == 4 * HEAD_DIM and k_cols == HEAD_DIM
     pieces = model // LANES
 
-    block, holder = prepare(hidden[:, 0], block_slot, slots_dev)
+    me_word = me.astype(jnp.int32).reshape(1)
+    block, holder, pair = prepare(hidden[:, 0], block_slot, slots_dev)
+    if fast:
+        keep, send = split_values((me_word // 2) % 2, value_store)
+        neighbour = swap(send, 2, devices)
+        stores = (keep, swap(keep, 1, devices), neighbour, swap(neighbour, 1, devices))
     order = [0]
     bit = devices // 2
     while bit:
@@ -424,40 +572,17 @@
         bit //= 2
         if bit:
             block = jnp.concatenate([block, other], axis=0)
-    me_word = me.astype(jnp.int32).reshape(1)
-    sent_pages = pick_pages(me_word, block, other, value_store, tuple(order))
-    block, other, sent_pages = lax.optimization_barrier((block, other, sent_pages))
-    fetched = exchange(sent_pages)
-    if fast:
-        bits = devices.bit_length() - 1
-        turn = [int(format(k, "b").zfill(bits)[::-1], 2) for k in order]
-    else:
-        turn = order
+    order = tuple(order)
+    if not fast:
+        sent_pages = pick_pages(me_word, block, other, value_store, order)
+        block, other, sent_pages = lax.optimization_barrier((block, other, sent_pages))
+        fetched = exchange(sent_pages)
     projected = project(
-        block,
-        other,
-        norm_gain.reshape(pieces, LANES),
-        query_weight,
-        kv_weight,
-        tuple(turn),
-        fast,
+        me_word, block, other, norm_gain.reshape(pieces, LANES), query_weight, kv_weight, order, fast
     )
     if fast:
-        near, far = projected
-        sent, kept, arrived = far[None], [near[None]], [near[None]]
-        places = [(0, 0)]
-        bit = 1
-        while bit < devices:
-            if bit > 1:
-                middle = kept[0].shape[1] // 2
-                sent = jnp.concatenate([part[:, middle:] for part in kept], axis=0)
-                kept = [part[:, :middle] for part in kept]
-            part = swap(sent, bit, devices)
-            places += [(len(arrived), row) for row in range(part.shape[0])]
-            arrived.append(part)
-            kept.append(part)
-            bit *= 2
-        where = jnp.bitwise_xor(me, jnp.arange(devices, dtype=jnp.int32))
+        columns = exchange(projected)
+        rows = plane_rows(me_word, block, other, order)
     else:
         targets = jnp.bitwise_xor(me, jnp.array(order, dtype=jnp.int32))
         columns = exchange(projected.reshape(devices, STEPS, q_cols + k_cols)[targets])
@@ -465,34 +590,30 @@
         query = query.transpose(1, 0, 2, 3).reshape(HEADS // 4, 8, HEAD_DIM)
         fresh = columns[:, :, q_cols:].transpose(1, 0, 2).reshape(STEPS, HEADS // 4, HEAD_DIM)
         fresh = jnp.pad(fresh.transpose(1, 0, 2), ((0, 0), (0, 8 - STEPS), (0, 0)))
-        arrived = [jnp.concatenate([query, fresh], axis=1)[:, None]]
-        places = [(0, row) for row in range(HEADS // 4)]
-        where = jnp.arange(HEADS // 4, dtype=jnp.int32)
-
-    cosine, sine = turn_tables(jnp.arange(seq, dtype=jnp.int32).astype(F32))
-    keys = make_keys(key_factors[0], key_basis[0], cosine, sine)
+        columns = jnp.concatenate([query, fresh], axis=1)
+
+    span = 2 * block_len
+    places = (pair[:, None] * span + jnp.arange(span, dtype=jnp.int32)[None, :]).reshape(-1)
+    cosine, sine = turn_tables(places.astype(F32))
+    keys = make_keys(pair, key_factors[0], key_basis[0], cosine, sine)
     picked = jnp.any(
-        selection[:, 0, :, None] == jnp.arange(pages, dtype=jnp.int32)[None, None, :], axis=1
+        selection[:, 0, :, None] == (places // block_len)[None, None, :], axis=1
     )
-    usable = jnp.repeat(picked, block_len, axis=1) & (
-        jnp.arange(seq, dtype=jnp.int32)[None, :] < lengths[0]
-    )
-    bias = jnp.where(usable, 0.0, -1e30).astype(F32)
+    bias = jnp.where(picked & (places < lengths[0])[None, :], 0.0, -1e30).astype(F32)
     new_cos, new_sin = turn_tables(
         (lengths[0] + jnp.arange(STEPS, dtype=jnp.int32)).astype(F32)
     )
-    heads = attend(
-        holder, where, keys, bias, new_cos, new_sin, fetched, tuple(places), arrived
-    )
-
     if fast:
-        rows = exchange(heads.reshape(devices, STEPS * 4, HEAD_DIM))
-        lhs = rows.reshape(devices, STEPS, 4 * HEAD_DIM).reshape(devices * STEPS, 4 * HEAD_DIM)
+        blocks = exchange(attend(columns, keys, bias, new_cos, new_sin, None, True))
+        parts = mix(me_word, rows, blocks, stores)
+        groups = [list(range(low, devices, PLANE)) for low in range(PLANE)]
+        lhs = exchange(parts, groups)
     else:
+        heads = attend(columns, keys, bias, new_cos, new_sin, fetched, False)
         flat = heads.reshape(HEADS // 4, STEPS, 4 * HEAD_DIM).transpose(1, 0, 2)
         flat = flat.reshape(STEPS, devices, model // devices).transpose(1, 0, 2)
         lhs = exchange(flat).reshape(devices * STEPS, model // devices)
-    partial = output(lhs, out_weight)
+    partial = output(lhs, out_weight, devices * STEPS, fast)
     arrived = exchange(partial.reshape(devices, STEPS * pieces, LANES))
     total = jnp.sum(arrived.astype(F32), axis=0).astype(BF16)
     return total.reshape(STEPS, 1, model)

time: 95.1 us -> 91.8 us (0.965)
  starting transfers between devices: 21.5 us -> 15.5 us
  local copies, waits for them, and re-layouts: 5.35 us -> 7.85 us
  waiting for transfers between devices: 19.1 us -> 16.7 us
  other arithmetic: 3.85 us -> 5.83 us
  Pallas kernels: 16.6 us -> 18.4 us
  blocking collectives: 27.2 us -> 25.8 us
    ppermute x8 -> x7, waiting for transfers between devices: 19.1 us -> 7.46 us  [swap(): return lax.ppermute(block, AXIS, [(i, i ^ bit) for i in range(devices)])]
    all_to_all x1 -> x2, waiting for transfers between devices: 0.01 us -> 9.26 us  [exchange(): lax.all_to_all(blocks, AXIS, split_axis=0, concat_axis=0, tiled=True, axi...]
    ppermute x8 -> x7, starting transfers between devices: 15.2 us -> 8.44 us  [swap(): return lax.ppermute(block, AXIS, [(i, i ^ bit) for i in range(devices)])]
    unnamed x16 -> x20, local copies, waits for them, and re-layouts: 4.47 us -> 7.12 us
    all_to_all x2, blocking collectives: 27.2 us -> 25.8 us  [exchange(): lax.all_to_all(blocks, AXIS, split_axis=0, concat_axis=0, tiled=True, axi...]
    pallas_call x4 -> x6, Pallas kernels: 10.8 us -> 11.9 us  [the longest x1 3.94 us: output(): pl.pallas_call(functools.partial(output_kernel, fast), in_specs=[whole(),...]
    all_to_all x1 -> x2, starting transfers between devices: 6.27 us -> 7.02 us  [exchange(): lax.all_to_all(blocks, AXIS, split_axis=0, concat_axis=0, tiled=True, axi...]
  transfers between devices with their start and end apart: 9 -> 9, of which waited for: 8 -> 5; matrix products, arithmetic and copies ran while one was open for 4% -> 8% of each run, Pallas kernels for 5% -> 12%
where the time goes in v5:
time: 91.8 us; the launch traced here: 90.9 us
  blocking collectives  25.8 us (28%)
  Pallas kernels  18.4 us (20%)
  waiting for transfers between devices  16.7 us (18%)
  starting transfers between devices  15.5 us (17%)
  local copies, waits for them, and re-layouts  7.85 us (9%)
  other arithmetic  5.83 us (6%)
    all_to_all x2, blocking collectives, exchange(): lax.all_to_all(blocks, AXIS, split_axis=0, concat_axis=0, tiled=True, axi...  25.8 us
    all_to_all x2, waiting for transfers between devices, exchange(): lax.all_to_all(blocks, AXIS, split_axis=0, concat_axis=0, tiled=True, axi...  9.26 us
    ppermute x7, starting transfers between devices, swap(): return lax.ppermute(block, AXIS, [(i, i ^ bit) for i in range(devices)])  8.44 us
    ppermute x7, waiting for transfers between devices, swap(): return lax.ppermute(block, AXIS, [(i, i ^ bit) for i in range(devices)])  7.46 us
    unnamed x20, local copies, waits for them, and re-layouts  7.12 us
    all_to_all x2, starting transfers between devices, exchange(): lax.all_to_all(blocks, AXIS, split_axis=0, concat_axis=0, tiled=True, axi...  7.02 us
    pallas_call x1, Pallas kernels, project(): pl.pallas_call(functools.partial(project_kernel, order, fast), in_specs=[...  4.98 us
    pallas_call x1, Pallas kernels, output(): pl.pallas_call(functools.partial(output_kernel, fast), in_specs=[whole(),...  3.94 us
  transfers between devices with their start and end apart: 9, of which 5 were waited for; matrix products, arithmetic and copies ran while one was open for 8% of the time, Pallas kernels for 12%

profile of v5, /device:TPU:0, one launch (start us, length us, event | category | flops | bytes accessed | tf_op | source)
XLA Modules:
  0.0 90.9 jit_solution(7273210620976380771)
XLA Ops:
  0.0 1.5 %prepare.1 = (bf16[1,144,128]{2,1,0:T(8,128)(2,1)}, s32[16]{0:T(128)}, s32[16]{0:T(128)}) custom-call(bf16[2,8192]{1,0:T(2,128)(2,1)} %bitcast.14, s32[1,32]{1,0:T(1,128)} %slots_ref.1), custom_call_target="tpu_custom_call" | custom-call | tf_op jit(solution)/shard_map/prepare/pallas_call | solution.py:74
  1.5 4.1 %collective-permute-start = (bf16[1,144,128]{2,1,0:T(8,128)(2,1)}, bf16[1,144,128]{2,1,0:T(8,128)(2,1)S(1)}, u32[]{:S(2)}, u32[]{:S(2)}) collective-permute-start(bf16[1,144,128]{2,1,0:T(8,128)(2,1)} %get-tuple-element.9), channel_id=1, source_target_pairs={{0,8},{1,9},{2,10},{3,11},{4,12},{5,13},{6,14},{7,15},{8,0},{9,1},... | collective-permute-start | bytes 110600 | tf_op jit(solution)/shard_map/ppermute | solution.py:528
  5.6 1.2 %copy-done.3 = bf16[32,16,1024]{2,1,0:T(8,128)(2,1)S(1)} copy-done((bf16[32,16,1024]{2,1,0:T(8,128)(2,1)S(1)}, bf16[32,16,1024]{2,1,0:T(8,128)(2,1)}, u32[]{:S(2)}) %copy-start.3) | copy-done | bytes 1048600
  7.1 1.5 %collective-permute-start.5 = (bf16[512,512]{1,0:T(8,128)(2,1)S(1)}, bf16[512,512]{1,0:T(8,128)(2,1)S(1)}, u32[]{:S(2)}, u32[]{:S(2)}) collective-permute-start(bf16[512,512]{1,0:T(8,128)(2,1)S(1)} %get-tuple-element.12), channel_id=1, source_target_pairs={{0,2},{1,3},{2,0},{3,1},{4,6},{5,7},{6,4},{7,5},{8,10},{9,11},{10,... | collective-permute-start | bytes 1572872 | tf_op jit(solution)/shard_map/ppermute | solution.py:528
  10.7 1.0 %fusion = (f32[512,64]{1,0:T(8,128)S(1)}, f32[512,64]{1,0:T(8,128)S(1)}, f32[512,64]{1,0:T(8,128)S(1)}) fusion(f32[64]{0:T(128)S(1)} %multiply_exponential_fusion, f32[512]{0:T(512)S(1)} %get-tuple-element.17), kind=kLoop, calls=%fused_computation.5 | loop fusion | flops 65536 | bytes 395520 | tf_op jit(solution)/shard_map/neg | solution.py:39
  11.9 1.0 %copy.13 = bf16[1,512,160]{2,1,0:T(8,128)(2,1)S(1)} copy(bf16[1,512,160]{1,2,0:T(8,128)(2,1)} %param.16) | data formatting | bytes 327680 | tf_op args[5]
  13.8 1.6 %collective-permute-start.1 = (bf16[2,144,128]{2,1,0:T(8,128)(2,1)S(1)}, bf16[2,144,128]{2,1,0:T(8,128)(2,1)S(1)}, u32[]{:S(2)}, u32[]{:S(2)}) collective-permute-start(bf16[2,144,128]{2,1,0:T(8,128)(2,1)S(1)} %pad_maximum_fusion.3), channel_id=1, source_target_pairs={{0,4},{1,5},{2,6},{3,7},{4,0},{5,1},{6,2},{7,3},{8,12},{9,13},{10,... | collective-permute-start | bytes 221192 | tf_op jit(solution)/shard_map/ppermute | solution.py:528
  16.1 2.3 %collective-permute-done.1 = bf16[2,144,128]{2,1,0:T(8,128)(2,1)S(1)} collective-permute-done((bf16[2,144,128]{2,1,0:T(8,128)(2,1)S(1)}, bf16[2,144,128]{2,1,0:T(8,128)(2,1)S(1)}, u32[]{:S(2)}, u32[]{:S(2)}) %collective-permute-start.1) | collective-permute-done | bytes 73760 | tf_op jit(solution)/shard_map/ppermute | solution.py:528
  19.9 4.9 %collective-permute-done.2 = bf16[4,144,128]{2,1,0:T(8,128)(2,1)S(1)} collective-permute-done((bf16[4,144,128]{2,1,0:T(8,128)(2,1)S(1)}, bf16[4,144,128]{2,1,0:T(8,128)(2,1)S(1)}, u32[]{:S(2)}, u32[]{:S(2)}) %collective-permute-start.2) | collective-permute-done | bytes 147488 | tf_op jit(solution)/shard_map/ppermute | solution.py:528
  26.5 1.7 %copy-done = bf16[8192,128]{1,0:T(8,128)(2,1)S(1)} copy-done((bf16[8192,128]{1,0:T(8,128)(2,1)S(1)}, bf16[8192,128]{1,0:T(8,128)(2,1)}, u32[]{:S(2)}) %copy-start) | copy-done | bytes 2097176
  28.9 5.0 %norm_project.1 = bf16[16,16,128]{2,1,0:T(8,128)(2,1)} custom-call(s32[1]{0:T(128)} %bitcast.me_ref, bf16[8,144,128]{2,1,0:T(8,128)(2,1)S(1)} %constant_dynamic-update-slice_fusion.first_ref, bf16[8,144,128]{2,1,0:T(8,128)(2,1)S(1)} %collective-permute-done.3.second_ref, bf16[64,128]{1,0:T(8,128)(2,1)S(1)} %bitcast.13, bf16[8192,512]{1,0:T(8,128)(2,1)} %wq_ref.1, ...), custom_call_target="tpu_custom_call" | custom-call | flops 335544320 | bytes 10485760 | tf_op jit(solution)/shard_map/norm_project/pallas_call | solution.py:348
  33.9 3.5 %all-to-all-start = ((bf16[16,16,128]{2,1,0:T(8,128)(2,1)}), bf16[16,16,128]{2,1,0:T(8,128)(2,1)S(1)}, u32[]{:S(2)}, u32[]{:S(2)}) async-start(bf16[16,16,128]{2,1,0:T(8,128)(2,1)} %norm_project.1), calls=%async_computation | async-start | bytes 131072 | tf_op jit(solution)/shard_map/all_to_all | solution.py:532
  37.4 1.0 %copy-done.4 = bf16[1,160,1024]{2,1,0:T(8,128)(2,1)S(1)} copy-done((bf16[1,160,1024]{2,1,0:T(8,128)(2,1)S(1)}, bf16[1,160,1024]{2,1,0:T(8,128)(2,1)}, u32[]{:S(2)}) %copy-start.4) | copy-done | bytes 327704
  38.4 1.3 %turned_keys.1.keys_ref = bf16[512,1024]{1,0:T(8,128)(2,1)S(1)} custom-call(s32[16]{0:T(128)S(1)} %copy-done.7, bf16[512,160]{1,0:T(8,128)(2,1)S(1)} %bitcast.11, bf16[160,1024]{1,0:T(8,128)(2,1)S(1)} %bitcast.12, f32[512,128]{1,0:T(8,128)S(1)} %get-tuple-element.21.cos_ref, f32[512,128]{1,0:T(8,128)S(1)} %get-tuple-element.22.sin_ref), custom_call_target="tpu_custom_call" | custom-call | flops 167772160 | bytes 2097152 | tf_op jit(solution)/shard_map/turned_keys/pallas_call | solution.py:255
  39.7 0.8 pad_maximum_fusion.4
  40.5 3.7 %all-to-all-done.columns_ref = bf16[16,16,128]{2,1,0:T(8,128)(2,1)S(1)} async-done(((bf16[16,16,128]{2,1,0:T(8,128)(2,1)}), bf16[16,16,128]{2,1,0:T(8,128)(2,1)S(1)}, u32[]{:S(2)}, u32[]{:S(2)}) %all-to-all-start) | async-done | bytes 65568 | tf_op jit(solution)/shard_map/all_to_all | solution.py:532
  44.2 1.3 %attend.1 = bf16[16,48,128]{2,1,0:T(8,128)(2,1)} custom-call(bf16[16,16,128]{2,1,0:T(8,128)(2,1)S(1)} %all-to-all-done.columns_ref, bf16[512,1024]{1,0:T(8,128)(2,1)S(1)} %turned_keys.1.keys_ref, f32[2,512]{1,0:T(2,128)S(1)} %and_select_fusion.bias_ref, f32[2,128]{1,0:T(2,128)S(1)} %get-tuple-element.23.cos_ref, f32[2,128]{1,0:T(2,128)S(1)} %get-tuple-element.24.sin_ref), custom_call_target="tpu_custom_call" | custom-call | flops 33554432 | bytes 2097152 | tf_op jit(solution)/shard_map/attend/pallas_call | solution.py:457
  45.6 3.5 %all-to-all-start.1 = ((bf16[16,48,128]{2,1,0:T(8,128)(2,1)}), bf16[16,48,128]{2,1,0:T(8,128)(2,1)S(1)}, u32[]{:S(2)}, u32[]{:S(2)}) async-start(bf16[16,48,128]{2,1,0:T(8,128)(2,1)} %attend.1), calls=%async_computation.1 | async-start | bytes 393216 | tf_op jit(solution)/shard_map/all_to_all | solution.py:532
  49.1 3.4 %plane_rows.1.rows_ref = s32[128]{0:T(128)} custom-call(s32[1]{0:T(128)} %bitcast.me_ref, bf16[8,144,128]{2,1,0:T(8,128)(2,1)} %copy-done.1, bf16[8,144,128]{2,1,0:T(8,128)(2,1)} %copy-done.2), custom_call_target="tpu_custom_call" | custom-call | tf_op jit(solution)/shard_map/plane_rows/pallas_call | solution.py:171
  52.5 5.5 %all-to-all-done.1.weights_ref = bf16[16,48,128]{2,1,0:T(8,128)(2,1)S(1)} async-done(((bf16[16,48,128]{2,1,0:T(8,128)(2,1)}), bf16[16,48,128]{2,1,0:T(8,128)(2,1)S(1)}, u32[]{:S(2)}, u32[]{:S(2)}) %all-to-all-start.1) | async-done | bytes 196640 | tf_op jit(solution)/shard_map/all_to_all | solution.py:532
  58.7 1.7 %mix_values.1 = bf16[4,128,128]{2,1,0:T(8,128)(2,1)S(1)} custom-call(s32[1]{0:T(128)} %bitcast.me_ref, s32[128]{0:T(128)S(1)} %copy-done.6, bf16[16,48,128]{2,1,0:T(8,128)(2,1)S(1)} %all-to-all-done.1.weights_ref, bf16[512,512]{1,0:T(8,128)(2,1)S(1)} %get-tuple-element.11.rest_0_, bf16[512,512]{1,0:T(8,128)(2,1)} %collective-permute-done.4.rest_1_, ...), custom_call_target="tpu_custom_call" | custom-call | flops 67108864 | bytes 4194304 | tf_op jit(solution)/shard_map/mix_values/pallas_call | solution.py:219
  60.4 8.5 %all_to_all.20.lhs_ref = bf16[4,128,128]{2,1,0:T(8,128)(2,1)S(1)} all-to-all(bf16[4,128,128]{2,1,0:T(8,128)(2,1)S(1)} %mix_values.1), channel_id=1, replica_groups={{0,4,8,12},{1,5,9,13},{2,6,10,14},{3,7,11,15},{16,20,24,28},{17,21,25,2..., dimensions={0} | all-to-all | bytes 262144 | tf_op jit(solution)/shard_map/all_to_all | solution.py:532
  68.9 3.9 %output_project.1 = bf16[2048,128]{1,0:T(8,128)(2,1)S(1)} custom-call(bf16[4,128,128]{2,1,0:T(8,128)(2,1)S(1)} %all_to_all.20.lhs_ref, bf16[512,8192]{1,0:T(8,128)(2,1)} %weight_ref.1), custom_call_target="tpu_custom_call" | custom-call | flops 268435456 | bytes 8388608 | tf_op jit(solution)/shard_map/output_project/pallas_call | solution.py:508
  72.9 17.3 %all_to_all.21 = bf16[16,128,128]{2,1,0:T(8,128)(2,1)S(1)} all-to-all(bf16[16,128,128]{2,1,0:T(8,128)(2,1)S(1)} %bitcast.10), channel_id=1, replica_groups=mesh['groups'=2,'session'=16] {'session'}, dimensions={0} | all-to-all | bytes 1048576 | tf_op jit(solution)/shard_map/all_to_all | solution.py:532
  (42 shorter events, 8.5 us)
Async XLA Ops:
  1.5 35.9 %copy-start.7 = (s32[16]{0:T(128)S(1)}, s32[16]{0:T(128)}, u32[]{:S(2)}) copy-start(s32[16]{0:T(128)} %get-tuple-element.10.pair_ref) | copy-start | bytes 196
  1.5 11.4 %collective-permute-start = (bf16[1,144,128]{2,1,0:T(8,128)(2,1)}, bf16[1,144,128]{2,1,0:T(8,128)(2,1)S(1)}, u32[]{:S(2)}, u32[]{:S(2)}) collective-permute-start(bf16[1,144,128]{2,1,0:T(8,128)(2,1)} %get-tuple-element.9), channel_id=1, source_target_pairs={{0,8},{1,9},{2,10},{3,11},{4,12},{5,13},{6,14},{7,15},{8,0},{9,1},... | collective-permute-start | bytes 110600 | tf_op jit(solution)/shard_map/ppermute | solution.py:528
  5.6 1.2 %copy-start.3 = (bf16[32,16,1024]{2,1,0:T(8,128)(2,1)S(1)}, bf16[32,16,1024]{2,1,0:T(8,128)(2,1)}, u32[]{:S(2)}) copy-start(bf16[32,16,1024]{2,1,0:T(8,128)(2,1)} %store_ref.1) | copy-start | bytes 3145732
  7.1 18.7 %collective-permute-start.5 = (bf16[512,512]{1,0:T(8,128)(2,1)S(1)}, bf16[512,512]{1,0:T(8,128)(2,1)S(1)}, u32[]{:S(2)}, u32[]{:S(2)}) collective-permute-start(bf16[512,512]{1,0:T(8,128)(2,1)S(1)} %get-tuple-element.12), channel_id=1, source_target_pairs={{0,2},{1,3},{2,0},{3,1},{4,6},{5,7},{6,4},{7,5},{8,10},{9,11},{10,... | collective-permute-start | bytes 1572872 | tf_op jit(solution)/shard_map/ppermute | solution.py:528
  8.6 43.9 %collective-permute-start.4 = (bf16[512,512]{1,0:T(8,128)(2,1)S(1)}, bf16[512,512]{1,0:T(8,128)(2,1)}, u32[]{:S(2)}, u32[]{:S(2)}) collective-permute-start(bf16[512,512]{1,0:T(8,128)(2,1)S(1)} %get-tuple-element.11.rest_0_), channel_id=1, source_target_pairs={{0,1},{1,0},{2,3},{3,2},{4,5},{5,4},{6,7},{7,6},{8,9},{9,8},{10,11... | collective-permute-start | bytes 1572872 | tf_op jit(solution)/shard_map/ppermute | solution.py:528
  13.8 4.7 %collective-permute-start.1 = (bf16[2,144,128]{2,1,0:T(8,128)(2,1)S(1)}, bf16[2,144,128]{2,1,0:T(8,128)(2,1)S(1)}, u32[]{:S(2)}, u32[]{:S(2)}) collective-permute-start(bf16[2,144,128]{2,1,0:T(8,128)(2,1)S(1)} %pad_maximum_fusion.3), channel_id=1, source_target_pairs={{0,4},{1,5},{2,6},{3,7},{4,0},{5,1},{6,2},{7,3},{8,12},{9,13},{10,... | collective-permute-start | bytes 221192 | tf_op jit(solution)/shard_map/ppermute | solution.py:528
  19.2 5.5 %collective-permute-start.2 = (bf16[4,144,128]{2,1,0:T(8,128)(2,1)S(1)}, bf16[4,144,128]{2,1,0:T(8,128)(2,1)S(1)}, u32[]{:S(2)}, u32[]{:S(2)}) collective-permute-start(bf16[4,144,128]{2,1,0:T(8,128)(2,1)S(1)} %pad_maximum_fusion.2), channel_id=1, source_target_pairs={{0,2},{1,3},{2,0},{3,1},{4,6},{5,7},{6,4},{7,5},{8,10},{9,11},{10,... | collective-permute-start | bytes 442376 | tf_op jit(solution)/shard_map/ppermute | solution.py:528
  24.8 24.3 %copy-start.1 = (bf16[8,144,128]{2,1,0:T(8,128)(2,1)}, bf16[8,144,128]{2,1,0:T(8,128)(2,1)S(1)}, u32[]{:S(2)}) copy-start(bf16[8,144,128]{2,1,0:T(8,128)(2,1)S(1)} %constant_dynamic-update-slice_fusion.first_ref) | copy-start | bytes 884740
  24.8 1.6 %collective-permute-start.3 = (bf16[8,144,128]{2,1,0:T(8,128)(2,1)S(1)}, bf16[8,144,128]{2,1,0:T(8,128)(2,1)S(1)}, u32[]{:S(2)}, u32[]{:S(2)}) collective-permute-start(bf16[8,144,128]{2,1,0:T(8,128)(2,1)S(1)} %constant_dynamic-update-slice_fusion.first_ref), channel_id=1, source_target_pairs={{0,1},{1,0},{2,3},{3,2},{4,5},{5,4},{6,7},{7,6},{8,9},{9,8},{10,11... | collective-permute-start | bytes 884744 | tf_op jit(solution)/shard_map/ppermute | solution.py:528
  25.7 32.3 %collective-permute-start.6 = (bf16[512,512]{1,0:T(8,128)(2,1)S(1)}, bf16[512,512]{1,0:T(8,128)(2,1)}, u32[]{:S(2)}, u32[]{:S(2)}) collective-permute-start(bf16[512,512]{1,0:T(8,128)(2,1)S(1)} %collective-permute-done.5.rest_2_), channel_id=1, source_target_pairs={{0,1},{1,0},{2,3},{3,2},{4,5},{5,4},{6,7},{7,6},{8,9},{9,8},{10,11... | collective-permute-start | bytes 1572872 | tf_op jit(solution)/shard_map/ppermute | solution.py:528
  26.5 22.6 %copy-start.2 = (bf16[8,144,128]{2,1,0:T(8,128)(2,1)}, bf16[8,144,128]{2,1,0:T(8,128)(2,1)S(1)}, u32[]{:S(2)}) copy-start(bf16[8,144,128]{2,1,0:T(8,128)(2,1)S(1)} %collective-permute-done.3.second_ref) | copy-start | bytes 884740
  26.5 1.7 %copy-start = (bf16[8192,128]{1,0:T(8,128)(2,1)S(1)}, bf16[8192,128]{1,0:T(8,128)(2,1)}, u32[]{:S(2)}) copy-start(bf16[8192,128]{1,0:T(8,128)(2,1)} %wk_ref.1) | copy-start | bytes 6291460
  28.2 0.7 copy-start.5
  33.9 10.4 %all-to-all-start = ((bf16[16,16,128]{2,1,0:T(8,128)(2,1)}), bf16[16,16,128]{2,1,0:T(8,128)(2,1)S(1)}, u32[]{:S(2)}, u32[]{:S(2)}) async-start(bf16[16,16,128]{2,1,0:T(8,128)(2,1)} %norm_project.1), calls=%async_computation | async-start | bytes 131072 | tf_op jit(solution)/shard_map/all_to_all | solution.py:532
  37.4 1.0 %copy-start.4 = (bf16[1,160,1024]{2,1,0:T(8,128)(2,1)S(1)}, bf16[1,160,1024]{2,1,0:T(8,128)(2,1)}, u32[]{:S(2)}) copy-start(bf16[1,160,1024]{2,1,0:T(8,128)(2,1)} %param.17) | copy-start | bytes 983044
  45.6 12.5 %all-to-all-start.1 = ((bf16[16,48,128]{2,1,0:T(8,128)(2,1)}), bf16[16,48,128]{2,1,0:T(8,128)(2,1)S(1)}, u32[]{:S(2)}, u32[]{:S(2)}) async-start(bf16[16,48,128]{2,1,0:T(8,128)(2,1)} %attend.1), calls=%async_computation.1 | async-start | bytes 393216 | tf_op jit(solution)/shard_map/all_to_all | solution.py:532
  58.0 0.7 copy-start.6

commit v6 on v5

--- a/solution.py
+++ b/solution.py
@@ -16,6 +16,7 @@
 LANES = 128
 EXTRA = 16
 PLANE = 4
+PROJECT_LIMIT = 61 * 2**20
 AXIS = "session"
 VMEM = pltpu.VMEM
 SMEM = pltpu.SMEM
@@ -44,8 +45,11 @@
     return pl.BlockSpec(memory_space=space)
 
 
-def prepare_kernel(slots_dev, hidden_ref, slots_ref, block_ref, holder_ref, pair_ref, wide_scr):
+def prepare_kernel(
+    slots_dev, hidden_ref, gain_ref, slots_ref, block_ref, scale_ref, holder_ref, pair_ref, wide_scr
+):
     steps, model = hidden_ref.shape
+    scale_ref[...] = gain_ref[...].astype(F32)
     pieces = model // LANES
     wide = hidden_ref[...].astype(F32)
     for step in range(steps):
@@ -67,22 +71,23 @@
     block_ref[0] = wide_scr[...].astype(BF16)
 
 
-def prepare(hidden, block_slot, slots_dev):
+def prepare(hidden, gain, block_slot, slots_dev):
     assert slots_dev <= 256
     steps, model = hidden.shape
     rows = steps * model // LANES + EXTRA
     return pl.pallas_call(
         functools.partial(prepare_kernel, slots_dev),
-        in_specs=[whole(), whole(SMEM)],
-        out_specs=(whole(), whole(SMEM), whole(SMEM)),
+        in_specs=[whole(), whole(), whole(SMEM)],
+        out_specs=(whole(), whole(), whole(SMEM), whole(SMEM)),
         out_shape=(
             jax.ShapeDtypeStruct((1, rows, LANES), BF16),
+            jax.ShapeDtypeStruct(gain.shape, F32),
             jax.ShapeDtypeStruct((block_slot.shape[1] // 2,), jnp.int32),
             jax.ShapeDtypeStruct((block_slot.shape[1] // 2,), jnp.int32),
         ),
         scratch_shapes=[VMEM((rows, LANES), F32)],
         name="prepare",
-    )(hidden, block_slot)
+    )(hidden, gain, block_slot)
 
 
 def pick_kernel(order, me_ref, first_ref, second_ref, store_ref, out_ref, table_scr, table_smem, sem):
@@ -305,7 +310,7 @@
     scale = lax.rsqrt(jnp.sum(squares, axis=1, keepdims=True) * (1.0 / depth) + 1e-05)
     for c in range(pieces):
         part = x_scr[pl.ds(c, count, stride=pieces), :]
-        gain = gain_ref[pl.ds(c, 1), :].astype(F32)
+        gain = gain_ref[c : c + 1, :]
         lhs_scr[:, c * LANES : (c + 1) * LANES] = (part * scale * gain).astype(BF16)
     q_sum = jnp.zeros((count, q_cols), F32)
     k_sum = jnp.zeros((count, k_cols), F32)
@@ -358,7 +363,7 @@
             VMEM((devices, 16, LANES) if fast else (8, LANES), F32),
             pltpu.SemaphoreType.DMA((2, chunks)),
         ],
-        compiler_params=pltpu.CompilerParams(vmem_limit_bytes=48 * 2**20),
+        compiler_params=pltpu.CompilerParams(vmem_limit_bytes=PROJECT_LIMIT),
         cost_estimate=pl.CostEstimate(
             flops=2 * rows * depth * (q_cols + k_cols),
             bytes_accessed=2 * depth * (q_cols + k_cols),
@@ -559,11 +564,9 @@
     pieces = model // LANES
 
     me_word = me.astype(jnp.int32).reshape(1)
-    block, holder, pair = prepare(hidden[:, 0], block_slot, slots_dev)
-    if fast:
-        keep, send = split_values((me_word // 2) % 2, value_store)
-        neighbour = swap(send, 2, devices)
-        stores = (keep, swap(keep, 1, devices), neighbour, swap(neighbour, 1, devices))
+    block, gain, holder, pair = prepare(
+        hidden[:, 0], norm_gain.reshape(pieces, LANES), block_slot, slots_dev
+    )
     order = [0]
     bit = devices // 2
     while bit:
@@ -572,15 +575,24 @@
         bit //= 2
         if bit:
             block = jnp.concatenate([block, other], axis=0)
+        if fast and bit == 2:
+            block, value_store = lax.optimization_barrier((block, value_store))
     order = tuple(order)
+    if fast:
+        x = lax.bitwise_and(lax.shift_right_logical(me_word, 1), 1)
+        keep, send = split_values(x, value_store)
+        block, other, send = lax.optimization_barrier((block, other, send))
+        neighbour = swap(send, 2, devices)
+        stores = (keep, swap(keep, 1, devices), neighbour, swap(neighbour, 1, devices))
     if not fast:
         sent_pages = pick_pages(me_word, block, other, value_store, order)
         block, other, sent_pages = lax.optimization_barrier((block, other, sent_pages))
         fetched = exchange(sent_pages)
     projected = project(
-        me_word, block, other, norm_gain.reshape(pieces, LANES), query_weight, kv_weight, order, fast
+        me_word, block, other, gain, query_weight, kv_weight, order, fast
     )
     if fast:
+        projected, pair = lax.optimization_barrier((projected, pair))
         columns = exchange(projected)
         rows = plane_rows(me_word, block, other, order)
     else:

time: 91.8 us -> 99.2 us (1.081)
  waiting for transfers between devices: 16.7 us -> 23.2 us
  starting transfers between devices: 15.5 us -> 21.3 us
  local copies, waits for them, and re-layouts: 7.85 us -> 4.4 us
  other arithmetic: 5.83 us -> 3.22 us
  Pallas kernels: 18.4 us -> 19.8 us
    ppermute x7, waiting for transfers between devices: 7.46 us -> 17.6 us  [swap(): return lax.ppermute(block, AXIS, [(i, i ^ bit) for i in range(devices)])]
    all_to_all x2, starting transfers between devices: 7.02 us -> 11.4 us  [exchange(): lax.all_to_all(blocks, AXIS, split_axis=0, concat_axis=0, tiled=True, axi...]
    all_to_all x2, waiting for transfers between devices: 9.26 us -> 5.59 us  [exchange(): lax.all_to_all(blocks, AXIS, split_axis=0, concat_axis=0, tiled=True, axi...]
    unnamed x20 -> x16, local copies, waits for them, and re-layouts: 7.12 us -> 3.67 us
    ppermute x7, starting transfers between devices: 8.44 us -> 9.93 us  [swap(): return lax.ppermute(block, AXIS, [(i, i ^ bit) for i in range(devices)])]
    pallas_call x1, Pallas kernels: 4.98 us -> 6.2 us  [project(): pl.pallas_call(functools.partial(project_kernel, order, fast), in_specs=[...]
  transfers between devices with their start and end apart: 9 -> 9, of which waited for: 5 -> 5; matrix products, arithmetic and copies ran while one was open for 8% -> 3% of each run, Pallas kernels for 12% -> 13%
where the time goes in v6:
time: 99.2 us; the launch traced here: 98.6 us
  blocking collectives  25.8 us (26%)
  waiting for transfers between devices  23.2 us (23%)
  starting transfers between devices  21.3 us (21%)
  Pallas kernels  19.8 us (20%)
  local copies, waits for them, and re-layouts  4.4 us (4%)
  other arithmetic  3.22 us (3%)
    all_to_all x2, blocking collectives, exchange(): lax.all_to_all(blocks, AXIS, split_axis=0, concat_axis=0, tiled=True, axi...  25.8 us
    ppermute x7, waiting for transfers between devices, swap(): return lax.ppermute(block, AXIS, [(i, i ^ bit) for i in range(devices)])  17.6 us
    all_to_all x2, starting transfers between devices, exchange(): lax.all_to_all(blocks, AXIS, split_axis=0, concat_axis=0, tiled=True, axi...  11.4 us
    ppermute x7, starting transfers between devices, swap(): return lax.ppermute(block, AXIS, [(i, i ^ bit) for i in range(devices)])  9.93 us
    pallas_call x1, Pallas kernels, project(): pl.pallas_call(functools.partial(project_kernel, order, fast), in_specs=[...  6.2 us
    all_to_all x2, waiting for transfers between devices, exchange(): lax.all_to_all(blocks, AXIS, split_axis=0, concat_axis=0, tiled=True, axi...  5.59 us
    pallas_call x1, Pallas kernels, output(): pl.pallas_call(functools.partial(output_kernel, fast), in_specs=[whole(),...  3.94 us
    unnamed x16, local copies, waits for them, and re-layouts  3.67 us
  transfers between devices with their start and end apart: 9, of which 5 were waited for; matrix products, arithmetic and copies ran while one was open for 3% of the time, Pallas kernels for 13%

profile of v6, /device:TPU:0, one launch (start us, length us, event | category | flops | bytes accessed | tf_op | source)
XLA Modules:
  0.0 98.6 jit_solution(14539261216558297414)
XLA Ops:
  0.0 1.6 %prepare.1 = (bf16[1,144,128]{2,1,0:T(8,128)(2,1)}, f32[64,128]{1,0:T(8,128)}, s32[16]{0:T(128)}, s32[16]{0:T(128)}) custom-call(bf16[2,8192]{1,0:T(2,128)(2,1)} %bitcast.13, bf16[64,128]{1,0:T(8,128)(2,1)} %bitcast.14, s32[1,32]{1,0:T(1,128)} %slots_ref.1), custom_call_target="tpu_custom_call" | custom-call | tf_op jit(solution)/shard_map/prepare/pallas_call | solution.py:78
  1.6 4.1 %collective-permute-start = (bf16[1,144,128]{2,1,0:T(8,128)(2,1)}, bf16[1,144,128]{2,1,0:T(8,128)(2,1)S(1)}, u32[]{:S(2)}, u32[]{:S(2)}) collective-permute-start(bf16[1,144,128]{2,1,0:T(8,128)(2,1)} %get-tuple-element.17), channel_id=1, source_target_pairs={{0,8},{1,9},{2,10},{3,11},{4,12},{5,13},{6,14},{7,15},{8,0},{9,1},... | collective-permute-start | bytes 110600 | tf_op jit(solution)/shard_map/ppermute | solution.py:533
  6.3 1.9 %collective-permute-done = bf16[1,144,128]{2,1,0:T(8,128)(2,1)S(1)} collective-permute-done((bf16[1,144,128]{2,1,0:T(8,128)(2,1)}, bf16[1,144,128]{2,1,0:T(8,128)(2,1)S(1)}, u32[]{:S(2)}, u32[]{:S(2)}) %collective-permute-start) | collective-permute-done | bytes 36896 | tf_op jit(solution)/shard_map/ppermute | solution.py:533
  9.0 1.5 %collective-permute-start.1 = (bf16[2,144,128]{2,1,0:T(8,128)(2,1)S(1)}, bf16[2,144,128]{2,1,0:T(8,128)(2,1)S(1)}, u32[]{:S(2)}, u32[]{:S(2)}) collective-permute-start(bf16[2,144,128]{2,1,0:T(8,128)(2,1)S(1)} %pad_maximum_fusion.3), channel_id=1, source_target_pairs={{0,4},{1,5},{2,6},{3,7},{4,0},{5,1},{6,2},{7,3},{8,12},{9,13},{10,... | collective-permute-start | bytes 221192 | tf_op jit(solution)/shard_map/ppermute | solution.py:533
  10.5 2.8 %collective-permute-done.1 = bf16[2,144,128]{2,1,0:T(8,128)(2,1)S(1)} collective-permute-done((bf16[2,144,128]{2,1,0:T(8,128)(2,1)S(1)}, bf16[2,144,128]{2,1,0:T(8,128)(2,1)S(1)}, u32[]{:S(2)}, u32[]{:S(2)}) %collective-permute-start.1) | collective-permute-done | bytes 73760 | tf_op jit(solution)/shard_map/ppermute | solution.py:533
  14.1 1.8 %collective-permute-start.2 = (bf16[4,144,128]{2,1,0:T(8,128)(2,1)S(1)}, bf16[4,144,128]{2,1,0:T(8,128)(2,1)S(1)}, u32[]{:S(2)}, u32[]{:S(2)}) collective-permute-start(bf16[4,144,128]{2,1,0:T(8,128)(2,1)S(1)} %pad_maximum_fusion.2), channel_id=1, source_target_pairs={{0,2},{1,3},{2,0},{3,1},{4,6},{5,7},{6,4},{7,5},{8,10},{9,11},{10,... | collective-permute-start | bytes 442376 | tf_op jit(solution)/shard_map/ppermute | solution.py:533
  15.9 1.0 %copy.13 = bf16[1,512,160]{2,1,0:T(8,128)(2,1)S(1)} copy(bf16[1,512,160]{1,2,0:T(8,128)(2,1)} %param.16) | data formatting | bytes 327680 | tf_op args[5]
  17.0 2.4 %collective-permute-done.2 = bf16[4,144,128]{2,1,0:T(8,128)(2,1)S(1)} collective-permute-done((bf16[4,144,128]{2,1,0:T(8,128)(2,1)S(1)}, bf16[4,144,128]{2,1,0:T(8,128)(2,1)S(1)}, u32[]{:S(2)}, u32[]{:S(2)}) %collective-permute-start.2) | collective-permute-done | bytes 147488 | tf_op jit(solution)/shard_map/ppermute | solution.py:533
  19.7 1.2 %copy-done = bf16[32,16,1024]{2,1,0:T(8,128)(2,1)S(1)} copy-done((bf16[32,16,1024]{2,1,0:T(8,128)(2,1)S(1)}, bf16[32,16,1024]{2,1,0:T(8,128)(2,1)}, u32[]{:S(2)}) %copy-start) | copy-done | bytes 1048600
  20.9 1.0 %split_values.1 = (bf16[512,512]{1,0:T(8,128)(2,1)S(1)}, bf16[512,512]{1,0:T(8,128)(2,1)}) custom-call(s32[1]{0:T(128)S(6)} %and.25.x_ref, bf16[32,16,1024]{2,1,0:T(8,128)(2,1)S(1)} %copy-done), custom_call_target="tpu_custom_call" | custom-call | tf_op jit(solution)/shard_map/split_values/pallas_call | solution.py:146
  23.1 6.2 %norm_project.1 = bf16[16,16,128]{2,1,0:T(8,128)(2,1)} custom-call(s32[1]{0:T(128)} %bitcast.me_ref, bf16[8,144,128]{2,1,0:T(8,128)(2,1)} %copy-done.4, bf16[8,144,128]{2,1,0:T(8,128)(2,1)} %copy-done.5, f32[64,128]{1,0:T(8,128)} %get-tuple-element.23.gain_ref, bf16[8192,512]{1,0:T(8,128)(2,1)} %wq_ref.1, bf16[8192,128]{1,0:T(8,128)(2,1)} %wk_ref.1), custom_call_target="tpu_custom_call" | custom-call | flops 335544320 | bytes 10485760 | tf_op jit(solution)/shard_map/norm_project/pallas_call | solution.py:353
  29.3 6.1 %all-to-all-start = ((bf16[16,16,128]{2,1,0:T(8,128)(2,1)}), bf16[16,16,128]{2,1,0:T(8,128)(2,1)S(1)}, u32[]{:S(2)}, u32[]{:S(2)}) async-start(bf16[16,16,128]{2,1,0:T(8,128)(2,1)} %norm_project.1), calls=%async_computation | async-start | bytes 131072 | tf_op jit(solution)/shard_map/all_to_all | solution.py:537
  35.6 2.0 %collective-permute-start.5 = (bf16[512,512]{1,0:T(8,128)(2,1)}, bf16[512,512]{1,0:T(8,128)(2,1)S(1)}, u32[]{:S(2)}, u32[]{:S(2)}) collective-permute-start(bf16[512,512]{1,0:T(8,128)(2,1)} %get-tuple-element.28), channel_id=1, source_target_pairs={{0,2},{1,3},{2,0},{3,1},{4,6},{5,7},{6,4},{7,5},{8,10},{9,11},{10,... | collective-permute-start | bytes 1572872 | tf_op jit(solution)/shard_map/ppermute | solution.py:533
  37.6 1.0 %fusion = (f32[512,64]{1,0:T(8,128)S(1)}, f32[512,64]{1,0:T(8,128)S(1)}, f32[512,64]{1,0:T(8,128)S(1)}) fusion(f32[64]{0:T(128)S(1)} %multiply_exponential_fusion, f32[512]{0:T(512)S(1)} %get-tuple-element.33), kind=kLoop, calls=%fused_computation.5 | loop fusion | flops 65536 | bytes 395520 | tf_op jit(solution)/shard_map/neg | solution.py:40
  38.8 1.4 %turned_keys.1.keys_ref = bf16[512,1024]{1,0:T(8,128)(2,1)S(1)} custom-call(s32[16]{0:T(128)S(1)} %copy-done.3, bf16[512,160]{1,0:T(8,128)(2,1)S(1)} %bitcast.11, bf16[160,1024]{1,0:T(8,128)(2,1)S(1)} %bitcast.12, f32[512,128]{1,0:T(8,128)S(1)} %get-tuple-element.37.cos_ref, f32[512,128]{1,0:T(8,128)S(1)} %get-tuple-element.38.sin_ref), custom_call_target="tpu_custom_call" | custom-call | flops 167772160 | bytes 2097152 | tf_op jit(solution)/shard_map/turned_keys/pallas_call | solution.py:260
  40.3 10.5 %collective-permute-done.5.rest_2_ = bf16[512,512]{1,0:T(8,128)(2,1)S(1)} collective-permute-done((bf16[512,512]{1,0:T(8,128)(2,1)}, bf16[512,512]{1,0:T(8,128)(2,1)S(1)}, u32[]{:S(2)}, u32[]{:S(2)}) %collective-permute-start.5) | collective-permute-done | bytes 524320 | tf_op jit(solution)/shard_map/ppermute | solution.py:533
  50.8 1.3 %attend.1 = bf16[16,48,128]{2,1,0:T(8,128)(2,1)} custom-call(bf16[16,16,128]{2,1,0:T(8,128)(2,1)S(1)} %all-to-all-done.columns_ref, bf16[512,1024]{1,0:T(8,128)(2,1)S(1)} %turned_keys.1.keys_ref, f32[2,512]{1,0:T(2,128)S(1)} %and_select_fusion.bias_ref, f32[2,128]{1,0:T(2,128)S(1)} %get-tuple-element.39.cos_ref, f32[2,128]{1,0:T(2,128)S(1)} %get-tuple-element.40.sin_ref), custom_call_target="tpu_custom_call" | custom-call | flops 33554432 | bytes 2097152 | tf_op jit(solution)/shard_map/attend/pallas_call | solution.py:462
  52.1 5.2 %all-to-all-start.1 = ((bf16[16,48,128]{2,1,0:T(8,128)(2,1)}), bf16[16,48,128]{2,1,0:T(8,128)(2,1)S(1)}, u32[]{:S(2)}, u32[]{:S(2)}) async-start(bf16[16,48,128]{2,1,0:T(8,128)(2,1)} %attend.1), calls=%async_computation.1 | async-start | bytes 393216 | tf_op jit(solution)/shard_map/all_to_all | solution.py:537
  57.3 3.4 %plane_rows.1.rows_ref = s32[128]{0:T(128)} custom-call(s32[1]{0:T(128)} %bitcast.me_ref, bf16[8,144,128]{2,1,0:T(8,128)(2,1)} %copy-done.4, bf16[8,144,128]{2,1,0:T(8,128)(2,1)} %copy-done.5), custom_call_target="tpu_custom_call" | custom-call | tf_op jit(solution)/shard_map/plane_rows/pallas_call | solution.py:176
  60.7 5.6 %all-to-all-done.1.weights_ref = bf16[16,48,128]{2,1,0:T(8,128)(2,1)S(1)} async-done(((bf16[16,48,128]{2,1,0:T(8,128)(2,1)}), bf16[16,48,128]{2,1,0:T(8,128)(2,1)S(1)}, u32[]{:S(2)}, u32[]{:S(2)}) %all-to-all-start.1) | async-done | bytes 196640 | tf_op jit(solution)/shard_map/all_to_all | solution.py:537
  67.0 1.1 %mix_values.1 = bf16[4,128,128]{2,1,0:T(8,128)(2,1)S(1)} custom-call(s32[1]{0:T(128)} %bitcast.me_ref, s32[128]{0:T(128)S(1)} %copy-done.2, bf16[16,48,128]{2,1,0:T(8,128)(2,1)S(1)} %all-to-all-done.1.weights_ref, bf16[512,512]{1,0:T(8,128)(2,1)S(1)} %get-tuple-element.27.rest_0_, bf16[512,512]{1,0:T(8,128)(2,1)S(1)} %collective-permute-done.4.rest_1_, ...), custom_call_target="tpu_custom_call" | custom-call | flops 67108864 | bytes 4194304 | tf_op jit(solution)/shard_map/mix_values/pallas_call | solution.py:224
  68.1 8.5 %all_to_all.20.lhs_ref = bf16[4,128,128]{2,1,0:T(8,128)(2,1)S(1)} all-to-all(bf16[4,128,128]{2,1,0:T(8,128)(2,1)S(1)} %mix_values.1), channel_id=1, replica_groups={{0,4,8,12},{1,5,9,13},{2,6,10,14},{3,7,11,15},{16,20,24,28},{17,21,25,2..., dimensions={0} | all-to-all | bytes 262144 | tf_op jit(solution)/shard_map/all_to_all | solution.py:537
  76.5 3.9 %output_project.1 = bf16[2048,128]{1,0:T(8,128)(2,1)S(1)} custom-call(bf16[4,128,128]{2,1,0:T(8,128)(2,1)S(1)} %all_to_all.20.lhs_ref, bf16[512,8192]{1,0:T(8,128)(2,1)} %weight_ref.1), custom_call_target="tpu_custom_call" | custom-call | flops 268435456 | bytes 8388608 | tf_op jit(solution)/shard_map/output_project/pallas_call | solution.py:513
  80.5 17.4 %all_to_all.21 = bf16[16,128,128]{2,1,0:T(8,128)(2,1)S(1)} all-to-all(bf16[16,128,128]{2,1,0:T(8,128)(2,1)S(1)} %bitcast.10), channel_id=1, replica_groups=mesh['groups'=2,'session'=16] {'session'}, dimensions={0} | all-to-all | bytes 1048576 | tf_op jit(solution)/shard_map/all_to_all | solution.py:537
  (38 shorter events, 4.9 us)
Async XLA Ops:
  0.0 38.8 %copy-start.1 = (bf16[1,160,1024]{2,1,0:T(8,128)(2,1)S(1)}, bf16[1,160,1024]{2,1,0:T(8,128)(2,1)}, u32[]{:S(2)}) copy-start(bf16[1,160,1024]{2,1,0:T(8,128)(2,1)} %param.17) | copy-start | bytes 983044
  1.6 33.9 %copy-start.3 = (s32[16]{0:T(128)S(1)}, s32[16]{0:T(128)}, u32[]{:S(2)}) copy-start(s32[16]{0:T(128)} %get-tuple-element.26.pair_ref) | copy-start | bytes 196
  1.6 6.6 %collective-permute-start = (bf16[1,144,128]{2,1,0:T(8,128)(2,1)}, bf16[1,144,128]{2,1,0:T(8,128)(2,1)S(1)}, u32[]{:S(2)}, u32[]{:S(2)}) collective-permute-start(bf16[1,144,128]{2,1,0:T(8,128)(2,1)} %get-tuple-element.17), channel_id=1, source_target_pairs={{0,8},{1,9},{2,10},{3,11},{4,12},{5,13},{6,14},{7,15},{8,0},{9,1},... | collective-permute-start | bytes 110600 | tf_op jit(solution)/shard_map/ppermute | solution.py:533
  9.0 4.4 %collective-permute-start.1 = (bf16[2,144,128]{2,1,0:T(8,128)(2,1)S(1)}, bf16[2,144,128]{2,1,0:T(8,128)(2,1)S(1)}, u32[]{:S(2)}, u32[]{:S(2)}) collective-permute-start(bf16[2,144,128]{2,1,0:T(8,128)(2,1)S(1)} %pad_maximum_fusion.3), channel_id=1, source_target_pairs={{0,4},{1,5},{2,6},{3,7},{4,0},{5,1},{6,2},{7,3},{8,12},{9,13},{10,... | collective-permute-start | bytes 221192 | tf_op jit(solution)/shard_map/ppermute | solution.py:533
  14.1 5.2 %collective-permute-start.2 = (bf16[4,144,128]{2,1,0:T(8,128)(2,1)S(1)}, bf16[4,144,128]{2,1,0:T(8,128)(2,1)S(1)}, u32[]{:S(2)}, u32[]{:S(2)}) collective-permute-start(bf16[4,144,128]{2,1,0:T(8,128)(2,1)S(1)} %pad_maximum_fusion.2), channel_id=1, source_target_pairs={{0,2},{1,3},{2,0},{3,1},{4,6},{5,7},{6,4},{7,5},{8,10},{9,11},{10,... | collective-permute-start | bytes 442376 | tf_op jit(solution)/shard_map/ppermute | solution.py:533
  19.4 3.0 %copy-start.4 = (bf16[8,144,128]{2,1,0:T(8,128)(2,1)}, bf16[8,144,128]{2,1,0:T(8,128)(2,1)S(1)}, u32[]{:S(2)}) copy-start(bf16[8,144,128]{2,1,0:T(8,128)(2,1)S(1)} %constant_dynamic-update-slice_fusion.first_ref) | copy-start | bytes 884740
  19.4 20.8 %copy-start.6 = (s32[2,1,16]{2,1,0:T(1,128)S(1)}, s32[2,1,16]{2,1,0:T(1,128)}, u32[]{:S(2)}) copy-start(s32[2,1,16]{2,1,0:T(1,128)} %param.21) | copy-start | bytes 388
  19.4 3.0 %collective-permute-start.3 = (bf16[8,144,128]{2,1,0:T(8,128)(2,1)S(1)}, bf16[8,144,128]{2,1,0:T(8,128)(2,1)S(1)}, u32[]{:S(2)}, u32[]{:S(2)}) collective-permute-start(bf16[8,144,128]{2,1,0:T(8,128)(2,1)S(1)} %constant_dynamic-update-slice_fusion.first_ref), channel_id=1, source_target_pairs={{0,1},{1,0},{2,3},{3,2},{4,5},{5,4},{6,7},{7,6},{8,9},{9,8},{10,11... | collective-permute-start | bytes 884744 | tf_op jit(solution)/shard_map/ppermute | solution.py:533
  19.7 1.2 %copy-start = (bf16[32,16,1024]{2,1,0:T(8,128)(2,1)S(1)}, bf16[32,16,1024]{2,1,0:T(8,128)(2,1)}, u32[]{:S(2)}) copy-start(bf16[32,16,1024]{2,1,0:T(8,128)(2,1)} %store_ref) | copy-start | bytes 3145732
  21.9 38.8 %collective-permute-start.4 = (bf16[512,512]{1,0:T(8,128)(2,1)S(1)}, bf16[512,512]{1,0:T(8,128)(2,1)S(1)}, u32[]{:S(2)}, u32[]{:S(2)}) collective-permute-start(bf16[512,512]{1,0:T(8,128)(2,1)S(1)} %get-tuple-element.27.rest_0_), channel_id=1, source_target_pairs={{0,1},{1,0},{2,3},{3,2},{4,5},{5,4},{6,7},{7,6},{8,9},{9,8},{10,11... | collective-permute-start | bytes 1572872 | tf_op jit(solution)/shard_map/ppermute | solution.py:533
  22.4 0.7 copy-start.5
  29.3 21.5 %all-to-all-start = ((bf16[16,16,128]{2,1,0:T(8,128)(2,1)}), bf16[16,16,128]{2,1,0:T(8,128)(2,1)S(1)}, u32[]{:S(2)}, u32[]{:S(2)}) async-start(bf16[16,16,128]{2,1,0:T(8,128)(2,1)} %norm_project.1), calls=%async_computation | async-start | bytes 131072 | tf_op jit(solution)/shard_map/all_to_all | solution.py:537
  35.6 15.1 %collective-permute-start.5 = (bf16[512,512]{1,0:T(8,128)(2,1)}, bf16[512,512]{1,0:T(8,128)(2,1)S(1)}, u32[]{:S(2)}, u32[]{:S(2)}) collective-permute-start(bf16[512,512]{1,0:T(8,128)(2,1)} %get-tuple-element.28), channel_id=1, source_target_pairs={{0,2},{1,3},{2,0},{3,1},{4,6},{5,7},{6,4},{7,5},{8,10},{9,11},{10,... | collective-permute-start | bytes 1572872 | tf_op jit(solution)/shard_map/ppermute | solution.py:533
  50.8 15.5 %collective-permute-start.6 = (bf16[512,512]{1,0:T(8,128)(2,1)S(1)}, bf16[512,512]{1,0:T(8,128)(2,1)S(1)}, u32[]{:S(2)}, u32[]{:S(2)}) collective-permute-start(bf16[512,512]{1,0:T(8,128)(2,1)S(1)} %collective-permute-done.5.rest_2_), channel_id=1, source_target_pairs={{0,1},{1,0},{2,3},{3,2},{4,5},{5,4},{6,7},{7,6},{8,9},{9,8},{10,11... | collective-permute-start | bytes 1572872 | tf_op jit(solution)/shard_map/ppermute | solution.py:533
  52.1 14.2 %all-to-all-start.1 = ((bf16[16,48,128]{2,1,0:T(8,128)(2,1)}), bf16[16,48,128]{2,1,0:T(8,128)(2,1)S(1)}, u32[]{:S(2)}, u32[]{:S(2)}) async-start(bf16[16,48,128]{2,1,0:T(8,128)(2,1)} %attend.1), calls=%async_computation.1 | async-start | bytes 393216 | tf_op jit(solution)/shard_map/all_to_all | solution.py:537
  66.3 0.7 copy-start.2

commit v7 on v6

--- a/solution.py
+++ b/solution.py
@@ -16,7 +16,8 @@
 LANES = 128
 EXTRA = 16
 PLANE = 4
-PROJECT_LIMIT = 61 * 2**20
+PAIRS = 8
+PROJECT_LIMIT = 48 * 2**20
 AXIS = "session"
 VMEM = pltpu.VMEM
 SMEM = pltpu.SMEM
@@ -39,6 +40,12 @@
         jnp.concatenate([cosine, cosine], axis=-1),
         jnp.concatenate([-sine, sine], axis=-1),
     )
+
+
+def origin(me, order, j):
+    if order is None:
+        return 2 * (j % PAIRS) + jnp.bitwise_xor(jnp.bitwise_and(me, 1), j // PAIRS)
+    return jnp.bitwise_xor(me, order[j])
 
 
 def whole(space=VMEM):
@@ -68,10 +75,12 @@
         pair = jnp.where(parity == 0, slot - base, slots_ref[0, 2 * m + 1] - base)
         table = jnp.where(lane == holder, pair, table)
     wide_scr[steps * pieces :, :] = table.astype(F32)
-    block_ref[0] = wide_scr[...].astype(BF16)
-
-
-def prepare(hidden, gain, block_slot, slots_dev):
+    block = wide_scr[...].astype(BF16)
+    for copy in range(block_ref.shape[0]):
+        block_ref[copy] = block
+
+
+def prepare(hidden, gain, block_slot, slots_dev, copies):
     assert slots_dev <= 256
     steps, model = hidden.shape
     rows = steps * model // LANES + EXTRA
@@ -80,7 +89,7 @@
         in_specs=[whole(), whole(), whole(SMEM)],
         out_specs=(whole(), whole(), whole(SMEM), whole(SMEM)),
         out_shape=(
-            jax.ShapeDtypeStruct((1, rows, LANES), BF16),
+            jax.ShapeDtypeStruct((copies, rows, LANES), BF16),
             jax.ShapeDtypeStruct(gain.shape, F32),
             jax.ShapeDtypeStruct((block_slot.shape[1] // 2,), jnp.int32),
             jax.ShapeDtypeStruct((block_slot.shape[1] // 2,), jnp.int32),
@@ -102,7 +111,7 @@
     copy.wait()
     me = me_ref[0]
     for j in range(2 * half):
-        target = jnp.bitwise_xor(me, order[j])
+        target = origin(me, order, j)
         for k in range(2):
             out_ref[target, k * block_len : (k + 1) * block_len, :] = store_ref[
                 table_smem[j, k, me]
@@ -165,7 +174,7 @@
     me = me_ref[0]
     plane = jnp.bitwise_and(me, -PLANE)
     for j in range(2 * half):
-        session = jnp.bitwise_xor(me, order[j])
+        session = origin(me, order, j)
         for k in range(2):
             for b in range(PLANE):
                 out_ref[session * (2 * PLANE) + k * PLANE + b] = table_smem[j, k, plane + b]
@@ -327,8 +336,8 @@
     me = me_ref[0]
     per = q_cols // LANES
     out_scr[...] = jnp.zeros_like(out_scr)
-    for j, other in enumerate(order):
-        place = jnp.bitwise_xor(me, other)
+    for j in range(2 * half):
+        place = origin(me, order, j)
         for step in range(STEPS):
             row = j * STEPS + step
             for c in range(per):
@@ -475,9 +484,10 @@
     )(*operands)
 
 
-def output_kernel(fast, lhs_ref, weight_ref, out_ref, weight_buf, out_scr, heads_scr, sems):
+def output_kernel(fast, me_ref, lhs_ref, weight_ref, *rest):
+    out_refs, (weight_buf, out_scr, heads_scr, sems) = rest[:-4], rest[-4:]
     chunks, _, span = weight_buf.shape
-    rows = out_ref.shape[0] * LANES // (chunks * span)
+    rows = out_scr.shape[0] * LANES // (chunks * span)
     pieces = chunks * span // LANES
     copies = []
     for i in range(chunks):
@@ -504,17 +514,30 @@
             out_scr[pl.ds(i * (span // LANES) + c, rows, stride=pieces), :] = part[
                 :, c * LANES : (c + 1) * LANES
             ]
-    out_ref[...] = out_scr[...].astype(BF16)
-
-
-def output(lhs, weight, rows, fast):
+    if not fast:
+        out_refs[0][...] = out_scr[...].astype(BF16)
+        return
+    low = jnp.bitwise_and(me_ref[0], 1)
+    for out_ref, core in zip(out_refs, (low, 1 - low)):
+        count, size, _ = out_ref.shape
+        for j in range(count):
+            part = pl.ds(pl.multiple_of((2 * j + core) * size, size), size)
+            out_ref[j] = out_scr[part, :].astype(BF16)
+
+
+def output(me, lhs, weight, rows, fast):
     depth, width = weight.shape
     chunks = 8
+    if fast:
+        shape = (rows // (2 * STEPS), STEPS * width // LANES, LANES)
+        shapes = (jax.ShapeDtypeStruct(shape, BF16),) * 2
+    else:
+        shapes = (jax.ShapeDtypeStruct((rows * width // LANES, LANES), BF16),)
     return pl.pallas_call(
         functools.partial(output_kernel, fast),
-        in_specs=[whole(), whole(pl.ANY)],
-        out_specs=whole(),
-        out_shape=jax.ShapeDtypeStruct((rows * width // LANES, LANES), BF16),
+        in_specs=[whole(SMEM), whole(), whole(pl.ANY)],
+        out_specs=(whole(),) * len(shapes),
+        out_shape=shapes,
         scratch_shapes=[
             VMEM((chunks, depth, width // chunks), BF16),
             VMEM((rows * width // LANES, LANES), F32),
@@ -526,7 +549,7 @@
             flops=2 * rows * depth * width, bytes_accessed=2 * depth * width, transcendentals=0
         ),
         name="output_project",
-    )(lhs, weight)
+    )(me, lhs, weight)
 
 
 def swap(block, bit, devices):
@@ -560,30 +583,32 @@
     model = hidden.shape[2]
     q_cols = query_weight.shape[1]
     k_cols = kv_weight.shape[1]
-    fast = q_cols == 4 * HEAD_DIM and k_cols == HEAD_DIM
+    fast = devices == 2 * PAIRS and q_cols == 4 * HEAD_DIM and k_cols == HEAD_DIM
     pieces = model // LANES
 
     me_word = me.astype(jnp.int32).reshape(1)
     block, gain, holder, pair = prepare(
-        hidden[:, 0], norm_gain.reshape(pieces, LANES), block_slot, slots_dev
-    )
-    order = [0]
-    bit = devices // 2
-    while bit:
-        other = swap(block, bit, devices)
-        order = order + [k ^ bit for k in order]
-        bit //= 2
-        if bit:
-            block = jnp.concatenate([block, other], axis=0)
-        if fast and bit == 2:
-            block, value_store = lax.optimization_barrier((block, value_store))
-    order = tuple(order)
-    if fast:
+        hidden[:, 0], norm_gain.reshape(pieces, LANES), block_slot, slots_dev, PAIRS if fast else 1
+    )
+    if fast:
+        same_core = [list(range(core, devices, 2)) for core in range(2)]
+        block = exchange(block, same_core)
+        other = swap(block, 1, devices)
+        order = None
         x = lax.bitwise_and(lax.shift_right_logical(me_word, 1), 1)
         keep, send = split_values(x, value_store)
-        block, other, send = lax.optimization_barrier((block, other, send))
         neighbour = swap(send, 2, devices)
         stores = (keep, swap(keep, 1, devices), neighbour, swap(neighbour, 1, devices))
+    else:
+        order = [0]
+        bit = devices // 2
+        while bit:
+            other = swap(block, bit, devices)
+            order = order + [k ^ bit for k in order]
+            bit //= 2
+            if bit:
+                block = jnp.concatenate([block, other], axis=0)
+        order = tuple(order)
     if not fast:
         sent_pages = pick_pages(me_word, block, other, value_store, order)
         block, other, sent_pages = lax.optimization_barrier((block, other, sent_pages))
@@ -592,7 +617,6 @@
         me_word, block, other, gain, query_weight, kv_weight, order, fast
     )
     if fast:
-        projected, pair = lax.optimization_barrier((projected, pair))
         columns = exchange(projected)
         rows = plane_rows(me_word, block, other, order)
     else:
@@ -625,8 +649,13 @@
         flat = heads.reshape(HEADS // 4, STEPS, 4 * HEAD_DIM).transpose(1, 0, 2)
         flat = flat.reshape(STEPS, devices, model // devices).transpose(1, 0, 2)
         lhs = exchange(flat).reshape(devices * STEPS, model // devices)
-    partial = output(lhs, out_weight, devices * STEPS, fast)
-    arrived = exchange(partial.reshape(devices, STEPS * pieces, LANES))
+    partial = output(me_word, lhs, out_weight, devices * STEPS, fast)
+    if fast:
+        near, far = partial
+        both = near.astype(F32) + swap(far, 1, devices).astype(F32)
+        arrived = exchange(both.astype(BF16), same_core)
+    else:
+        arrived = exchange(partial[0].reshape(devices, STEPS * pieces, LANES))
     total = jnp.sum(arrived.astype(F32), axis=0).astype(BF16)
     return total.reshape(STEPS, 1, model)
 

time: 99.2 us -> 88.9 us (0.90)
  blocking collectives: 25.8 us -> 20.4 us
  starting transfers between devices: 21.3 us -> 17.2 us
  waiting for transfers between devices: 23.2 us -> 19.7 us
  local copies, waits for them, and re-layouts: 4.4 us -> 7.07 us
  Pallas kernels: 19.8 us -> 18.4 us
  other arithmetic: 3.22 us -> 4.35 us
    ppermute x7 -> x5, waiting for transfers between devices: 17.6 us -> 8.73 us  [swap(): return lax.ppermute(block, AXIS, [(i, i ^ bit) for i in range(devices)])]
    ppermute x7 -> x5, starting transfers between devices: 9.93 us -> 2.16 us  [swap(): return lax.ppermute(block, AXIS, [(i, i ^ bit) for i in range(devices)])]
    all_to_all x2, blocking collectives: 25.8 us -> 20.4 us  [exchange(): lax.all_to_all(blocks, AXIS, split_axis=0, concat_axis=0, tiled=True, axi...]
    all_to_all x2 -> x3, waiting for transfers between devices: 5.59 us -> 11 us  [exchange(): lax.all_to_all(blocks, AXIS, split_axis=0, concat_axis=0, tiled=True, axi...]
    all_to_all x2 -> x3, starting transfers between devices: 11.4 us -> 15.1 us  [exchange(): lax.all_to_all(blocks, AXIS, split_axis=0, concat_axis=0, tiled=True, axi...]
    unnamed x16 -> x17, local copies, waits for them, and re-layouts: 3.67 us -> 6.36 us
    concatenate x2 -> x0, other arithmetic: 1.56 us -> none  [local(): block = jnp.concatenate([block, other], axis=0)]
    pallas_call x1, Pallas kernels: 6.2 us -> 4.95 us  [project(): pl.pallas_call(functools.partial(project_kernel, order, fast), in_specs=[...]
  transfers between devices with their start and end apart: 9 -> 8, of which waited for: 5 -> 5; matrix products, arithmetic and copies ran while one was open for 3% -> 6% of each run, Pallas kernels for 13% -> 13%
where the time goes in v7:
time: 88.9 us; the launch traced here: 88.1 us
  blocking collectives  20.4 us (23%)
  waiting for transfers between devices  19.7 us (22%)
  Pallas kernels  18.4 us (21%)
  starting transfers between devices  17.2 us (19%)
  local copies, waits for them, and re-layouts  7.07 us (8%)
  other arithmetic  4.35 us (5%)
    all_to_all x2, blocking collectives, exchange(): lax.all_to_all(blocks, AXIS, split_axis=0, concat_axis=0, tiled=True, axi...  20.4 us
    all_to_all x3, starting transfers between devices, exchange(): lax.all_to_all(blocks, AXIS, split_axis=0, concat_axis=0, tiled=True, axi...  15.1 us
    all_to_all x3, waiting for transfers between devices, exchange(): lax.all_to_all(blocks, AXIS, split_axis=0, concat_axis=0, tiled=True, axi...  11 us
    ppermute x5, waiting for transfers between devices, swap(): return lax.ppermute(block, AXIS, [(i, i ^ bit) for i in range(devices)])  8.73 us
    unnamed x17, local copies, waits for them, and re-layouts  6.36 us
    pallas_call x1, Pallas kernels, project(): pl.pallas_call(functools.partial(project_kernel, order, fast), in_specs=[...  4.95 us
    pallas_call x1, Pallas kernels, output(): pl.pallas_call(functools.partial(output_kernel, fast), in_specs=[whole(SM...  3.93 us
    pallas_call x1, Pallas kernels, plane_rows(): pl.pallas_call(functools.partial(rows_kernel, order), in_specs=[whole(SME...  3.37 us
  transfers between devices with their start and end apart: 8, of which 5 were waited for; matrix products, arithmetic and copies ran while one was open for 6% of the time, Pallas kernels for 13%

profile of v7, /device:TPU:0, one launch (start us, length us, event | category | flops | bytes accessed | tf_op | source)
XLA Modules:
  0.0 88.1 jit_solution(10330209303883097659)
XLA Ops:
  0.0 1.6 %prepare.1 = (bf16[8,144,128]{2,1,0:T(8,128)(2,1)}, f32[64,128]{1,0:T(8,128)}, s32[16]{0:T(128)}, s32[16]{0:T(128)}) custom-call(bf16[2,8192]{1,0:T(2,128)(2,1)} %bitcast.11, bf16[64,128]{1,0:T(8,128)(2,1)} %bitcast.12, s32[1,32]{1,0:T(1,128)} %slots_ref.1), custom_call_target="tpu_custom_call" | custom-call | tf_op jit(solution)/shard_map/prepare/pallas_call | solution.py:87
  1.6 7.3 %all-to-all-start = ((bf16[8,144,128]{2,1,0:T(8,128)(2,1)}), bf16[8,144,128]{2,1,0:T(8,128)(2,1)S(1)}, u32[]{:S(2)}, u32[]{:S(2)}) async-start(bf16[8,144,128]{2,1,0:T(8,128)(2,1)} %get-tuple-element.12), calls=%async_computation | async-start | bytes 589824 | tf_op jit(solution)/shard_map/all_to_all | solution.py:560
  8.9 1.2 %copy-done.3 = bf16[32,16,1024]{2,1,0:T(8,128)(2,1)S(1)} copy-done((bf16[32,16,1024]{2,1,0:T(8,128)(2,1)S(1)}, bf16[32,16,1024]{2,1,0:T(8,128)(2,1)}, u32[]{:S(2)}) %copy-start.3) | copy-done | bytes 1048600
  10.3 2.1 %collective-permute-start.2 = (bf16[512,512]{1,0:T(8,128)(2,1)S(1)}, bf16[512,512]{1,0:T(8,128)(2,1)S(1)}, u32[]{:S(2)}, u32[]{:S(2)}) collective-permute-start(bf16[512,512]{1,0:T(8,128)(2,1)S(1)} %get-tuple-element.16), channel_id=1, source_target_pairs={{0,2},{1,3},{2,0},{3,1},{4,6},{5,7},{6,4},{7,5},{8,10},{9,11},{10,... | collective-permute-start | bytes 1572872 | tf_op jit(solution)/shard_map/ppermute | solution.py:556
  13.1 1.0 %copy.13 = bf16[1,512,160]{2,1,0:T(8,128)(2,1)S(1)} copy(bf16[1,512,160]{1,2,0:T(8,128)(2,1)} %param.16) | data formatting | bytes 327680 | tf_op args[5]
  14.9 1.0 %fusion = (f32[512,64]{1,0:T(8,128)S(1)}, f32[512,64]{1,0:T(8,128)S(1)}, f32[512,64]{1,0:T(8,128)S(1)}) fusion(f32[64]{0:T(128)S(1)} %multiply_exponential_fusion, f32[512]{0:T(512)S(1)} %get-tuple-element.23), kind=kLoop, calls=%fused_computation.5 | loop fusion | flops 65536 | bytes 395520 | tf_op jit(solution)/shard_map/neg | solution.py:41
  16.8 1.7 %all-to-all-done.first_ref = bf16[8,144,128]{2,1,0:T(8,128)(2,1)S(1)} async-done(((bf16[8,144,128]{2,1,0:T(8,128)(2,1)}), bf16[8,144,128]{2,1,0:T(8,128)(2,1)S(1)}, u32[]{:S(2)}, u32[]{:S(2)}) %all-to-all-start) | async-done | bytes 294944 | tf_op jit(solution)/shard_map/all_to_all | solution.py:560
  19.3 7.2 %collective-permute-done.2.rest_2_ = bf16[512,512]{1,0:T(8,128)(2,1)S(1)} collective-permute-done((bf16[512,512]{1,0:T(8,128)(2,1)S(1)}, bf16[512,512]{1,0:T(8,128)(2,1)S(1)}, u32[]{:S(2)}, u32[]{:S(2)}) %collective-permute-start.2) | collective-permute-done | bytes 524320 | tf_op jit(solution)/shard_map/ppermute | solution.py:556
  26.6 1.7 %copy-done.1 = bf16[8192,128]{1,0:T(8,128)(2,1)S(1)} copy-done((bf16[8192,128]{1,0:T(8,128)(2,1)S(1)}, bf16[8192,128]{1,0:T(8,128)(2,1)}, u32[]{:S(2)}) %copy-start.1) | copy-done | bytes 2097176
  29.0 5.0 %norm_project.1 = bf16[16,16,128]{2,1,0:T(8,128)(2,1)} custom-call(s32[1]{0:T(128)} %bitcast.me_ref, bf16[8,144,128]{2,1,0:T(8,128)(2,1)S(1)} %all-to-all-done.first_ref, bf16[8,144,128]{2,1,0:T(8,128)(2,1)S(1)} %collective-permute-done.second_ref, f32[64,128]{1,0:T(8,128)S(1)} %copy-done.5, bf16[8192,512]{1,0:T(8,128)(2,1)} %wq_ref.1, ...), custom_call_target="tpu_custom_call" | custom-call | flops 335544320 | bytes 10485760 | tf_op jit(solution)/shard_map/norm_project/pallas_call | solution.py:362
  34.0 4.3 %all-to-all-start.1 = ((bf16[16,16,128]{2,1,0:T(8,128)(2,1)}), bf16[16,16,128]{2,1,0:T(8,128)(2,1)S(1)}, u32[]{:S(2)}, u32[]{:S(2)}) async-start(bf16[16,16,128]{2,1,0:T(8,128)(2,1)} %norm_project.1), calls=%async_computation.1 | async-start | bytes 131072 | tf_op jit(solution)/shard_map/all_to_all | solution.py:560
  38.3 1.0 %copy-done.4 = bf16[1,160,1024]{2,1,0:T(8,128)(2,1)S(1)} copy-done((bf16[1,160,1024]{2,1,0:T(8,128)(2,1)S(1)}, bf16[1,160,1024]{2,1,0:T(8,128)(2,1)}, u32[]{:S(2)}) %copy-start.4) | copy-done | bytes 327704
  39.2 1.3 %turned_keys.1.keys_ref = bf16[512,1024]{1,0:T(8,128)(2,1)S(1)} custom-call(s32[16]{0:T(128)S(1)} %copy-done.7, bf16[512,160]{1,0:T(8,128)(2,1)S(1)} %bitcast.9, bf16[160,1024]{1,0:T(8,128)(2,1)S(1)} %bitcast.10, f32[512,128]{1,0:T(8,128)S(1)} %get-tuple-element.27.cos_ref, f32[512,128]{1,0:T(8,128)S(1)} %get-tuple-element.28.sin_ref), custom_call_target="tpu_custom_call" | custom-call | flops 167772160 | bytes 2097152 | tf_op jit(solution)/shard_map/turned_keys/pallas_call | solution.py:269
  40.6 0.8 pad_maximum_fusion.2
  41.4 3.8 %all-to-all-done.1.columns_ref = bf16[16,16,128]{2,1,0:T(8,128)(2,1)S(1)} async-done(((bf16[16,16,128]{2,1,0:T(8,128)(2,1)}), bf16[16,16,128]{2,1,0:T(8,128)(2,1)S(1)}, u32[]{:S(2)}, u32[]{:S(2)}) %all-to-all-start.1) | async-done | bytes 65568 | tf_op jit(solution)/shard_map/all_to_all | solution.py:560
  45.2 1.3 %attend.1 = bf16[16,48,128]{2,1,0:T(8,128)(2,1)} custom-call(bf16[16,16,128]{2,1,0:T(8,128)(2,1)S(1)} %all-to-all-done.1.columns_ref, bf16[512,1024]{1,0:T(8,128)(2,1)S(1)} %turned_keys.1.keys_ref, f32[2,512]{1,0:T(2,128)S(1)} %and_select_fusion.bias_ref, f32[2,128]{1,0:T(2,128)S(1)} %get-tuple-element.29.cos_ref, f32[2,128]{1,0:T(2,128)S(1)} %get-tuple-element.30.sin_ref), custom_call_target="tpu_custom_call" | custom-call | flops 33554432 | bytes 2097152 | tf_op jit(solution)/shard_map/attend/pallas_call | solution.py:471
  46.5 3.5 %all-to-all-start.2 = ((bf16[16,48,128]{2,1,0:T(8,128)(2,1)}), bf16[16,48,128]{2,1,0:T(8,128)(2,1)S(1)}, u32[]{:S(2)}, u32[]{:S(2)}) async-start(bf16[16,48,128]{2,1,0:T(8,128)(2,1)} %attend.1), calls=%async_computation.2 | async-start | bytes 393216 | tf_op jit(solution)/shard_map/all_to_all | solution.py:560
  50.0 3.4 %plane_rows.1.rows_ref = s32[128]{0:T(128)} custom-call(s32[1]{0:T(128)} %bitcast.me_ref, bf16[8,144,128]{2,1,0:T(8,128)(2,1)} %copy-done, bf16[8,144,128]{2,1,0:T(8,128)(2,1)} %copy-done.2), custom_call_target="tpu_custom_call" | custom-call | tf_op jit(solution)/shard_map/plane_rows/pallas_call | solution.py:185
  53.4 5.5 %all-to-all-done.2.weights_ref = bf16[16,48,128]{2,1,0:T(8,128)(2,1)S(1)} async-done(((bf16[16,48,128]{2,1,0:T(8,128)(2,1)}), bf16[16,48,128]{2,1,0:T(8,128)(2,1)S(1)}, u32[]{:S(2)}, u32[]{:S(2)}) %all-to-all-start.2) | async-done | bytes 196640 | tf_op jit(solution)/shard_map/all_to_all | solution.py:560
  59.6 1.7 %mix_values.1 = bf16[4,128,128]{2,1,0:T(8,128)(2,1)S(1)} custom-call(s32[1]{0:T(128)} %bitcast.me_ref, s32[128]{0:T(128)S(1)} %copy-done.6, bf16[16,48,128]{2,1,0:T(8,128)(2,1)S(1)} %all-to-all-done.2.weights_ref, bf16[512,512]{1,0:T(8,128)(2,1)S(1)} %get-tuple-element.15.rest_0_, bf16[512,512]{1,0:T(8,128)(2,1)} %collective-permute-done.1.rest_1_, ...), custom_call_target="tpu_custom_call" | custom-call | flops 67108864 | bytes 4194304 | tf_op jit(solution)/shard_map/mix_values/pallas_call | solution.py:233
  61.3 8.5 %all_to_all.25.lhs_ref = bf16[4,128,128]{2,1,0:T(8,128)(2,1)S(1)} all-to-all(bf16[4,128,128]{2,1,0:T(8,128)(2,1)S(1)} %mix_values.1), channel_id=1, replica_groups={{0,4,8,12},{1,5,9,13},{2,6,10,14},{3,7,11,15},{16,20,24,28},{17,21,25,2..., dimensions={0} | all-to-all | bytes 262144 | tf_op jit(solution)/shard_map/all_to_all | solution.py:560
  69.8 3.9 %output_project.1 = (bf16[8,128,128]{2,1,0:T(8,128)(2,1)S(1)}, bf16[8,128,128]{2,1,0:T(8,128)(2,1)S(1)}) custom-call(s32[1]{0:T(128)} %bitcast.me_ref, bf16[4,128,128]{2,1,0:T(8,128)(2,1)S(1)} %all_to_all.25.lhs_ref, bf16[512,8192]{1,0:T(8,128)(2,1)} %weight_ref.1), custom_call_target="tpu_custom_call" | custom-call | flops 268435456 | bytes 8388608 | tf_op jit(solution)/shard_map/output_project/pallas_call | solution.py:536
  73.8 1.5 %collective-permute-done.4 = bf16[8,128,128]{2,1,0:T(8,128)(2,1)S(1)} collective-permute-done((bf16[8,128,128]{2,1,0:T(8,128)(2,1)S(1)}, bf16[8,128,128]{2,1,0:T(8,128)(2,1)S(1)}, u32[]{:S(2)}, u32[]{:S(2)}) %collective-permute-start.4) | collective-permute-done | bytes 262176 | tf_op jit(solution)/shard_map/ppermute | solution.py:556
  75.4 12.0 %all_to_all.26 = bf16[8,128,128]{2,1,0:T(8,128)(2,1)S(1)} all-to-all(bf16[8,128,128]{2,1,0:T(8,128)(2,1)S(1)} %add_convert_fusion), channel_id=1, replica_groups={{0,2,4,6,8,10,12,14},{1,3,5,7,9,11,13,15},{16,18,20,22,24,26,28,30},{17..., dimensions={0} | all-to-all | bytes 524288 | tf_op jit(solution)/shard_map/all_to_all | solution.py:560
  (35 shorter events, 5.0 us)
Async XLA Ops:
  1.6 36.6 %copy-start.7 = (s32[16]{0:T(128)S(1)}, s32[16]{0:T(128)}, u32[]{:S(2)}) copy-start(s32[16]{0:T(128)} %get-tuple-element.14.pair_ref) | copy-start | bytes 196
  1.6 16.9 %all-to-all-start = ((bf16[8,144,128]{2,1,0:T(8,128)(2,1)}), bf16[8,144,128]{2,1,0:T(8,128)(2,1)S(1)}, u32[]{:S(2)}, u32[]{:S(2)}) async-start(bf16[8,144,128]{2,1,0:T(8,128)(2,1)} %get-tuple-element.12), calls=%async_computation | async-start | bytes 589824 | tf_op jit(solution)/shard_map/all_to_all | solution.py:560
  8.9 1.2 %copy-start.3 = (bf16[32,16,1024]{2,1,0:T(8,128)(2,1)S(1)}, bf16[32,16,1024]{2,1,0:T(8,128)(2,1)}, u32[]{:S(2)}) copy-start(bf16[32,16,1024]{2,1,0:T(8,128)(2,1)} %store_ref.1) | copy-start | bytes 3145732
  10.3 16.2 %collective-permute-start.2 = (bf16[512,512]{1,0:T(8,128)(2,1)S(1)}, bf16[512,512]{1,0:T(8,128)(2,1)S(1)}, u32[]{:S(2)}, u32[]{:S(2)}) collective-permute-start(bf16[512,512]{1,0:T(8,128)(2,1)S(1)} %get-tuple-element.16), channel_id=1, source_target_pairs={{0,2},{1,3},{2,0},{3,1},{4,6},{5,7},{6,4},{7,5},{8,10},{9,11},{10,... | collective-permute-start | bytes 1572872 | tf_op jit(solution)/shard_map/ppermute | solution.py:556
  12.4 41.0 %collective-permute-start.1 = (bf16[512,512]{1,0:T(8,128)(2,1)S(1)}, bf16[512,512]{1,0:T(8,128)(2,1)}, u32[]{:S(2)}, u32[]{:S(2)}) collective-permute-start(bf16[512,512]{1,0:T(8,128)(2,1)S(1)} %get-tuple-element.15.rest_0_), channel_id=1, source_target_pairs={{0,1},{1,0},{2,3},{3,2},{4,5},{5,4},{6,7},{7,6},{8,9},{9,8},{10,11... | collective-permute-start | bytes 1572872 | tf_op jit(solution)/shard_map/ppermute | solution.py:556
  18.5 31.5 %copy-start = (bf16[8,144,128]{2,1,0:T(8,128)(2,1)}, bf16[8,144,128]{2,1,0:T(8,128)(2,1)S(1)}, u32[]{:S(2)}) copy-start(bf16[8,144,128]{2,1,0:T(8,128)(2,1)S(1)} %all-to-all-done.first_ref) | copy-start | bytes 884740
  18.5 8.0 %collective-permute-start = (bf16[8,144,128]{2,1,0:T(8,128)(2,1)S(1)}, bf16[8,144,128]{2,1,0:T(8,128)(2,1)S(1)}, u32[]{:S(2)}, u32[]{:S(2)}) collective-permute-start(bf16[8,144,128]{2,1,0:T(8,128)(2,1)S(1)} %all-to-all-done.first_ref), channel_id=1, source_target_pairs={{0,1},{1,0},{2,3},{3,2},{4,5},{5,4},{6,7},{7,6},{8,9},{9,8},{10,11... | collective-permute-start | bytes 884744 | tf_op jit(solution)/shard_map/ppermute | solution.py:556
  26.6 26.9 %collective-permute-start.3 = (bf16[512,512]{1,0:T(8,128)(2,1)S(1)}, bf16[512,512]{1,0:T(8,128)(2,1)}, u32[]{:S(2)}, u32[]{:S(2)}) collective-permute-start(bf16[512,512]{1,0:T(8,128)(2,1)S(1)} %collective-permute-done.2.rest_2_), channel_id=1, source_target_pairs={{0,1},{1,0},{2,3},{3,2},{4,5},{5,4},{6,7},{7,6},{8,9},{9,8},{10,11... | collective-permute-start | bytes 1572872 | tf_op jit(solution)/shard_map/ppermute | solution.py:556
  26.6 23.4 %copy-start.2 = (bf16[8,144,128]{2,1,0:T(8,128)(2,1)}, bf16[8,144,128]{2,1,0:T(8,128)(2,1)S(1)}, u32[]{:S(2)}) copy-start(bf16[8,144,128]{2,1,0:T(8,128)(2,1)S(1)} %collective-permute-done.second_ref) | copy-start | bytes 884740
  26.6 1.7 %copy-start.1 = (bf16[8192,128]{1,0:T(8,128)(2,1)S(1)}, bf16[8192,128]{1,0:T(8,128)(2,1)}, u32[]{:S(2)}) copy-start(bf16[8192,128]{1,0:T(8,128)(2,1)} %wk_ref.1) | copy-start | bytes 6291460
  28.3 0.8 copy-start.5
  34.0 11.2 %all-to-all-start.1 = ((bf16[16,16,128]{2,1,0:T(8,128)(2,1)}), bf16[16,16,128]{2,1,0:T(8,128)(2,1)S(1)}, u32[]{:S(2)}, u32[]{:S(2)}) async-start(bf16[16,16,128]{2,1,0:T(8,128)(2,1)} %norm_project.1), calls=%async_computation.1 | async-start | bytes 131072 | tf_op jit(solution)/shard_map/all_to_all | solution.py:560
  38.3 1.0 %copy-start.4 = (bf16[1,160,1024]{2,1,0:T(8,128)(2,1)S(1)}, bf16[1,160,1024]{2,1,0:T(8,128)(2,1)}, u32[]{:S(2)}) copy-start(bf16[1,160,1024]{2,1,0:T(8,128)(2,1)} %param.17) | copy-start | bytes 983044
  46.5 12.5 %all-to-all-start.2 = ((bf16[16,48,128]{2,1,0:T(8,128)(2,1)}), bf16[16,48,128]{2,1,0:T(8,128)(2,1)S(1)}, u32[]{:S(2)}, u32[]{:S(2)}) async-start(bf16[16,48,128]{2,1,0:T(8,128)(2,1)} %attend.1), calls=%async_computation.2 | async-start | bytes 393216 | tf_op jit(solution)/shard_map/all_to_all | solution.py:560
  59.0 0.7 copy-start.6
  73.7 1.6 %collective-permute-start.4 = (bf16[8,128,128]{2,1,0:T(8,128)(2,1)S(1)}, bf16[8,128,128]{2,1,0:T(8,128)(2,1)S(1)}, u32[]{:S(2)}, u32[]{:S(2)}) collective-permute-start(bf16[8,128,128]{2,1,0:T(8,128)(2,1)S(1)} %get-tuple-element.18), channel_id=1, source_target_pairs={{0,1},{1,0},{2,3},{3,2},{4,5},{5,4},{6,7},{7,6},{8,9},{9,8},{10,11... | collective-permute-start | bytes 786440 | tf_op jit(solution)/shard_map/ppermute | solution.py:556

commit v8 on v7

--- a/solution.py
+++ b/solution.py
@@ -53,12 +53,13 @@
 
 
 def prepare_kernel(
-    slots_dev, hidden_ref, gain_ref, slots_ref, block_ref, scale_ref, holder_ref, pair_ref, wide_scr
+    slots_dev, hidden_ref, gain_ref, slots_ref, block_ref, holder_ref, pair_ref, wide_scr
 ):
     steps, model = hidden_ref.shape
-    scale_ref[...] = gain_ref[...].astype(F32)
     pieces = model // LANES
     wide = hidden_ref[...].astype(F32)
+    scale = lax.rsqrt(jnp.mean(wide * wide, axis=1, keepdims=True) + 1e-05)
+    wide = wide * scale * gain_ref[...].astype(F32)
     for step in range(steps):
         for c in range(pieces):
             row = step * pieces + c
@@ -87,10 +88,9 @@
     return pl.pallas_call(
         functools.partial(prepare_kernel, slots_dev),
         in_specs=[whole(), whole(), whole(SMEM)],
-        out_specs=(whole(), whole(), whole(SMEM), whole(SMEM)),
+        out_specs=(whole(), whole(SMEM), whole(SMEM)),
         out_shape=(
             jax.ShapeDtypeStruct((copies, rows, LANES), BF16),
-            jax.ShapeDtypeStruct(gain.shape, F32),
             jax.ShapeDtypeStruct((block_slot.shape[1] // 2,), jnp.int32),
             jax.ShapeDtypeStruct((block_slot.shape[1] // 2,), jnp.int32),
         ),
@@ -160,40 +160,6 @@
         compiler_params=pltpu.CompilerParams(vmem_limit_bytes=16 * 2**20),
         name="split_values",
     )(x, store)
-
-
-def rows_kernel(order, me_ref, first_ref, second_ref, out_ref, table_scr, table_smem, sem):
-    half, rows, _ = first_ref.shape
-    for j in range(2 * half):
-        source = first_ref if j < half else second_ref
-        asked = source[j % half, rows - EXTRA :, :].astype(F32)
-        table_scr[j] = asked[:8].astype(jnp.int32)
-    copy = pltpu.make_async_copy(table_scr, table_smem, sem)
-    copy.start()
-    copy.wait()
-    me = me_ref[0]
-    plane = jnp.bitwise_and(me, -PLANE)
-    for j in range(2 * half):
-        session = origin(me, order, j)
-        for k in range(2):
-            for b in range(PLANE):
-                out_ref[session * (2 * PLANE) + k * PLANE + b] = table_smem[j, k, plane + b]
-
-
-def plane_rows(me, first, second, order):
-    count = 2 * first.shape[0]
-    return pl.pallas_call(
-        functools.partial(rows_kernel, order),
-        in_specs=[whole(SMEM), whole(), whole()],
-        out_specs=whole(SMEM),
-        out_shape=jax.ShapeDtypeStruct((count * 2 * PLANE,), jnp.int32),
-        scratch_shapes=[
-            VMEM((count, 8, LANES), jnp.int32),
-            SMEM((count, 8, LANES), jnp.int32),
-            pltpu.SemaphoreType.DMA(()),
-        ],
-        name="plane_rows",
-    )(me, first, second)
 
 
 def mix_kernel(me_ref, rows_ref, weights_ref, *rest):
@@ -288,9 +254,12 @@
 
 
 def project_kernel(
-    order, fast, me_ref, first_ref, second_ref, gain_ref, wq_ref, wk_ref, out_ref,
-    x_scr, lhs_scr, wq_buf, wk_buf, out_scr, sems,
+    order, fast, me_ref, first_ref, second_ref, wq_ref, wk_ref, out_ref, *rest
 ):
+    if fast:
+        rows_ref, x_scr, lhs_scr, wq_buf, wk_buf, out_scr, sems, *asked_scr = rest
+    else:
+        x_scr, lhs_scr, wq_buf, wk_buf, out_scr, sems = rest
     depth, q_cols = wq_ref.shape
     k_cols = wk_ref.shape[1]
     chunks = wq_buf.shape[0]
@@ -312,15 +281,17 @@
     for j in range(2 * half):
         source = first_ref if j < half else second_ref
         x_scr[j * rows : (j + 1) * rows] = source[j % half, :rows, :].astype(F32)
-    squares = jnp.zeros((count, LANES), F32)
+    if fast:
+        table_scr, table_smem, table_sem = asked_scr
+        for j in range(2 * half):
+            source = first_ref if j < half else second_ref
+            asked = source[j % half, rows:, :].astype(F32)
+            table_scr[2 * j : 2 * j + 2, :] = asked[:2].astype(jnp.int32)
+        table_copy = pltpu.make_async_copy(table_scr, table_smem, table_sem)
+        table_copy.start()
     for c in range(pieces):
         part = x_scr[pl.ds(c, count, stride=pieces), :]
-        squares = squares + part * part
-    scale = lax.rsqrt(jnp.sum(squares, axis=1, keepdims=True) * (1.0 / depth) + 1e-05)
-    for c in range(pieces):
-        part = x_scr[pl.ds(c, count, stride=pieces), :]
-        gain = gain_ref[c : c + 1, :]
-        lhs_scr[:, c * LANES : (c + 1) * LANES] = (part * scale * gain).astype(BF16)
+        lhs_scr[:, c * LANES : (c + 1) * LANES] = part.astype(BF16)
     q_sum = jnp.zeros((count, q_cols), F32)
     k_sum = jnp.zeros((count, k_cols), F32)
     for i in range(chunks):
@@ -348,9 +319,16 @@
                 row : row + 1, :
             ]
     out_ref[...] = out_scr[...].astype(BF16)
-
-
-def project(me, first, second, gain, query_weight, kv_weight, order, fast):
+    table_copy.wait()
+    plane = jnp.bitwise_and(me, -PLANE)
+    for j in range(2 * half):
+        place = origin(me, order, j) * (2 * PLANE)
+        for k in range(2):
+            for b in range(PLANE):
+                rows_ref[place + k * PLANE + b] = table_smem[2 * j + k, plane + b]
+
+
+def project(me, first, second, query_weight, kv_weight, order, fast):
     depth, q_cols = query_weight.shape
     k_cols = kv_weight.shape[1]
     pieces = depth // LANES
@@ -361,9 +339,16 @@
     shape = (devices, 16, LANES) if fast else (rows, q_cols + k_cols)
     return pl.pallas_call(
         functools.partial(project_kernel, order, fast),
-        in_specs=[whole(SMEM), whole(), whole(), whole(), whole(pl.ANY), whole(pl.ANY)],
-        out_specs=whole(),
-        out_shape=jax.ShapeDtypeStruct(shape, BF16),
+        in_specs=[whole(SMEM), whole(), whole(), whole(pl.ANY), whole(pl.ANY)],
+        out_specs=(whole(), whole(SMEM)) if fast else whole(),
+        out_shape=(
+            (
+                jax.ShapeDtypeStruct(shape, BF16),
+                jax.ShapeDtypeStruct((devices * 2 * PLANE,), jnp.int32),
+            )
+            if fast
+            else jax.ShapeDtypeStruct(shape, BF16)
+        ),
         scratch_shapes=[
             VMEM((rows * pieces, LANES), F32),
             VMEM((rows, depth), BF16),
@@ -371,7 +356,16 @@
             VMEM((chunks, span, k_cols), BF16),
             VMEM((devices, 16, LANES) if fast else (8, LANES), F32),
             pltpu.SemaphoreType.DMA((2, chunks)),
-        ],
+        ]
+        + (
+            [
+                VMEM((2 * devices, LANES), jnp.int32),
+                SMEM((2 * devices, LANES), jnp.int32),
+                pltpu.SemaphoreType.DMA(()),
+            ]
+            if fast
+            else []
+        ),
         compiler_params=pltpu.CompilerParams(vmem_limit_bytes=PROJECT_LIMIT),
         cost_estimate=pl.CostEstimate(
             flops=2 * rows * depth * (q_cols + k_cols),
@@ -379,7 +373,7 @@
             transcendentals=0,
         ),
         name="norm_project",
-    )(me, first, second, gain, query_weight, kv_weight)
+    )(me, first, second, query_weight, kv_weight)
 
 
 def attend_kernel(fast, columns_ref, keys_ref, bias_ref, cos_ref, sin_ref, *rest):
@@ -587,8 +581,8 @@
     pieces = model // LANES
 
     me_word = me.astype(jnp.int32).reshape(1)
-    block, gain, holder, pair = prepare(
-        hidden[:, 0], norm_gain.reshape(pieces, LANES), block_slot, slots_dev, PAIRS if fast else 1
+    block, holder, pair = prepare(
+        hidden[:, 0], norm_gain.reshape(1, model), block_slot, slots_dev, PAIRS if fast else 1
     )
     if fast:
         same_core = [list(range(core, devices, 2)) for core in range(2)]
@@ -598,7 +592,6 @@
         x = lax.bitwise_and(lax.shift_right_logical(me_word, 1), 1)
         keep, send = split_values(x, value_store)
         neighbour = swap(send, 2, devices)
-        stores = (keep, swap(keep, 1, devices), neighbour, swap(neighbour, 1, devices))
     else:
         order = [0]
         bit = devices // 2
@@ -614,11 +607,13 @@
         block, other, sent_pages = lax.optimization_barrier((block, other, sent_pages))
         fetched = exchange(sent_pages)
     projected = project(
-        me_word, block, other, gain, query_weight, kv_weight, order, fast
-    )
-    if fast:
+        me_word, block, other, query_weight, kv_weight, order, fast
+    )
+    if fast:
+        projected, rows = projected
+        projected, neighbour, pair = lax.optimization_barrier((projected, neighbour, pair))
+        stores = (keep, swap(keep, 1, devices), neighbour, swap(neighbour, 1, devices))
         columns = exchange(projected)
-        rows = plane_rows(me_word, block, other, order)
     else:
         targets = jnp.bitwise_xor(me, jnp.array(order, dtype=jnp.int32))
         columns = exchange(projected.reshape(devices, STEPS, q_cols + k_cols)[targets])

time: 88.9 us -> 81.4 us (0.916)
  Pallas kernels: 18.4 us -> 14.7 us
  other arithmetic: 4.35 us -> 1.7 us
    ppermute x5, waiting for transfers between devices: 8.73 us -> 2.92 us  [swap(): return lax.ppermute(block, AXIS, [(i, i ^ bit) for i in range(devices)])]
    all_to_all x3, waiting for transfers between devices: 11 us -> 15.9 us  [exchange(): lax.all_to_all(blocks, AXIS, split_axis=0, concat_axis=0, tiled=True, axi...]
    pallas_call x1 -> x0, Pallas kernels: 3.37 us -> none  [plane_rows(): pl.pallas_call(functools.partial(rows_kernel, order), in_specs=[whole(SME...]
    unnamed x17 -> x11, local copies, waits for them, and re-layouts: 6.36 us -> 4.84 us
    reshape x0 -> x1, local copies, waits for them, and re-layouts: none -> 1.36 us  [local(): norm_gain.reshape(1, model)]
  transfers between devices with their start and end apart: 8 -> 8, of which waited for: 5 -> 5; matrix products, arithmetic and copies ran while one was open for 6% -> 3% of each run, Pallas kernels for 13% -> 10%
where the time goes in v8:
time: 81.4 us; the launch traced here: 80.7 us
  blocking collectives  20.4 us (25%)
  waiting for transfers between devices  18.9 us (23%)
  starting transfers between devices  17.3 us (21%)
  Pallas kernels  14.7 us (18%)
  local copies, waits for them, and re-layouts  6.91 us (8%)
  other arithmetic  1.7 us (2%)
  between operations  0.83 us (1%)
    all_to_all x2, blocking collectives, exchange(): lax.all_to_all(blocks, AXIS, split_axis=0, concat_axis=0, tiled=True, axi...  20.4 us
    all_to_all x3, waiting for transfers between devices, exchange(): lax.all_to_all(blocks, AXIS, split_axis=0, concat_axis=0, tiled=True, axi...  15.9 us
    all_to_all x3, starting transfers between devices, exchange(): lax.all_to_all(blocks, AXIS, split_axis=0, concat_axis=0, tiled=True, axi...  14.6 us
    pallas_call x1, Pallas kernels, project(): pl.pallas_call(functools.partial(project_kernel, order, fast), in_specs=[...  5.12 us
    unnamed x11, local copies, waits for them, and re-layouts  4.84 us
    pallas_call x1, Pallas kernels, output(): pl.pallas_call(functools.partial(output_kernel, fast), in_specs=[whole(SM...  3.94 us
    ppermute x5, waiting for transfers between devices, swap(): return lax.ppermute(block, AXIS, [(i, i ^ bit) for i in range(devices)])  2.92 us
    ppermute x5, starting transfers between devices, swap(): return lax.ppermute(block, AXIS, [(i, i ^ bit) for i in range(devices)])  2.63 us
  transfers between devices with their start and end apart: 8, of which 5 were waited for; matrix products, arithmetic and copies ran while one was open for 3% of the time, Pallas kernels for 10%

profile of v8, /device:TPU:0, one launch (start us, length us, event | category | flops | bytes accessed | tf_op | source)
XLA Modules:
  0.0 80.7 jit_solution(9406973424401799826)
XLA Ops:
  0.0 1.4 %reshape.72.gain_ref = bf16[1,8192]{1,0:T(2,128)(2,1)} reshape(bf16[8192]{0:T(1024)(128)(2,1)} %param.12) | data formatting | bytes 32768 | tf_op jit(solution)/shard_map/reshape | solution.py:585
  1.4 1.7 %prepare.1 = (bf16[8,144,128]{2,1,0:T(8,128)(2,1)}, s32[16]{0:T(128)}, s32[16]{0:T(128)}) custom-call(bf16[2,8192]{1,0:T(2,128)(2,1)} %bitcast.10, bf16[1,8192]{1,0:T(2,128)(2,1)} %reshape.72.gain_ref, s32[1,32]{1,0:T(1,128)} %slots_ref.1), custom_call_target="tpu_custom_call" | custom-call | tf_op jit(solution)/shard_map/prepare/pallas_call | solution.py:88
  3.1 7.3 %all-to-all-start = ((bf16[8,144,128]{2,1,0:T(8,128)(2,1)}), bf16[8,144,128]{2,1,0:T(8,128)(2,1)S(1)}, u32[]{:S(2)}, u32[]{:S(2)}) async-start(bf16[8,144,128]{2,1,0:T(8,128)(2,1)} %get-tuple-element.16), calls=%async_computation | async-start | bytes 589824 | tf_op jit(solution)/shard_map/all_to_all | solution.py:554
  10.4 1.2 %copy-done.1 = bf16[32,16,1024]{2,1,0:T(8,128)(2,1)S(1)} copy-done((bf16[32,16,1024]{2,1,0:T(8,128)(2,1)S(1)}, bf16[32,16,1024]{2,1,0:T(8,128)(2,1)}, u32[]{:S(2)}) %copy-start.1) | copy-done | bytes 1048600
  11.8 2.1 %collective-permute-start.1 = (bf16[512,512]{1,0:T(8,128)(2,1)S(1)}, bf16[512,512]{1,0:T(8,128)(2,1)S(1)}, u32[]{:S(2)}, u32[]{:S(2)}) collective-permute-start(bf16[512,512]{1,0:T(8,128)(2,1)S(1)} %get-tuple-element.19), channel_id=1, source_target_pairs={{0,2},{1,3},{2,0},{3,1},{4,6},{5,7},{6,4},{7,5},{8,10},{9,11},{10,... | collective-permute-start | bytes 1572872 | tf_op jit(solution)/shard_map/ppermute | solution.py:550
  13.9 1.1 %copy.13 = bf16[1,512,160]{2,1,0:T(8,128)(2,1)S(1)} copy(bf16[1,512,160]{1,2,0:T(8,128)(2,1)} %param.16) | data formatting | bytes 327680 | tf_op args[5]
  15.6 4.4 %all-to-all-done.first_ref = bf16[8,144,128]{2,1,0:T(8,128)(2,1)S(1)} async-done(((bf16[8,144,128]{2,1,0:T(8,128)(2,1)}), bf16[8,144,128]{2,1,0:T(8,128)(2,1)S(1)}, u32[]{:S(2)}, u32[]{:S(2)}) %all-to-all-start) | async-done | bytes 294944 | tf_op jit(solution)/shard_map/all_to_all | solution.py:554
  20.2 1.4 %collective-permute-done.second_ref = bf16[8,144,128]{2,1,0:T(8,128)(2,1)S(1)} collective-permute-done((bf16[8,144,128]{2,1,0:T(8,128)(2,1)S(1)}, bf16[8,144,128]{2,1,0:T(8,128)(2,1)S(1)}, u32[]{:S(2)}, u32[]{:S(2)}) %collective-permute-start) | collective-permute-done | bytes 294944 | tf_op jit(solution)/shard_map/ppermute | solution.py:550
  21.6 1.6 %copy-done = bf16[8192,128]{1,0:T(8,128)(2,1)S(1)} copy-done((bf16[8192,128]{1,0:T(8,128)(2,1)S(1)}, bf16[8192,128]{1,0:T(8,128)(2,1)}, u32[]{:S(2)}) %copy-start) | copy-done | bytes 2097176
  23.2 5.1 %norm_project.1 = (bf16[16,16,128]{2,1,0:T(8,128)(2,1)}, s32[128]{0:T(128)S(1)}) custom-call(s32[1]{0:T(128)} %bitcast.me_ref, bf16[8,144,128]{2,1,0:T(8,128)(2,1)S(1)} %all-to-all-done.first_ref, bf16[8,144,128]{2,1,0:T(8,128)(2,1)S(1)} %collective-permute-done.second_ref, bf16[8192,512]{1,0:T(8,128)(2,1)} %wq_ref.1, bf16[8192,128]{1,0:T(8,128)(2,1)S(1)} %copy-done), custom_call_target="tpu_custom_call" | custom-call | flops 335544320 | bytes 10485760 | tf_op jit(solution)/shard_map/norm_project/pallas_call | solution.py:340
  28.3 3.8 %all-to-all-start.1 = ((bf16[16,16,128]{2,1,0:T(8,128)(2,1)}), bf16[16,16,128]{2,1,0:T(8,128)(2,1)S(1)}, u32[]{:S(2)}, u32[]{:S(2)}) async-start(bf16[16,16,128]{2,1,0:T(8,128)(2,1)} %get-tuple-element.21), calls=%async_computation.1 | async-start | bytes 131072 | tf_op jit(solution)/shard_map/all_to_all | solution.py:554
  32.4 1.0 %fusion = (f32[512,64]{1,0:T(8,128)S(1)}, f32[512,64]{1,0:T(8,128)S(1)}, f32[512,64]{1,0:T(8,128)S(1)}) fusion(f32[64]{0:T(128)S(1)} %multiply_exponential_fusion, f32[512]{0:T(512)S(1)} %get-tuple-element.31), kind=kLoop, calls=%fused_computation.5 | loop fusion | flops 65536 | bytes 395520 | tf_op jit(solution)/shard_map/neg | solution.py:41
  34.2 1.0 %copy-done.2 = bf16[1,160,1024]{2,1,0:T(8,128)(2,1)S(1)} copy-done((bf16[1,160,1024]{2,1,0:T(8,128)(2,1)S(1)}, bf16[1,160,1024]{2,1,0:T(8,128)(2,1)}, u32[]{:S(2)}) %copy-start.2) | copy-done | bytes 327704
  35.1 1.3 %turned_keys.1.keys_ref = bf16[512,1024]{1,0:T(8,128)(2,1)S(1)} custom-call(s32[16]{0:T(128)S(1)} %copy-done.3, bf16[512,160]{1,0:T(8,128)(2,1)S(1)} %bitcast.8, bf16[160,1024]{1,0:T(8,128)(2,1)S(1)} %bitcast.9, f32[512,128]{1,0:T(8,128)S(1)} %get-tuple-element.35.cos_ref, f32[512,128]{1,0:T(8,128)S(1)} %get-tuple-element.36.sin_ref), custom_call_target="tpu_custom_call" | custom-call | flops 167772160 | bytes 2097152 | tf_op jit(solution)/shard_map/turned_keys/pallas_call | solution.py:235
  36.5 2.6 %all-to-all-done.1.columns_ref = bf16[16,16,128]{2,1,0:T(8,128)(2,1)S(1)} async-done(((bf16[16,16,128]{2,1,0:T(8,128)(2,1)}), bf16[16,16,128]{2,1,0:T(8,128)(2,1)S(1)}, u32[]{:S(2)}, u32[]{:S(2)}) %all-to-all-start.1) | async-done | bytes 65568 | tf_op jit(solution)/shard_map/all_to_all | solution.py:554
  39.1 1.3 %attend.1 = bf16[16,48,128]{2,1,0:T(8,128)(2,1)} custom-call(bf16[16,16,128]{2,1,0:T(8,128)(2,1)S(1)} %all-to-all-done.1.columns_ref, bf16[512,1024]{1,0:T(8,128)(2,1)S(1)} %turned_keys.1.keys_ref, f32[2,512]{1,0:T(2,128)S(1)} %and_select_fusion.bias_ref, f32[2,128]{1,0:T(2,128)S(1)} %get-tuple-element.37.cos_ref, f32[2,128]{1,0:T(2,128)S(1)} %get-tuple-element.38.sin_ref), custom_call_target="tpu_custom_call" | custom-call | flops 33554432 | bytes 2097152 | tf_op jit(solution)/shard_map/attend/pallas_call | solution.py:465
  40.4 3.5 %all-to-all-start.2 = ((bf16[16,48,128]{2,1,0:T(8,128)(2,1)}), bf16[16,48,128]{2,1,0:T(8,128)(2,1)S(1)}, u32[]{:S(2)}, u32[]{:S(2)}) async-start(bf16[16,48,128]{2,1,0:T(8,128)(2,1)} %attend.1), calls=%async_computation.2 | async-start | bytes 393216 | tf_op jit(solution)/shard_map/all_to_all | solution.py:554
  43.9 9.0 %all-to-all-done.2.weights_ref = bf16[16,48,128]{2,1,0:T(8,128)(2,1)S(1)} async-done(((bf16[16,48,128]{2,1,0:T(8,128)(2,1)}), bf16[16,48,128]{2,1,0:T(8,128)(2,1)S(1)}, u32[]{:S(2)}, u32[]{:S(2)}) %all-to-all-start.2) | async-done | bytes 196640 | tf_op jit(solution)/shard_map/all_to_all | solution.py:554
  52.9 1.1 %mix_values.1 = bf16[4,128,128]{2,1,0:T(8,128)(2,1)S(1)} custom-call(s32[1]{0:T(128)} %bitcast.me_ref, s32[128]{0:T(128)S(1)} %get-tuple-element.17.rows_ref, bf16[16,48,128]{2,1,0:T(8,128)(2,1)S(1)} %all-to-all-done.2.weights_ref, bf16[512,512]{1,0:T(8,128)(2,1)S(1)} %get-tuple-element.23.rest_0_, bf16[512,512]{1,0:T(8,128)(2,1)S(1)} %collective-permute-done.2.rest_1_, ...), custom_call_target="tpu_custom_call" | custom-call | flops 67108864 | bytes 4194304 | tf_op jit(solution)/shard_map/mix_values/pallas_call | solution.py:199
  54.0 8.5 %all_to_all.25.lhs_ref = bf16[4,128,128]{2,1,0:T(8,128)(2,1)S(1)} all-to-all(bf16[4,128,128]{2,1,0:T(8,128)(2,1)S(1)} %mix_values.1), channel_id=1, replica_groups={{0,4,8,12},{1,5,9,13},{2,6,10,14},{3,7,11,15},{16,20,24,28},{17,21,25,2..., dimensions={0} | all-to-all | bytes 262144 | tf_op jit(solution)/shard_map/all_to_all | solution.py:554
  62.4 3.9 %output_project.1 = (bf16[8,128,128]{2,1,0:T(8,128)(2,1)S(1)}, bf16[8,128,128]{2,1,0:T(8,128)(2,1)S(1)}) custom-call(s32[1]{0:T(128)} %bitcast.me_ref, bf16[4,128,128]{2,1,0:T(8,128)(2,1)S(1)} %all_to_all.25.lhs_ref, bf16[512,8192]{1,0:T(8,128)(2,1)} %weight_ref.1), custom_call_target="tpu_custom_call" | custom-call | flops 268435456 | bytes 8388608 | tf_op jit(solution)/shard_map/output_project/pallas_call | solution.py:530
  66.4 1.5 %collective-permute-done.4 = bf16[8,128,128]{2,1,0:T(8,128)(2,1)S(1)} collective-permute-done((bf16[8,128,128]{2,1,0:T(8,128)(2,1)S(1)}, bf16[8,128,128]{2,1,0:T(8,128)(2,1)S(1)}, u32[]{:S(2)}, u32[]{:S(2)}) %collective-permute-start.4) | collective-permute-done | bytes 262176 | tf_op jit(solution)/shard_map/ppermute | solution.py:550
  68.0 12.0 %all_to_all.26 = bf16[8,128,128]{2,1,0:T(8,128)(2,1)S(1)} all-to-all(bf16[8,128,128]{2,1,0:T(8,128)(2,1)S(1)} %add_convert_fusion), channel_id=1, replica_groups={{0,2,4,6,8,10,12,14},{1,3,5,7,9,11,13,15},{16,18,20,22,24,26,28,30},{17..., dimensions={0} | all-to-all | bytes 524288 | tf_op jit(solution)/shard_map/all_to_all | solution.py:554
  80.1 0.6 reshape.73
  (29 shorter events, 1.6 us)
Async XLA Ops:
  0.0 33.9 %copy-start.4 = (s32[2,1,16]{2,1,0:T(1,128)S(1)}, s32[2,1,16]{2,1,0:T(1,128)}, u32[]{:S(2)}) copy-start(s32[2,1,16]{2,1,0:T(1,128)} %param.21) | copy-start | bytes 388
  3.1 29.1 %copy-start.3 = (s32[16]{0:T(128)S(1)}, s32[16]{0:T(128)}, u32[]{:S(2)}) copy-start(s32[16]{0:T(128)} %get-tuple-element.22.pair_ref) | copy-start | bytes 196
  3.1 16.9 %all-to-all-start = ((bf16[8,144,128]{2,1,0:T(8,128)(2,1)}), bf16[8,144,128]{2,1,0:T(8,128)(2,1)S(1)}, u32[]{:S(2)}, u32[]{:S(2)}) async-start(bf16[8,144,128]{2,1,0:T(8,128)(2,1)} %get-tuple-element.16), calls=%async_computation | async-start | bytes 589824 | tf_op jit(solution)/shard_map/all_to_all | solution.py:554
  10.4 1.2 %copy-start.1 = (bf16[32,16,1024]{2,1,0:T(8,128)(2,1)S(1)}, bf16[32,16,1024]{2,1,0:T(8,128)(2,1)}, u32[]{:S(2)}) copy-start(bf16[32,16,1024]{2,1,0:T(8,128)(2,1)} %store_ref.1) | copy-start | bytes 3145732
  11.8 16.5 %collective-permute-start.1 = (bf16[512,512]{1,0:T(8,128)(2,1)S(1)}, bf16[512,512]{1,0:T(8,128)(2,1)S(1)}, u32[]{:S(2)}, u32[]{:S(2)}) collective-permute-start(bf16[512,512]{1,0:T(8,128)(2,1)S(1)} %get-tuple-element.19), channel_id=1, source_target_pairs={{0,2},{1,3},{2,0},{3,1},{4,6},{5,7},{6,4},{7,5},{8,10},{9,11},{10,... | collective-permute-start | bytes 1572872 | tf_op jit(solution)/shard_map/ppermute | solution.py:550
  13.9 30.0 %collective-permute-start.2 = (bf16[512,512]{1,0:T(8,128)(2,1)S(1)}, bf16[512,512]{1,0:T(8,128)(2,1)S(1)}, u32[]{:S(2)}, u32[]{:S(2)}) collective-permute-start(bf16[512,512]{1,0:T(8,128)(2,1)S(1)} %get-tuple-element.23.rest_0_), channel_id=1, source_target_pairs={{0,1},{1,0},{2,3},{3,2},{4,5},{5,4},{6,7},{7,6},{8,9},{9,8},{10,11... | collective-permute-start | bytes 1572872 | tf_op jit(solution)/shard_map/ppermute | solution.py:550
  20.0 1.6 %collective-permute-start = (bf16[8,144,128]{2,1,0:T(8,128)(2,1)S(1)}, bf16[8,144,128]{2,1,0:T(8,128)(2,1)S(1)}, u32[]{:S(2)}, u32[]{:S(2)}) collective-permute-start(bf16[8,144,128]{2,1,0:T(8,128)(2,1)S(1)} %all-to-all-done.first_ref), channel_id=1, source_target_pairs={{0,1},{1,0},{2,3},{3,2},{4,5},{5,4},{6,7},{7,6},{8,9},{9,8},{10,11... | collective-permute-start | bytes 884744 | tf_op jit(solution)/shard_map/ppermute | solution.py:550
  21.6 1.6 %copy-start = (bf16[8192,128]{1,0:T(8,128)(2,1)S(1)}, bf16[8192,128]{1,0:T(8,128)(2,1)}, u32[]{:S(2)}) copy-start(bf16[8192,128]{1,0:T(8,128)(2,1)} %wk_ref.1) | copy-start | bytes 6291460
  28.3 10.8 %all-to-all-start.1 = ((bf16[16,16,128]{2,1,0:T(8,128)(2,1)}), bf16[16,16,128]{2,1,0:T(8,128)(2,1)S(1)}, u32[]{:S(2)}, u32[]{:S(2)}) async-start(bf16[16,16,128]{2,1,0:T(8,128)(2,1)} %get-tuple-element.21), calls=%async_computation.1 | async-start | bytes 131072 | tf_op jit(solution)/shard_map/all_to_all | solution.py:554
  33.4 19.5 %collective-permute-start.3 = (bf16[512,512]{1,0:T(8,128)(2,1)S(1)}, bf16[512,512]{1,0:T(8,128)(2,1)S(1)}, u32[]{:S(2)}, u32[]{:S(2)}) collective-permute-start(bf16[512,512]{1,0:T(8,128)(2,1)S(1)} %collective-permute-done.1.rest_2_), channel_id=1, source_target_pairs={{0,1},{1,0},{2,3},{3,2},{4,5},{5,4},{6,7},{7,6},{8,9},{9,8},{10,11... | collective-permute-start | bytes 1572872 | tf_op jit(solution)/shard_map/ppermute | solution.py:550
  34.2 1.0 %copy-start.2 = (bf16[1,160,1024]{2,1,0:T(8,128)(2,1)S(1)}, bf16[1,160,1024]{2,1,0:T(8,128)(2,1)}, u32[]{:S(2)}) copy-start(bf16[1,160,1024]{2,1,0:T(8,128)(2,1)} %param.17) | copy-start | bytes 983044
  40.4 12.5 %all-to-all-start.2 = ((bf16[16,48,128]{2,1,0:T(8,128)(2,1)}), bf16[16,48,128]{2,1,0:T(8,128)(2,1)S(1)}, u32[]{:S(2)}, u32[]{:S(2)}) async-start(bf16[16,48,128]{2,1,0:T(8,128)(2,1)} %attend.1), calls=%async_computation.2 | async-start | bytes 393216 | tf_op jit(solution)/shard_map/all_to_all | solution.py:554
  66.4 1.6 %collective-permute-start.4 = (bf16[8,128,128]{2,1,0:T(8,128)(2,1)S(1)}, bf16[8,128,128]{2,1,0:T(8,128)(2,1)S(1)}, u32[]{:S(2)}, u32[]{:S(2)}) collective-permute-start(bf16[8,128,128]{2,1,0:T(8,128)(2,1)S(1)} %get-tuple-element.26), channel_id=1, source_target_pairs={{0,1},{1,0},{2,3},{3,2},{4,5},{5,4},{6,7},{7,6},{8,9},{9,8},{10,11... | collective-permute-start | bytes 786440 | tf_op jit(solution)/shard_map/ppermute | solution.py:550

commit v9 on v8

--- a/solution.py
+++ b/solution.py
@@ -17,7 +17,7 @@
 EXTRA = 16
 PLANE = 4
 PAIRS = 8
-PROJECT_LIMIT = 48 * 2**20
+PROJECT_LIMIT = 52 * 2**20
 AXIS = "session"
 VMEM = pltpu.VMEM
 SMEM = pltpu.SMEM
@@ -59,7 +59,7 @@
     pieces = model // LANES
     wide = hidden_ref[...].astype(F32)
     scale = lax.rsqrt(jnp.mean(wide * wide, axis=1, keepdims=True) + 1e-05)
-    wide = wide * scale * gain_ref[...].astype(F32)
+    wide = wide * scale
     for step in range(steps):
         for c in range(pieces):
             row = step * pieces + c
@@ -76,6 +76,10 @@
         pair = jnp.where(parity == 0, slot - base, slots_ref[0, 2 * m + 1] - base)
         table = jnp.where(lane == holder, pair, table)
     wide_scr[steps * pieces :, :] = table.astype(F32)
+    gain = gain_ref[...].astype(F32)
+    for step in range(steps):
+        rows = slice(step * pieces, (step + 1) * pieces)
+        wide_scr[rows, :] = wide_scr[rows, :] * gain
     block = wide_scr[...].astype(BF16)
     for copy in range(block_ref.shape[0]):
         block_ref[copy] = block
@@ -582,7 +586,7 @@
 
     me_word = me.astype(jnp.int32).reshape(1)
     block, holder, pair = prepare(
-        hidden[:, 0], norm_gain.reshape(1, model), block_slot, slots_dev, PAIRS if fast else 1
+        hidden[:, 0], norm_gain.reshape(pieces, LANES), block_slot, slots_dev, PAIRS if fast else 1
     )
     if fast:
         same_core = [list(range(core, devices, 2)) for core in range(2)]

time: 81.4 us -> 80 us (0.983)
  local copies, waits for them, and re-layouts: 6.91 us -> 3.96 us
  waiting for transfers between devices: 18.9 us -> 20 us
    unnamed x11 -> x9, local copies, waits for them, and re-layouts: 4.84 us -> 3.25 us
    reshape x1 -> x0, local copies, waits for them, and re-layouts: 1.36 us -> none  [local(): norm_gain.reshape(1, model)]
    ppermute x5, waiting for transfers between devices: 2.92 us -> 4.11 us  [swap(): return lax.ppermute(block, AXIS, [(i, i ^ bit) for i in range(devices)])]
  transfers between devices with their start and end apart: 8 -> 8, of which waited for: 5 -> 6; matrix products, arithmetic and copies ran while one was open for 3% -> 3% of each run, Pallas kernels for 10% -> 10%
where the time goes in v9:
time: 80 us; the launch traced here: 79.4 us
  blocking collectives  20.4 us (25%)
  waiting for transfers between devices  20 us (25%)
  starting transfers between devices  17.6 us (22%)
  Pallas kernels  14.8 us (18%)
  local copies, waits for them, and re-layouts  3.96 us (5%)
  other arithmetic  1.7 us (2%)
  between operations  0.83 us (1%)
    all_to_all x2, blocking collectives, exchange(): lax.all_to_all(blocks, AXIS, split_axis=0, concat_axis=0, tiled=True, axi...  20.4 us
    all_to_all x3, waiting for transfers between devices, exchange(): lax.all_to_all(blocks, AXIS, split_axis=0, concat_axis=0, tiled=True, axi...  15.9 us
    all_to_all x3, starting transfers between devices, exchange(): lax.all_to_all(blocks, AXIS, split_axis=0, concat_axis=0, tiled=True, axi...  14.9 us
    pallas_call x1, Pallas kernels, project(): pl.pallas_call(functools.partial(project_kernel, order, fast), in_specs=[...  5.23 us
    ppermute x5, waiting for transfers between devices, swap(): return lax.ppermute(block, AXIS, [(i, i ^ bit) for i in range(devices)])  4.11 us
    pallas_call x1, Pallas kernels, output(): pl.pallas_call(functools.partial(output_kernel, fast), in_specs=[whole(SM...  3.94 us
    unnamed x9, local copies, waits for them, and re-layouts  3.25 us
    ppermute x5, starting transfers between devices, swap(): return lax.ppermute(block, AXIS, [(i, i ^ bit) for i in range(devices)])  2.63 us
  transfers between devices with their start and end apart: 8, of which 6 were waited for; matrix products, arithmetic and copies ran while one was open for 3% of the time, Pallas kernels for 10%

profile of v9, /device:TPU:0, one launch (start us, length us, event | category | flops | bytes accessed | tf_op | source)
XLA Modules:
  0.0 79.4 jit_solution(3056557597022749688)
XLA Ops:
  0.0 1.7 %prepare.1 = (bf16[8,144,128]{2,1,0:T(8,128)(2,1)}, s32[16]{0:T(128)}, s32[16]{0:T(128)}) custom-call(bf16[2,8192]{1,0:T(2,128)(2,1)} %bitcast.11, bf16[64,128]{1,0:T(8,128)(2,1)} %bitcast.12, s32[1,32]{1,0:T(1,128)} %slots_ref.1), custom_call_target="tpu_custom_call" | custom-call | tf_op jit(solution)/shard_map/prepare/pallas_call | solution.py:92
  1.8 7.3 %all-to-all-start = ((bf16[8,144,128]{2,1,0:T(8,128)(2,1)}), bf16[8,144,128]{2,1,0:T(8,128)(2,1)S(1)}, u32[]{:S(2)}, u32[]{:S(2)}) async-start(bf16[8,144,128]{2,1,0:T(8,128)(2,1)} %get-tuple-element.16), calls=%async_computation | async-start | bytes 589824 | tf_op jit(solution)/shard_map/all_to_all | solution.py:558
  9.0 1.2 %copy-done = bf16[32,16,1024]{2,1,0:T(8,128)(2,1)S(1)} copy-done((bf16[32,16,1024]{2,1,0:T(8,128)(2,1)S(1)}, bf16[32,16,1024]{2,1,0:T(8,128)(2,1)}, u32[]{:S(2)}) %copy-start) | copy-done | bytes 1048600
  10.5 2.1 %collective-permute-start.1 = (bf16[512,512]{1,0:T(8,128)(2,1)S(1)}, bf16[512,512]{1,0:T(8,128)(2,1)S(1)}, u32[]{:S(2)}, u32[]{:S(2)}) collective-permute-start(bf16[512,512]{1,0:T(8,128)(2,1)S(1)} %get-tuple-element.19), channel_id=1, source_target_pairs={{0,2},{1,3},{2,0},{3,1},{4,6},{5,7},{6,4},{7,5},{8,10},{9,11},{10,... | collective-permute-start | bytes 1572872 | tf_op jit(solution)/shard_map/ppermute | solution.py:554
  12.5 1.1 %copy.13 = bf16[1,512,160]{2,1,0:T(8,128)(2,1)S(1)} copy(bf16[1,512,160]{1,2,0:T(8,128)(2,1)} %param.16) | data formatting | bytes 327680 | tf_op args[5]
  14.3 4.4 %all-to-all-done.first_ref = bf16[8,144,128]{2,1,0:T(8,128)(2,1)S(1)} async-done(((bf16[8,144,128]{2,1,0:T(8,128)(2,1)}), bf16[8,144,128]{2,1,0:T(8,128)(2,1)S(1)}, u32[]{:S(2)}, u32[]{:S(2)}) %all-to-all-start) | async-done | bytes 294944 | tf_op jit(solution)/shard_map/all_to_all | solution.py:558
  18.8 1.4 %collective-permute-done.second_ref = bf16[8,144,128]{2,1,0:T(8,128)(2,1)S(1)} collective-permute-done((bf16[8,144,128]{2,1,0:T(8,128)(2,1)S(1)}, bf16[8,144,128]{2,1,0:T(8,128)(2,1)S(1)}, u32[]{:S(2)}, u32[]{:S(2)}) %collective-permute-start) | collective-permute-done | bytes 294944 | tf_op jit(solution)/shard_map/ppermute | solution.py:554
  20.2 5.2 %norm_project.1 = (bf16[16,16,128]{2,1,0:T(8,128)(2,1)}, s32[128]{0:T(128)S(1)}) custom-call(s32[1]{0:T(128)} %bitcast.me_ref, bf16[8,144,128]{2,1,0:T(8,128)(2,1)S(1)} %all-to-all-done.first_ref, bf16[8,144,128]{2,1,0:T(8,128)(2,1)S(1)} %collective-permute-done.second_ref, bf16[8192,512]{1,0:T(8,128)(2,1)} %wq_ref.1, bf16[8192,128]{1,0:T(8,128)(2,1)} %wk_ref.1), custom_call_target="tpu_custom_call" | custom-call | flops 335544320 | bytes 10485760 | tf_op jit(solution)/shard_map/norm_project/pallas_call | solution.py:344
  25.5 1.2 %collective-permute-done.1.rest_2_ = bf16[512,512]{1,0:T(8,128)(2,1)S(1)} collective-permute-done((bf16[512,512]{1,0:T(8,128)(2,1)S(1)}, bf16[512,512]{1,0:T(8,128)(2,1)S(1)}, u32[]{:S(2)}, u32[]{:S(2)}) %collective-permute-start.1) | collective-permute-done | bytes 524320 | tf_op jit(solution)/shard_map/ppermute | solution.py:554
  26.7 4.1 %all-to-all-start.1 = ((bf16[16,16,128]{2,1,0:T(8,128)(2,1)}), bf16[16,16,128]{2,1,0:T(8,128)(2,1)S(1)}, u32[]{:S(2)}, u32[]{:S(2)}) async-start(bf16[16,16,128]{2,1,0:T(8,128)(2,1)} %get-tuple-element.21), calls=%async_computation.1 | async-start | bytes 131072 | tf_op jit(solution)/shard_map/all_to_all | solution.py:558
  31.0 1.0 %fusion = (f32[512,64]{1,0:T(8,128)S(1)}, f32[512,64]{1,0:T(8,128)S(1)}, f32[512,64]{1,0:T(8,128)S(1)}) fusion(f32[64]{0:T(128)S(1)} %multiply_exponential_fusion, f32[512]{0:T(512)S(1)} %get-tuple-element.31), kind=kLoop, calls=%fused_computation.5 | loop fusion | flops 65536 | bytes 395520 | tf_op jit(solution)/shard_map/neg | solution.py:41
  32.0 0.5 collective-permute-start.3
  32.8 1.0 %copy-done.1 = bf16[1,160,1024]{2,1,0:T(8,128)(2,1)S(1)} copy-done((bf16[1,160,1024]{2,1,0:T(8,128)(2,1)S(1)}, bf16[1,160,1024]{2,1,0:T(8,128)(2,1)}, u32[]{:S(2)}) %copy-start.1) | copy-done | bytes 327704
  33.8 1.3 %turned_keys.1.keys_ref = bf16[512,1024]{1,0:T(8,128)(2,1)S(1)} custom-call(s32[16]{0:T(128)S(1)} %copy-done.2, bf16[512,160]{1,0:T(8,128)(2,1)S(1)} %bitcast.9, bf16[160,1024]{1,0:T(8,128)(2,1)S(1)} %bitcast.10, f32[512,128]{1,0:T(8,128)S(1)} %get-tuple-element.35.cos_ref, f32[512,128]{1,0:T(8,128)S(1)} %get-tuple-element.36.sin_ref), custom_call_target="tpu_custom_call" | custom-call | flops 167772160 | bytes 2097152 | tf_op jit(solution)/shard_map/turned_keys/pallas_call | solution.py:239
  35.1 2.6 %all-to-all-done.1.columns_ref = bf16[16,16,128]{2,1,0:T(8,128)(2,1)S(1)} async-done(((bf16[16,16,128]{2,1,0:T(8,128)(2,1)}), bf16[16,16,128]{2,1,0:T(8,128)(2,1)S(1)}, u32[]{:S(2)}, u32[]{:S(2)}) %all-to-all-start.1) | async-done | bytes 65568 | tf_op jit(solution)/shard_map/all_to_all | solution.py:558
  37.7 1.3 %attend.1 = bf16[16,48,128]{2,1,0:T(8,128)(2,1)} custom-call(bf16[16,16,128]{2,1,0:T(8,128)(2,1)S(1)} %all-to-all-done.1.columns_ref, bf16[512,1024]{1,0:T(8,128)(2,1)S(1)} %turned_keys.1.keys_ref, f32[2,512]{1,0:T(2,128)S(1)} %and_select_fusion.bias_ref, f32[2,128]{1,0:T(2,128)S(1)} %get-tuple-element.37.cos_ref, f32[2,128]{1,0:T(2,128)S(1)} %get-tuple-element.38.sin_ref), custom_call_target="tpu_custom_call" | custom-call | flops 33554432 | bytes 2097152 | tf_op jit(solution)/shard_map/attend/pallas_call | solution.py:469
  39.0 3.5 %all-to-all-start.2 = ((bf16[16,48,128]{2,1,0:T(8,128)(2,1)}), bf16[16,48,128]{2,1,0:T(8,128)(2,1)S(1)}, u32[]{:S(2)}, u32[]{:S(2)}) async-start(bf16[16,48,128]{2,1,0:T(8,128)(2,1)} %attend.1), calls=%async_computation.2 | async-start | bytes 393216 | tf_op jit(solution)/shard_map/all_to_all | solution.py:558
  42.6 9.0 %all-to-all-done.2.weights_ref = bf16[16,48,128]{2,1,0:T(8,128)(2,1)S(1)} async-done(((bf16[16,48,128]{2,1,0:T(8,128)(2,1)}), bf16[16,48,128]{2,1,0:T(8,128)(2,1)S(1)}, u32[]{:S(2)}, u32[]{:S(2)}) %all-to-all-start.2) | async-done | bytes 196640 | tf_op jit(solution)/shard_map/all_to_all | solution.py:558
  51.5 1.1 %mix_values.1 = bf16[4,128,128]{2,1,0:T(8,128)(2,1)S(1)} custom-call(s32[1]{0:T(128)} %bitcast.me_ref, s32[128]{0:T(128)S(1)} %get-tuple-element.17.rows_ref, bf16[16,48,128]{2,1,0:T(8,128)(2,1)S(1)} %all-to-all-done.2.weights_ref, bf16[512,512]{1,0:T(8,128)(2,1)S(1)} %get-tuple-element.23.rest_0_, bf16[512,512]{1,0:T(8,128)(2,1)S(1)} %collective-permute-done.2.rest_1_, ...), custom_call_target="tpu_custom_call" | custom-call | flops 67108864 | bytes 4194304 | tf_op jit(solution)/shard_map/mix_values/pallas_call | solution.py:203
  52.6 8.5 %all_to_all.25.lhs_ref = bf16[4,128,128]{2,1,0:T(8,128)(2,1)S(1)} all-to-all(bf16[4,128,128]{2,1,0:T(8,128)(2,1)S(1)} %mix_values.1), channel_id=1, replica_groups={{0,4,8,12},{1,5,9,13},{2,6,10,14},{3,7,11,15},{16,20,24,28},{17,21,25,2..., dimensions={0} | all-to-all | bytes 262144 | tf_op jit(solution)/shard_map/all_to_all | solution.py:558
  61.1 3.9 %output_project.1 = (bf16[8,128,128]{2,1,0:T(8,128)(2,1)S(1)}, bf16[8,128,128]{2,1,0:T(8,128)(2,1)S(1)}) custom-call(s32[1]{0:T(128)} %bitcast.me_ref, bf16[4,128,128]{2,1,0:T(8,128)(2,1)S(1)} %all_to_all.25.lhs_ref, bf16[512,8192]{1,0:T(8,128)(2,1)} %weight_ref.1), custom_call_target="tpu_custom_call" | custom-call | flops 268435456 | bytes 8388608 | tf_op jit(solution)/shard_map/output_project/pallas_call | solution.py:534
  65.1 1.5 %collective-permute-done.4 = bf16[8,128,128]{2,1,0:T(8,128)(2,1)S(1)} collective-permute-done((bf16[8,128,128]{2,1,0:T(8,128)(2,1)S(1)}, bf16[8,128,128]{2,1,0:T(8,128)(2,1)S(1)}, u32[]{:S(2)}, u32[]{:S(2)}) %collective-permute-start.4) | collective-permute-done | bytes 262176 | tf_op jit(solution)/shard_map/ppermute | solution.py:554
  66.7 12.0 %all_to_all.26 = bf16[8,128,128]{2,1,0:T(8,128)(2,1)S(1)} all-to-all(bf16[8,128,128]{2,1,0:T(8,128)(2,1)S(1)} %add_convert_fusion), channel_id=1, replica_groups={{0,2,4,6,8,10,12,14},{1,3,5,7,9,11,13,15},{16,18,20,22,24,26,28,30},{17..., dimensions={0} | all-to-all | bytes 524288 | tf_op jit(solution)/shard_map/all_to_all | solution.py:558
  78.7 0.6 reshape.73
  (26 shorter events, 1.1 us)
Async XLA Ops:
  0.0 32.5 %copy-start.3 = (s32[2,1,16]{2,1,0:T(1,128)S(1)}, s32[2,1,16]{2,1,0:T(1,128)}, u32[]{:S(2)}) copy-start(s32[2,1,16]{2,1,0:T(1,128)} %param.21) | copy-start | bytes 388
  1.8 29.1 %copy-start.2 = (s32[16]{0:T(128)S(1)}, s32[16]{0:T(128)}, u32[]{:S(2)}) copy-start(s32[16]{0:T(128)} %get-tuple-element.22.pair_ref) | copy-start | bytes 196
  1.8 16.9 %all-to-all-start = ((bf16[8,144,128]{2,1,0:T(8,128)(2,1)}), bf16[8,144,128]{2,1,0:T(8,128)(2,1)S(1)}, u32[]{:S(2)}, u32[]{:S(2)}) async-start(bf16[8,144,128]{2,1,0:T(8,128)(2,1)} %get-tuple-element.16), calls=%async_computation | async-start | bytes 589824 | tf_op jit(solution)/shard_map/all_to_all | solution.py:558
  9.0 1.2 %copy-start = (bf16[32,16,1024]{2,1,0:T(8,128)(2,1)S(1)}, bf16[32,16,1024]{2,1,0:T(8,128)(2,1)}, u32[]{:S(2)}) copy-start(bf16[32,16,1024]{2,1,0:T(8,128)(2,1)} %store_ref.1) | copy-start | bytes 3145732
  10.5 16.2 %collective-permute-start.1 = (bf16[512,512]{1,0:T(8,128)(2,1)S(1)}, bf16[512,512]{1,0:T(8,128)(2,1)S(1)}, u32[]{:S(2)}, u32[]{:S(2)}) collective-permute-start(bf16[512,512]{1,0:T(8,128)(2,1)S(1)} %get-tuple-element.19), channel_id=1, source_target_pairs={{0,2},{1,3},{2,0},{3,1},{4,6},{5,7},{6,4},{7,5},{8,10},{9,11},{10,... | collective-permute-start | bytes 1572872 | tf_op jit(solution)/shard_map/ppermute | solution.py:554
  12.5 30.0 %collective-permute-start.2 = (bf16[512,512]{1,0:T(8,128)(2,1)S(1)}, bf16[512,512]{1,0:T(8,128)(2,1)S(1)}, u32[]{:S(2)}, u32[]{:S(2)}) collective-permute-start(bf16[512,512]{1,0:T(8,128)(2,1)S(1)} %get-tuple-element.23.rest_0_), channel_id=1, source_target_pairs={{0,1},{1,0},{2,3},{3,2},{4,5},{5,4},{6,7},{7,6},{8,9},{9,8},{10,11... | collective-permute-start | bytes 1572872 | tf_op jit(solution)/shard_map/ppermute | solution.py:554
  18.6 1.6 %collective-permute-start = (bf16[8,144,128]{2,1,0:T(8,128)(2,1)S(1)}, bf16[8,144,128]{2,1,0:T(8,128)(2,1)S(1)}, u32[]{:S(2)}, u32[]{:S(2)}) collective-permute-start(bf16[8,144,128]{2,1,0:T(8,128)(2,1)S(1)} %all-to-all-done.first_ref), channel_id=1, source_target_pairs={{0,1},{1,0},{2,3},{3,2},{4,5},{5,4},{6,7},{7,6},{8,9},{9,8},{10,11... | collective-permute-start | bytes 884744 | tf_op jit(solution)/shard_map/ppermute | solution.py:554
  26.7 11.1 %all-to-all-start.1 = ((bf16[16,16,128]{2,1,0:T(8,128)(2,1)}), bf16[16,16,128]{2,1,0:T(8,128)(2,1)S(1)}, u32[]{:S(2)}, u32[]{:S(2)}) async-start(bf16[16,16,128]{2,1,0:T(8,128)(2,1)} %get-tuple-element.21), calls=%async_computation.1 | async-start | bytes 131072 | tf_op jit(solution)/shard_map/all_to_all | solution.py:558
  32.0 19.5 %collective-permute-start.3 = (bf16[512,512]{1,0:T(8,128)(2,1)S(1)}, bf16[512,512]{1,0:T(8,128)(2,1)S(1)}, u32[]{:S(2)}, u32[]{:S(2)}) collective-permute-start(bf16[512,512]{1,0:T(8,128)(2,1)S(1)} %collective-permute-done.1.rest_2_), channel_id=1, source_target_pairs={{0,1},{1,0},{2,3},{3,2},{4,5},{5,4},{6,7},{7,6},{8,9},{9,8},{10,11... | collective-permute-start | bytes 1572872 | tf_op jit(solution)/shard_map/ppermute | solution.py:554
  32.8 1.0 %copy-start.1 = (bf16[1,160,1024]{2,1,0:T(8,128)(2,1)S(1)}, bf16[1,160,1024]{2,1,0:T(8,128)(2,1)}, u32[]{:S(2)}) copy-start(bf16[1,160,1024]{2,1,0:T(8,128)(2,1)} %param.17) | copy-start | bytes 983044
  39.0 12.5 %all-to-all-start.2 = ((bf16[16,48,128]{2,1,0:T(8,128)(2,1)}), bf16[16,48,128]{2,1,0:T(8,128)(2,1)S(1)}, u32[]{:S(2)}, u32[]{:S(2)}) async-start(bf16[16,48,128]{2,1,0:T(8,128)(2,1)} %attend.1), calls=%async_computation.2 | async-start | bytes 393216 | tf_op jit(solution)/shard_map/all_to_all | solution.py:558
  65.0 1.6 %collective-permute-start.4 = (bf16[8,128,128]{2,1,0:T(8,128)(2,1)S(1)}, bf16[8,128,128]{2,1,0:T(8,128)(2,1)S(1)}, u32[]{:S(2)}, u32[]{:S(2)}) collective-permute-start(bf16[8,128,128]{2,1,0:T(8,128)(2,1)S(1)} %get-tuple-element.26), channel_id=1, source_target_pairs={{0,1},{1,0},{2,3},{3,2},{4,5},{5,4},{6,7},{7,6},{8,9},{9,8},{10,11... | collective-permute-start | bytes 786440 | tf_op jit(solution)/shard_map/ppermute | solution.py:554

commit v10 on v9

--- a/solution.py
+++ b/solution.py
@@ -17,7 +17,7 @@
 EXTRA = 16
 PLANE = 4
 PAIRS = 8
-PROJECT_LIMIT = 52 * 2**20
+PROJECT_LIMIT = 48 * 2**20
 AXIS = "session"
 VMEM = pltpu.VMEM
 SMEM = pltpu.SMEM
@@ -167,12 +167,13 @@
 
 
 def mix_kernel(me_ref, rows_ref, weights_ref, *rest):
-    stores, (out_ref, values_scr, sum_scr) = rest[:PLANE], rest[PLANE:]
+    stores, (values_scr, sum_scr) = rest[:PLANE], rest[-2:]
+    out_refs = rest[PLANE:-2]
     me = me_ref[0]
     low = jnp.bitwise_and(me, PLANE - 1)
     z_me = lax.div(me, PLANE)
     sessions = weights_ref.shape[0]
-    planes = out_ref.shape[0]
+    planes = len(out_refs)
     block_len = values_scr.shape[1] // (2 * PLANE)
     for session in range(sessions):
         for q, store in enumerate(stores):
@@ -193,7 +194,8 @@
             sum_scr[z, mine, :] = product[z * 8 : (z + 1) * 8, z * LANES : (z + 1) * LANES]
         recent = block[planes * 8 :].astype(F32)
         sum_scr[z_me, mine, :] += recent[:8]
-    out_ref[...] = sum_scr[...].astype(BF16)
+    for q, out_ref in enumerate(out_refs):
+        out_ref[...] = sum_scr[jnp.bitwise_xor(z_me, q)].astype(BF16)
 
 
 def mix(me, rows, weights, stores):
@@ -203,8 +205,8 @@
     return pl.pallas_call(
         mix_kernel,
         in_specs=[whole(SMEM)] * 2 + [whole()] * (1 + PLANE),
-        out_specs=whole(),
-        out_shape=jax.ShapeDtypeStruct(shape, BF16),
+        out_specs=(whole(),) * planes,
+        out_shape=(jax.ShapeDtypeStruct(shape[1:], BF16),) * planes,
         scratch_shapes=[VMEM((sessions, LANES, planes * LANES), BF16), VMEM(shape, F32)],
         compiler_params=pltpu.CompilerParams(vmem_limit_bytes=16 * 2**20),
         cost_estimate=pl.CostEstimate(
@@ -255,6 +257,35 @@
         ),
         name="turned_keys",
     )(pair, factors, basis, cosine, sine)
+
+
+def fetch_kernel(source_ref, target_ref, sems):
+    parts = sems.shape[0]
+    span = source_ref.shape[0] // parts
+    copies = []
+    for part in range(parts):
+        rows = pl.ds(part * span, span)
+        copies.append(
+            pltpu.make_async_copy(source_ref.at[rows, :], target_ref.at[rows, :], sems.at[part])
+        )
+        copies[-1].start()
+    for copy in copies:
+        copy.wait()
+
+
+def fetch(weight, limit):
+    return pl.pallas_call(
+        fetch_kernel,
+        in_specs=[whole(pl.ANY)],
+        out_specs=whole(pl.ANY),
+        out_shape=jax.ShapeDtypeStruct(weight.shape, weight.dtype),
+        scratch_shapes=[pltpu.SemaphoreType.DMA((4,))],
+        compiler_params=pltpu.CompilerParams(vmem_limit_bytes=limit * 2**20),
+        cost_estimate=pl.CostEstimate(
+            flops=0, bytes_accessed=2 * weight.size, transcendentals=0
+        ),
+        name="fetch_weight",
+    )(weight)
 
 
 def project_kernel(
@@ -482,32 +513,28 @@
     )(*operands)
 
 
-def output_kernel(fast, me_ref, lhs_ref, weight_ref, *rest):
-    out_refs, (weight_buf, out_scr, heads_scr, sems) = rest[:-4], rest[-4:]
-    chunks, _, span = weight_buf.shape
+def output_kernel(fast, count, me_ref, weight_ref, *rest):
+    lhs_refs, rest = rest[:count], rest[count:]
+    out_refs, (out_scr, heads_scr) = rest[:-2], rest[-2:]
+    chunks = 8
+    span = weight_ref.shape[1] // chunks
     rows = out_scr.shape[0] * LANES // (chunks * span)
     pieces = chunks * span // LANES
-    copies = []
-    for i in range(chunks):
-        copy = pltpu.make_async_copy(
-            weight_ref.at[:, pl.ds(i * span, span)], weight_buf.at[i], sems.at[i]
-        )
-        copy.start()
-        copies.append(copy)
     if fast:
         per = heads_scr.shape[0] // rows
-        total = lhs_ref[0].astype(F32)
-        for z in range(1, lhs_ref.shape[0]):
-            total = total + lhs_ref[z].astype(F32)
+        total = lhs_refs[0][...].astype(F32)
+        for lhs_ref in lhs_refs[1:]:
+            total = total + lhs_ref[...].astype(F32)
         heads_scr[...] = total
         lhs = jnp.concatenate(
             [heads_scr[pl.ds(g, rows, stride=per), :].astype(BF16) for g in range(per)], axis=1
         )
     else:
-        lhs = lhs_ref[...]
+        lhs = lhs_refs[0][...]
     for i in range(chunks):
-        copies[i].wait()
-        part = jnp.dot(lhs, weight_buf[i], preferred_element_type=F32)
+        part = jnp.dot(
+            lhs, weight_ref[:, i * span : (i + 1) * span], preferred_element_type=F32
+        )
         for c in range(span // LANES):
             out_scr[pl.ds(i * (span // LANES) + c, rows, stride=pieces), :] = part[
                 :, c * LANES : (c + 1) * LANES
@@ -525,29 +552,26 @@
 
 def output(me, lhs, weight, rows, fast):
     depth, width = weight.shape
-    chunks = 8
     if fast:
         shape = (rows // (2 * STEPS), STEPS * width // LANES, LANES)
         shapes = (jax.ShapeDtypeStruct(shape, BF16),) * 2
     else:
         shapes = (jax.ShapeDtypeStruct((rows * width // LANES, LANES), BF16),)
     return pl.pallas_call(
-        functools.partial(output_kernel, fast),
-        in_specs=[whole(SMEM), whole(), whole(pl.ANY)],
+        functools.partial(output_kernel, fast, len(lhs)),
+        in_specs=[whole(SMEM)] + [whole()] * (1 + len(lhs)),
         out_specs=(whole(),) * len(shapes),
         out_shape=shapes,
         scratch_shapes=[
-            VMEM((chunks, depth, width // chunks), BF16),
             VMEM((rows * width // LANES, LANES), F32),
-            VMEM(lhs.shape[1:] if fast else (8, LANES), F32),
-            pltpu.SemaphoreType.DMA((chunks,)),
+            VMEM(lhs[0].shape if fast else (8, LANES), F32),
         ],
-        compiler_params=pltpu.CompilerParams(vmem_limit_bytes=48 * 2**20),
+        compiler_params=pltpu.CompilerParams(vmem_limit_bytes=24 * 2**20),
         cost_estimate=pl.CostEstimate(
             flops=2 * rows * depth * width, bytes_accessed=2 * depth * width, transcendentals=0
         ),
         name="output_project",
-    )(me, lhs, weight)
+    )(me, weight, *lhs)
 
 
 def swap(block, bit, devices):
@@ -591,6 +615,8 @@
     if fast:
         same_core = [list(range(core, devices, 2)) for core in range(2)]
         block = exchange(block, same_core)
+        block, kv_weight = lax.optimization_barrier((block, kv_weight))
+        kv_weight = fetch(kv_weight, 50)
         other = swap(block, 1, devices)
         order = None
         x = lax.bitwise_and(lax.shift_right_logical(me_word, 1), 1)
@@ -606,6 +632,8 @@
             if bit:
                 block = jnp.concatenate([block, other], axis=0)
         order = tuple(order)
+    span = 2 * block_len
+    places = (pair[:, None] * span + jnp.arange(span, dtype=jnp.int32)[None, :]).reshape(-1)
     if not fast:
         sent_pages = pick_pages(me_word, block, other, value_store, order)
         block, other, sent_pages = lax.optimization_barrier((block, other, sent_pages))
@@ -615,8 +643,7 @@
     )
     if fast:
         projected, rows = projected
-        projected, neighbour, pair = lax.optimization_barrier((projected, neighbour, pair))
-        stores = (keep, swap(keep, 1, devices), neighbour, swap(neighbour, 1, devices))
+        projected, places = lax.optimization_barrier((projected, places))
         columns = exchange(projected)
     else:
         targets = jnp.bitwise_xor(me, jnp.array(order, dtype=jnp.int32))
@@ -627,8 +654,6 @@
         fresh = jnp.pad(fresh.transpose(1, 0, 2), ((0, 0), (0, 8 - STEPS), (0, 0)))
         columns = jnp.concatenate([query, fresh], axis=1)
 
-    span = 2 * block_len
-    places = (pair[:, None] * span + jnp.arange(span, dtype=jnp.int32)[None, :]).reshape(-1)
     cosine, sine = turn_tables(places.astype(F32))
     keys = make_keys(pair, key_factors[0], key_basis[0], cosine, sine)
     picked = jnp.any(
@@ -639,15 +664,19 @@
         (lengths[0] + jnp.arange(STEPS, dtype=jnp.int32)).astype(F32)
     )
     if fast:
-        blocks = exchange(attend(columns, keys, bias, new_cos, new_sin, None, True))
+        blocks = attend(columns, keys, bias, new_cos, new_sin, None, True)
+        blocks, neighbour = lax.optimization_barrier((blocks, neighbour))
+        stores = (keep, swap(keep, 1, devices), neighbour, swap(neighbour, 1, devices))
+        blocks = exchange(blocks)
         parts = mix(me_word, rows, blocks, stores)
-        groups = [list(range(low, devices, PLANE)) for low in range(PLANE)]
-        lhs = exchange(parts, groups)
+        (*parts, out_weight) = lax.optimization_barrier((*parts, out_weight))
+        out_weight = fetch(out_weight, 43)
+        lhs = [parts[0]] + [swap(parts[q], q * PLANE, devices) for q in range(1, len(parts))]
     else:
         heads = attend(columns, keys, bias, new_cos, new_sin, fetched, False)
         flat = heads.reshape(HEADS // 4, STEPS, 4 * HEAD_DIM).transpose(1, 0, 2)
         flat = flat.reshape(STEPS, devices, model // devices).transpose(1, 0, 2)
-        lhs = exchange(flat).reshape(devices * STEPS, model // devices)
+        lhs = [exchange(flat).reshape(devices * STEPS, model // devices)]
     partial = output(me_word, lhs, out_weight, devices * STEPS, fast)
     if fast:
         near, far = partial

time: 80 us -> 76.4 us (0.955)
  blocking collectives: 20.4 us -> 12.5 us
  Pallas kernels: 14.8 us -> 18.5 us
  starting transfers between devices: 17.6 us -> 21.1 us
  waiting for transfers between devices: 20 us -> 17.6 us
  local copies, waits for them, and re-layouts: 3.96 us -> 2.99 us
    all_to_all x2 -> x1, blocking collectives: 20.4 us -> 12.5 us  [exchange(): lax.all_to_all(blocks, AXIS, split_axis=0, concat_axis=0, tiled=True, axi...]
    ppermute x5 -> x8, starting transfers between devices: 2.63 us -> 6.54 us  [swap(): return lax.ppermute(block, AXIS, [(i, i ^ bit) for i in range(devices)])]
    pallas_call x1 -> x3, Pallas kernels: 3.94 us -> 6.88 us  [the longest x2 5.1 us: fetch(): pl.pallas_call(fetch_kernel, in_specs=[whole(pl.ANY)], out_specs=whole(pl...]
    ppermute x5 -> x8, waiting for transfers between devices: 4.11 us -> 1.54 us  [swap(): return lax.ppermute(block, AXIS, [(i, i ^ bit) for i in range(devices)])]
    unnamed x9, local copies, waits for them, and re-layouts: 3.25 us -> 2.28 us
    pallas_call x1, Pallas kernels: 0.19 us -> 1 us  [split_values(): pl.pallas_call(split_kernel, in_specs=[whole(SMEM), whole()], out_specs=(...]
  transfers between devices with their start and end apart: 8 -> 11, of which waited for: 6 -> 4; matrix products, arithmetic and copies ran while one was open for 3% -> 4% of each run, Pallas kernels for 10% -> 18%
where the time goes in v10:
time: 76.4 us; the launch traced here: 75.8 us
  starting transfers between devices  21.1 us (28%)
  Pallas kernels  18.5 us (24%)
  waiting for transfers between devices  17.6 us (23%)
  blocking collectives  12.5 us (16%)
  local copies, waits for them, and re-layouts  2.99 us (4%)
  other arithmetic  2.32 us (3%)
  between operations  0.88 us (1%)
    all_to_all x3, waiting for transfers between devices, exchange(): lax.all_to_all(blocks, AXIS, split_axis=0, concat_axis=0, tiled=True, axi...  16 us
    all_to_all x3, starting transfers between devices, exchange(): lax.all_to_all(blocks, AXIS, split_axis=0, concat_axis=0, tiled=True, axi...  14.6 us
    all_to_all x1, blocking collectives, exchange(): lax.all_to_all(blocks, AXIS, split_axis=0, concat_axis=0, tiled=True, axi...  12.5 us
    ppermute x8, starting transfers between devices, swap(): return lax.ppermute(block, AXIS, [(i, i ^ bit) for i in range(devices)])  6.54 us
    pallas_call x1, Pallas kernels, project(): pl.pallas_call(functools.partial(project_kernel, order, fast), in_specs=[...  5.13 us
    pallas_call x2, Pallas kernels, fetch(): pl.pallas_call(fetch_kernel, in_specs=[whole(pl.ANY)], out_specs=whole(pl...  5.1 us
    unnamed x9, local copies, waits for them, and re-layouts  2.28 us
    pallas_call x1, Pallas kernels, output(): pl.pallas_call(functools.partial(output_kernel, fast, len(lhs)), in_specs...  1.78 us
  transfers between devices with their start and end apart: 11, of which 4 were waited for; matrix products, arithmetic and copies ran while one was open for 4% of the time, Pallas kernels for 18%

profile of v10, /device:TPU:0, one launch (start us, length us, event | category | flops | bytes accessed | tf_op | source)
XLA Modules:
  0.0 75.8 jit_solution(11115624373729648545)
XLA Ops:
  0.0 1.7 %prepare.1 = (bf16[8,144,128]{2,1,0:T(8,128)(2,1)}, s32[16]{0:T(128)}, s32[16]{0:T(128)}) custom-call(bf16[2,8192]{1,0:T(2,128)(2,1)} %bitcast.11, bf16[64,128]{1,0:T(8,128)(2,1)} %bitcast.12, s32[1,32]{1,0:T(1,128)} %slots_ref.1), custom_call_target="tpu_custom_call" | custom-call | tf_op jit(solution)/shard_map/prepare/pallas_call | solution.py:92
  1.8 7.3 %all-to-all-start = ((bf16[8,144,128]{2,1,0:T(8,128)(2,1)}), bf16[8,144,128]{2,1,0:T(8,128)(2,1)S(1)}, u32[]{:S(2)}, u32[]{:S(2)}) async-start(bf16[8,144,128]{2,1,0:T(8,128)(2,1)} %get-tuple-element.28), calls=%async_computation | async-start | bytes 589824 | tf_op jit(solution)/shard_map/all_to_all | solution.py:582
  9.0 1.2 %copy-done = bf16[32,16,1024]{2,1,0:T(8,128)(2,1)S(1)} copy-done((bf16[32,16,1024]{2,1,0:T(8,128)(2,1)S(1)}, bf16[32,16,1024]{2,1,0:T(8,128)(2,1)}, u32[]{:S(2)}) %copy-start) | copy-done | bytes 1048600
  10.2 1.0 %split_values.1 = (bf16[512,512]{1,0:T(8,128)(2,1)S(1)}, bf16[512,512]{1,0:T(8,128)(2,1)}) custom-call(s32[1]{0:T(128)S(6)} %and.20.x_ref, bf16[32,16,1024]{2,1,0:T(8,128)(2,1)S(1)} %copy-done), custom_call_target="tpu_custom_call" | custom-call | tf_op jit(solution)/shard_map/split_values/pallas_call | solution.py:159
  11.2 2.0 %collective-permute-start.1 = (bf16[512,512]{1,0:T(8,128)(2,1)}, bf16[512,512]{1,0:T(8,128)(2,1)S(1)}, u32[]{:S(2)}, u32[]{:S(2)}) collective-permute-start(bf16[512,512]{1,0:T(8,128)(2,1)} %get-tuple-element.36), channel_id=1, source_target_pairs={{0,2},{1,3},{2,0},{3,1},{4,6},{5,7},{6,4},{7,5},{8,10},{9,11},{10,... | collective-permute-start | bytes 1572872 | tf_op jit(solution)/shard_map/ppermute | solution.py:578
  14.5 1.0 %copy.13 = bf16[1,512,160]{2,1,0:T(8,128)(2,1)S(1)} copy(bf16[1,512,160]{1,2,0:T(8,128)(2,1)} %param.16) | data formatting | bytes 327680 | tf_op args[5]
  15.8 2.9 %all-to-all-done.first_ref = bf16[8,144,128]{2,1,0:T(8,128)(2,1)S(1)} async-done(((bf16[8,144,128]{2,1,0:T(8,128)(2,1)}), bf16[8,144,128]{2,1,0:T(8,128)(2,1)S(1)}, u32[]{:S(2)}, u32[]{:S(2)}) %all-to-all-start) | async-done | bytes 294944 | tf_op jit(solution)/shard_map/all_to_all | solution.py:582
  18.8 1.6 %fetch_weight.2.wk_ref = bf16[8192,128]{1,0:T(8,128)(2,1)S(1)} custom-call(bf16[8192,128]{1,0:T(8,128)(2,1)} %source_ref), custom_call_target="tpu_custom_call" | custom-call | bytes 2097152 | tf_op jit(solution)/shard_map/fetch_weight/pallas_call | solution.py:277
  20.5 5.1 %norm_project.1 = (bf16[16,16,128]{2,1,0:T(8,128)(2,1)}, s32[128]{0:T(128)S(1)}) custom-call(s32[1]{0:T(128)} %bitcast.me_ref, bf16[8,144,128]{2,1,0:T(8,128)(2,1)S(1)} %all-to-all-done.first_ref, bf16[8,144,128]{2,1,0:T(8,128)(2,1)S(1)} %collective-permute-done.second_ref, bf16[8192,512]{1,0:T(8,128)(2,1)} %wq_ref.1, bf16[8192,128]{1,0:T(8,128)(2,1)S(1)} %fetch_weight.2.wk_ref), custom_call_target="tpu_custom_call" | custom-call | flops 335544320 | bytes 10485760 | tf_op jit(solution)/shard_map/norm_project/pallas_call | solution.py:375
  25.6 3.8 %all-to-all-start.1 = ((bf16[16,16,128]{2,1,0:T(8,128)(2,1)}), bf16[16,16,128]{2,1,0:T(8,128)(2,1)S(1)}, u32[]{:S(2)}, u32[]{:S(2)}) async-start(bf16[16,16,128]{2,1,0:T(8,128)(2,1)} %get-tuple-element.34), calls=%async_computation.1 | async-start | bytes 131072 | tf_op jit(solution)/shard_map/all_to_all | solution.py:582
  29.4 1.0 %fusion = (f32[512,64]{1,0:T(8,128)S(1)}, f32[512,64]{1,0:T(8,128)S(1)}, f32[512,64]{1,0:T(8,128)S(1)}) fusion(f32[64]{0:T(128)S(1)} %multiply_exponential_fusion, f32[512]{0:T(512)S(1)} %get-tuple-element.55), kind=kLoop, calls=%fused_computation.5 | loop fusion | flops 65536 | bytes 395520 | tf_op jit(solution)/shard_map/neg | solution.py:41
  30.7 1.3 %turned_keys.1.keys_ref = bf16[512,1024]{1,0:T(8,128)(2,1)S(1)} custom-call(s32[16]{0:T(128)S(1)} %copy-done.2, bf16[512,160]{1,0:T(8,128)(2,1)S(1)} %bitcast.9, bf16[160,1024]{1,0:T(8,128)(2,1)S(1)} %bitcast.10, f32[512,128]{1,0:T(8,128)S(1)} %get-tuple-element.59.cos_ref, f32[512,128]{1,0:T(8,128)S(1)} %get-tuple-element.60.sin_ref), custom_call_target="tpu_custom_call" | custom-call | flops 167772160 | bytes 2097152 | tf_op jit(solution)/shard_map/turned_keys/pallas_call | solution.py:241
  32.1 4.2 %all-to-all-done.1.columns_ref = bf16[16,16,128]{2,1,0:T(8,128)(2,1)S(1)} async-done(((bf16[16,16,128]{2,1,0:T(8,128)(2,1)}), bf16[16,16,128]{2,1,0:T(8,128)(2,1)S(1)}, u32[]{:S(2)}, u32[]{:S(2)}) %all-to-all-start.1) | async-done | bytes 65568 | tf_op jit(solution)/shard_map/all_to_all | solution.py:582
  36.3 1.3 %attend.1 = bf16[16,48,128]{2,1,0:T(8,128)(2,1)} custom-call(bf16[16,16,128]{2,1,0:T(8,128)(2,1)S(1)} %all-to-all-done.1.columns_ref, bf16[512,1024]{1,0:T(8,128)(2,1)S(1)} %turned_keys.1.keys_ref, f32[2,512]{1,0:T(2,128)S(1)} %and_select_fusion.bias_ref, f32[2,128]{1,0:T(2,128)S(1)} %get-tuple-element.61.cos_ref, f32[2,128]{1,0:T(2,128)S(1)} %get-tuple-element.62.sin_ref), custom_call_target="tpu_custom_call" | custom-call | flops 33554432 | bytes 2097152 | tf_op jit(solution)/shard_map/attend/pallas_call | solution.py:500
  37.7 3.5 %all-to-all-start.2 = ((bf16[16,48,128]{2,1,0:T(8,128)(2,1)}), bf16[16,48,128]{2,1,0:T(8,128)(2,1)S(1)}, u32[]{:S(2)}, u32[]{:S(2)}) async-start(bf16[16,48,128]{2,1,0:T(8,128)(2,1)} %attend.1), calls=%async_computation.2 | async-start | bytes 393216 | tf_op jit(solution)/shard_map/all_to_all | solution.py:582
  41.2 9.0 %all-to-all-done.2.weights_ref = bf16[16,48,128]{2,1,0:T(8,128)(2,1)S(1)} async-done(((bf16[16,48,128]{2,1,0:T(8,128)(2,1)}), bf16[16,48,128]{2,1,0:T(8,128)(2,1)S(1)}, u32[]{:S(2)}, u32[]{:S(2)}) %all-to-all-start.2) | async-done | bytes 196640 | tf_op jit(solution)/shard_map/all_to_all | solution.py:582
  50.2 1.1 %mix_values.1 = (bf16[128,128]{1,0:T(8,128)(2,1)S(1)}, bf16[128,128]{1,0:T(8,128)(2,1)S(1)}, bf16[128,128]{1,0:T(8,128)(2,1)S(1)}, bf16[128,128]{1,0:T(8,128)(2,1)S(1)}) custom-call(s32[1]{0:T(128)} %bitcast.me_ref, s32[128]{0:T(128)S(1)} %get-tuple-element.31.rows_ref, bf16[16,48,128]{2,1,0:T(8,128)(2,1)S(1)} %all-to-all-done.2.weights_ref, ...), custom_call_target="tpu_custom_call" | custom-call | flops 67108864 | bytes 4194304 | tf_op jit(solution)/shard_map/mix_values/pallas_call | solution.py:205
  51.3 1.4 %collective-permute-start.5 = (bf16[128,128]{1,0:T(8,128)(2,1)S(1)}, bf16[128,128]{1,0:T(8,128)(2,1)S(1)}, u32[]{:S(2)}, u32[]{:S(2)}) collective-permute-start(bf16[128,128]{1,0:T(8,128)(2,1)S(1)} %get-tuple-element.47), channel_id=1, source_target_pairs={{0,8},{1,9},{2,10},{3,11},{4,12},{5,13},{6,14},{7,15},{8,0},{9,1},... | collective-permute-start | bytes 98312 | tf_op jit(solution)/shard_map/ppermute | solution.py:578
  52.7 3.0 %collective-permute-start.6 = (bf16[128,128]{1,0:T(8,128)(2,1)S(1)}, bf16[128,128]{1,0:T(8,128)(2,1)S(1)}, u32[]{:S(2)}, u32[]{:S(2)}) collective-permute-start(bf16[128,128]{1,0:T(8,128)(2,1)S(1)} %get-tuple-element.48), channel_id=1, source_target_pairs={{0,12},{1,13},{2,14},{3,15},{4,8},{5,9},{6,10},{7,11},{8,4},{9,5},... | collective-permute-start | bytes 98312 | tf_op jit(solution)/shard_map/ppermute | solution.py:578
  55.7 3.5 %fetch_weight.3.weight_ref = bf16[512,8192]{1,0:T(8,128)(2,1)S(1)} custom-call(bf16[512,8192]{1,0:T(8,128)(2,1)} %source_ref.1), custom_call_target="tpu_custom_call" | custom-call | bytes 8388608 | tf_op jit(solution)/shard_map/fetch_weight/pallas_call | solution.py:277
  59.2 1.8 %output_project.1 = (bf16[8,128,128]{2,1,0:T(8,128)(2,1)S(1)}, bf16[8,128,128]{2,1,0:T(8,128)(2,1)S(1)}) custom-call(s32[1]{0:T(128)} %bitcast.me_ref, bf16[512,8192]{1,0:T(8,128)(2,1)S(1)} %fetch_weight.3.weight_ref, bf16[128,128]{1,0:T(8,128)(2,1)S(1)} %get-tuple-element.45.rest_0_, bf16[128,128]{1,0:T(8,128)(2,1)S(1)} %collective-permute-done.4.rest_1_, ...), custom_call_target="tpu_custom_call" | custom-call | flops 268435456 | bytes 8388608 | tf_op jit(solution)/shard_map/output_project/pallas_call | solution.py:560
  61.1 1.5 %collective-permute-done.7 = bf16[8,128,128]{2,1,0:T(8,128)(2,1)S(1)} collective-permute-done((bf16[8,128,128]{2,1,0:T(8,128)(2,1)S(1)}, bf16[8,128,128]{2,1,0:T(8,128)(2,1)S(1)}, u32[]{:S(2)}, u32[]{:S(2)}) %collective-permute-start.7) | collective-permute-done | bytes 262176 | tf_op jit(solution)/shard_map/ppermute | solution.py:578
  62.7 12.5 %all_to_all.20 = bf16[8,128,128]{2,1,0:T(8,128)(2,1)S(1)} all-to-all(bf16[8,128,128]{2,1,0:T(8,128)(2,1)S(1)} %add_convert_fusion), channel_id=1, replica_groups={{0,2,4,6,8,10,12,14},{1,3,5,7,9,11,13,15},{16,18,20,22,24,26,28,30},{17..., dimensions={0} | all-to-all | bytes 524288 | tf_op jit(solution)/shard_map/all_to_all | solution.py:582
  75.2 0.6 reshape.32
  (33 shorter events, 1.6 us)
Async XLA Ops:
  1.8 16.9 %all-to-all-start = ((bf16[8,144,128]{2,1,0:T(8,128)(2,1)}), bf16[8,144,128]{2,1,0:T(8,128)(2,1)S(1)}, u32[]{:S(2)}, u32[]{:S(2)}) async-start(bf16[8,144,128]{2,1,0:T(8,128)(2,1)} %get-tuple-element.28), calls=%async_computation | async-start | bytes 589824 | tf_op jit(solution)/shard_map/all_to_all | solution.py:582
  9.0 1.2 %copy-start = (bf16[32,16,1024]{2,1,0:T(8,128)(2,1)S(1)}, bf16[32,16,1024]{2,1,0:T(8,128)(2,1)}, u32[]{:S(2)}) copy-start(bf16[32,16,1024]{2,1,0:T(8,128)(2,1)} %store_ref.1) | copy-start | bytes 3145732
  11.2 26.4 %collective-permute-start.1 = (bf16[512,512]{1,0:T(8,128)(2,1)}, bf16[512,512]{1,0:T(8,128)(2,1)S(1)}, u32[]{:S(2)}, u32[]{:S(2)}) collective-permute-start(bf16[512,512]{1,0:T(8,128)(2,1)} %get-tuple-element.36), channel_id=1, source_target_pairs={{0,2},{1,3},{2,0},{3,1},{4,6},{5,7},{6,4},{7,5},{8,10},{9,11},{10,... | collective-permute-start | bytes 1572872 | tf_op jit(solution)/shard_map/ppermute | solution.py:578
  13.3 27.9 %collective-permute-start.2 = (bf16[512,512]{1,0:T(8,128)(2,1)S(1)}, bf16[512,512]{1,0:T(8,128)(2,1)S(1)}, u32[]{:S(2)}, u32[]{:S(2)}) collective-permute-start(bf16[512,512]{1,0:T(8,128)(2,1)S(1)} %get-tuple-element.38.rest_0_), channel_id=1, source_target_pairs={{0,1},{1,0},{2,3},{3,2},{4,5},{5,4},{6,7},{7,6},{8,9},{9,8},{10,11... | collective-permute-start | bytes 1572872 | tf_op jit(solution)/shard_map/ppermute | solution.py:578
  18.6 1.8 %collective-permute-start = (bf16[8,144,128]{2,1,0:T(8,128)(2,1)S(1)}, bf16[8,144,128]{2,1,0:T(8,128)(2,1)S(1)}, u32[]{:S(2)}, u32[]{:S(2)}) collective-permute-start(bf16[8,144,128]{2,1,0:T(8,128)(2,1)S(1)} %all-to-all-done.first_ref), channel_id=1, source_target_pairs={{0,1},{1,0},{2,3},{3,2},{4,5},{5,4},{6,7},{7,6},{8,9},{9,8},{10,11... | collective-permute-start | bytes 884744 | tf_op jit(solution)/shard_map/ppermute | solution.py:578
  18.8 11.8 %copy-start.1 = (bf16[1,160,1024]{2,1,0:T(8,128)(2,1)S(1)}, bf16[1,160,1024]{2,1,0:T(8,128)(2,1)}, u32[]{:S(2)}) copy-start(bf16[1,160,1024]{2,1,0:T(8,128)(2,1)} %param.17) | copy-start | bytes 983044
  18.8 11.8 %copy-start.2 = (s32[16]{0:T(128)S(1)}, s32[16]{0:T(128)}, u32[]{:S(2)}) copy-start(s32[16]{0:T(128)} %get-tuple-element.33.pair_ref) | copy-start | bytes 196
  20.4 11.6 %copy-start.3 = (s32[2,1,16]{2,1,0:T(1,128)S(1)}, s32[2,1,16]{2,1,0:T(1,128)}, u32[]{:S(2)}) copy-start(s32[2,1,16]{2,1,0:T(1,128)} %param.21) | copy-start | bytes 388
  25.6 10.7 %all-to-all-start.1 = ((bf16[16,16,128]{2,1,0:T(8,128)(2,1)}), bf16[16,16,128]{2,1,0:T(8,128)(2,1)S(1)}, u32[]{:S(2)}, u32[]{:S(2)}) async-start(bf16[16,16,128]{2,1,0:T(8,128)(2,1)} %get-tuple-element.34), calls=%async_computation.1 | async-start | bytes 131072 | tf_op jit(solution)/shard_map/all_to_all | solution.py:582
  37.7 12.5 %collective-permute-start.3 = (bf16[512,512]{1,0:T(8,128)(2,1)S(1)}, bf16[512,512]{1,0:T(8,128)(2,1)S(1)}, u32[]{:S(2)}, u32[]{:S(2)}) collective-permute-start(bf16[512,512]{1,0:T(8,128)(2,1)S(1)} %collective-permute-done.1.rest_2_), channel_id=1, source_target_pairs={{0,1},{1,0},{2,3},{3,2},{4,5},{5,4},{6,7},{7,6},{8,9},{9,8},{10,11... | collective-permute-start | bytes 1572872 | tf_op jit(solution)/shard_map/ppermute | solution.py:578
  37.7 12.5 %all-to-all-start.2 = ((bf16[16,48,128]{2,1,0:T(8,128)(2,1)}), bf16[16,48,128]{2,1,0:T(8,128)(2,1)S(1)}, u32[]{:S(2)}, u32[]{:S(2)}) async-start(bf16[16,48,128]{2,1,0:T(8,128)(2,1)} %attend.1), calls=%async_computation.2 | async-start | bytes 393216 | tf_op jit(solution)/shard_map/all_to_all | solution.py:582
  51.2 8.0 %collective-permute-start.4 = (bf16[128,128]{1,0:T(8,128)(2,1)S(1)}, bf16[128,128]{1,0:T(8,128)(2,1)S(1)}, u32[]{:S(2)}, u32[]{:S(2)}) collective-permute-start(bf16[128,128]{1,0:T(8,128)(2,1)S(1)} %get-tuple-element.46), channel_id=1, source_target_pairs={{0,4},{1,5},{2,6},{3,7},{4,0},{5,1},{6,2},{7,3},{8,12},{9,13},{10,... | collective-permute-start | bytes 98312 | tf_op jit(solution)/shard_map/ppermute | solution.py:578
  51.3 7.9 %collective-permute-start.5 = (bf16[128,128]{1,0:T(8,128)(2,1)S(1)}, bf16[128,128]{1,0:T(8,128)(2,1)S(1)}, u32[]{:S(2)}, u32[]{:S(2)}) collective-permute-start(bf16[128,128]{1,0:T(8,128)(2,1)S(1)} %get-tuple-element.47), channel_id=1, source_target_pairs={{0,8},{1,9},{2,10},{3,11},{4,12},{5,13},{6,14},{7,15},{8,0},{9,1},... | collective-permute-start | bytes 98312 | tf_op jit(solution)/shard_map/ppermute | solution.py:578
  52.7 6.5 %collective-permute-start.6 = (bf16[128,128]{1,0:T(8,128)(2,1)S(1)}, bf16[128,128]{1,0:T(8,128)(2,1)S(1)}, u32[]{:S(2)}, u32[]{:S(2)}) collective-permute-start(bf16[128,128]{1,0:T(8,128)(2,1)S(1)} %get-tuple-element.48), channel_id=1, source_target_pairs={{0,12},{1,13},{2,14},{3,15},{4,8},{5,9},{6,10},{7,11},{8,4},{9,5},... | collective-permute-start | bytes 98312 | tf_op jit(solution)/shard_map/ppermute | solution.py:578
  61.0 1.6 %collective-permute-start.7 = (bf16[8,128,128]{2,1,0:T(8,128)(2,1)S(1)}, bf16[8,128,128]{2,1,0:T(8,128)(2,1)S(1)}, u32[]{:S(2)}, u32[]{:S(2)}) collective-permute-start(bf16[8,128,128]{2,1,0:T(8,128)(2,1)S(1)} %get-tuple-element.50), channel_id=1, source_target_pairs={{0,1},{1,0},{2,3},{3,2},{4,5},{5,4},{6,7},{7,6},{8,9},{9,8},{10,11... | collective-permute-start | bytes 786440 | tf_op jit(solution)/shard_map/ppermute | solution.py:578

commit v11 on v10

--- a/solution.py
+++ b/solution.py
@@ -166,9 +166,12 @@
     )(x, store)
 
 
-def mix_kernel(me_ref, rows_ref, weights_ref, *rest):
-    stores, (values_scr, sum_scr) = rest[:PLANE], rest[-2:]
-    out_refs = rest[PLANE:-2]
+def mix_kernel(me_ref, rows_ref, weights_ref, matrix_ref, *rest):
+    stores, (head_ref, values_scr, sum_scr, sem) = rest[:PLANE], rest[-4:]
+    out_refs = rest[PLANE:-4]
+    columns = pl.ds(0, head_ref.shape[1])
+    copy = pltpu.make_async_copy(matrix_ref.at[:, columns], head_ref, sem)
+    copy.start()
     me = me_ref[0]
     low = jnp.bitwise_and(me, PLANE - 1)
     z_me = lax.div(me, PLANE)
@@ -196,26 +199,32 @@
         sum_scr[z_me, mine, :] += recent[:8]
     for q, out_ref in enumerate(out_refs):
         out_ref[...] = sum_scr[jnp.bitwise_xor(z_me, q)].astype(BF16)
-
-
-def mix(me, rows, weights, stores):
+    copy.wait()
+
+
+def mix(me, rows, weights, matrix, stores):
     sessions = weights.shape[0]
     planes = stores[0].shape[1] // LANES
     shape = (planes, sessions * 8, LANES)
+    head = jax.ShapeDtypeStruct((matrix.shape[0], matrix.shape[1] // 4), matrix.dtype)
     return pl.pallas_call(
         mix_kernel,
-        in_specs=[whole(SMEM)] * 2 + [whole()] * (1 + PLANE),
-        out_specs=(whole(),) * planes,
-        out_shape=(jax.ShapeDtypeStruct(shape[1:], BF16),) * planes,
-        scratch_shapes=[VMEM((sessions, LANES, planes * LANES), BF16), VMEM(shape, F32)],
-        compiler_params=pltpu.CompilerParams(vmem_limit_bytes=16 * 2**20),
+        in_specs=[whole(SMEM)] * 2 + [whole(), whole(pl.ANY)] + [whole()] * PLANE,
+        out_specs=(whole(),) * planes + (whole(pl.ANY),),
+        out_shape=(jax.ShapeDtypeStruct(shape[1:], BF16),) * planes + (head,),
+        scratch_shapes=[
+            VMEM((sessions, LANES, planes * LANES), BF16),
+            VMEM(shape, F32),
+            pltpu.SemaphoreType.DMA(()),
+        ],
+        compiler_params=pltpu.CompilerParams(vmem_limit_bytes=46 * 2**20),
         cost_estimate=pl.CostEstimate(
             flops=2 * sessions * 32 * LANES * planes * LANES,
             bytes_accessed=4 * stores[0].size * PLANE,
             transcendentals=0,
         ),
         name="mix_values",
-    )(me, rows, weights, *stores)
+    )(me, rows, weights, matrix, *stores)
 
 
 def keys_kernel(pair_ref, factors_ref, basis_ref, cos_ref, sin_ref, out_ref, rows_scr):
@@ -261,28 +270,31 @@
 
 def fetch_kernel(source_ref, target_ref, sems):
     parts = sems.shape[0]
-    span = source_ref.shape[0] // parts
+    rows, width = target_ref.shape
+    columns = pl.ds(source_ref.shape[1] - width, width)
     copies = []
     for part in range(parts):
-        rows = pl.ds(part * span, span)
+        mine = pl.ds(part * (rows // parts), rows // parts)
         copies.append(
-            pltpu.make_async_copy(source_ref.at[rows, :], target_ref.at[rows, :], sems.at[part])
+            pltpu.make_async_copy(
+                source_ref.at[mine, columns], target_ref.at[mine, :], sems.at[part]
+            )
         )
         copies[-1].start()
     for copy in copies:
         copy.wait()
 
 
-def fetch(weight, limit):
+def fetch(weight, limit, width):
     return pl.pallas_call(
         fetch_kernel,
         in_specs=[whole(pl.ANY)],
         out_specs=whole(pl.ANY),
-        out_shape=jax.ShapeDtypeStruct(weight.shape, weight.dtype),
+        out_shape=jax.ShapeDtypeStruct((weight.shape[0], width), weight.dtype),
         scratch_shapes=[pltpu.SemaphoreType.DMA((4,))],
         compiler_params=pltpu.CompilerParams(vmem_limit_bytes=limit * 2**20),
         cost_estimate=pl.CostEstimate(
-            flops=0, bytes_accessed=2 * weight.size, transcendentals=0
+            flops=0, bytes_accessed=2 * weight.shape[0] * width, transcendentals=0
         ),
         name="fetch_weight",
     )(weight)
@@ -292,9 +304,9 @@
     order, fast, me_ref, first_ref, second_ref, wq_ref, wk_ref, out_ref, *rest
 ):
     if fast:
-        rows_ref, x_scr, lhs_scr, wq_buf, wk_buf, out_scr, sems, *asked_scr = rest
+        rows_ref, x_scr, lhs_scr, wq_buf, out_scr, sems, *asked_scr = rest
     else:
-        x_scr, lhs_scr, wq_buf, wk_buf, out_scr, sems = rest
+        x_scr, lhs_scr, wq_buf, out_scr, sems = rest
     depth, q_cols = wq_ref.shape
     k_cols = wk_ref.shape[1]
     chunks = wq_buf.shape[0]
@@ -303,13 +315,8 @@
     copies = []
     for i in range(chunks):
         rows = pl.ds(i * span, span)
-        pair = (
-            pltpu.make_async_copy(wq_ref.at[rows, :], wq_buf.at[i], sems.at[0, i]),
-            pltpu.make_async_copy(wk_ref.at[rows, :], wk_buf.at[i], sems.at[1, i]),
-        )
-        for copy in pair:
-            copy.start()
-        copies.append(pair)
+        copies.append(pltpu.make_async_copy(wq_ref.at[rows, :], wq_buf.at[i], sems.at[i]))
+        copies[-1].start()
     half = first_ref.shape[0]
     count = 2 * half * STEPS
     rows = STEPS * pieces
@@ -330,11 +337,12 @@
     q_sum = jnp.zeros((count, q_cols), F32)
     k_sum = jnp.zeros((count, k_cols), F32)
     for i in range(chunks):
-        for copy in copies[i]:
-            copy.wait()
+        copies[i].wait()
         lhs = lhs_scr[:, i * span : (i + 1) * span]
         q_sum = q_sum + jnp.dot(lhs, wq_buf[i], preferred_element_type=F32)
-        k_sum = k_sum + jnp.dot(lhs, wk_buf[i], preferred_element_type=F32)
+        k_sum = k_sum + jnp.dot(
+            lhs, wk_ref[i * span : (i + 1) * span, :], preferred_element_type=F32
+        )
     if not fast:
         out_ref[:, :q_cols] = q_sum.astype(BF16)
         out_ref[:, q_cols:] = k_sum.astype(BF16)
@@ -374,7 +382,7 @@
     shape = (devices, 16, LANES) if fast else (rows, q_cols + k_cols)
     return pl.pallas_call(
         functools.partial(project_kernel, order, fast),
-        in_specs=[whole(SMEM), whole(), whole(), whole(pl.ANY), whole(pl.ANY)],
+        in_specs=[whole(SMEM), whole(), whole(), whole(pl.ANY), whole()],
         out_specs=(whole(), whole(SMEM)) if fast else whole(),
         out_shape=(
             (
@@ -388,9 +396,8 @@
             VMEM((rows * pieces, LANES), F32),
             VMEM((rows, depth), BF16),
             VMEM((chunks, span, q_cols), BF16),
-            VMEM((chunks, span, k_cols), BF16),
             VMEM((devices, 16, LANES) if fast else (8, LANES), F32),
-            pltpu.SemaphoreType.DMA((2, chunks)),
+            pltpu.SemaphoreType.DMA((chunks,)),
         ]
         + (
             [
@@ -513,11 +520,12 @@
     )(*operands)
 
 
-def output_kernel(fast, count, me_ref, weight_ref, *rest):
-    lhs_refs, rest = rest[:count], rest[count:]
+def output_kernel(fast, count, parts, me_ref, *rest):
+    lhs_refs, weight_refs, rest = rest[:count], rest[count : count + parts], rest[count + parts :]
     out_refs, (out_scr, heads_scr) = rest[:-2], rest[-2:]
     chunks = 8
-    span = weight_ref.shape[1] // chunks
+    span = sum(weight_ref.shape[1] for weight_ref in weight_refs) // chunks
+    places = [(w, c) for w in weight_refs for c in range(0, w.shape[1], span)]
     rows = out_scr.shape[0] * LANES // (chunks * span)
     pieces = chunks * span // LANES
     if fast:
@@ -532,9 +540,8 @@
     else:
         lhs = lhs_refs[0][...]
     for i in range(chunks):
-        part = jnp.dot(
-            lhs, weight_ref[:, i * span : (i + 1) * span], preferred_element_type=F32
-        )
+        weight_ref, first = places[i]
+        part = jnp.dot(lhs, weight_ref[:, first : first + span], preferred_element_type=F32)
         for c in range(span // LANES):
             out_scr[pl.ds(i * (span // LANES) + c, rows, stride=pieces), :] = part[
                 :, c * LANES : (c + 1) * LANES
@@ -550,16 +557,17 @@
             out_ref[j] = out_scr[part, :].astype(BF16)
 
 
-def output(me, lhs, weight, rows, fast):
-    depth, width = weight.shape
+def output(me, lhs, weights, rows, fast):
+    depth = weights[0].shape[0]
+    width = sum(weight.shape[1] for weight in weights)
     if fast:
         shape = (rows // (2 * STEPS), STEPS * width // LANES, LANES)
         shapes = (jax.ShapeDtypeStruct(shape, BF16),) * 2
     else:
         shapes = (jax.ShapeDtypeStruct((rows * width // LANES, LANES), BF16),)
     return pl.pallas_call(
-        functools.partial(output_kernel, fast, len(lhs)),
-        in_specs=[whole(SMEM)] + [whole()] * (1 + len(lhs)),
+        functools.partial(output_kernel, fast, len(lhs), len(weights)),
+        in_specs=[whole(SMEM)] + [whole()] * (len(weights) + len(lhs)),
         out_specs=(whole(),) * len(shapes),
         out_shape=shapes,
         scratch_shapes=[
@@ -571,7 +579,7 @@
             flops=2 * rows * depth * width, bytes_accessed=2 * depth * width, transcendentals=0
         ),
         name="output_project",
-    )(me, weight, *lhs)
+    )(me, *lhs, *weights)
 
 
 def swap(block, bit, devices):
@@ -616,7 +624,7 @@
         same_core = [list(range(core, devices, 2)) for core in range(2)]
         block = exchange(block, same_core)
         block, kv_weight = lax.optimization_barrier((block, kv_weight))
-        kv_weight = fetch(kv_weight, 50)
+        kv_weight = fetch(kv_weight, 50, k_cols)
         other = swap(block, 1, devices)
         order = None
         x = lax.bitwise_and(lax.shift_right_logical(me_word, 1), 1)
@@ -668,15 +676,16 @@
         blocks, neighbour = lax.optimization_barrier((blocks, neighbour))
         stores = (keep, swap(keep, 1, devices), neighbour, swap(neighbour, 1, devices))
         blocks = exchange(blocks)
-        parts = mix(me_word, rows, blocks, stores)
+        (*parts, first_weight) = mix(me_word, rows, blocks, out_weight, stores)
         (*parts, out_weight) = lax.optimization_barrier((*parts, out_weight))
-        out_weight = fetch(out_weight, 43)
+        out_weight = [first_weight, fetch(out_weight, 43, model - first_weight.shape[1])]
         lhs = [parts[0]] + [swap(parts[q], q * PLANE, devices) for q in range(1, len(parts))]
     else:
         heads = attend(columns, keys, bias, new_cos, new_sin, fetched, False)
         flat = heads.reshape(HEADS // 4, STEPS, 4 * HEAD_DIM).transpose(1, 0, 2)
         flat = flat.reshape(STEPS, devices, model // devices).transpose(1, 0, 2)
         lhs = [exchange(flat).reshape(devices * STEPS, model // devices)]
+        out_weight = [out_weight]
     partial = output(me_word, lhs, out_weight, devices * STEPS, fast)
     if fast:
         near, far = partial

time: 76.4 us -> 77.8 us (1.018)
    pallas_call x2, Pallas kernels: 2.86 us -> 4.3 us  [the longest x1 2.52 us: mix(): pl.pallas_call(mix_kernel, in_specs=[whole(SMEM)] * 2 + [whole(), whole(p...]
  transfers between devices with their start and end apart: 11 -> 11, of which waited for: 4 -> 4; matrix products, arithmetic and copies ran while one was open for 4% -> 4% of each run, Pallas kernels for 18% -> 17%
where the time goes in v11:
time: 77.8 us; the launch traced here: 77.2 us
  starting transfers between devices  21.1 us (27%)
  Pallas kernels  19.2 us (25%)
  waiting for transfers between devices  17.6 us (23%)
  blocking collectives  13.1 us (17%)
  local copies, waits for them, and re-layouts  3 us (4%)
  other arithmetic  2.32 us (3%)
  between operations  0.89 us (1%)
    all_to_all x3, waiting for transfers between devices, exchange(): lax.all_to_all(blocks, AXIS, split_axis=0, concat_axis=0, tiled=True, axi...  16 us
    all_to_all x3, starting transfers between devices, exchange(): lax.all_to_all(blocks, AXIS, split_axis=0, concat_axis=0, tiled=True, axi...  14.6 us
    all_to_all x1, blocking collectives, exchange(): lax.all_to_all(blocks, AXIS, split_axis=0, concat_axis=0, tiled=True, axi...  13.1 us
    ppermute x8, starting transfers between devices, swap(): return lax.ppermute(block, AXIS, [(i, i ^ bit) for i in range(devices)])  6.54 us
    pallas_call x1, Pallas kernels, project(): pl.pallas_call(functools.partial(project_kernel, order, fast), in_specs=[...  5.07 us
    pallas_call x2, Pallas kernels, fetch(): pl.pallas_call(fetch_kernel, in_specs=[whole(pl.ANY)], out_specs=whole(pl...  4.42 us
    pallas_call x1, Pallas kernels, mix(): pl.pallas_call(mix_kernel, in_specs=[whole(SMEM)] * 2 + [whole(), whole(p...  2.52 us
    unnamed x9, local copies, waits for them, and re-layouts  2.29 us
  transfers between devices with their start and end apart: 11, of which 4 were waited for; matrix products, arithmetic and copies ran while one was open for 4% of the time, Pallas kernels for 17%

profile of v11, /device:TPU:0, one launch (start us, length us, event | category | flops | bytes accessed | tf_op | source)
XLA Modules:
  0.0 77.2 jit_solution(14686130152698928925)
XLA Ops:
  0.0 1.7 %prepare.1 = (bf16[8,144,128]{2,1,0:T(8,128)(2,1)}, s32[16]{0:T(128)}, s32[16]{0:T(128)}) custom-call(bf16[2,8192]{1,0:T(2,128)(2,1)} %bitcast.11, bf16[64,128]{1,0:T(8,128)(2,1)} %bitcast.12, s32[1,32]{1,0:T(1,128)} %slots_ref.1), custom_call_target="tpu_custom_call" | custom-call | tf_op jit(solution)/shard_map/prepare/pallas_call | solution.py:92
  1.8 7.3 %all-to-all-start = ((bf16[8,144,128]{2,1,0:T(8,128)(2,1)}), bf16[8,144,128]{2,1,0:T(8,128)(2,1)S(1)}, u32[]{:S(2)}, u32[]{:S(2)}) async-start(bf16[8,144,128]{2,1,0:T(8,128)(2,1)} %get-tuple-element.29), calls=%async_computation | async-start | bytes 589824 | tf_op jit(solution)/shard_map/all_to_all | solution.py:590
  9.0 1.2 %copy-done = bf16[32,16,1024]{2,1,0:T(8,128)(2,1)S(1)} copy-done((bf16[32,16,1024]{2,1,0:T(8,128)(2,1)S(1)}, bf16[32,16,1024]{2,1,0:T(8,128)(2,1)}, u32[]{:S(2)}) %copy-start) | copy-done | bytes 1048600
  10.2 1.0 %split_values.1 = (bf16[512,512]{1,0:T(8,128)(2,1)S(1)}, bf16[512,512]{1,0:T(8,128)(2,1)}) custom-call(s32[1]{0:T(128)S(6)} %and.20.x_ref, bf16[32,16,1024]{2,1,0:T(8,128)(2,1)S(1)} %copy-done), custom_call_target="tpu_custom_call" | custom-call | tf_op jit(solution)/shard_map/split_values/pallas_call | solution.py:159
  11.2 2.0 %collective-permute-start.1 = (bf16[512,512]{1,0:T(8,128)(2,1)}, bf16[512,512]{1,0:T(8,128)(2,1)S(1)}, u32[]{:S(2)}, u32[]{:S(2)}) collective-permute-start(bf16[512,512]{1,0:T(8,128)(2,1)} %get-tuple-element.37), channel_id=1, source_target_pairs={{0,2},{1,3},{2,0},{3,1},{4,6},{5,7},{6,4},{7,5},{8,10},{9,11},{10,... | collective-permute-start | bytes 1572872 | tf_op jit(solution)/shard_map/ppermute | solution.py:586
  14.5 1.0 %copy.13 = bf16[1,512,160]{2,1,0:T(8,128)(2,1)S(1)} copy(bf16[1,512,160]{1,2,0:T(8,128)(2,1)} %param.16) | data formatting | bytes 327680 | tf_op args[5]
  15.8 2.9 %all-to-all-done.first_ref = bf16[8,144,128]{2,1,0:T(8,128)(2,1)S(1)} async-done(((bf16[8,144,128]{2,1,0:T(8,128)(2,1)}), bf16[8,144,128]{2,1,0:T(8,128)(2,1)S(1)}, u32[]{:S(2)}, u32[]{:S(2)}) %all-to-all-start) | async-done | bytes 294944 | tf_op jit(solution)/shard_map/all_to_all | solution.py:590
  18.8 1.6 %fetch_weight.2.wk_ref = bf16[8192,128]{1,0:T(8,128)(2,1)S(1)} custom-call(bf16[8192,128]{1,0:T(8,128)(2,1)} %source_ref), custom_call_target="tpu_custom_call" | custom-call | bytes 2097152 | tf_op jit(solution)/shard_map/fetch_weight/pallas_call | solution.py:289
  20.4 5.1 %norm_project.1 = (bf16[16,16,128]{2,1,0:T(8,128)(2,1)}, s32[128]{0:T(128)S(1)}) custom-call(s32[1]{0:T(128)} %bitcast.me_ref, bf16[8,144,128]{2,1,0:T(8,128)(2,1)S(1)} %all-to-all-done.first_ref, bf16[8,144,128]{2,1,0:T(8,128)(2,1)S(1)} %collective-permute-done.second_ref, bf16[8192,512]{1,0:T(8,128)(2,1)} %wq_ref.1, bf16[8192,128]{1,0:T(8,128)(2,1)S(1)} %fetch_weight.2.wk_ref), custom_call_target="tpu_custom_call" | custom-call | flops 335544320 | bytes 10485760 | tf_op jit(solution)/shard_map/norm_project/pallas_call | solution.py:383
  25.5 3.8 %all-to-all-start.1 = ((bf16[16,16,128]{2,1,0:T(8,128)(2,1)}), bf16[16,16,128]{2,1,0:T(8,128)(2,1)S(1)}, u32[]{:S(2)}, u32[]{:S(2)}) async-start(bf16[16,16,128]{2,1,0:T(8,128)(2,1)} %get-tuple-element.35), calls=%async_computation.1 | async-start | bytes 131072 | tf_op jit(solution)/shard_map/all_to_all | solution.py:590
  29.3 1.0 %fusion = (f32[512,64]{1,0:T(8,128)S(1)}, f32[512,64]{1,0:T(8,128)S(1)}, f32[512,64]{1,0:T(8,128)S(1)}) fusion(f32[64]{0:T(128)S(1)} %multiply_exponential_fusion, f32[512]{0:T(512)S(1)} %get-tuple-element.57), kind=kLoop, calls=%fused_computation.5 | loop fusion | flops 65536 | bytes 395520 | tf_op jit(solution)/shard_map/neg | solution.py:41
  30.6 1.3 %turned_keys.1.keys_ref = bf16[512,1024]{1,0:T(8,128)(2,1)S(1)} custom-call(s32[16]{0:T(128)S(1)} %copy-done.2, bf16[512,160]{1,0:T(8,128)(2,1)S(1)} %bitcast.9, bf16[160,1024]{1,0:T(8,128)(2,1)S(1)} %bitcast.10, f32[512,128]{1,0:T(8,128)S(1)} %get-tuple-element.61.cos_ref, f32[512,128]{1,0:T(8,128)S(1)} %get-tuple-element.62.sin_ref), custom_call_target="tpu_custom_call" | custom-call | flops 167772160 | bytes 2097152 | tf_op jit(solution)/shard_map/turned_keys/pallas_call | solution.py:250
  32.0 4.2 %all-to-all-done.1.columns_ref = bf16[16,16,128]{2,1,0:T(8,128)(2,1)S(1)} async-done(((bf16[16,16,128]{2,1,0:T(8,128)(2,1)}), bf16[16,16,128]{2,1,0:T(8,128)(2,1)S(1)}, u32[]{:S(2)}, u32[]{:S(2)}) %all-to-all-start.1) | async-done | bytes 65568 | tf_op jit(solution)/shard_map/all_to_all | solution.py:590
  36.2 1.3 %attend.1 = bf16[16,48,128]{2,1,0:T(8,128)(2,1)} custom-call(bf16[16,16,128]{2,1,0:T(8,128)(2,1)S(1)} %all-to-all-done.1.columns_ref, bf16[512,1024]{1,0:T(8,128)(2,1)S(1)} %turned_keys.1.keys_ref, f32[2,512]{1,0:T(2,128)S(1)} %and_select_fusion.bias_ref, f32[2,128]{1,0:T(2,128)S(1)} %get-tuple-element.63.cos_ref, f32[2,128]{1,0:T(2,128)S(1)} %get-tuple-element.64.sin_ref), custom_call_target="tpu_custom_call" | custom-call | flops 33554432 | bytes 2097152 | tf_op jit(solution)/shard_map/attend/pallas_call | solution.py:507
  37.6 3.5 %all-to-all-start.2 = ((bf16[16,48,128]{2,1,0:T(8,128)(2,1)}), bf16[16,48,128]{2,1,0:T(8,128)(2,1)S(1)}, u32[]{:S(2)}, u32[]{:S(2)}) async-start(bf16[16,48,128]{2,1,0:T(8,128)(2,1)} %attend.1), calls=%async_computation.2 | async-start | bytes 393216 | tf_op jit(solution)/shard_map/all_to_all | solution.py:590
  41.1 9.0 %all-to-all-done.2.weights_ref = bf16[16,48,128]{2,1,0:T(8,128)(2,1)S(1)} async-done(((bf16[16,48,128]{2,1,0:T(8,128)(2,1)}), bf16[16,48,128]{2,1,0:T(8,128)(2,1)S(1)}, u32[]{:S(2)}, u32[]{:S(2)}) %all-to-all-start.2) | async-done | bytes 196640 | tf_op jit(solution)/shard_map/all_to_all | solution.py:590
  50.1 2.5 %mix_values.1 = (bf16[128,128]{1,0:T(8,128)(2,1)S(1)}, bf16[128,128]{1,0:T(8,128)(2,1)S(1)}, bf16[128,128]{1,0:T(8,128)(2,1)S(1)}, bf16[128,128]{1,0:T(8,128)(2,1)S(1)}, bf16[512,2048]{1,0:T(8,128)(2,1)S(1)}) custom-call(s32[1]{0:T(128)} %bitcast.me_ref, s32[128]{0:T(128)S(1)} %get-tuple-element.32.rows_ref, ...), custom_call_target="tpu_custom_call" | custom-call | flops 67108864 | bytes 4194304 | tf_op jit(solution)/shard_map/mix_values/pallas_call | solution.py:210
  52.7 1.4 %collective-permute-start.5 = (bf16[128,128]{1,0:T(8,128)(2,1)S(1)}, bf16[128,128]{1,0:T(8,128)(2,1)S(1)}, u32[]{:S(2)}, u32[]{:S(2)}) collective-permute-start(bf16[128,128]{1,0:T(8,128)(2,1)S(1)} %get-tuple-element.47), channel_id=1, source_target_pairs={{0,8},{1,9},{2,10},{3,11},{4,12},{5,13},{6,14},{7,15},{8,0},{9,1},... | collective-permute-start | bytes 98312 | tf_op jit(solution)/shard_map/ppermute | solution.py:586
  54.0 3.0 %collective-permute-start.6 = (bf16[128,128]{1,0:T(8,128)(2,1)S(1)}, bf16[128,128]{1,0:T(8,128)(2,1)S(1)}, u32[]{:S(2)}, u32[]{:S(2)}) collective-permute-start(bf16[128,128]{1,0:T(8,128)(2,1)S(1)} %get-tuple-element.48), channel_id=1, source_target_pairs={{0,12},{1,13},{2,14},{3,15},{4,8},{5,9},{6,10},{7,11},{8,4},{9,5},... | collective-permute-start | bytes 98312 | tf_op jit(solution)/shard_map/ppermute | solution.py:586
  57.0 2.9 %fetch_weight.3.rest_5_ = bf16[512,6144]{1,0:T(8,128)(2,1)S(1)} custom-call(bf16[512,8192]{1,0:T(8,128)(2,1)} %source_ref.1), custom_call_target="tpu_custom_call" | custom-call | bytes 6291456 | tf_op jit(solution)/shard_map/fetch_weight/pallas_call | solution.py:289
  59.9 1.8 %output_project.1 = (bf16[8,128,128]{2,1,0:T(8,128)(2,1)S(1)}, bf16[8,128,128]{2,1,0:T(8,128)(2,1)S(1)}) custom-call(s32[1]{0:T(128)} %bitcast.me_ref, bf16[128,128]{1,0:T(8,128)(2,1)S(1)} %get-tuple-element.45.rest_0_, bf16[128,128]{1,0:T(8,128)(2,1)S(1)} %collective-permute-done.4.rest_1_, bf16[128,128]{1,0:T(8,128)(2,1)S(1)} %collective-permute-done.5.rest_2_, ...), custom_call_target="tpu_custom_call" | custom-call | flops 268435456 | bytes 8388608 | tf_op jit(solution)/shard_map/output_project/pallas_call | solution.py:568
  61.8 1.5 %collective-permute-done.7 = bf16[8,128,128]{2,1,0:T(8,128)(2,1)S(1)} collective-permute-done((bf16[8,128,128]{2,1,0:T(8,128)(2,1)S(1)}, bf16[8,128,128]{2,1,0:T(8,128)(2,1)S(1)}, u32[]{:S(2)}, u32[]{:S(2)}) %collective-permute-start.7) | collective-permute-done | bytes 262176 | tf_op jit(solution)/shard_map/ppermute | solution.py:586
  63.4 13.1 %all_to_all.20 = bf16[8,128,128]{2,1,0:T(8,128)(2,1)S(1)} all-to-all(bf16[8,128,128]{2,1,0:T(8,128)(2,1)S(1)} %add_convert_fusion), channel_id=1, replica_groups={{0,2,4,6,8,10,12,14},{1,3,5,7,9,11,13,15},{16,18,20,22,24,26,28,30},{17..., dimensions={0} | all-to-all | bytes 524288 | tf_op jit(solution)/shard_map/all_to_all | solution.py:590
  76.6 0.6 reshape.32
  (33 shorter events, 1.6 us)
Async XLA Ops:
  1.8 16.9 %all-to-all-start = ((bf16[8,144,128]{2,1,0:T(8,128)(2,1)}), bf16[8,144,128]{2,1,0:T(8,128)(2,1)S(1)}, u32[]{:S(2)}, u32[]{:S(2)}) async-start(bf16[8,144,128]{2,1,0:T(8,128)(2,1)} %get-tuple-element.29), calls=%async_computation | async-start | bytes 589824 | tf_op jit(solution)/shard_map/all_to_all | solution.py:590
  9.0 1.2 %copy-start = (bf16[32,16,1024]{2,1,0:T(8,128)(2,1)S(1)}, bf16[32,16,1024]{2,1,0:T(8,128)(2,1)}, u32[]{:S(2)}) copy-start(bf16[32,16,1024]{2,1,0:T(8,128)(2,1)} %store_ref.1) | copy-start | bytes 3145732
  11.2 26.3 %collective-permute-start.1 = (bf16[512,512]{1,0:T(8,128)(2,1)}, bf16[512,512]{1,0:T(8,128)(2,1)S(1)}, u32[]{:S(2)}, u32[]{:S(2)}) collective-permute-start(bf16[512,512]{1,0:T(8,128)(2,1)} %get-tuple-element.37), channel_id=1, source_target_pairs={{0,2},{1,3},{2,0},{3,1},{4,6},{5,7},{6,4},{7,5},{8,10},{9,11},{10,... | collective-permute-start | bytes 1572872 | tf_op jit(solution)/shard_map/ppermute | solution.py:586
  13.3 27.8 %collective-permute-start.2 = (bf16[512,512]{1,0:T(8,128)(2,1)S(1)}, bf16[512,512]{1,0:T(8,128)(2,1)S(1)}, u32[]{:S(2)}, u32[]{:S(2)}) collective-permute-start(bf16[512,512]{1,0:T(8,128)(2,1)S(1)} %get-tuple-element.39.rest_0_), channel_id=1, source_target_pairs={{0,1},{1,0},{2,3},{3,2},{4,5},{5,4},{6,7},{7,6},{8,9},{9,8},{10,11... | collective-permute-start | bytes 1572872 | tf_op jit(solution)/shard_map/ppermute | solution.py:586
  18.6 1.8 %collective-permute-start = (bf16[8,144,128]{2,1,0:T(8,128)(2,1)S(1)}, bf16[8,144,128]{2,1,0:T(8,128)(2,1)S(1)}, u32[]{:S(2)}, u32[]{:S(2)}) collective-permute-start(bf16[8,144,128]{2,1,0:T(8,128)(2,1)S(1)} %all-to-all-done.first_ref), channel_id=1, source_target_pairs={{0,1},{1,0},{2,3},{3,2},{4,5},{5,4},{6,7},{7,6},{8,9},{9,8},{10,11... | collective-permute-start | bytes 884744 | tf_op jit(solution)/shard_map/ppermute | solution.py:586
  20.4 10.2 %copy-start.1 = (bf16[1,160,1024]{2,1,0:T(8,128)(2,1)S(1)}, bf16[1,160,1024]{2,1,0:T(8,128)(2,1)}, u32[]{:S(2)}) copy-start(bf16[1,160,1024]{2,1,0:T(8,128)(2,1)} %param.17) | copy-start | bytes 983044
  20.4 10.2 %copy-start.2 = (s32[16]{0:T(128)S(1)}, s32[16]{0:T(128)}, u32[]{:S(2)}) copy-start(s32[16]{0:T(128)} %get-tuple-element.34.pair_ref) | copy-start | bytes 196
  20.4 11.5 %copy-start.3 = (s32[2,1,16]{2,1,0:T(1,128)S(1)}, s32[2,1,16]{2,1,0:T(1,128)}, u32[]{:S(2)}) copy-start(s32[2,1,16]{2,1,0:T(1,128)} %param.21) | copy-start | bytes 388
  25.5 10.7 %all-to-all-start.1 = ((bf16[16,16,128]{2,1,0:T(8,128)(2,1)}), bf16[16,16,128]{2,1,0:T(8,128)(2,1)S(1)}, u32[]{:S(2)}, u32[]{:S(2)}) async-start(bf16[16,16,128]{2,1,0:T(8,128)(2,1)} %get-tuple-element.35), calls=%async_computation.1 | async-start | bytes 131072 | tf_op jit(solution)/shard_map/all_to_all | solution.py:590
  37.6 12.5 %collective-permute-start.3 = (bf16[512,512]{1,0:T(8,128)(2,1)S(1)}, bf16[512,512]{1,0:T(8,128)(2,1)S(1)}, u32[]{:S(2)}, u32[]{:S(2)}) collective-permute-start(bf16[512,512]{1,0:T(8,128)(2,1)S(1)} %collective-permute-done.1.rest_2_), channel_id=1, source_target_pairs={{0,1},{1,0},{2,3},{3,2},{4,5},{5,4},{6,7},{7,6},{8,9},{9,8},{10,11... | collective-permute-start | bytes 1572872 | tf_op jit(solution)/shard_map/ppermute | solution.py:586
  37.6 12.5 %all-to-all-start.2 = ((bf16[16,48,128]{2,1,0:T(8,128)(2,1)}), bf16[16,48,128]{2,1,0:T(8,128)(2,1)S(1)}, u32[]{:S(2)}, u32[]{:S(2)}) async-start(bf16[16,48,128]{2,1,0:T(8,128)(2,1)} %attend.1), calls=%async_computation.2 | async-start | bytes 393216 | tf_op jit(solution)/shard_map/all_to_all | solution.py:590
  52.6 7.3 %collective-permute-start.4 = (bf16[128,128]{1,0:T(8,128)(2,1)S(1)}, bf16[128,128]{1,0:T(8,128)(2,1)S(1)}, u32[]{:S(2)}, u32[]{:S(2)}) collective-permute-start(bf16[128,128]{1,0:T(8,128)(2,1)S(1)} %get-tuple-element.46), channel_id=1, source_target_pairs={{0,4},{1,5},{2,6},{3,7},{4,0},{5,1},{6,2},{7,3},{8,12},{9,13},{10,... | collective-permute-start | bytes 98312 | tf_op jit(solution)/shard_map/ppermute | solution.py:586
  52.7 7.3 %collective-permute-start.5 = (bf16[128,128]{1,0:T(8,128)(2,1)S(1)}, bf16[128,128]{1,0:T(8,128)(2,1)S(1)}, u32[]{:S(2)}, u32[]{:S(2)}) collective-permute-start(bf16[128,128]{1,0:T(8,128)(2,1)S(1)} %get-tuple-element.47), channel_id=1, source_target_pairs={{0,8},{1,9},{2,10},{3,11},{4,12},{5,13},{6,14},{7,15},{8,0},{9,1},... | collective-permute-start | bytes 98312 | tf_op jit(solution)/shard_map/ppermute | solution.py:586
  54.0 5.9 %collective-permute-start.6 = (bf16[128,128]{1,0:T(8,128)(2,1)S(1)}, bf16[128,128]{1,0:T(8,128)(2,1)S(1)}, u32[]{:S(2)}, u32[]{:S(2)}) collective-permute-start(bf16[128,128]{1,0:T(8,128)(2,1)S(1)} %get-tuple-element.48), channel_id=1, source_target_pairs={{0,12},{1,13},{2,14},{3,15},{4,8},{5,9},{6,10},{7,11},{8,4},{9,5},... | collective-permute-start | bytes 98312 | tf_op jit(solution)/shard_map/ppermute | solution.py:586
  61.7 1.6 %collective-permute-start.7 = (bf16[8,128,128]{2,1,0:T(8,128)(2,1)S(1)}, bf16[8,128,128]{2,1,0:T(8,128)(2,1)S(1)}, u32[]{:S(2)}, u32[]{:S(2)}) collective-permute-start(bf16[8,128,128]{2,1,0:T(8,128)(2,1)S(1)} %get-tuple-element.52), channel_id=1, source_target_pairs={{0,1},{1,0},{2,3},{3,2},{4,5},{5,4},{6,7},{7,6},{8,9},{9,8},{10,11... | collective-permute-start | bytes 786440 | tf_op jit(solution)/shard_map/ppermute | solution.py:586

commit v12 on v10

--- a/solution.py
+++ b/solution.py
@@ -261,28 +261,31 @@
 
 def fetch_kernel(source_ref, target_ref, sems):
     parts = sems.shape[0]
-    span = source_ref.shape[0] // parts
+    rows, width = target_ref.shape
+    columns = pl.ds(source_ref.shape[1] - width, width)
     copies = []
     for part in range(parts):
-        rows = pl.ds(part * span, span)
+        mine = pl.ds(part * (rows // parts), rows // parts)
         copies.append(
-            pltpu.make_async_copy(source_ref.at[rows, :], target_ref.at[rows, :], sems.at[part])
+            pltpu.make_async_copy(
+                source_ref.at[mine, columns], target_ref.at[mine, :], sems.at[part]
+            )
         )
         copies[-1].start()
     for copy in copies:
         copy.wait()
 
 
-def fetch(weight, limit):
+def fetch(weight, limit, width):
     return pl.pallas_call(
         fetch_kernel,
         in_specs=[whole(pl.ANY)],
         out_specs=whole(pl.ANY),
-        out_shape=jax.ShapeDtypeStruct(weight.shape, weight.dtype),
+        out_shape=jax.ShapeDtypeStruct((weight.shape[0], width), weight.dtype),
         scratch_shapes=[pltpu.SemaphoreType.DMA((4,))],
         compiler_params=pltpu.CompilerParams(vmem_limit_bytes=limit * 2**20),
         cost_estimate=pl.CostEstimate(
-            flops=0, bytes_accessed=2 * weight.size, transcendentals=0
+            flops=0, bytes_accessed=2 * weight.shape[0] * width, transcendentals=0
         ),
         name="fetch_weight",
     )(weight)
@@ -292,9 +295,9 @@
     order, fast, me_ref, first_ref, second_ref, wq_ref, wk_ref, out_ref, *rest
 ):
     if fast:
-        rows_ref, x_scr, lhs_scr, wq_buf, wk_buf, out_scr, sems, *asked_scr = rest
+        rows_ref, x_scr, lhs_scr, wq_buf, out_scr, sems, *asked_scr = rest
     else:
-        x_scr, lhs_scr, wq_buf, wk_buf, out_scr, sems = rest
+        x_scr, lhs_scr, wq_buf, out_scr, sems = rest
     depth, q_cols = wq_ref.shape
     k_cols = wk_ref.shape[1]
     chunks = wq_buf.shape[0]
@@ -303,13 +306,8 @@
     copies = []
     for i in range(chunks):
         rows = pl.ds(i * span, span)
-        pair = (
-            pltpu.make_async_copy(wq_ref.at[rows, :], wq_buf.at[i], sems.at[0, i]),
-            pltpu.make_async_copy(wk_ref.at[rows, :], wk_buf.at[i], sems.at[1, i]),
-        )
-        for copy in pair:
-            copy.start()
-        copies.append(pair)
+        copies.append(pltpu.make_async_copy(wq_ref.at[rows, :], wq_buf.at[i], sems.at[i]))
+        copies[-1].start()
     half = first_ref.shape[0]
     count = 2 * half * STEPS
     rows = STEPS * pieces
@@ -330,11 +328,12 @@
     q_sum = jnp.zeros((count, q_cols), F32)
     k_sum = jnp.zeros((count, k_cols), F32)
     for i in range(chunks):
-        for copy in copies[i]:
-            copy.wait()
+        copies[i].wait()
         lhs = lhs_scr[:, i * span : (i + 1) * span]
         q_sum = q_sum + jnp.dot(lhs, wq_buf[i], preferred_element_type=F32)
-        k_sum = k_sum + jnp.dot(lhs, wk_buf[i], preferred_element_type=F32)
+        k_sum = k_sum + jnp.dot(
+            lhs, wk_ref[i * span : (i + 1) * span, :], preferred_element_type=F32
+        )
     if not fast:
         out_ref[:, :q_cols] = q_sum.astype(BF16)
         out_ref[:, q_cols:] = k_sum.astype(BF16)
@@ -374,7 +373,7 @@
     shape = (devices, 16, LANES) if fast else (rows, q_cols + k_cols)
     return pl.pallas_call(
         functools.partial(project_kernel, order, fast),
-        in_specs=[whole(SMEM), whole(), whole(), whole(pl.ANY), whole(pl.ANY)],
+        in_specs=[whole(SMEM), whole(), whole(), whole(pl.ANY), whole()],
         out_specs=(whole(), whole(SMEM)) if fast else whole(),
         out_shape=(
             (
@@ -388,9 +387,8 @@
             VMEM((rows * pieces, LANES), F32),
             VMEM((rows, depth), BF16),
             VMEM((chunks, span, q_cols), BF16),
-            VMEM((chunks, span, k_cols), BF16),
             VMEM((devices, 16, LANES) if fast else (8, LANES), F32),
-            pltpu.SemaphoreType.DMA((2, chunks)),
+            pltpu.SemaphoreType.DMA((chunks,)),
         ]
         + (
             [
@@ -513,9 +511,12 @@
     )(*operands)
 
 
-def output_kernel(fast, count, me_ref, weight_ref, *rest):
+def output_kernel(fast, count, me_ref, weight_ref, last_ref, *rest):
     lhs_refs, rest = rest[:count], rest[count:]
-    out_refs, (out_scr, heads_scr) = rest[:-2], rest[-2:]
+    out_refs, (head_buf, out_scr, heads_scr, sem) = rest[:-4], rest[-4:]
+    width = head_buf.shape[1]
+    head_copy = pltpu.make_async_copy(weight_ref.at[:, pl.ds(0, width)], head_buf, sem)
+    head_copy.start()
     chunks = 8
     span = weight_ref.shape[1] // chunks
     rows = out_scr.shape[0] * LANES // (chunks * span)
@@ -531,9 +532,13 @@
         )
     else:
         lhs = lhs_refs[0][...]
-    for i in range(chunks):
+    first = width // span
+    for i in (*range(first, chunks), *range(first)):
+        if i == 0:
+            head_copy.wait()
+        source, place = (last_ref, i - first) if i >= first else (head_buf, i)
         part = jnp.dot(
-            lhs, weight_ref[:, i * span : (i + 1) * span], preferred_element_type=F32
+            lhs, source[:, place * span : (place + 1) * span], preferred_element_type=F32
         )
         for c in range(span // LANES):
             out_scr[pl.ds(i * (span // LANES) + c, rows, stride=pieces), :] = part[
@@ -550,7 +555,7 @@
             out_ref[j] = out_scr[part, :].astype(BF16)
 
 
-def output(me, lhs, weight, rows, fast):
+def output(me, lhs, weight, last, rows, fast):
     depth, width = weight.shape
     if fast:
         shape = (rows // (2 * STEPS), STEPS * width // LANES, LANES)
@@ -559,19 +564,21 @@
         shapes = (jax.ShapeDtypeStruct((rows * width // LANES, LANES), BF16),)
     return pl.pallas_call(
         functools.partial(output_kernel, fast, len(lhs)),
-        in_specs=[whole(SMEM)] + [whole()] * (1 + len(lhs)),
+        in_specs=[whole(SMEM), whole(pl.ANY)] + [whole()] * (1 + len(lhs)),
         out_specs=(whole(),) * len(shapes),
         out_shape=shapes,
         scratch_shapes=[
+            VMEM((depth, width - last.shape[1]), BF16),
             VMEM((rows * width // LANES, LANES), F32),
             VMEM(lhs[0].shape if fast else (8, LANES), F32),
+            pltpu.SemaphoreType.DMA(()),
         ],
-        compiler_params=pltpu.CompilerParams(vmem_limit_bytes=24 * 2**20),
+        compiler_params=pltpu.CompilerParams(vmem_limit_bytes=46 * 2**20),
         cost_estimate=pl.CostEstimate(
             flops=2 * rows * depth * width, bytes_accessed=2 * depth * width, transcendentals=0
         ),
         name="output_project",
-    )(me, weight, *lhs)
+    )(me, weight, last, *lhs)
 
 
 def swap(block, bit, devices):
@@ -616,7 +623,7 @@
         same_core = [list(range(core, devices, 2)) for core in range(2)]
         block = exchange(block, same_core)
         block, kv_weight = lax.optimization_barrier((block, kv_weight))
-        kv_weight = fetch(kv_weight, 50)
+        kv_weight = fetch(kv_weight, 50, k_cols)
         other = swap(block, 1, devices)
         order = None
         x = lax.bitwise_and(lax.shift_right_logical(me_word, 1), 1)
@@ -670,14 +677,15 @@
         blocks = exchange(blocks)
         parts = mix(me_word, rows, blocks, stores)
         (*parts, out_weight) = lax.optimization_barrier((*parts, out_weight))
-        out_weight = fetch(out_weight, 43)
+        last_weight = fetch(out_weight, 43, model - model // 4)
         lhs = [parts[0]] + [swap(parts[q], q * PLANE, devices) for q in range(1, len(parts))]
     else:
         heads = attend(columns, keys, bias, new_cos, new_sin, fetched, False)
         flat = heads.reshape(HEADS // 4, STEPS, 4 * HEAD_DIM).transpose(1, 0, 2)
         flat = flat.reshape(STEPS, devices, model // devices).transpose(1, 0, 2)
         lhs = [exchange(flat).reshape(devices * STEPS, model // devices)]
-    partial = output(me_word, lhs, out_weight, devices * STEPS, fast)
+        last_weight = out_weight[:, model // 4 :]
+    partial = output(me_word, lhs, out_weight, last_weight, devices * STEPS, fast)
     if fast:
         near, far = partial
         both = near.astype(F32) + swap(far, 1, devices).astype(F32)

time: 76.4 us -> 77.8 us (1.018)
    pallas_call x1, Pallas kernels: 1.78 us -> 3.28 us  [output(): pl.pallas_call(functools.partial(output_kernel, fast, len(lhs)), in_specs...]
  transfers between devices with their start and end apart: 11 -> 11, of which waited for: 4 -> 4; matrix products, arithmetic and copies ran while one was open for 4% -> 4% of each run, Pallas kernels for 18% -> 17%
where the time goes in v12:
time: 77.8 us; the launch traced here: 77.2 us
  starting transfers between devices  21.1 us (27%)
  Pallas kernels  19.2 us (25%)
  waiting for transfers between devices  17.6 us (23%)
  blocking collectives  13.1 us (17%)
  local copies, waits for them, and re-layouts  3 us (4%)
  other arithmetic  2.32 us (3%)
  between operations  0.89 us (1%)
    all_to_all x3, waiting for transfers between devices, exchange(): lax.all_to_all(blocks, AXIS, split_axis=0, concat_axis=0, tiled=True, axi...  16 us
    all_to_all x3, starting transfers between devices, exchange(): lax.all_to_all(blocks, AXIS, split_axis=0, concat_axis=0, tiled=True, axi...  14.6 us
    all_to_all x1, blocking collectives, exchange(): lax.all_to_all(blocks, AXIS, split_axis=0, concat_axis=0, tiled=True, axi...  13.1 us
    ppermute x8, starting transfers between devices, swap(): return lax.ppermute(block, AXIS, [(i, i ^ bit) for i in range(devices)])  6.54 us
    pallas_call x1, Pallas kernels, project(): pl.pallas_call(functools.partial(project_kernel, order, fast), in_specs=[...  5.07 us
    pallas_call x2, Pallas kernels, fetch(): pl.pallas_call(fetch_kernel, in_specs=[whole(pl.ANY)], out_specs=whole(pl...  4.42 us
    pallas_call x1, Pallas kernels, output(): pl.pallas_call(functools.partial(output_kernel, fast, len(lhs)), in_specs...  3.28 us
    unnamed x9, local copies, waits for them, and re-layouts  2.29 us
  transfers between devices with their start and end apart: 11, of which 4 were waited for; matrix products, arithmetic and copies ran while one was open for 4% of the time, Pallas kernels for 17%

profile of v12, /device:TPU:0, one launch (start us, length us, event | category | flops | bytes accessed | tf_op | source)
XLA Modules:
  0.0 77.2 jit_solution(9972705488902649055)
XLA Ops:
  0.0 1.7 %prepare.1 = (bf16[8,144,128]{2,1,0:T(8,128)(2,1)}, s32[16]{0:T(128)}, s32[16]{0:T(128)}) custom-call(bf16[2,8192]{1,0:T(2,128)(2,1)} %bitcast.11, bf16[64,128]{1,0:T(8,128)(2,1)} %bitcast.12, s32[1,32]{1,0:T(1,128)} %slots_ref.1), custom_call_target="tpu_custom_call" | custom-call | tf_op jit(solution)/shard_map/prepare/pallas_call | solution.py:92
  1.8 7.3 %all-to-all-start = ((bf16[8,144,128]{2,1,0:T(8,128)(2,1)}), bf16[8,144,128]{2,1,0:T(8,128)(2,1)S(1)}, u32[]{:S(2)}, u32[]{:S(2)}) async-start(bf16[8,144,128]{2,1,0:T(8,128)(2,1)} %get-tuple-element.28), calls=%async_computation | async-start | bytes 589824 | tf_op jit(solution)/shard_map/all_to_all | solution.py:589
  9.0 1.2 %copy-done = bf16[32,16,1024]{2,1,0:T(8,128)(2,1)S(1)} copy-done((bf16[32,16,1024]{2,1,0:T(8,128)(2,1)S(1)}, bf16[32,16,1024]{2,1,0:T(8,128)(2,1)}, u32[]{:S(2)}) %copy-start) | copy-done | bytes 1048600
  10.2 1.0 %split_values.1 = (bf16[512,512]{1,0:T(8,128)(2,1)S(1)}, bf16[512,512]{1,0:T(8,128)(2,1)}) custom-call(s32[1]{0:T(128)S(6)} %and.20.x_ref, bf16[32,16,1024]{2,1,0:T(8,128)(2,1)S(1)} %copy-done), custom_call_target="tpu_custom_call" | custom-call | tf_op jit(solution)/shard_map/split_values/pallas_call | solution.py:159
  11.2 2.0 %collective-permute-start.1 = (bf16[512,512]{1,0:T(8,128)(2,1)}, bf16[512,512]{1,0:T(8,128)(2,1)S(1)}, u32[]{:S(2)}, u32[]{:S(2)}) collective-permute-start(bf16[512,512]{1,0:T(8,128)(2,1)} %get-tuple-element.36), channel_id=1, source_target_pairs={{0,2},{1,3},{2,0},{3,1},{4,6},{5,7},{6,4},{7,5},{8,10},{9,11},{10,... | collective-permute-start | bytes 1572872 | tf_op jit(solution)/shard_map/ppermute | solution.py:585
  14.5 1.0 %copy.13 = bf16[1,512,160]{2,1,0:T(8,128)(2,1)S(1)} copy(bf16[1,512,160]{1,2,0:T(8,128)(2,1)} %param.16) | data formatting | bytes 327680 | tf_op args[5]
  15.8 2.9 %all-to-all-done.first_ref = bf16[8,144,128]{2,1,0:T(8,128)(2,1)S(1)} async-done(((bf16[8,144,128]{2,1,0:T(8,128)(2,1)}), bf16[8,144,128]{2,1,0:T(8,128)(2,1)S(1)}, u32[]{:S(2)}, u32[]{:S(2)}) %all-to-all-start) | async-done | bytes 294944 | tf_op jit(solution)/shard_map/all_to_all | solution.py:589
  18.8 1.6 %fetch_weight.2.wk_ref = bf16[8192,128]{1,0:T(8,128)(2,1)S(1)} custom-call(bf16[8192,128]{1,0:T(8,128)(2,1)} %source_ref), custom_call_target="tpu_custom_call" | custom-call | bytes 2097152 | tf_op jit(solution)/shard_map/fetch_weight/pallas_call | solution.py:280
  20.4 5.1 %norm_project.1 = (bf16[16,16,128]{2,1,0:T(8,128)(2,1)}, s32[128]{0:T(128)S(1)}) custom-call(s32[1]{0:T(128)} %bitcast.me_ref, bf16[8,144,128]{2,1,0:T(8,128)(2,1)S(1)} %all-to-all-done.first_ref, bf16[8,144,128]{2,1,0:T(8,128)(2,1)S(1)} %collective-permute-done.second_ref, bf16[8192,512]{1,0:T(8,128)(2,1)} %wq_ref.1, bf16[8192,128]{1,0:T(8,128)(2,1)S(1)} %fetch_weight.2.wk_ref), custom_call_target="tpu_custom_call" | custom-call | flops 335544320 | bytes 10485760 | tf_op jit(solution)/shard_map/norm_project/pallas_call | solution.py:374
  25.5 3.8 %all-to-all-start.1 = ((bf16[16,16,128]{2,1,0:T(8,128)(2,1)}), bf16[16,16,128]{2,1,0:T(8,128)(2,1)S(1)}, u32[]{:S(2)}, u32[]{:S(2)}) async-start(bf16[16,16,128]{2,1,0:T(8,128)(2,1)} %get-tuple-element.34), calls=%async_computation.1 | async-start | bytes 131072 | tf_op jit(solution)/shard_map/all_to_all | solution.py:589
  29.3 1.0 %fusion = (f32[512,64]{1,0:T(8,128)S(1)}, f32[512,64]{1,0:T(8,128)S(1)}, f32[512,64]{1,0:T(8,128)S(1)}) fusion(f32[64]{0:T(128)S(1)} %multiply_exponential_fusion, f32[512]{0:T(512)S(1)} %get-tuple-element.55), kind=kLoop, calls=%fused_computation.5 | loop fusion | flops 65536 | bytes 395520 | tf_op jit(solution)/shard_map/neg | solution.py:41
  30.6 1.3 %turned_keys.1.keys_ref = bf16[512,1024]{1,0:T(8,128)(2,1)S(1)} custom-call(s32[16]{0:T(128)S(1)} %copy-done.2, bf16[512,160]{1,0:T(8,128)(2,1)S(1)} %bitcast.9, bf16[160,1024]{1,0:T(8,128)(2,1)S(1)} %bitcast.10, f32[512,128]{1,0:T(8,128)S(1)} %get-tuple-element.59.cos_ref, f32[512,128]{1,0:T(8,128)S(1)} %get-tuple-element.60.sin_ref), custom_call_target="tpu_custom_call" | custom-call | flops 167772160 | bytes 2097152 | tf_op jit(solution)/shard_map/turned_keys/pallas_call | solution.py:241
  32.0 4.2 %all-to-all-done.1.columns_ref = bf16[16,16,128]{2,1,0:T(8,128)(2,1)S(1)} async-done(((bf16[16,16,128]{2,1,0:T(8,128)(2,1)}), bf16[16,16,128]{2,1,0:T(8,128)(2,1)S(1)}, u32[]{:S(2)}, u32[]{:S(2)}) %all-to-all-start.1) | async-done | bytes 65568 | tf_op jit(solution)/shard_map/all_to_all | solution.py:589
  36.2 1.3 %attend.1 = bf16[16,48,128]{2,1,0:T(8,128)(2,1)} custom-call(bf16[16,16,128]{2,1,0:T(8,128)(2,1)S(1)} %all-to-all-done.1.columns_ref, bf16[512,1024]{1,0:T(8,128)(2,1)S(1)} %turned_keys.1.keys_ref, f32[2,512]{1,0:T(2,128)S(1)} %and_select_fusion.bias_ref, f32[2,128]{1,0:T(2,128)S(1)} %get-tuple-element.61.cos_ref, f32[2,128]{1,0:T(2,128)S(1)} %get-tuple-element.62.sin_ref), custom_call_target="tpu_custom_call" | custom-call | flops 33554432 | bytes 2097152 | tf_op jit(solution)/shard_map/attend/pallas_call | solution.py:498
  37.6 3.5 %all-to-all-start.2 = ((bf16[16,48,128]{2,1,0:T(8,128)(2,1)}), bf16[16,48,128]{2,1,0:T(8,128)(2,1)S(1)}, u32[]{:S(2)}, u32[]{:S(2)}) async-start(bf16[16,48,128]{2,1,0:T(8,128)(2,1)} %attend.1), calls=%async_computation.2 | async-start | bytes 393216 | tf_op jit(solution)/shard_map/all_to_all | solution.py:589
  41.1 9.0 %all-to-all-done.2.weights_ref = bf16[16,48,128]{2,1,0:T(8,128)(2,1)S(1)} async-done(((bf16[16,48,128]{2,1,0:T(8,128)(2,1)}), bf16[16,48,128]{2,1,0:T(8,128)(2,1)S(1)}, u32[]{:S(2)}, u32[]{:S(2)}) %all-to-all-start.2) | async-done | bytes 196640 | tf_op jit(solution)/shard_map/all_to_all | solution.py:589
  50.1 1.1 %mix_values.1 = (bf16[128,128]{1,0:T(8,128)(2,1)S(1)}, bf16[128,128]{1,0:T(8,128)(2,1)S(1)}, bf16[128,128]{1,0:T(8,128)(2,1)S(1)}, bf16[128,128]{1,0:T(8,128)(2,1)S(1)}) custom-call(s32[1]{0:T(128)} %bitcast.me_ref, s32[128]{0:T(128)S(1)} %get-tuple-element.31.rows_ref, bf16[16,48,128]{2,1,0:T(8,128)(2,1)S(1)} %all-to-all-done.2.weights_ref, ...), custom_call_target="tpu_custom_call" | custom-call | flops 67108864 | bytes 4194304 | tf_op jit(solution)/shard_map/mix_values/pallas_call | solution.py:205
  51.2 1.4 %collective-permute-start.5 = (bf16[128,128]{1,0:T(8,128)(2,1)S(1)}, bf16[128,128]{1,0:T(8,128)(2,1)S(1)}, u32[]{:S(2)}, u32[]{:S(2)}) collective-permute-start(bf16[128,128]{1,0:T(8,128)(2,1)S(1)} %get-tuple-element.47), channel_id=1, source_target_pairs={{0,8},{1,9},{2,10},{3,11},{4,12},{5,13},{6,14},{7,15},{8,0},{9,1},... | collective-permute-start | bytes 98312 | tf_op jit(solution)/shard_map/ppermute | solution.py:585
  52.6 3.0 %collective-permute-start.6 = (bf16[128,128]{1,0:T(8,128)(2,1)S(1)}, bf16[128,128]{1,0:T(8,128)(2,1)S(1)}, u32[]{:S(2)}, u32[]{:S(2)}) collective-permute-start(bf16[128,128]{1,0:T(8,128)(2,1)S(1)} %get-tuple-element.48), channel_id=1, source_target_pairs={{0,12},{1,13},{2,14},{3,15},{4,8},{5,9},{6,10},{7,11},{8,4},{9,5},... | collective-permute-start | bytes 98312 | tf_op jit(solution)/shard_map/ppermute | solution.py:585
  55.6 2.9 %fetch_weight.3.last_ref = bf16[512,6144]{1,0:T(8,128)(2,1)S(1)} custom-call(bf16[512,8192]{1,0:T(8,128)(2,1)} %weight_ref), custom_call_target="tpu_custom_call" | custom-call | bytes 6291456 | tf_op jit(solution)/shard_map/fetch_weight/pallas_call | solution.py:280
  58.5 3.3 %output_project.1 = (bf16[8,128,128]{2,1,0:T(8,128)(2,1)S(1)}, bf16[8,128,128]{2,1,0:T(8,128)(2,1)S(1)}) custom-call(s32[1]{0:T(128)} %bitcast.me_ref, bf16[512,8192]{1,0:T(8,128)(2,1)} %weight_ref, bf16[512,6144]{1,0:T(8,128)(2,1)S(1)} %fetch_weight.3.last_ref, bf16[128,128]{1,0:T(8,128)(2,1)S(1)} %get-tuple-element.45.rest_0_, ...), custom_call_target="tpu_custom_call" | custom-call | flops 268435456 | bytes 8388608 | tf_op jit(solution)/shard_map/output_project/pallas_call | solution.py:565
  61.9 1.5 %collective-permute-done.7 = bf16[8,128,128]{2,1,0:T(8,128)(2,1)S(1)} collective-permute-done((bf16[8,128,128]{2,1,0:T(8,128)(2,1)S(1)}, bf16[8,128,128]{2,1,0:T(8,128)(2,1)S(1)}, u32[]{:S(2)}, u32[]{:S(2)}) %collective-permute-start.7) | collective-permute-done | bytes 262176 | tf_op jit(solution)/shard_map/ppermute | solution.py:585
  63.5 13.1 %all_to_all.20 = bf16[8,128,128]{2,1,0:T(8,128)(2,1)S(1)} all-to-all(bf16[8,128,128]{2,1,0:T(8,128)(2,1)S(1)} %add_convert_fusion), channel_id=1, replica_groups={{0,2,4,6,8,10,12,14},{1,3,5,7,9,11,13,15},{16,18,20,22,24,26,28,30},{17..., dimensions={0} | all-to-all | bytes 524288 | tf_op jit(solution)/shard_map/all_to_all | solution.py:589
  76.6 0.6 reshape.32
  (33 shorter events, 1.6 us)
Async XLA Ops:
  1.8 16.9 %all-to-all-start = ((bf16[8,144,128]{2,1,0:T(8,128)(2,1)}), bf16[8,144,128]{2,1,0:T(8,128)(2,1)S(1)}, u32[]{:S(2)}, u32[]{:S(2)}) async-start(bf16[8,144,128]{2,1,0:T(8,128)(2,1)} %get-tuple-element.28), calls=%async_computation | async-start | bytes 589824 | tf_op jit(solution)/shard_map/all_to_all | solution.py:589
  9.0 1.2 %copy-start = (bf16[32,16,1024]{2,1,0:T(8,128)(2,1)S(1)}, bf16[32,16,1024]{2,1,0:T(8,128)(2,1)}, u32[]{:S(2)}) copy-start(bf16[32,16,1024]{2,1,0:T(8,128)(2,1)} %store_ref.1) | copy-start | bytes 3145732
  11.2 26.3 %collective-permute-start.1 = (bf16[512,512]{1,0:T(8,128)(2,1)}, bf16[512,512]{1,0:T(8,128)(2,1)S(1)}, u32[]{:S(2)}, u32[]{:S(2)}) collective-permute-start(bf16[512,512]{1,0:T(8,128)(2,1)} %get-tuple-element.36), channel_id=1, source_target_pairs={{0,2},{1,3},{2,0},{3,1},{4,6},{5,7},{6,4},{7,5},{8,10},{9,11},{10,... | collective-permute-start | bytes 1572872 | tf_op jit(solution)/shard_map/ppermute | solution.py:585
  13.3 27.8 %collective-permute-start.2 = (bf16[512,512]{1,0:T(8,128)(2,1)S(1)}, bf16[512,512]{1,0:T(8,128)(2,1)S(1)}, u32[]{:S(2)}, u32[]{:S(2)}) collective-permute-start(bf16[512,512]{1,0:T(8,128)(2,1)S(1)} %get-tuple-element.38.rest_0_), channel_id=1, source_target_pairs={{0,1},{1,0},{2,3},{3,2},{4,5},{5,4},{6,7},{7,6},{8,9},{9,8},{10,11... | collective-permute-start | bytes 1572872 | tf_op jit(solution)/shard_map/ppermute | solution.py:585
  18.6 1.8 %collective-permute-start = (bf16[8,144,128]{2,1,0:T(8,128)(2,1)S(1)}, bf16[8,144,128]{2,1,0:T(8,128)(2,1)S(1)}, u32[]{:S(2)}, u32[]{:S(2)}) collective-permute-start(bf16[8,144,128]{2,1,0:T(8,128)(2,1)S(1)} %all-to-all-done.first_ref), channel_id=1, source_target_pairs={{0,1},{1,0},{2,3},{3,2},{4,5},{5,4},{6,7},{7,6},{8,9},{9,8},{10,11... | collective-permute-start | bytes 884744 | tf_op jit(solution)/shard_map/ppermute | solution.py:585
  20.4 10.2 %copy-start.1 = (bf16[1,160,1024]{2,1,0:T(8,128)(2,1)S(1)}, bf16[1,160,1024]{2,1,0:T(8,128)(2,1)}, u32[]{:S(2)}) copy-start(bf16[1,160,1024]{2,1,0:T(8,128)(2,1)} %param.17) | copy-start | bytes 983044
  20.4 10.2 %copy-start.2 = (s32[16]{0:T(128)S(1)}, s32[16]{0:T(128)}, u32[]{:S(2)}) copy-start(s32[16]{0:T(128)} %get-tuple-element.33.pair_ref) | copy-start | bytes 196
  20.4 11.5 %copy-start.3 = (s32[2,1,16]{2,1,0:T(1,128)S(1)}, s32[2,1,16]{2,1,0:T(1,128)}, u32[]{:S(2)}) copy-start(s32[2,1,16]{2,1,0:T(1,128)} %param.21) | copy-start | bytes 388
  25.5 10.7 %all-to-all-start.1 = ((bf16[16,16,128]{2,1,0:T(8,128)(2,1)}), bf16[16,16,128]{2,1,0:T(8,128)(2,1)S(1)}, u32[]{:S(2)}, u32[]{:S(2)}) async-start(bf16[16,16,128]{2,1,0:T(8,128)(2,1)} %get-tuple-element.34), calls=%async_computation.1 | async-start | bytes 131072 | tf_op jit(solution)/shard_map/all_to_all | solution.py:589
  37.6 12.5 %collective-permute-start.3 = (bf16[512,512]{1,0:T(8,128)(2,1)S(1)}, bf16[512,512]{1,0:T(8,128)(2,1)S(1)}, u32[]{:S(2)}, u32[]{:S(2)}) collective-permute-start(bf16[512,512]{1,0:T(8,128)(2,1)S(1)} %collective-permute-done.1.rest_2_), channel_id=1, source_target_pairs={{0,1},{1,0},{2,3},{3,2},{4,5},{5,4},{6,7},{7,6},{8,9},{9,8},{10,11... | collective-permute-start | bytes 1572872 | tf_op jit(solution)/shard_map/ppermute | solution.py:585
  37.6 12.5 %all-to-all-start.2 = ((bf16[16,48,128]{2,1,0:T(8,128)(2,1)}), bf16[16,48,128]{2,1,0:T(8,128)(2,1)S(1)}, u32[]{:S(2)}, u32[]{:S(2)}) async-start(bf16[16,48,128]{2,1,0:T(8,128)(2,1)} %attend.1), calls=%async_computation.2 | async-start | bytes 393216 | tf_op jit(solution)/shard_map/all_to_all | solution.py:589
  51.1 7.3 %collective-permute-start.4 = (bf16[128,128]{1,0:T(8,128)(2,1)S(1)}, bf16[128,128]{1,0:T(8,128)(2,1)S(1)}, u32[]{:S(2)}, u32[]{:S(2)}) collective-permute-start(bf16[128,128]{1,0:T(8,128)(2,1)S(1)} %get-tuple-element.46), channel_id=1, source_target_pairs={{0,4},{1,5},{2,6},{3,7},{4,0},{5,1},{6,2},{7,3},{8,12},{9,13},{10,... | collective-permute-start | bytes 98312 | tf_op jit(solution)/shard_map/ppermute | solution.py:585
  51.2 7.3 %collective-permute-start.5 = (bf16[128,128]{1,0:T(8,128)(2,1)S(1)}, bf16[128,128]{1,0:T(8,128)(2,1)S(1)}, u32[]{:S(2)}, u32[]{:S(2)}) collective-permute-start(bf16[128,128]{1,0:T(8,128)(2,1)S(1)} %get-tuple-element.47), channel_id=1, source_target_pairs={{0,8},{1,9},{2,10},{3,11},{4,12},{5,13},{6,14},{7,15},{8,0},{9,1},... | collective-permute-start | bytes 98312 | tf_op jit(solution)/shard_map/ppermute | solution.py:585
  52.6 5.9 %collective-permute-start.6 = (bf16[128,128]{1,0:T(8,128)(2,1)S(1)}, bf16[128,128]{1,0:T(8,128)(2,1)S(1)}, u32[]{:S(2)}, u32[]{:S(2)}) collective-permute-start(bf16[128,128]{1,0:T(8,128)(2,1)S(1)} %get-tuple-element.48), channel_id=1, source_target_pairs={{0,12},{1,13},{2,14},{3,15},{4,8},{5,9},{6,10},{7,11},{8,4},{9,5},... | collective-permute-start | bytes 98312 | tf_op jit(solution)/shard_map/ppermute | solution.py:585
  61.8 1.6 %collective-permute-start.7 = (bf16[8,128,128]{2,1,0:T(8,128)(2,1)S(1)}, bf16[8,128,128]{2,1,0:T(8,128)(2,1)S(1)}, u32[]{:S(2)}, u32[]{:S(2)}) collective-permute-start(bf16[8,128,128]{2,1,0:T(8,128)(2,1)S(1)} %get-tuple-element.50), channel_id=1, source_target_pairs={{0,1},{1,0},{2,3},{3,2},{4,5},{5,4},{6,7},{7,6},{8,9},{9,8},{10,11... | collective-permute-start | bytes 786440 | tf_op jit(solution)/shard_map/ppermute | solution.py:585

commit v13 on v12

--- a/solution.py
+++ b/solution.py
@@ -515,8 +515,16 @@
     lhs_refs, rest = rest[:count], rest[count:]
     out_refs, (head_buf, out_scr, heads_scr, sem) = rest[:-4], rest[-4:]
     width = head_buf.shape[1]
-    head_copy = pltpu.make_async_copy(weight_ref.at[:, pl.ds(0, width)], head_buf, sem)
-    head_copy.start()
+    depth = head_buf.shape[0] // sem.shape[0]
+    head_copies = []
+    for i in range(sem.shape[0]):
+        mine = pl.ds(i * depth, depth)
+        head_copies.append(
+            pltpu.make_async_copy(
+                weight_ref.at[mine, pl.ds(0, width)], head_buf.at[mine, :], sem.at[i]
+            )
+        )
+        head_copies[-1].start()
     chunks = 8
     span = weight_ref.shape[1] // chunks
     rows = out_scr.shape[0] * LANES // (chunks * span)
@@ -535,7 +543,8 @@
     first = width // span
     for i in (*range(first, chunks), *range(first)):
         if i == 0:
-            head_copy.wait()
+            for copy in head_copies:
+                copy.wait()
         source, place = (last_ref, i - first) if i >= first else (head_buf, i)
         part = jnp.dot(
             lhs, source[:, place * span : (place + 1) * span], preferred_element_type=F32
@@ -571,7 +580,7 @@
             VMEM((depth, width - last.shape[1]), BF16),
             VMEM((rows * width // LANES, LANES), F32),
             VMEM(lhs[0].shape if fast else (8, LANES), F32),
-            pltpu.SemaphoreType.DMA(()),
+            pltpu.SemaphoreType.DMA((4 if fast else 1,)),
         ],
         compiler_params=pltpu.CompilerParams(vmem_limit_bytes=46 * 2**20),
         cost_estimate=pl.CostEstimate(

time: 77.8 us -> 77.8 us (level)
  no operation moved by 1% of the time
where the time goes in v13:
time: 77.8 us; the launch traced here: 77.2 us
  starting transfers between devices  21.1 us (27%)
  Pallas kernels  19.2 us (25%)
  waiting for transfers between devices  17.6 us (23%)
  blocking collectives  13.1 us (17%)
  local copies, waits for them, and re-layouts  3 us (4%)
  other arithmetic  2.32 us (3%)
  between operations  0.89 us (1%)
    all_to_all x3, waiting for transfers between devices, exchange(): lax.all_to_all(blocks, AXIS, split_axis=0, concat_axis=0, tiled=True, axi...  16 us
    all_to_all x3, starting transfers between devices, exchange(): lax.all_to_all(blocks, AXIS, split_axis=0, concat_axis=0, tiled=True, axi...  14.6 us
    all_to_all x1, blocking collectives, exchange(): lax.all_to_all(blocks, AXIS, split_axis=0, concat_axis=0, tiled=True, axi...  13.1 us
    ppermute x8, starting transfers between devices, swap(): return lax.ppermute(block, AXIS, [(i, i ^ bit) for i in range(devices)])  6.54 us
    pallas_call x1, Pallas kernels, project(): pl.pallas_call(functools.partial(project_kernel, order, fast), in_specs=[...  5.07 us
    pallas_call x2, Pallas kernels, fetch(): pl.pallas_call(fetch_kernel, in_specs=[whole(pl.ANY)], out_specs=whole(pl...  4.42 us
    pallas_call x1, Pallas kernels, output(): pl.pallas_call(functools.partial(output_kernel, fast, len(lhs)), in_specs...  3.23 us
    unnamed x9, local copies, waits for them, and re-layouts  2.29 us
  transfers between devices with their start and end apart: 11, of which 4 were waited for; matrix products, arithmetic and copies ran while one was open for 4% of the time, Pallas kernels for 17%

profile of v13, /device:TPU:0, one launch (start us, length us, event | category | flops | bytes accessed | tf_op | source)
XLA Modules:
  0.0 77.2 jit_solution(13317030583943269076)
XLA Ops:
  0.0 1.7 %prepare.1 = (bf16[8,144,128]{2,1,0:T(8,128)(2,1)}, s32[16]{0:T(128)}, s32[16]{0:T(128)}) custom-call(bf16[2,8192]{1,0:T(2,128)(2,1)} %bitcast.11, bf16[64,128]{1,0:T(8,128)(2,1)} %bitcast.12, s32[1,32]{1,0:T(1,128)} %slots_ref.1), custom_call_target="tpu_custom_call" | custom-call | tf_op jit(solution)/shard_map/prepare/pallas_call | solution.py:92
  1.8 7.3 %all-to-all-start = ((bf16[8,144,128]{2,1,0:T(8,128)(2,1)}), bf16[8,144,128]{2,1,0:T(8,128)(2,1)S(1)}, u32[]{:S(2)}, u32[]{:S(2)}) async-start(bf16[8,144,128]{2,1,0:T(8,128)(2,1)} %get-tuple-element.28), calls=%async_computation | async-start | bytes 589824 | tf_op jit(solution)/shard_map/all_to_all | solution.py:598
  9.0 1.2 %copy-done = bf16[32,16,1024]{2,1,0:T(8,128)(2,1)S(1)} copy-done((bf16[32,16,1024]{2,1,0:T(8,128)(2,1)S(1)}, bf16[32,16,1024]{2,1,0:T(8,128)(2,1)}, u32[]{:S(2)}) %copy-start) | copy-done | bytes 1048600
  10.2 1.0 %split_values.1 = (bf16[512,512]{1,0:T(8,128)(2,1)S(1)}, bf16[512,512]{1,0:T(8,128)(2,1)}) custom-call(s32[1]{0:T(128)S(6)} %and.20.x_ref, bf16[32,16,1024]{2,1,0:T(8,128)(2,1)S(1)} %copy-done), custom_call_target="tpu_custom_call" | custom-call | tf_op jit(solution)/shard_map/split_values/pallas_call | solution.py:159
  11.2 2.0 %collective-permute-start.1 = (bf16[512,512]{1,0:T(8,128)(2,1)}, bf16[512,512]{1,0:T(8,128)(2,1)S(1)}, u32[]{:S(2)}, u32[]{:S(2)}) collective-permute-start(bf16[512,512]{1,0:T(8,128)(2,1)} %get-tuple-element.36), channel_id=1, source_target_pairs={{0,2},{1,3},{2,0},{3,1},{4,6},{5,7},{6,4},{7,5},{8,10},{9,11},{10,... | collective-permute-start | bytes 1572872 | tf_op jit(solution)/shard_map/ppermute | solution.py:594
  14.5 1.0 %copy.13 = bf16[1,512,160]{2,1,0:T(8,128)(2,1)S(1)} copy(bf16[1,512,160]{1,2,0:T(8,128)(2,1)} %param.16) | data formatting | bytes 327680 | tf_op args[5]
  15.8 2.9 %all-to-all-done.first_ref = bf16[8,144,128]{2,1,0:T(8,128)(2,1)S(1)} async-done(((bf16[8,144,128]{2,1,0:T(8,128)(2,1)}), bf16[8,144,128]{2,1,0:T(8,128)(2,1)S(1)}, u32[]{:S(2)}, u32[]{:S(2)}) %all-to-all-start) | async-done | bytes 294944 | tf_op jit(solution)/shard_map/all_to_all | solution.py:598
  18.8 1.6 %fetch_weight.2.wk_ref = bf16[8192,128]{1,0:T(8,128)(2,1)S(1)} custom-call(bf16[8192,128]{1,0:T(8,128)(2,1)} %source_ref), custom_call_target="tpu_custom_call" | custom-call | bytes 2097152 | tf_op jit(solution)/shard_map/fetch_weight/pallas_call | solution.py:280
  20.4 5.1 %norm_project.1 = (bf16[16,16,128]{2,1,0:T(8,128)(2,1)}, s32[128]{0:T(128)S(1)}) custom-call(s32[1]{0:T(128)} %bitcast.me_ref, bf16[8,144,128]{2,1,0:T(8,128)(2,1)S(1)} %all-to-all-done.first_ref, bf16[8,144,128]{2,1,0:T(8,128)(2,1)S(1)} %collective-permute-done.second_ref, bf16[8192,512]{1,0:T(8,128)(2,1)} %wq_ref.1, bf16[8192,128]{1,0:T(8,128)(2,1)S(1)} %fetch_weight.2.wk_ref), custom_call_target="tpu_custom_call" | custom-call | flops 335544320 | bytes 10485760 | tf_op jit(solution)/shard_map/norm_project/pallas_call | solution.py:374
  25.5 3.8 %all-to-all-start.1 = ((bf16[16,16,128]{2,1,0:T(8,128)(2,1)}), bf16[16,16,128]{2,1,0:T(8,128)(2,1)S(1)}, u32[]{:S(2)}, u32[]{:S(2)}) async-start(bf16[16,16,128]{2,1,0:T(8,128)(2,1)} %get-tuple-element.34), calls=%async_computation.1 | async-start | bytes 131072 | tf_op jit(solution)/shard_map/all_to_all | solution.py:598
  29.3 1.0 %fusion = (f32[512,64]{1,0:T(8,128)S(1)}, f32[512,64]{1,0:T(8,128)S(1)}, f32[512,64]{1,0:T(8,128)S(1)}) fusion(f32[64]{0:T(128)S(1)} %multiply_exponential_fusion, f32[512]{0:T(512)S(1)} %get-tuple-element.55), kind=kLoop, calls=%fused_computation.5 | loop fusion | flops 65536 | bytes 395520 | tf_op jit(solution)/shard_map/neg | solution.py:41
  30.6 1.3 %turned_keys.1.keys_ref = bf16[512,1024]{1,0:T(8,128)(2,1)S(1)} custom-call(s32[16]{0:T(128)S(1)} %copy-done.2, bf16[512,160]{1,0:T(8,128)(2,1)S(1)} %bitcast.9, bf16[160,1024]{1,0:T(8,128)(2,1)S(1)} %bitcast.10, f32[512,128]{1,0:T(8,128)S(1)} %get-tuple-element.59.cos_ref, f32[512,128]{1,0:T(8,128)S(1)} %get-tuple-element.60.sin_ref), custom_call_target="tpu_custom_call" | custom-call | flops 167772160 | bytes 2097152 | tf_op jit(solution)/shard_map/turned_keys/pallas_call | solution.py:241
  32.0 4.2 %all-to-all-done.1.columns_ref = bf16[16,16,128]{2,1,0:T(8,128)(2,1)S(1)} async-done(((bf16[16,16,128]{2,1,0:T(8,128)(2,1)}), bf16[16,16,128]{2,1,0:T(8,128)(2,1)S(1)}, u32[]{:S(2)}, u32[]{:S(2)}) %all-to-all-start.1) | async-done | bytes 65568 | tf_op jit(solution)/shard_map/all_to_all | solution.py:598
  36.2 1.3 %attend.1 = bf16[16,48,128]{2,1,0:T(8,128)(2,1)} custom-call(bf16[16,16,128]{2,1,0:T(8,128)(2,1)S(1)} %all-to-all-done.1.columns_ref, bf16[512,1024]{1,0:T(8,128)(2,1)S(1)} %turned_keys.1.keys_ref, f32[2,512]{1,0:T(2,128)S(1)} %and_select_fusion.bias_ref, f32[2,128]{1,0:T(2,128)S(1)} %get-tuple-element.61.cos_ref, f32[2,128]{1,0:T(2,128)S(1)} %get-tuple-element.62.sin_ref), custom_call_target="tpu_custom_call" | custom-call | flops 33554432 | bytes 2097152 | tf_op jit(solution)/shard_map/attend/pallas_call | solution.py:498
  37.6 3.5 %all-to-all-start.2 = ((bf16[16,48,128]{2,1,0:T(8,128)(2,1)}), bf16[16,48,128]{2,1,0:T(8,128)(2,1)S(1)}, u32[]{:S(2)}, u32[]{:S(2)}) async-start(bf16[16,48,128]{2,1,0:T(8,128)(2,1)} %attend.1), calls=%async_computation.2 | async-start | bytes 393216 | tf_op jit(solution)/shard_map/all_to_all | solution.py:598
  41.1 9.0 %all-to-all-done.2.weights_ref = bf16[16,48,128]{2,1,0:T(8,128)(2,1)S(1)} async-done(((bf16[16,48,128]{2,1,0:T(8,128)(2,1)}), bf16[16,48,128]{2,1,0:T(8,128)(2,1)S(1)}, u32[]{:S(2)}, u32[]{:S(2)}) %all-to-all-start.2) | async-done | bytes 196640 | tf_op jit(solution)/shard_map/all_to_all | solution.py:598
  50.1 1.1 %mix_values.1 = (bf16[128,128]{1,0:T(8,128)(2,1)S(1)}, bf16[128,128]{1,0:T(8,128)(2,1)S(1)}, bf16[128,128]{1,0:T(8,128)(2,1)S(1)}, bf16[128,128]{1,0:T(8,128)(2,1)S(1)}) custom-call(s32[1]{0:T(128)} %bitcast.me_ref, s32[128]{0:T(128)S(1)} %get-tuple-element.31.rows_ref, bf16[16,48,128]{2,1,0:T(8,128)(2,1)S(1)} %all-to-all-done.2.weights_ref, ...), custom_call_target="tpu_custom_call" | custom-call | flops 67108864 | bytes 4194304 | tf_op jit(solution)/shard_map/mix_values/pallas_call | solution.py:205
  51.2 1.4 %collective-permute-start.5 = (bf16[128,128]{1,0:T(8,128)(2,1)S(1)}, bf16[128,128]{1,0:T(8,128)(2,1)S(1)}, u32[]{:S(2)}, u32[]{:S(2)}) collective-permute-start(bf16[128,128]{1,0:T(8,128)(2,1)S(1)} %get-tuple-element.47), channel_id=1, source_target_pairs={{0,8},{1,9},{2,10},{3,11},{4,12},{5,13},{6,14},{7,15},{8,0},{9,1},... | collective-permute-start | bytes 98312 | tf_op jit(solution)/shard_map/ppermute | solution.py:594
  52.6 3.0 %collective-permute-start.6 = (bf16[128,128]{1,0:T(8,128)(2,1)S(1)}, bf16[128,128]{1,0:T(8,128)(2,1)S(1)}, u32[]{:S(2)}, u32[]{:S(2)}) collective-permute-start(bf16[128,128]{1,0:T(8,128)(2,1)S(1)} %get-tuple-element.48), channel_id=1, source_target_pairs={{0,12},{1,13},{2,14},{3,15},{4,8},{5,9},{6,10},{7,11},{8,4},{9,5},... | collective-permute-start | bytes 98312 | tf_op jit(solution)/shard_map/ppermute | solution.py:594
  55.6 2.9 %fetch_weight.3.last_ref = bf16[512,6144]{1,0:T(8,128)(2,1)S(1)} custom-call(bf16[512,8192]{1,0:T(8,128)(2,1)} %weight_ref), custom_call_target="tpu_custom_call" | custom-call | bytes 6291456 | tf_op jit(solution)/shard_map/fetch_weight/pallas_call | solution.py:280
  58.5 3.2 %output_project.1 = (bf16[8,128,128]{2,1,0:T(8,128)(2,1)S(1)}, bf16[8,128,128]{2,1,0:T(8,128)(2,1)S(1)}) custom-call(s32[1]{0:T(128)} %bitcast.me_ref, bf16[512,8192]{1,0:T(8,128)(2,1)} %weight_ref, bf16[512,6144]{1,0:T(8,128)(2,1)S(1)} %fetch_weight.3.last_ref, bf16[128,128]{1,0:T(8,128)(2,1)S(1)} %get-tuple-element.45.rest_0_, ...), custom_call_target="tpu_custom_call" | custom-call | flops 268435456 | bytes 8388608 | tf_op jit(solution)/shard_map/output_project/pallas_call | solution.py:574
  61.8 1.5 %collective-permute-done.7 = bf16[8,128,128]{2,1,0:T(8,128)(2,1)S(1)} collective-permute-done((bf16[8,128,128]{2,1,0:T(8,128)(2,1)S(1)}, bf16[8,128,128]{2,1,0:T(8,128)(2,1)S(1)}, u32[]{:S(2)}, u32[]{:S(2)}) %collective-permute-start.7) | collective-permute-done | bytes 262176 | tf_op jit(solution)/shard_map/ppermute | solution.py:594
  63.4 13.1 %all_to_all.20 = bf16[8,128,128]{2,1,0:T(8,128)(2,1)S(1)} all-to-all(bf16[8,128,128]{2,1,0:T(8,128)(2,1)S(1)} %add_convert_fusion), channel_id=1, replica_groups={{0,2,4,6,8,10,12,14},{1,3,5,7,9,11,13,15},{16,18,20,22,24,26,28,30},{17..., dimensions={0} | all-to-all | bytes 524288 | tf_op jit(solution)/shard_map/all_to_all | solution.py:598
  76.6 0.6 reshape.32
  (33 shorter events, 1.6 us)
Async XLA Ops:
  1.8 16.9 %all-to-all-start = ((bf16[8,144,128]{2,1,0:T(8,128)(2,1)}), bf16[8,144,128]{2,1,0:T(8,128)(2,1)S(1)}, u32[]{:S(2)}, u32[]{:S(2)}) async-start(bf16[8,144,128]{2,1,0:T(8,128)(2,1)} %get-tuple-element.28), calls=%async_computation | async-start | bytes 589824 | tf_op jit(solution)/shard_map/all_to_all | solution.py:598
  9.0 1.2 %copy-start = (bf16[32,16,1024]{2,1,0:T(8,128)(2,1)S(1)}, bf16[32,16,1024]{2,1,0:T(8,128)(2,1)}, u32[]{:S(2)}) copy-start(bf16[32,16,1024]{2,1,0:T(8,128)(2,1)} %store_ref.1) | copy-start | bytes 3145732
  11.2 26.3 %collective-permute-start.1 = (bf16[512,512]{1,0:T(8,128)(2,1)}, bf16[512,512]{1,0:T(8,128)(2,1)S(1)}, u32[]{:S(2)}, u32[]{:S(2)}) collective-permute-start(bf16[512,512]{1,0:T(8,128)(2,1)} %get-tuple-element.36), channel_id=1, source_target_pairs={{0,2},{1,3},{2,0},{3,1},{4,6},{5,7},{6,4},{7,5},{8,10},{9,11},{10,... | collective-permute-start | bytes 1572872 | tf_op jit(solution)/shard_map/ppermute | solution.py:594
  13.3 27.8 %collective-permute-start.2 = (bf16[512,512]{1,0:T(8,128)(2,1)S(1)}, bf16[512,512]{1,0:T(8,128)(2,1)S(1)}, u32[]{:S(2)}, u32[]{:S(2)}) collective-permute-start(bf16[512,512]{1,0:T(8,128)(2,1)S(1)} %get-tuple-element.38.rest_0_), channel_id=1, source_target_pairs={{0,1},{1,0},{2,3},{3,2},{4,5},{5,4},{6,7},{7,6},{8,9},{9,8},{10,11... | collective-permute-start | bytes 1572872 | tf_op jit(solution)/shard_map/ppermute | solution.py:594
  18.6 1.8 %collective-permute-start = (bf16[8,144,128]{2,1,0:T(8,128)(2,1)S(1)}, bf16[8,144,128]{2,1,0:T(8,128)(2,1)S(1)}, u32[]{:S(2)}, u32[]{:S(2)}) collective-permute-start(bf16[8,144,128]{2,1,0:T(8,128)(2,1)S(1)} %all-to-all-done.first_ref), channel_id=1, source_target_pairs={{0,1},{1,0},{2,3},{3,2},{4,5},{5,4},{6,7},{7,6},{8,9},{9,8},{10,11... | collective-permute-start | bytes 884744 | tf_op jit(solution)/shard_map/ppermute | solution.py:594
  20.4 10.2 %copy-start.1 = (bf16[1,160,1024]{2,1,0:T(8,128)(2,1)S(1)}, bf16[1,160,1024]{2,1,0:T(8,128)(2,1)}, u32[]{:S(2)}) copy-start(bf16[1,160,1024]{2,1,0:T(8,128)(2,1)} %param.17) | copy-start | bytes 983044
  20.4 10.2 %copy-start.2 = (s32[16]{0:T(128)S(1)}, s32[16]{0:T(128)}, u32[]{:S(2)}) copy-start(s32[16]{0:T(128)} %get-tuple-element.33.pair_ref) | copy-start | bytes 196
  20.4 11.5 %copy-start.3 = (s32[2,1,16]{2,1,0:T(1,128)S(1)}, s32[2,1,16]{2,1,0:T(1,128)}, u32[]{:S(2)}) copy-start(s32[2,1,16]{2,1,0:T(1,128)} %param.21) | copy-start | bytes 388
  25.5 10.7 %all-to-all-start.1 = ((bf16[16,16,128]{2,1,0:T(8,128)(2,1)}), bf16[16,16,128]{2,1,0:T(8,128)(2,1)S(1)}, u32[]{:S(2)}, u32[]{:S(2)}) async-start(bf16[16,16,128]{2,1,0:T(8,128)(2,1)} %get-tuple-element.34), calls=%async_computation.1 | async-start | bytes 131072 | tf_op jit(solution)/shard_map/all_to_all | solution.py:598
  37.6 12.5 %collective-permute-start.3 = (bf16[512,512]{1,0:T(8,128)(2,1)S(1)}, bf16[512,512]{1,0:T(8,128)(2,1)S(1)}, u32[]{:S(2)}, u32[]{:S(2)}) collective-permute-start(bf16[512,512]{1,0:T(8,128)(2,1)S(1)} %collective-permute-done.1.rest_2_), channel_id=1, source_target_pairs={{0,1},{1,0},{2,3},{3,2},{4,5},{5,4},{6,7},{7,6},{8,9},{9,8},{10,11... | collective-permute-start | bytes 1572872 | tf_op jit(solution)/shard_map/ppermute | solution.py:594
  37.6 12.5 %all-to-all-start.2 = ((bf16[16,48,128]{2,1,0:T(8,128)(2,1)}), bf16[16,48,128]{2,1,0:T(8,128)(2,1)S(1)}, u32[]{:S(2)}, u32[]{:S(2)}) async-start(bf16[16,48,128]{2,1,0:T(8,128)(2,1)} %attend.1), calls=%async_computation.2 | async-start | bytes 393216 | tf_op jit(solution)/shard_map/all_to_all | solution.py:598
  51.1 7.3 %collective-permute-start.4 = (bf16[128,128]{1,0:T(8,128)(2,1)S(1)}, bf16[128,128]{1,0:T(8,128)(2,1)S(1)}, u32[]{:S(2)}, u32[]{:S(2)}) collective-permute-start(bf16[128,128]{1,0:T(8,128)(2,1)S(1)} %get-tuple-element.46), channel_id=1, source_target_pairs={{0,4},{1,5},{2,6},{3,7},{4,0},{5,1},{6,2},{7,3},{8,12},{9,13},{10,... | collective-permute-start | bytes 98312 | tf_op jit(solution)/shard_map/ppermute | solution.py:594
  51.2 7.3 %collective-permute-start.5 = (bf16[128,128]{1,0:T(8,128)(2,1)S(1)}, bf16[128,128]{1,0:T(8,128)(2,1)S(1)}, u32[]{:S(2)}, u32[]{:S(2)}) collective-permute-start(bf16[128,128]{1,0:T(8,128)(2,1)S(1)} %get-tuple-element.47), channel_id=1, source_target_pairs={{0,8},{1,9},{2,10},{3,11},{4,12},{5,13},{6,14},{7,15},{8,0},{9,1},... | collective-permute-start | bytes 98312 | tf_op jit(solution)/shard_map/ppermute | solution.py:594
  52.6 5.9 %collective-permute-start.6 = (bf16[128,128]{1,0:T(8,128)(2,1)S(1)}, bf16[128,128]{1,0:T(8,128)(2,1)S(1)}, u32[]{:S(2)}, u32[]{:S(2)}) collective-permute-start(bf16[128,128]{1,0:T(8,128)(2,1)S(1)} %get-tuple-element.48), channel_id=1, source_target_pairs={{0,12},{1,13},{2,14},{3,15},{4,8},{5,9},{6,10},{7,11},{8,4},{9,5},... | collective-permute-start | bytes 98312 | tf_op jit(solution)/shard_map/ppermute | solution.py:594
  61.7 1.6 %collective-permute-start.7 = (bf16[8,128,128]{2,1,0:T(8,128)(2,1)S(1)}, bf16[8,128,128]{2,1,0:T(8,128)(2,1)S(1)}, u32[]{:S(2)}, u32[]{:S(2)}) collective-permute-start(bf16[8,128,128]{2,1,0:T(8,128)(2,1)S(1)} %get-tuple-element.50), channel_id=1, source_target_pairs={{0,1},{1,0},{2,3},{3,2},{4,5},{5,4},{6,7},{7,6},{8,9},{9,8},{10,11... | collective-permute-start | bytes 786440 | tf_op jit(solution)/shard_map/ppermute | solution.py:594

commit v14 on v10

--- a/solution.py
+++ b/solution.py
@@ -292,9 +292,9 @@
     order, fast, me_ref, first_ref, second_ref, wq_ref, wk_ref, out_ref, *rest
 ):
     if fast:
-        rows_ref, x_scr, lhs_scr, wq_buf, wk_buf, out_scr, sems, *asked_scr = rest
+        rows_ref, x_scr, lhs_scr, wq_buf, out_scr, sems, *asked_scr = rest
     else:
-        x_scr, lhs_scr, wq_buf, wk_buf, out_scr, sems = rest
+        x_scr, lhs_scr, wq_buf, out_scr, sems = rest
     depth, q_cols = wq_ref.shape
     k_cols = wk_ref.shape[1]
     chunks = wq_buf.shape[0]
@@ -303,13 +303,8 @@
     copies = []
     for i in range(chunks):
         rows = pl.ds(i * span, span)
-        pair = (
-            pltpu.make_async_copy(wq_ref.at[rows, :], wq_buf.at[i], sems.at[0, i]),
-            pltpu.make_async_copy(wk_ref.at[rows, :], wk_buf.at[i], sems.at[1, i]),
-        )
-        for copy in pair:
-            copy.start()
-        copies.append(pair)
+        copies.append(pltpu.make_async_copy(wq_ref.at[rows, :], wq_buf.at[i], sems.at[i]))
+        copies[-1].start()
     half = first_ref.shape[0]
     count = 2 * half * STEPS
     rows = STEPS * pieces
@@ -330,11 +325,12 @@
     q_sum = jnp.zeros((count, q_cols), F32)
     k_sum = jnp.zeros((count, k_cols), F32)
     for i in range(chunks):
-        for copy in copies[i]:
-            copy.wait()
+        copies[i].wait()
         lhs = lhs_scr[:, i * span : (i + 1) * span]
         q_sum = q_sum + jnp.dot(lhs, wq_buf[i], preferred_element_type=F32)
-        k_sum = k_sum + jnp.dot(lhs, wk_buf[i], preferred_element_type=F32)
+        k_sum = k_sum + jnp.dot(
+            lhs, wk_ref[i * span : (i + 1) * span, :], preferred_element_type=F32
+        )
     if not fast:
         out_ref[:, :q_cols] = q_sum.astype(BF16)
         out_ref[:, q_cols:] = k_sum.astype(BF16)
@@ -374,7 +370,7 @@
     shape = (devices, 16, LANES) if fast else (rows, q_cols + k_cols)
     return pl.pallas_call(
         functools.partial(project_kernel, order, fast),
-        in_specs=[whole(SMEM), whole(), whole(), whole(pl.ANY), whole(pl.ANY)],
+        in_specs=[whole(SMEM), whole(), whole(), whole(pl.ANY), whole()],
         out_specs=(whole(), whole(SMEM)) if fast else whole(),
         out_shape=(
             (
@@ -388,9 +384,8 @@
             VMEM((rows * pieces, LANES), F32),
             VMEM((rows, depth), BF16),
             VMEM((chunks, span, q_cols), BF16),
-            VMEM((chunks, span, k_cols), BF16),
             VMEM((devices, 16, LANES) if fast else (8, LANES), F32),
-            pltpu.SemaphoreType.DMA((2, chunks)),
+            pltpu.SemaphoreType.DMA((chunks,)),
         ]
         + (
             [

time: 76.4 us -> 76.3 us (level)
  no operation moved by 1% of the time
where the time goes in v14:
time: 76.3 us; the launch traced here: 75.7 us
  starting transfers between devices  21.1 us (28%)
  Pallas kernels  18.4 us (24%)
  waiting for transfers between devices  17.6 us (23%)
  blocking collectives  12.5 us (16%)
  local copies, waits for them, and re-layouts  2.99 us (4%)
  other arithmetic  2.32 us (3%)
  between operations  0.88 us (1%)
    all_to_all x3, waiting for transfers between devices, exchange(): lax.all_to_all(blocks, AXIS, split_axis=0, concat_axis=0, tiled=True, axi...  16 us
    all_to_all x3, starting transfers between devices, exchange(): lax.all_to_all(blocks, AXIS, split_axis=0, concat_axis=0, tiled=True, axi...  14.6 us
    all_to_all x1, blocking collectives, exchange(): lax.all_to_all(blocks, AXIS, split_axis=0, concat_axis=0, tiled=True, axi...  12.5 us
    ppermute x8, starting transfers between devices, swap(): return lax.ppermute(block, AXIS, [(i, i ^ bit) for i in range(devices)])  6.54 us
    pallas_call x2, Pallas kernels, fetch(): pl.pallas_call(fetch_kernel, in_specs=[whole(pl.ANY)], out_specs=whole(pl...  5.1 us
    pallas_call x1, Pallas kernels, project(): pl.pallas_call(functools.partial(project_kernel, order, fast), in_specs=[...  5.03 us
    unnamed x9, local copies, waits for them, and re-layouts  2.28 us
    pallas_call x1, Pallas kernels, output(): pl.pallas_call(functools.partial(output_kernel, fast, len(lhs)), in_specs...  1.78 us
  transfers between devices with their start and end apart: 11, of which 4 were waited for; matrix products, arithmetic and copies ran while one was open for 4% of the time, Pallas kernels for 18%

profile of v14, /device:TPU:0, one launch (start us, length us, event | category | flops | bytes accessed | tf_op | source)
XLA Modules:
  0.0 75.7 jit_solution(14891779116035771348)
XLA Ops:
  0.0 1.7 %prepare.1 = (bf16[8,144,128]{2,1,0:T(8,128)(2,1)}, s32[16]{0:T(128)}, s32[16]{0:T(128)}) custom-call(bf16[2,8192]{1,0:T(2,128)(2,1)} %bitcast.11, bf16[64,128]{1,0:T(8,128)(2,1)} %bitcast.12, s32[1,32]{1,0:T(1,128)} %slots_ref.1), custom_call_target="tpu_custom_call" | custom-call | tf_op jit(solution)/shard_map/prepare/pallas_call | solution.py:92
  1.8 7.3 %all-to-all-start = ((bf16[8,144,128]{2,1,0:T(8,128)(2,1)}), bf16[8,144,128]{2,1,0:T(8,128)(2,1)S(1)}, u32[]{:S(2)}, u32[]{:S(2)}) async-start(bf16[8,144,128]{2,1,0:T(8,128)(2,1)} %get-tuple-element.28), calls=%async_computation | async-start | bytes 589824 | tf_op jit(solution)/shard_map/all_to_all | solution.py:577
  9.0 1.2 %copy-done = bf16[32,16,1024]{2,1,0:T(8,128)(2,1)S(1)} copy-done((bf16[32,16,1024]{2,1,0:T(8,128)(2,1)S(1)}, bf16[32,16,1024]{2,1,0:T(8,128)(2,1)}, u32[]{:S(2)}) %copy-start) | copy-done | bytes 1048600
  10.2 1.0 %split_values.1 = (bf16[512,512]{1,0:T(8,128)(2,1)S(1)}, bf16[512,512]{1,0:T(8,128)(2,1)}) custom-call(s32[1]{0:T(128)S(6)} %and.20.x_ref, bf16[32,16,1024]{2,1,0:T(8,128)(2,1)S(1)} %copy-done), custom_call_target="tpu_custom_call" | custom-call | tf_op jit(solution)/shard_map/split_values/pallas_call | solution.py:159
  11.2 2.0 %collective-permute-start.1 = (bf16[512,512]{1,0:T(8,128)(2,1)}, bf16[512,512]{1,0:T(8,128)(2,1)S(1)}, u32[]{:S(2)}, u32[]{:S(2)}) collective-permute-start(bf16[512,512]{1,0:T(8,128)(2,1)} %get-tuple-element.36), channel_id=1, source_target_pairs={{0,2},{1,3},{2,0},{3,1},{4,6},{5,7},{6,4},{7,5},{8,10},{9,11},{10,... | collective-permute-start | bytes 1572872 | tf_op jit(solution)/shard_map/ppermute | solution.py:573
  14.5 1.0 %copy.13 = bf16[1,512,160]{2,1,0:T(8,128)(2,1)S(1)} copy(bf16[1,512,160]{1,2,0:T(8,128)(2,1)} %param.16) | data formatting | bytes 327680 | tf_op args[5]
  15.8 2.9 %all-to-all-done.first_ref = bf16[8,144,128]{2,1,0:T(8,128)(2,1)S(1)} async-done(((bf16[8,144,128]{2,1,0:T(8,128)(2,1)}), bf16[8,144,128]{2,1,0:T(8,128)(2,1)S(1)}, u32[]{:S(2)}, u32[]{:S(2)}) %all-to-all-start) | async-done | bytes 294944 | tf_op jit(solution)/shard_map/all_to_all | solution.py:577
  18.8 1.6 %fetch_weight.2.wk_ref = bf16[8192,128]{1,0:T(8,128)(2,1)S(1)} custom-call(bf16[8192,128]{1,0:T(8,128)(2,1)} %source_ref), custom_call_target="tpu_custom_call" | custom-call | bytes 2097152 | tf_op jit(solution)/shard_map/fetch_weight/pallas_call | solution.py:277
  20.5 5.0 %norm_project.1 = (bf16[16,16,128]{2,1,0:T(8,128)(2,1)}, s32[128]{0:T(128)S(1)}) custom-call(s32[1]{0:T(128)} %bitcast.me_ref, bf16[8,144,128]{2,1,0:T(8,128)(2,1)S(1)} %all-to-all-done.first_ref, bf16[8,144,128]{2,1,0:T(8,128)(2,1)S(1)} %collective-permute-done.second_ref, bf16[8192,512]{1,0:T(8,128)(2,1)} %wq_ref.1, bf16[8192,128]{1,0:T(8,128)(2,1)S(1)} %fetch_weight.2.wk_ref), custom_call_target="tpu_custom_call" | custom-call | flops 335544320 | bytes 10485760 | tf_op jit(solution)/shard_map/norm_project/pallas_call | solution.py:371
  25.5 3.8 %all-to-all-start.1 = ((bf16[16,16,128]{2,1,0:T(8,128)(2,1)}), bf16[16,16,128]{2,1,0:T(8,128)(2,1)S(1)}, u32[]{:S(2)}, u32[]{:S(2)}) async-start(bf16[16,16,128]{2,1,0:T(8,128)(2,1)} %get-tuple-element.34), calls=%async_computation.1 | async-start | bytes 131072 | tf_op jit(solution)/shard_map/all_to_all | solution.py:577
  29.3 1.0 %fusion = (f32[512,64]{1,0:T(8,128)S(1)}, f32[512,64]{1,0:T(8,128)S(1)}, f32[512,64]{1,0:T(8,128)S(1)}) fusion(f32[64]{0:T(128)S(1)} %multiply_exponential_fusion, f32[512]{0:T(512)S(1)} %get-tuple-element.55), kind=kLoop, calls=%fused_computation.5 | loop fusion | flops 65536 | bytes 395520 | tf_op jit(solution)/shard_map/neg | solution.py:41
  30.6 1.3 %turned_keys.1.keys_ref = bf16[512,1024]{1,0:T(8,128)(2,1)S(1)} custom-call(s32[16]{0:T(128)S(1)} %copy-done.2, bf16[512,160]{1,0:T(8,128)(2,1)S(1)} %bitcast.9, bf16[160,1024]{1,0:T(8,128)(2,1)S(1)} %bitcast.10, f32[512,128]{1,0:T(8,128)S(1)} %get-tuple-element.59.cos_ref, f32[512,128]{1,0:T(8,128)S(1)} %get-tuple-element.60.sin_ref), custom_call_target="tpu_custom_call" | custom-call | flops 167772160 | bytes 2097152 | tf_op jit(solution)/shard_map/turned_keys/pallas_call | solution.py:241
  32.0 4.2 %all-to-all-done.1.columns_ref = bf16[16,16,128]{2,1,0:T(8,128)(2,1)S(1)} async-done(((bf16[16,16,128]{2,1,0:T(8,128)(2,1)}), bf16[16,16,128]{2,1,0:T(8,128)(2,1)S(1)}, u32[]{:S(2)}, u32[]{:S(2)}) %all-to-all-start.1) | async-done | bytes 65568 | tf_op jit(solution)/shard_map/all_to_all | solution.py:577
  36.2 1.3 %attend.1 = bf16[16,48,128]{2,1,0:T(8,128)(2,1)} custom-call(bf16[16,16,128]{2,1,0:T(8,128)(2,1)S(1)} %all-to-all-done.1.columns_ref, bf16[512,1024]{1,0:T(8,128)(2,1)S(1)} %turned_keys.1.keys_ref, f32[2,512]{1,0:T(2,128)S(1)} %and_select_fusion.bias_ref, f32[2,128]{1,0:T(2,128)S(1)} %get-tuple-element.61.cos_ref, f32[2,128]{1,0:T(2,128)S(1)} %get-tuple-element.62.sin_ref), custom_call_target="tpu_custom_call" | custom-call | flops 33554432 | bytes 2097152 | tf_op jit(solution)/shard_map/attend/pallas_call | solution.py:495
  37.6 3.5 %all-to-all-start.2 = ((bf16[16,48,128]{2,1,0:T(8,128)(2,1)}), bf16[16,48,128]{2,1,0:T(8,128)(2,1)S(1)}, u32[]{:S(2)}, u32[]{:S(2)}) async-start(bf16[16,48,128]{2,1,0:T(8,128)(2,1)} %attend.1), calls=%async_computation.2 | async-start | bytes 393216 | tf_op jit(solution)/shard_map/all_to_all | solution.py:577
  41.1 9.0 %all-to-all-done.2.weights_ref = bf16[16,48,128]{2,1,0:T(8,128)(2,1)S(1)} async-done(((bf16[16,48,128]{2,1,0:T(8,128)(2,1)}), bf16[16,48,128]{2,1,0:T(8,128)(2,1)S(1)}, u32[]{:S(2)}, u32[]{:S(2)}) %all-to-all-start.2) | async-done | bytes 196640 | tf_op jit(solution)/shard_map/all_to_all | solution.py:577
  50.1 1.1 %mix_values.1 = (bf16[128,128]{1,0:T(8,128)(2,1)S(1)}, bf16[128,128]{1,0:T(8,128)(2,1)S(1)}, bf16[128,128]{1,0:T(8,128)(2,1)S(1)}, bf16[128,128]{1,0:T(8,128)(2,1)S(1)}) custom-call(s32[1]{0:T(128)} %bitcast.me_ref, s32[128]{0:T(128)S(1)} %get-tuple-element.31.rows_ref, bf16[16,48,128]{2,1,0:T(8,128)(2,1)S(1)} %all-to-all-done.2.weights_ref, ...), custom_call_target="tpu_custom_call" | custom-call | flops 67108864 | bytes 4194304 | tf_op jit(solution)/shard_map/mix_values/pallas_call | solution.py:205
  51.2 1.4 %collective-permute-start.5 = (bf16[128,128]{1,0:T(8,128)(2,1)S(1)}, bf16[128,128]{1,0:T(8,128)(2,1)S(1)}, u32[]{:S(2)}, u32[]{:S(2)}) collective-permute-start(bf16[128,128]{1,0:T(8,128)(2,1)S(1)} %get-tuple-element.47), channel_id=1, source_target_pairs={{0,8},{1,9},{2,10},{3,11},{4,12},{5,13},{6,14},{7,15},{8,0},{9,1},... | collective-permute-start | bytes 98312 | tf_op jit(solution)/shard_map/ppermute | solution.py:573
  52.6 3.0 %collective-permute-start.6 = (bf16[128,128]{1,0:T(8,128)(2,1)S(1)}, bf16[128,128]{1,0:T(8,128)(2,1)S(1)}, u32[]{:S(2)}, u32[]{:S(2)}) collective-permute-start(bf16[128,128]{1,0:T(8,128)(2,1)S(1)} %get-tuple-element.48), channel_id=1, source_target_pairs={{0,12},{1,13},{2,14},{3,15},{4,8},{5,9},{6,10},{7,11},{8,4},{9,5},... | collective-permute-start | bytes 98312 | tf_op jit(solution)/shard_map/ppermute | solution.py:573
  55.6 3.5 %fetch_weight.3.weight_ref = bf16[512,8192]{1,0:T(8,128)(2,1)S(1)} custom-call(bf16[512,8192]{1,0:T(8,128)(2,1)} %source_ref.1), custom_call_target="tpu_custom_call" | custom-call | bytes 8388608 | tf_op jit(solution)/shard_map/fetch_weight/pallas_call | solution.py:277
  59.1 1.8 %output_project.1 = (bf16[8,128,128]{2,1,0:T(8,128)(2,1)S(1)}, bf16[8,128,128]{2,1,0:T(8,128)(2,1)S(1)}) custom-call(s32[1]{0:T(128)} %bitcast.me_ref, bf16[512,8192]{1,0:T(8,128)(2,1)S(1)} %fetch_weight.3.weight_ref, bf16[128,128]{1,0:T(8,128)(2,1)S(1)} %get-tuple-element.45.rest_0_, bf16[128,128]{1,0:T(8,128)(2,1)S(1)} %collective-permute-done.4.rest_1_, ...), custom_call_target="tpu_custom_call" | custom-call | flops 268435456 | bytes 8388608 | tf_op jit(solution)/shard_map/output_project/pallas_call | solution.py:555
  61.0 1.5 %collective-permute-done.7 = bf16[8,128,128]{2,1,0:T(8,128)(2,1)S(1)} collective-permute-done((bf16[8,128,128]{2,1,0:T(8,128)(2,1)S(1)}, bf16[8,128,128]{2,1,0:T(8,128)(2,1)S(1)}, u32[]{:S(2)}, u32[]{:S(2)}) %collective-permute-start.7) | collective-permute-done | bytes 262176 | tf_op jit(solution)/shard_map/ppermute | solution.py:573
  62.6 12.5 %all_to_all.20 = bf16[8,128,128]{2,1,0:T(8,128)(2,1)S(1)} all-to-all(bf16[8,128,128]{2,1,0:T(8,128)(2,1)S(1)} %add_convert_fusion), channel_id=1, replica_groups={{0,2,4,6,8,10,12,14},{1,3,5,7,9,11,13,15},{16,18,20,22,24,26,28,30},{17..., dimensions={0} | all-to-all | bytes 524288 | tf_op jit(solution)/shard_map/all_to_all | solution.py:577
  75.1 0.6 reshape.32
  (33 shorter events, 1.6 us)
Async XLA Ops:
  1.8 16.9 %all-to-all-start = ((bf16[8,144,128]{2,1,0:T(8,128)(2,1)}), bf16[8,144,128]{2,1,0:T(8,128)(2,1)S(1)}, u32[]{:S(2)}, u32[]{:S(2)}) async-start(bf16[8,144,128]{2,1,0:T(8,128)(2,1)} %get-tuple-element.28), calls=%async_computation | async-start | bytes 589824 | tf_op jit(solution)/shard_map/all_to_all | solution.py:577
  9.0 1.2 %copy-start = (bf16[32,16,1024]{2,1,0:T(8,128)(2,1)S(1)}, bf16[32,16,1024]{2,1,0:T(8,128)(2,1)}, u32[]{:S(2)}) copy-start(bf16[32,16,1024]{2,1,0:T(8,128)(2,1)} %store_ref.1) | copy-start | bytes 3145732
  11.2 26.3 %collective-permute-start.1 = (bf16[512,512]{1,0:T(8,128)(2,1)}, bf16[512,512]{1,0:T(8,128)(2,1)S(1)}, u32[]{:S(2)}, u32[]{:S(2)}) collective-permute-start(bf16[512,512]{1,0:T(8,128)(2,1)} %get-tuple-element.36), channel_id=1, source_target_pairs={{0,2},{1,3},{2,0},{3,1},{4,6},{5,7},{6,4},{7,5},{8,10},{9,11},{10,... | collective-permute-start | bytes 1572872 | tf_op jit(solution)/shard_map/ppermute | solution.py:573
  13.3 27.8 %collective-permute-start.2 = (bf16[512,512]{1,0:T(8,128)(2,1)S(1)}, bf16[512,512]{1,0:T(8,128)(2,1)S(1)}, u32[]{:S(2)}, u32[]{:S(2)}) collective-permute-start(bf16[512,512]{1,0:T(8,128)(2,1)S(1)} %get-tuple-element.38.rest_0_), channel_id=1, source_target_pairs={{0,1},{1,0},{2,3},{3,2},{4,5},{5,4},{6,7},{7,6},{8,9},{9,8},{10,11... | collective-permute-start | bytes 1572872 | tf_op jit(solution)/shard_map/ppermute | solution.py:573
  18.6 1.8 %collective-permute-start = (bf16[8,144,128]{2,1,0:T(8,128)(2,1)S(1)}, bf16[8,144,128]{2,1,0:T(8,128)(2,1)S(1)}, u32[]{:S(2)}, u32[]{:S(2)}) collective-permute-start(bf16[8,144,128]{2,1,0:T(8,128)(2,1)S(1)} %all-to-all-done.first_ref), channel_id=1, source_target_pairs={{0,1},{1,0},{2,3},{3,2},{4,5},{5,4},{6,7},{7,6},{8,9},{9,8},{10,11... | collective-permute-start | bytes 884744 | tf_op jit(solution)/shard_map/ppermute | solution.py:573
  18.8 11.7 %copy-start.1 = (bf16[1,160,1024]{2,1,0:T(8,128)(2,1)S(1)}, bf16[1,160,1024]{2,1,0:T(8,128)(2,1)}, u32[]{:S(2)}) copy-start(bf16[1,160,1024]{2,1,0:T(8,128)(2,1)} %param.17) | copy-start | bytes 983044
  18.8 11.7 %copy-start.2 = (s32[16]{0:T(128)S(1)}, s32[16]{0:T(128)}, u32[]{:S(2)}) copy-start(s32[16]{0:T(128)} %get-tuple-element.33.pair_ref) | copy-start | bytes 196
  20.4 11.5 %copy-start.3 = (s32[2,1,16]{2,1,0:T(1,128)S(1)}, s32[2,1,16]{2,1,0:T(1,128)}, u32[]{:S(2)}) copy-start(s32[2,1,16]{2,1,0:T(1,128)} %param.21) | copy-start | bytes 388
  25.5 10.7 %all-to-all-start.1 = ((bf16[16,16,128]{2,1,0:T(8,128)(2,1)}), bf16[16,16,128]{2,1,0:T(8,128)(2,1)S(1)}, u32[]{:S(2)}, u32[]{:S(2)}) async-start(bf16[16,16,128]{2,1,0:T(8,128)(2,1)} %get-tuple-element.34), calls=%async_computation.1 | async-start | bytes 131072 | tf_op jit(solution)/shard_map/all_to_all | solution.py:577
  37.6 12.5 %collective-permute-start.3 = (bf16[512,512]{1,0:T(8,128)(2,1)S(1)}, bf16[512,512]{1,0:T(8,128)(2,1)S(1)}, u32[]{:S(2)}, u32[]{:S(2)}) collective-permute-start(bf16[512,512]{1,0:T(8,128)(2,1)S(1)} %collective-permute-done.1.rest_2_), channel_id=1, source_target_pairs={{0,1},{1,0},{2,3},{3,2},{4,5},{5,4},{6,7},{7,6},{8,9},{9,8},{10,11... | collective-permute-start | bytes 1572872 | tf_op jit(solution)/shard_map/ppermute | solution.py:573
  37.6 12.5 %all-to-all-start.2 = ((bf16[16,48,128]{2,1,0:T(8,128)(2,1)}), bf16[16,48,128]{2,1,0:T(8,128)(2,1)S(1)}, u32[]{:S(2)}, u32[]{:S(2)}) async-start(bf16[16,48,128]{2,1,0:T(8,128)(2,1)} %attend.1), calls=%async_computation.2 | async-start | bytes 393216 | tf_op jit(solution)/shard_map/all_to_all | solution.py:577
  51.1 8.0 %collective-permute-start.4 = (bf16[128,128]{1,0:T(8,128)(2,1)S(1)}, bf16[128,128]{1,0:T(8,128)(2,1)S(1)}, u32[]{:S(2)}, u32[]{:S(2)}) collective-permute-start(bf16[128,128]{1,0:T(8,128)(2,1)S(1)} %get-tuple-element.46), channel_id=1, source_target_pairs={{0,4},{1,5},{2,6},{3,7},{4,0},{5,1},{6,2},{7,3},{8,12},{9,13},{10,... | collective-permute-start | bytes 98312 | tf_op jit(solution)/shard_map/ppermute | solution.py:573
  51.2 7.9 %collective-permute-start.5 = (bf16[128,128]{1,0:T(8,128)(2,1)S(1)}, bf16[128,128]{1,0:T(8,128)(2,1)S(1)}, u32[]{:S(2)}, u32[]{:S(2)}) collective-permute-start(bf16[128,128]{1,0:T(8,128)(2,1)S(1)} %get-tuple-element.47), channel_id=1, source_target_pairs={{0,8},{1,9},{2,10},{3,11},{4,12},{5,13},{6,14},{7,15},{8,0},{9,1},... | collective-permute-start | bytes 98312 | tf_op jit(solution)/shard_map/ppermute | solution.py:573
  52.6 6.5 %collective-permute-start.6 = (bf16[128,128]{1,0:T(8,128)(2,1)S(1)}, bf16[128,128]{1,0:T(8,128)(2,1)S(1)}, u32[]{:S(2)}, u32[]{:S(2)}) collective-permute-start(bf16[128,128]{1,0:T(8,128)(2,1)S(1)} %get-tuple-element.48), channel_id=1, source_target_pairs={{0,12},{1,13},{2,14},{3,15},{4,8},{5,9},{6,10},{7,11},{8,4},{9,5},... | collective-permute-start | bytes 98312 | tf_op jit(solution)/shard_map/ppermute | solution.py:573
  60.9 1.6 %collective-permute-start.7 = (bf16[8,128,128]{2,1,0:T(8,128)(2,1)S(1)}, bf16[8,128,128]{2,1,0:T(8,128)(2,1)S(1)}, u32[]{:S(2)}, u32[]{:S(2)}) collective-permute-start(bf16[8,128,128]{2,1,0:T(8,128)(2,1)S(1)} %get-tuple-element.50), channel_id=1, source_target_pairs={{0,1},{1,0},{2,3},{3,2},{4,5},{5,4},{6,7},{7,6},{8,9},{9,8},{10,11... | collective-permute-start | bytes 786440 | tf_op jit(solution)/shard_map/ppermute | solution.py:573

commit v15 on v14

--- a/solution.py
+++ b/solution.py
@@ -301,10 +301,17 @@
     span = depth // chunks
     pieces = depth // LANES
     copies = []
+    parts = sems.shape[1]
     for i in range(chunks):
-        rows = pl.ds(i * span, span)
-        copies.append(pltpu.make_async_copy(wq_ref.at[rows, :], wq_buf.at[i], sems.at[i]))
-        copies[-1].start()
+        copies.append([])
+        for part in range(parts):
+            copy = pltpu.make_async_copy(
+                wq_ref.at[pl.ds(i * span + part * (span // parts), span // parts), :],
+                wq_buf.at[i, pl.ds(part * (span // parts), span // parts), :],
+                sems.at[i, part],
+            )
+            copy.start()
+            copies[-1].append(copy)
     half = first_ref.shape[0]
     count = 2 * half * STEPS
     rows = STEPS * pieces
@@ -322,10 +329,21 @@
     for c in range(pieces):
         part = x_scr[pl.ds(c, count, stride=pieces), :]
         lhs_scr[:, c * LANES : (c + 1) * LANES] = part.astype(BF16)
+    if fast:
+        me = me_ref[0]
+        out_scr[...] = jnp.zeros_like(out_scr)
+        table_copy.wait()
+        plane = jnp.bitwise_and(me, -PLANE)
+        for j in range(2 * half):
+            place = origin(me, order, j) * (2 * PLANE)
+            for k in range(2):
+                for b in range(PLANE):
+                    rows_ref[place + k * PLANE + b] = table_smem[2 * j + k, plane + b]
     q_sum = jnp.zeros((count, q_cols), F32)
     k_sum = jnp.zeros((count, k_cols), F32)
     for i in range(chunks):
-        copies[i].wait()
+        for copy in copies[i]:
+            copy.wait()
         lhs = lhs_scr[:, i * span : (i + 1) * span]
         q_sum = q_sum + jnp.dot(lhs, wq_buf[i], preferred_element_type=F32)
         k_sum = k_sum + jnp.dot(
@@ -335,9 +353,7 @@
         out_ref[:, :q_cols] = q_sum.astype(BF16)
         out_ref[:, q_cols:] = k_sum.astype(BF16)
         return
-    me = me_ref[0]
     per = q_cols // LANES
-    out_scr[...] = jnp.zeros_like(out_scr)
     for j in range(2 * half):
         place = origin(me, order, j)
         for step in range(STEPS):
@@ -350,13 +366,6 @@
                 row : row + 1, :
             ]
     out_ref[...] = out_scr[...].astype(BF16)
-    table_copy.wait()
-    plane = jnp.bitwise_and(me, -PLANE)
-    for j in range(2 * half):
-        place = origin(me, order, j) * (2 * PLANE)
-        for k in range(2):
-            for b in range(PLANE):
-                rows_ref[place + k * PLANE + b] = table_smem[2 * j + k, plane + b]
 
 
 def project(me, first, second, query_weight, kv_weight, order, fast):
@@ -385,7 +394,7 @@
             VMEM((rows, depth), BF16),
             VMEM((chunks, span, q_cols), BF16),
             VMEM((devices, 16, LANES) if fast else (8, LANES), F32),
-            pltpu.SemaphoreType.DMA((chunks,)),
+            pltpu.SemaphoreType.DMA((chunks, 4)),
         ]
         + (
             [

time: 76.3 us -> 76.4 us (level)
  no operation moved by 1% of the time
where the time goes in v15:
time: 76.4 us; the launch traced here: 75.8 us
  starting transfers between devices  21.1 us (28%)
  Pallas kernels  18.4 us (24%)
  waiting for transfers between devices  17.6 us (23%)
  blocking collectives  12.5 us (16%)
  local copies, waits for them, and re-layouts  2.99 us (4%)
  other arithmetic  2.32 us (3%)
  between operations  0.88 us (1%)
    all_to_all x3, waiting for transfers between devices, exchange(): lax.all_to_all(blocks, AXIS, split_axis=0, concat_axis=0, tiled=True, axi...  16 us
    all_to_all x3, starting transfers between devices, exchange(): lax.all_to_all(blocks, AXIS, split_axis=0, concat_axis=0, tiled=True, axi...  14.6 us
    all_to_all x1, blocking collectives, exchange(): lax.all_to_all(blocks, AXIS, split_axis=0, concat_axis=0, tiled=True, axi...  12.5 us
    ppermute x8, starting transfers between devices, swap(): return lax.ppermute(block, AXIS, [(i, i ^ bit) for i in range(devices)])  6.54 us
    pallas_call x2, Pallas kernels, fetch(): pl.pallas_call(fetch_kernel, in_specs=[whole(pl.ANY)], out_specs=whole(pl...  5.1 us
    pallas_call x1, Pallas kernels, project(): pl.pallas_call(functools.partial(project_kernel, order, fast), in_specs=[...  5.08 us
    unnamed x9, local copies, waits for them, and re-layouts  2.28 us
    pallas_call x1, Pallas kernels, output(): pl.pallas_call(functools.partial(output_kernel, fast, len(lhs)), in_specs...  1.78 us
  transfers between devices with their start and end apart: 11, of which 4 were waited for; matrix products, arithmetic and copies ran while one was open for 4% of the time, Pallas kernels for 18%

profile of v15, /device:TPU:0, one launch (start us, length us, event | category | flops | bytes accessed | tf_op | source)
XLA Modules:
  0.0 75.8 jit_solution(3138138897166435256)
XLA Ops:
  0.0 1.7 %prepare.1 = (bf16[8,144,128]{2,1,0:T(8,128)(2,1)}, s32[16]{0:T(128)}, s32[16]{0:T(128)}) custom-call(bf16[2,8192]{1,0:T(2,128)(2,1)} %bitcast.11, bf16[64,128]{1,0:T(8,128)(2,1)} %bitcast.12, s32[1,32]{1,0:T(1,128)} %slots_ref.1), custom_call_target="tpu_custom_call" | custom-call | tf_op jit(solution)/shard_map/prepare/pallas_call | solution.py:92
  1.8 7.3 %all-to-all-start = ((bf16[8,144,128]{2,1,0:T(8,128)(2,1)}), bf16[8,144,128]{2,1,0:T(8,128)(2,1)S(1)}, u32[]{:S(2)}, u32[]{:S(2)}) async-start(bf16[8,144,128]{2,1,0:T(8,128)(2,1)} %get-tuple-element.28), calls=%async_computation | async-start | bytes 589824 | tf_op jit(solution)/shard_map/all_to_all | solution.py:586
  9.0 1.2 %copy-done = bf16[32,16,1024]{2,1,0:T(8,128)(2,1)S(1)} copy-done((bf16[32,16,1024]{2,1,0:T(8,128)(2,1)S(1)}, bf16[32,16,1024]{2,1,0:T(8,128)(2,1)}, u32[]{:S(2)}) %copy-start) | copy-done | bytes 1048600
  10.2 1.0 %split_values.1 = (bf16[512,512]{1,0:T(8,128)(2,1)S(1)}, bf16[512,512]{1,0:T(8,128)(2,1)}) custom-call(s32[1]{0:T(128)S(6)} %and.20.x_ref, bf16[32,16,1024]{2,1,0:T(8,128)(2,1)S(1)} %copy-done), custom_call_target="tpu_custom_call" | custom-call | tf_op jit(solution)/shard_map/split_values/pallas_call | solution.py:159
  11.2 2.0 %collective-permute-start.1 = (bf16[512,512]{1,0:T(8,128)(2,1)}, bf16[512,512]{1,0:T(8,128)(2,1)S(1)}, u32[]{:S(2)}, u32[]{:S(2)}) collective-permute-start(bf16[512,512]{1,0:T(8,128)(2,1)} %get-tuple-element.36), channel_id=1, source_target_pairs={{0,2},{1,3},{2,0},{3,1},{4,6},{5,7},{6,4},{7,5},{8,10},{9,11},{10,... | collective-permute-start | bytes 1572872 | tf_op jit(solution)/shard_map/ppermute | solution.py:582
  14.5 1.0 %copy.13 = bf16[1,512,160]{2,1,0:T(8,128)(2,1)S(1)} copy(bf16[1,512,160]{1,2,0:T(8,128)(2,1)} %param.16) | data formatting | bytes 327680 | tf_op args[5]
  15.8 2.9 %all-to-all-done.first_ref = bf16[8,144,128]{2,1,0:T(8,128)(2,1)S(1)} async-done(((bf16[8,144,128]{2,1,0:T(8,128)(2,1)}), bf16[8,144,128]{2,1,0:T(8,128)(2,1)S(1)}, u32[]{:S(2)}, u32[]{:S(2)}) %all-to-all-start) | async-done | bytes 294944 | tf_op jit(solution)/shard_map/all_to_all | solution.py:586
  18.8 1.6 %fetch_weight.2.wk_ref = bf16[8192,128]{1,0:T(8,128)(2,1)S(1)} custom-call(bf16[8192,128]{1,0:T(8,128)(2,1)} %source_ref), custom_call_target="tpu_custom_call" | custom-call | bytes 2097152 | tf_op jit(solution)/shard_map/fetch_weight/pallas_call | solution.py:277
  20.5 5.1 %norm_project.1 = (bf16[16,16,128]{2,1,0:T(8,128)(2,1)}, s32[128]{0:T(128)S(1)}) custom-call(s32[1]{0:T(128)} %bitcast.me_ref, bf16[8,144,128]{2,1,0:T(8,128)(2,1)S(1)} %all-to-all-done.first_ref, bf16[8,144,128]{2,1,0:T(8,128)(2,1)S(1)} %collective-permute-done.second_ref, bf16[8192,512]{1,0:T(8,128)(2,1)} %wq_ref.1, bf16[8192,128]{1,0:T(8,128)(2,1)S(1)} %fetch_weight.2.wk_ref), custom_call_target="tpu_custom_call" | custom-call | flops 335544320 | bytes 10485760 | tf_op jit(solution)/shard_map/norm_project/pallas_call | solution.py:380
  25.6 3.8 %all-to-all-start.1 = ((bf16[16,16,128]{2,1,0:T(8,128)(2,1)}), bf16[16,16,128]{2,1,0:T(8,128)(2,1)S(1)}, u32[]{:S(2)}, u32[]{:S(2)}) async-start(bf16[16,16,128]{2,1,0:T(8,128)(2,1)} %get-tuple-element.34), calls=%async_computation.1 | async-start | bytes 131072 | tf_op jit(solution)/shard_map/all_to_all | solution.py:586
  29.4 1.0 %fusion = (f32[512,64]{1,0:T(8,128)S(1)}, f32[512,64]{1,0:T(8,128)S(1)}, f32[512,64]{1,0:T(8,128)S(1)}) fusion(f32[64]{0:T(128)S(1)} %multiply_exponential_fusion, f32[512]{0:T(512)S(1)} %get-tuple-element.55), kind=kLoop, calls=%fused_computation.5 | loop fusion | flops 65536 | bytes 395520 | tf_op jit(solution)/shard_map/neg | solution.py:41
  30.6 1.3 %turned_keys.1.keys_ref = bf16[512,1024]{1,0:T(8,128)(2,1)S(1)} custom-call(s32[16]{0:T(128)S(1)} %copy-done.2, bf16[512,160]{1,0:T(8,128)(2,1)S(1)} %bitcast.9, bf16[160,1024]{1,0:T(8,128)(2,1)S(1)} %bitcast.10, f32[512,128]{1,0:T(8,128)S(1)} %get-tuple-element.59.cos_ref, f32[512,128]{1,0:T(8,128)S(1)} %get-tuple-element.60.sin_ref), custom_call_target="tpu_custom_call" | custom-call | flops 167772160 | bytes 2097152 | tf_op jit(solution)/shard_map/turned_keys/pallas_call | solution.py:241
  32.1 4.2 %all-to-all-done.1.columns_ref = bf16[16,16,128]{2,1,0:T(8,128)(2,1)S(1)} async-done(((bf16[16,16,128]{2,1,0:T(8,128)(2,1)}), bf16[16,16,128]{2,1,0:T(8,128)(2,1)S(1)}, u32[]{:S(2)}, u32[]{:S(2)}) %all-to-all-start.1) | async-done | bytes 65568 | tf_op jit(solution)/shard_map/all_to_all | solution.py:586
  36.3 1.3 %attend.1 = bf16[16,48,128]{2,1,0:T(8,128)(2,1)} custom-call(bf16[16,16,128]{2,1,0:T(8,128)(2,1)S(1)} %all-to-all-done.1.columns_ref, bf16[512,1024]{1,0:T(8,128)(2,1)S(1)} %turned_keys.1.keys_ref, f32[2,512]{1,0:T(2,128)S(1)} %and_select_fusion.bias_ref, f32[2,128]{1,0:T(2,128)S(1)} %get-tuple-element.61.cos_ref, f32[2,128]{1,0:T(2,128)S(1)} %get-tuple-element.62.sin_ref), custom_call_target="tpu_custom_call" | custom-call | flops 33554432 | bytes 2097152 | tf_op jit(solution)/shard_map/attend/pallas_call | solution.py:504
  37.6 3.5 %all-to-all-start.2 = ((bf16[16,48,128]{2,1,0:T(8,128)(2,1)}), bf16[16,48,128]{2,1,0:T(8,128)(2,1)S(1)}, u32[]{:S(2)}, u32[]{:S(2)}) async-start(bf16[16,48,128]{2,1,0:T(8,128)(2,1)} %attend.1), calls=%async_computation.2 | async-start | bytes 393216 | tf_op jit(solution)/shard_map/all_to_all | solution.py:586
  41.1 9.0 %all-to-all-done.2.weights_ref = bf16[16,48,128]{2,1,0:T(8,128)(2,1)S(1)} async-done(((bf16[16,48,128]{2,1,0:T(8,128)(2,1)}), bf16[16,48,128]{2,1,0:T(8,128)(2,1)S(1)}, u32[]{:S(2)}, u32[]{:S(2)}) %all-to-all-start.2) | async-done | bytes 196640 | tf_op jit(solution)/shard_map/all_to_all | solution.py:586
  50.1 1.1 %mix_values.1 = (bf16[128,128]{1,0:T(8,128)(2,1)S(1)}, bf16[128,128]{1,0:T(8,128)(2,1)S(1)}, bf16[128,128]{1,0:T(8,128)(2,1)S(1)}, bf16[128,128]{1,0:T(8,128)(2,1)S(1)}) custom-call(s32[1]{0:T(128)} %bitcast.me_ref, s32[128]{0:T(128)S(1)} %get-tuple-element.31.rows_ref, bf16[16,48,128]{2,1,0:T(8,128)(2,1)S(1)} %all-to-all-done.2.weights_ref, ...), custom_call_target="tpu_custom_call" | custom-call | flops 67108864 | bytes 4194304 | tf_op jit(solution)/shard_map/mix_values/pallas_call | solution.py:205
  51.3 1.4 %collective-permute-start.5 = (bf16[128,128]{1,0:T(8,128)(2,1)S(1)}, bf16[128,128]{1,0:T(8,128)(2,1)S(1)}, u32[]{:S(2)}, u32[]{:S(2)}) collective-permute-start(bf16[128,128]{1,0:T(8,128)(2,1)S(1)} %get-tuple-element.47), channel_id=1, source_target_pairs={{0,8},{1,9},{2,10},{3,11},{4,12},{5,13},{6,14},{7,15},{8,0},{9,1},... | collective-permute-start | bytes 98312 | tf_op jit(solution)/shard_map/ppermute | solution.py:582
  52.6 3.0 %collective-permute-start.6 = (bf16[128,128]{1,0:T(8,128)(2,1)S(1)}, bf16[128,128]{1,0:T(8,128)(2,1)S(1)}, u32[]{:S(2)}, u32[]{:S(2)}) collective-permute-start(bf16[128,128]{1,0:T(8,128)(2,1)S(1)} %get-tuple-element.48), channel_id=1, source_target_pairs={{0,12},{1,13},{2,14},{3,15},{4,8},{5,9},{6,10},{7,11},{8,4},{9,5},... | collective-permute-start | bytes 98312 | tf_op jit(solution)/shard_map/ppermute | solution.py:582
  55.6 3.5 %fetch_weight.3.weight_ref = bf16[512,8192]{1,0:T(8,128)(2,1)S(1)} custom-call(bf16[512,8192]{1,0:T(8,128)(2,1)} %source_ref.1), custom_call_target="tpu_custom_call" | custom-call | bytes 8388608 | tf_op jit(solution)/shard_map/fetch_weight/pallas_call | solution.py:277
  59.2 1.8 %output_project.1 = (bf16[8,128,128]{2,1,0:T(8,128)(2,1)S(1)}, bf16[8,128,128]{2,1,0:T(8,128)(2,1)S(1)}) custom-call(s32[1]{0:T(128)} %bitcast.me_ref, bf16[512,8192]{1,0:T(8,128)(2,1)S(1)} %fetch_weight.3.weight_ref, bf16[128,128]{1,0:T(8,128)(2,1)S(1)} %get-tuple-element.45.rest_0_, bf16[128,128]{1,0:T(8,128)(2,1)S(1)} %collective-permute-done.4.rest_1_, ...), custom_call_target="tpu_custom_call" | custom-call | flops 268435456 | bytes 8388608 | tf_op jit(solution)/shard_map/output_project/pallas_call | solution.py:564
  61.1 1.5 %collective-permute-done.7 = bf16[8,128,128]{2,1,0:T(8,128)(2,1)S(1)} collective-permute-done((bf16[8,128,128]{2,1,0:T(8,128)(2,1)S(1)}, bf16[8,128,128]{2,1,0:T(8,128)(2,1)S(1)}, u32[]{:S(2)}, u32[]{:S(2)}) %collective-permute-start.7) | collective-permute-done | bytes 262176 | tf_op jit(solution)/shard_map/ppermute | solution.py:582
  62.7 12.5 %all_to_all.20 = bf16[8,128,128]{2,1,0:T(8,128)(2,1)S(1)} all-to-all(bf16[8,128,128]{2,1,0:T(8,128)(2,1)S(1)} %add_convert_fusion), channel_id=1, replica_groups={{0,2,4,6,8,10,12,14},{1,3,5,7,9,11,13,15},{16,18,20,22,24,26,28,30},{17..., dimensions={0} | all-to-all | bytes 524288 | tf_op jit(solution)/shard_map/all_to_all | solution.py:586
  75.2 0.6 reshape.32
  (33 shorter events, 1.6 us)
Async XLA Ops:
  1.8 16.9 %all-to-all-start = ((bf16[8,144,128]{2,1,0:T(8,128)(2,1)}), bf16[8,144,128]{2,1,0:T(8,128)(2,1)S(1)}, u32[]{:S(2)}, u32[]{:S(2)}) async-start(bf16[8,144,128]{2,1,0:T(8,128)(2,1)} %get-tuple-element.28), calls=%async_computation | async-start | bytes 589824 | tf_op jit(solution)/shard_map/all_to_all | solution.py:586
  9.0 1.2 %copy-start = (bf16[32,16,1024]{2,1,0:T(8,128)(2,1)S(1)}, bf16[32,16,1024]{2,1,0:T(8,128)(2,1)}, u32[]{:S(2)}) copy-start(bf16[32,16,1024]{2,1,0:T(8,128)(2,1)} %store_ref.1) | copy-start | bytes 3145732
  11.2 26.4 %collective-permute-start.1 = (bf16[512,512]{1,0:T(8,128)(2,1)}, bf16[512,512]{1,0:T(8,128)(2,1)S(1)}, u32[]{:S(2)}, u32[]{:S(2)}) collective-permute-start(bf16[512,512]{1,0:T(8,128)(2,1)} %get-tuple-element.36), channel_id=1, source_target_pairs={{0,2},{1,3},{2,0},{3,1},{4,6},{5,7},{6,4},{7,5},{8,10},{9,11},{10,... | collective-permute-start | bytes 1572872 | tf_op jit(solution)/shard_map/ppermute | solution.py:582
  13.3 27.9 %collective-permute-start.2 = (bf16[512,512]{1,0:T(8,128)(2,1)S(1)}, bf16[512,512]{1,0:T(8,128)(2,1)S(1)}, u32[]{:S(2)}, u32[]{:S(2)}) collective-permute-start(bf16[512,512]{1,0:T(8,128)(2,1)S(1)} %get-tuple-element.38.rest_0_), channel_id=1, source_target_pairs={{0,1},{1,0},{2,3},{3,2},{4,5},{5,4},{6,7},{7,6},{8,9},{9,8},{10,11... | collective-permute-start | bytes 1572872 | tf_op jit(solution)/shard_map/ppermute | solution.py:582
  18.6 1.8 %collective-permute-start = (bf16[8,144,128]{2,1,0:T(8,128)(2,1)S(1)}, bf16[8,144,128]{2,1,0:T(8,128)(2,1)S(1)}, u32[]{:S(2)}, u32[]{:S(2)}) collective-permute-start(bf16[8,144,128]{2,1,0:T(8,128)(2,1)S(1)} %all-to-all-done.first_ref), channel_id=1, source_target_pairs={{0,1},{1,0},{2,3},{3,2},{4,5},{5,4},{6,7},{7,6},{8,9},{9,8},{10,11... | collective-permute-start | bytes 884744 | tf_op jit(solution)/shard_map/ppermute | solution.py:582
  18.8 11.8 %copy-start.1 = (bf16[1,160,1024]{2,1,0:T(8,128)(2,1)S(1)}, bf16[1,160,1024]{2,1,0:T(8,128)(2,1)}, u32[]{:S(2)}) copy-start(bf16[1,160,1024]{2,1,0:T(8,128)(2,1)} %param.17) | copy-start | bytes 983044
  18.8 11.8 %copy-start.2 = (s32[16]{0:T(128)S(1)}, s32[16]{0:T(128)}, u32[]{:S(2)}) copy-start(s32[16]{0:T(128)} %get-tuple-element.33.pair_ref) | copy-start | bytes 196
  20.4 11.5 %copy-start.3 = (s32[2,1,16]{2,1,0:T(1,128)S(1)}, s32[2,1,16]{2,1,0:T(1,128)}, u32[]{:S(2)}) copy-start(s32[2,1,16]{2,1,0:T(1,128)} %param.21) | copy-start | bytes 388
  25.6 10.7 %all-to-all-start.1 = ((bf16[16,16,128]{2,1,0:T(8,128)(2,1)}), bf16[16,16,128]{2,1,0:T(8,128)(2,1)S(1)}, u32[]{:S(2)}, u32[]{:S(2)}) async-start(bf16[16,16,128]{2,1,0:T(8,128)(2,1)} %get-tuple-element.34), calls=%async_computation.1 | async-start | bytes 131072 | tf_op jit(solution)/shard_map/all_to_all | solution.py:586
  37.6 12.5 %collective-permute-start.3 = (bf16[512,512]{1,0:T(8,128)(2,1)S(1)}, bf16[512,512]{1,0:T(8,128)(2,1)S(1)}, u32[]{:S(2)}, u32[]{:S(2)}) collective-permute-start(bf16[512,512]{1,0:T(8,128)(2,1)S(1)} %collective-permute-done.1.rest_2_), channel_id=1, source_target_pairs={{0,1},{1,0},{2,3},{3,2},{4,5},{5,4},{6,7},{7,6},{8,9},{9,8},{10,11... | collective-permute-start | bytes 1572872 | tf_op jit(solution)/shard_map/ppermute | solution.py:582
  37.6 12.5 %all-to-all-start.2 = ((bf16[16,48,128]{2,1,0:T(8,128)(2,1)}), bf16[16,48,128]{2,1,0:T(8,128)(2,1)S(1)}, u32[]{:S(2)}, u32[]{:S(2)}) async-start(bf16[16,48,128]{2,1,0:T(8,128)(2,1)} %attend.1), calls=%async_computation.2 | async-start | bytes 393216 | tf_op jit(solution)/shard_map/all_to_all | solution.py:586
  51.2 8.0 %collective-permute-start.4 = (bf16[128,128]{1,0:T(8,128)(2,1)S(1)}, bf16[128,128]{1,0:T(8,128)(2,1)S(1)}, u32[]{:S(2)}, u32[]{:S(2)}) collective-permute-start(bf16[128,128]{1,0:T(8,128)(2,1)S(1)} %get-tuple-element.46), channel_id=1, source_target_pairs={{0,4},{1,5},{2,6},{3,7},{4,0},{5,1},{6,2},{7,3},{8,12},{9,13},{10,... | collective-permute-start | bytes 98312 | tf_op jit(solution)/shard_map/ppermute | solution.py:582
  51.3 7.9 %collective-permute-start.5 = (bf16[128,128]{1,0:T(8,128)(2,1)S(1)}, bf16[128,128]{1,0:T(8,128)(2,1)S(1)}, u32[]{:S(2)}, u32[]{:S(2)}) collective-permute-start(bf16[128,128]{1,0:T(8,128)(2,1)S(1)} %get-tuple-element.47), channel_id=1, source_target_pairs={{0,8},{1,9},{2,10},{3,11},{4,12},{5,13},{6,14},{7,15},{8,0},{9,1},... | collective-permute-start | bytes 98312 | tf_op jit(solution)/shard_map/ppermute | solution.py:582
  52.6 6.5 %collective-permute-start.6 = (bf16[128,128]{1,0:T(8,128)(2,1)S(1)}, bf16[128,128]{1,0:T(8,128)(2,1)S(1)}, u32[]{:S(2)}, u32[]{:S(2)}) collective-permute-start(bf16[128,128]{1,0:T(8,128)(2,1)S(1)} %get-tuple-element.48), channel_id=1, source_target_pairs={{0,12},{1,13},{2,14},{3,15},{4,8},{5,9},{6,10},{7,11},{8,4},{9,5},... | collective-permute-start | bytes 98312 | tf_op jit(solution)/shard_map/ppermute | solution.py:582
  61.0 1.6 %collective-permute-start.7 = (bf16[8,128,128]{2,1,0:T(8,128)(2,1)S(1)}, bf16[8,128,128]{2,1,0:T(8,128)(2,1)S(1)}, u32[]{:S(2)}, u32[]{:S(2)}) collective-permute-start(bf16[8,128,128]{2,1,0:T(8,128)(2,1)S(1)} %get-tuple-element.50), channel_id=1, source_target_pairs={{0,1},{1,0},{2,3},{3,2},{4,5},{5,4},{6,7},{7,6},{8,9},{9,8},{10,11... | collective-permute-start | bytes 786440 | tf_op jit(solution)/shard_map/ppermute | solution.py:582

commit v16 on v15

--- a/solution.py
+++ b/solution.py
@@ -619,12 +619,12 @@
     if fast:
         same_core = [list(range(core, devices, 2)) for core in range(2)]
         block = exchange(block, same_core)
-        block, kv_weight = lax.optimization_barrier((block, kv_weight))
+        x = lax.bitwise_and(lax.shift_right_logical(me_word, 1), 1)
+        keep, send = split_values(x, value_store)
+        block, kv_weight, send = lax.optimization_barrier((block, kv_weight, send))
         kv_weight = fetch(kv_weight, 50)
         other = swap(block, 1, devices)
         order = None
-        x = lax.bitwise_and(lax.shift_right_logical(me_word, 1), 1)
-        keep, send = split_values(x, value_store)
         neighbour = swap(send, 2, devices)
     else:
         order = [0]

time: 76.4 us -> 77.4 us (1.013)
  waiting for transfers between devices: 17.6 us -> 19.6 us
  starting transfers between devices: 21.1 us -> 20.3 us
    all_to_all x3, waiting for transfers between devices: 16 us -> 18 us  [exchange(): lax.all_to_all(blocks, AXIS, split_axis=0, concat_axis=0, tiled=True, axi...]
where the time goes in v16:
time: 77.4 us; the launch traced here: 76.8 us
  starting transfers between devices  20.3 us (26%)
  waiting for transfers between devices  19.6 us (25%)
  Pallas kernels  18.4 us (24%)
  blocking collectives  12.5 us (16%)
  local copies, waits for them, and re-layouts  2.99 us (4%)
  other arithmetic  2.32 us (3%)
  between operations  0.88 us (1%)
    all_to_all x3, waiting for transfers between devices, exchange(): lax.all_to_all(blocks, AXIS, split_axis=0, concat_axis=0, tiled=True, axi...  18 us
    all_to_all x3, starting transfers between devices, exchange(): lax.all_to_all(blocks, AXIS, split_axis=0, concat_axis=0, tiled=True, axi...  14.3 us
    all_to_all x1, blocking collectives, exchange(): lax.all_to_all(blocks, AXIS, split_axis=0, concat_axis=0, tiled=True, axi...  12.5 us
    ppermute x8, starting transfers between devices, swap(): return lax.ppermute(block, AXIS, [(i, i ^ bit) for i in range(devices)])  5.96 us
    pallas_call x1, Pallas kernels, project(): pl.pallas_call(functools.partial(project_kernel, order, fast), in_specs=[...  5.08 us
    pallas_call x2, Pallas kernels, fetch(): pl.pallas_call(fetch_kernel, in_specs=[whole(pl.ANY)], out_specs=whole(pl...  5.05 us
    unnamed x9, local copies, waits for them, and re-layouts  2.28 us
    pallas_call x1, Pallas kernels, output(): pl.pallas_call(functools.partial(output_kernel, fast, len(lhs)), in_specs...  1.78 us
  transfers between devices with their start and end apart: 11, of which 4 were waited for; matrix products, arithmetic and copies ran while one was open for 4% of the time, Pallas kernels for 18%

profile of v16, /device:TPU:0, one launch (start us, length us, event | category | flops | bytes accessed | tf_op | source)
XLA Modules:
  0.0 76.8 jit_solution(7033590987275206672)
XLA Ops:
  0.0 1.7 %prepare.1 = (bf16[8,144,128]{2,1,0:T(8,128)(2,1)}, s32[16]{0:T(128)}, s32[16]{0:T(128)}) custom-call(bf16[2,8192]{1,0:T(2,128)(2,1)} %bitcast.11, bf16[64,128]{1,0:T(8,128)(2,1)} %bitcast.12, s32[1,32]{1,0:T(1,128)} %slots_ref.1), custom_call_target="tpu_custom_call" | custom-call | tf_op jit(solution)/shard_map/prepare/pallas_call | solution.py:92
  1.8 7.3 %all-to-all-start = ((bf16[8,144,128]{2,1,0:T(8,128)(2,1)}), bf16[8,144,128]{2,1,0:T(8,128)(2,1)S(1)}, u32[]{:S(2)}, u32[]{:S(2)}) async-start(bf16[8,144,128]{2,1,0:T(8,128)(2,1)} %get-tuple-element.29), calls=%async_computation | async-start | bytes 589824 | tf_op jit(solution)/shard_map/all_to_all | solution.py:586
  9.0 1.2 %copy-done = bf16[32,16,1024]{2,1,0:T(8,128)(2,1)S(1)} copy-done((bf16[32,16,1024]{2,1,0:T(8,128)(2,1)S(1)}, bf16[32,16,1024]{2,1,0:T(8,128)(2,1)}, u32[]{:S(2)}) %copy-start) | copy-done | bytes 1048600
  10.2 1.0 %split_values.1 = (bf16[512,512]{1,0:T(8,128)(2,1)S(1)}, bf16[512,512]{1,0:T(8,128)(2,1)}) custom-call(s32[1]{0:T(128)S(6)} %and.17.x_ref, bf16[32,16,1024]{2,1,0:T(8,128)(2,1)S(1)} %copy-done), custom_call_target="tpu_custom_call" | custom-call | tf_op jit(solution)/shard_map/split_values/pallas_call | solution.py:159
  12.5 1.0 %copy.13 = bf16[1,512,160]{2,1,0:T(8,128)(2,1)S(1)} copy(bf16[1,512,160]{1,2,0:T(8,128)(2,1)} %param.16) | data formatting | bytes 327680 | tf_op args[5]
  13.7 4.9 %all-to-all-done.first_ref = bf16[8,144,128]{2,1,0:T(8,128)(2,1)S(1)} async-done(((bf16[8,144,128]{2,1,0:T(8,128)(2,1)}), bf16[8,144,128]{2,1,0:T(8,128)(2,1)S(1)}, u32[]{:S(2)}, u32[]{:S(2)}) %all-to-all-start) | async-done | bytes 294944 | tf_op jit(solution)/shard_map/all_to_all | solution.py:586
  18.8 1.4 %collective-permute-start.1 = (bf16[512,512]{1,0:T(8,128)(2,1)}, bf16[512,512]{1,0:T(8,128)(2,1)S(1)}, u32[]{:S(2)}, u32[]{:S(2)}) collective-permute-start(bf16[512,512]{1,0:T(8,128)(2,1)} %get-tuple-element.38), channel_id=1, source_target_pairs={{0,2},{1,3},{2,0},{3,1},{4,6},{5,7},{6,4},{7,5},{8,10},{9,11},{10,... | collective-permute-start | bytes 1572872 | tf_op jit(solution)/shard_map/ppermute | solution.py:582
  20.3 1.5 %fetch_weight.2.wk_ref = bf16[8192,128]{1,0:T(8,128)(2,1)S(1)} custom-call(bf16[8192,128]{1,0:T(8,128)(2,1)} %source_ref), custom_call_target="tpu_custom_call" | custom-call | bytes 2097152 | tf_op jit(solution)/shard_map/fetch_weight/pallas_call | solution.py:277
  21.9 5.1 %norm_project.1 = (bf16[16,16,128]{2,1,0:T(8,128)(2,1)}, s32[128]{0:T(128)S(1)}) custom-call(s32[1]{0:T(128)} %bitcast.me_ref, bf16[8,144,128]{2,1,0:T(8,128)(2,1)S(1)} %all-to-all-done.first_ref, bf16[8,144,128]{2,1,0:T(8,128)(2,1)S(1)} %collective-permute-done.second_ref, bf16[8192,512]{1,0:T(8,128)(2,1)} %wq_ref.1, bf16[8192,128]{1,0:T(8,128)(2,1)S(1)} %fetch_weight.2.wk_ref), custom_call_target="tpu_custom_call" | custom-call | flops 335544320 | bytes 10485760 | tf_op jit(solution)/shard_map/norm_project/pallas_call | solution.py:380
  27.0 3.5 %all-to-all-start.1 = ((bf16[16,16,128]{2,1,0:T(8,128)(2,1)}), bf16[16,16,128]{2,1,0:T(8,128)(2,1)S(1)}, u32[]{:S(2)}, u32[]{:S(2)}) async-start(bf16[16,16,128]{2,1,0:T(8,128)(2,1)} %get-tuple-element.36), calls=%async_computation.1 | async-start | bytes 131072 | tf_op jit(solution)/shard_map/all_to_all | solution.py:586
  30.5 1.0 %fusion = (f32[512,64]{1,0:T(8,128)S(1)}, f32[512,64]{1,0:T(8,128)S(1)}, f32[512,64]{1,0:T(8,128)S(1)}) fusion(f32[64]{0:T(128)S(1)} %multiply_exponential_fusion, f32[512]{0:T(512)S(1)} %get-tuple-element.57), kind=kLoop, calls=%fused_computation.5 | loop fusion | flops 65536 | bytes 395520 | tf_op jit(solution)/shard_map/neg | solution.py:41
  31.7 1.3 %turned_keys.1.keys_ref = bf16[512,1024]{1,0:T(8,128)(2,1)S(1)} custom-call(s32[16]{0:T(128)S(1)} %copy-done.2, bf16[512,160]{1,0:T(8,128)(2,1)S(1)} %bitcast.9, bf16[160,1024]{1,0:T(8,128)(2,1)S(1)} %bitcast.10, f32[512,128]{1,0:T(8,128)S(1)} %get-tuple-element.61.cos_ref, f32[512,128]{1,0:T(8,128)S(1)} %get-tuple-element.62.sin_ref), custom_call_target="tpu_custom_call" | custom-call | flops 167772160 | bytes 2097152 | tf_op jit(solution)/shard_map/turned_keys/pallas_call | solution.py:241
  33.1 4.2 %all-to-all-done.1.columns_ref = bf16[16,16,128]{2,1,0:T(8,128)(2,1)S(1)} async-done(((bf16[16,16,128]{2,1,0:T(8,128)(2,1)}), bf16[16,16,128]{2,1,0:T(8,128)(2,1)S(1)}, u32[]{:S(2)}, u32[]{:S(2)}) %all-to-all-start.1) | async-done | bytes 65568 | tf_op jit(solution)/shard_map/all_to_all | solution.py:586
  37.3 1.3 %attend.1 = bf16[16,48,128]{2,1,0:T(8,128)(2,1)} custom-call(bf16[16,16,128]{2,1,0:T(8,128)(2,1)S(1)} %all-to-all-done.1.columns_ref, bf16[512,1024]{1,0:T(8,128)(2,1)S(1)} %turned_keys.1.keys_ref, f32[2,512]{1,0:T(2,128)S(1)} %and_select_fusion.bias_ref, f32[2,128]{1,0:T(2,128)S(1)} %get-tuple-element.63.cos_ref, f32[2,128]{1,0:T(2,128)S(1)} %get-tuple-element.64.sin_ref), custom_call_target="tpu_custom_call" | custom-call | flops 33554432 | bytes 2097152 | tf_op jit(solution)/shard_map/attend/pallas_call | solution.py:504
  38.6 3.5 %all-to-all-start.2 = ((bf16[16,48,128]{2,1,0:T(8,128)(2,1)}), bf16[16,48,128]{2,1,0:T(8,128)(2,1)S(1)}, u32[]{:S(2)}, u32[]{:S(2)}) async-start(bf16[16,48,128]{2,1,0:T(8,128)(2,1)} %attend.1), calls=%async_computation.2 | async-start | bytes 393216 | tf_op jit(solution)/shard_map/all_to_all | solution.py:586
  42.2 9.0 %all-to-all-done.2.weights_ref = bf16[16,48,128]{2,1,0:T(8,128)(2,1)S(1)} async-done(((bf16[16,48,128]{2,1,0:T(8,128)(2,1)}), bf16[16,48,128]{2,1,0:T(8,128)(2,1)S(1)}, u32[]{:S(2)}, u32[]{:S(2)}) %all-to-all-start.2) | async-done | bytes 196640 | tf_op jit(solution)/shard_map/all_to_all | solution.py:586
  51.1 1.1 %mix_values.1 = (bf16[128,128]{1,0:T(8,128)(2,1)S(1)}, bf16[128,128]{1,0:T(8,128)(2,1)S(1)}, bf16[128,128]{1,0:T(8,128)(2,1)S(1)}, bf16[128,128]{1,0:T(8,128)(2,1)S(1)}) custom-call(s32[1]{0:T(128)} %bitcast.me_ref, s32[128]{0:T(128)S(1)} %get-tuple-element.33.rows_ref, bf16[16,48,128]{2,1,0:T(8,128)(2,1)S(1)} %all-to-all-done.2.weights_ref, ...), custom_call_target="tpu_custom_call" | custom-call | flops 67108864 | bytes 4194304 | tf_op jit(solution)/shard_map/mix_values/pallas_call | solution.py:205
  52.3 1.4 %collective-permute-start.5 = (bf16[128,128]{1,0:T(8,128)(2,1)S(1)}, bf16[128,128]{1,0:T(8,128)(2,1)S(1)}, u32[]{:S(2)}, u32[]{:S(2)}) collective-permute-start(bf16[128,128]{1,0:T(8,128)(2,1)S(1)} %get-tuple-element.49), channel_id=1, source_target_pairs={{0,8},{1,9},{2,10},{3,11},{4,12},{5,13},{6,14},{7,15},{8,0},{9,1},... | collective-permute-start | bytes 98312 | tf_op jit(solution)/shard_map/ppermute | solution.py:582
  53.7 3.0 %collective-permute-start.6 = (bf16[128,128]{1,0:T(8,128)(2,1)S(1)}, bf16[128,128]{1,0:T(8,128)(2,1)S(1)}, u32[]{:S(2)}, u32[]{:S(2)}) collective-permute-start(bf16[128,128]{1,0:T(8,128)(2,1)S(1)} %get-tuple-element.50), channel_id=1, source_target_pairs={{0,12},{1,13},{2,14},{3,15},{4,8},{5,9},{6,10},{7,11},{8,4},{9,5},... | collective-permute-start | bytes 98312 | tf_op jit(solution)/shard_map/ppermute | solution.py:582
  56.7 3.5 %fetch_weight.3.weight_ref = bf16[512,8192]{1,0:T(8,128)(2,1)S(1)} custom-call(bf16[512,8192]{1,0:T(8,128)(2,1)} %source_ref.1), custom_call_target="tpu_custom_call" | custom-call | bytes 8388608 | tf_op jit(solution)/shard_map/fetch_weight/pallas_call | solution.py:277
  60.2 1.8 %output_project.1 = (bf16[8,128,128]{2,1,0:T(8,128)(2,1)S(1)}, bf16[8,128,128]{2,1,0:T(8,128)(2,1)S(1)}) custom-call(s32[1]{0:T(128)} %bitcast.me_ref, bf16[512,8192]{1,0:T(8,128)(2,1)S(1)} %fetch_weight.3.weight_ref, bf16[128,128]{1,0:T(8,128)(2,1)S(1)} %get-tuple-element.47.rest_0_, bf16[128,128]{1,0:T(8,128)(2,1)S(1)} %collective-permute-done.4.rest_1_, ...), custom_call_target="tpu_custom_call" | custom-call | flops 268435456 | bytes 8388608 | tf_op jit(solution)/shard_map/output_project/pallas_call | solution.py:564
  62.1 1.5 %collective-permute-done.7 = bf16[8,128,128]{2,1,0:T(8,128)(2,1)S(1)} collective-permute-done((bf16[8,128,128]{2,1,0:T(8,128)(2,1)S(1)}, bf16[8,128,128]{2,1,0:T(8,128)(2,1)S(1)}, u32[]{:S(2)}, u32[]{:S(2)}) %collective-permute-start.7) | collective-permute-done | bytes 262176 | tf_op jit(solution)/shard_map/ppermute | solution.py:582
  63.7 12.5 %all_to_all.20 = bf16[8,128,128]{2,1,0:T(8,128)(2,1)S(1)} all-to-all(bf16[8,128,128]{2,1,0:T(8,128)(2,1)S(1)} %add_convert_fusion), channel_id=1, replica_groups={{0,2,4,6,8,10,12,14},{1,3,5,7,9,11,13,15},{16,18,20,22,24,26,28,30},{17..., dimensions={0} | all-to-all | bytes 524288 | tf_op jit(solution)/shard_map/all_to_all | solution.py:586
  76.2 0.6 reshape.32
  (33 shorter events, 1.6 us)
Async XLA Ops:
  1.8 16.9 %all-to-all-start = ((bf16[8,144,128]{2,1,0:T(8,128)(2,1)}), bf16[8,144,128]{2,1,0:T(8,128)(2,1)S(1)}, u32[]{:S(2)}, u32[]{:S(2)}) async-start(bf16[8,144,128]{2,1,0:T(8,128)(2,1)} %get-tuple-element.29), calls=%async_computation | async-start | bytes 589824 | tf_op jit(solution)/shard_map/all_to_all | solution.py:586
  9.0 1.2 %copy-start = (bf16[32,16,1024]{2,1,0:T(8,128)(2,1)S(1)}, bf16[32,16,1024]{2,1,0:T(8,128)(2,1)}, u32[]{:S(2)}) copy-start(bf16[32,16,1024]{2,1,0:T(8,128)(2,1)} %store_ref.1) | copy-start | bytes 3145732
  11.2 30.9 %collective-permute-start.2 = (bf16[512,512]{1,0:T(8,128)(2,1)S(1)}, bf16[512,512]{1,0:T(8,128)(2,1)S(1)}, u32[]{:S(2)}, u32[]{:S(2)}) collective-permute-start(bf16[512,512]{1,0:T(8,128)(2,1)S(1)} %get-tuple-element.40.rest_0_), channel_id=1, source_target_pairs={{0,1},{1,0},{2,3},{3,2},{4,5},{5,4},{6,7},{7,6},{8,9},{9,8},{10,11... | collective-permute-start | bytes 1572872 | tf_op jit(solution)/shard_map/ppermute | solution.py:582
  18.6 3.2 %collective-permute-start = (bf16[8,144,128]{2,1,0:T(8,128)(2,1)S(1)}, bf16[8,144,128]{2,1,0:T(8,128)(2,1)S(1)}, u32[]{:S(2)}, u32[]{:S(2)}) collective-permute-start(bf16[8,144,128]{2,1,0:T(8,128)(2,1)S(1)} %all-to-all-done.first_ref), channel_id=1, source_target_pairs={{0,1},{1,0},{2,3},{3,2},{4,5},{5,4},{6,7},{7,6},{8,9},{9,8},{10,11... | collective-permute-start | bytes 884744 | tf_op jit(solution)/shard_map/ppermute | solution.py:582
  18.8 12.8 %copy-start.1 = (bf16[1,160,1024]{2,1,0:T(8,128)(2,1)S(1)}, bf16[1,160,1024]{2,1,0:T(8,128)(2,1)}, u32[]{:S(2)}) copy-start(bf16[1,160,1024]{2,1,0:T(8,128)(2,1)} %param.17) | copy-start | bytes 983044
  18.8 12.8 %copy-start.2 = (s32[16]{0:T(128)S(1)}, s32[16]{0:T(128)}, u32[]{:S(2)}) copy-start(s32[16]{0:T(128)} %get-tuple-element.35.pair_ref) | copy-start | bytes 196
  18.8 19.8 %collective-permute-start.1 = (bf16[512,512]{1,0:T(8,128)(2,1)}, bf16[512,512]{1,0:T(8,128)(2,1)S(1)}, u32[]{:S(2)}, u32[]{:S(2)}) collective-permute-start(bf16[512,512]{1,0:T(8,128)(2,1)} %get-tuple-element.38), channel_id=1, source_target_pairs={{0,2},{1,3},{2,0},{3,1},{4,6},{5,7},{6,4},{7,5},{8,10},{9,11},{10,... | collective-permute-start | bytes 1572872 | tf_op jit(solution)/shard_map/ppermute | solution.py:582
  21.8 11.2 %copy-start.3 = (s32[2,1,16]{2,1,0:T(1,128)S(1)}, s32[2,1,16]{2,1,0:T(1,128)}, u32[]{:S(2)}) copy-start(s32[2,1,16]{2,1,0:T(1,128)} %param.21) | copy-start | bytes 388
  27.0 10.4 %all-to-all-start.1 = ((bf16[16,16,128]{2,1,0:T(8,128)(2,1)}), bf16[16,16,128]{2,1,0:T(8,128)(2,1)S(1)}, u32[]{:S(2)}, u32[]{:S(2)}) async-start(bf16[16,16,128]{2,1,0:T(8,128)(2,1)} %get-tuple-element.36), calls=%async_computation.1 | async-start | bytes 131072 | tf_op jit(solution)/shard_map/all_to_all | solution.py:586
  38.6 12.5 %collective-permute-start.3 = (bf16[512,512]{1,0:T(8,128)(2,1)S(1)}, bf16[512,512]{1,0:T(8,128)(2,1)S(1)}, u32[]{:S(2)}, u32[]{:S(2)}) collective-permute-start(bf16[512,512]{1,0:T(8,128)(2,1)S(1)} %collective-permute-done.1.rest_2_), channel_id=1, source_target_pairs={{0,1},{1,0},{2,3},{3,2},{4,5},{5,4},{6,7},{7,6},{8,9},{9,8},{10,11... | collective-permute-start | bytes 1572872 | tf_op jit(solution)/shard_map/ppermute | solution.py:582
  38.6 12.5 %all-to-all-start.2 = ((bf16[16,48,128]{2,1,0:T(8,128)(2,1)}), bf16[16,48,128]{2,1,0:T(8,128)(2,1)S(1)}, u32[]{:S(2)}, u32[]{:S(2)}) async-start(bf16[16,48,128]{2,1,0:T(8,128)(2,1)} %attend.1), calls=%async_computation.2 | async-start | bytes 393216 | tf_op jit(solution)/shard_map/all_to_all | solution.py:586
  52.2 8.0 %collective-permute-start.4 = (bf16[128,128]{1,0:T(8,128)(2,1)S(1)}, bf16[128,128]{1,0:T(8,128)(2,1)S(1)}, u32[]{:S(2)}, u32[]{:S(2)}) collective-permute-start(bf16[128,128]{1,0:T(8,128)(2,1)S(1)} %get-tuple-element.48), channel_id=1, source_target_pairs={{0,4},{1,5},{2,6},{3,7},{4,0},{5,1},{6,2},{7,3},{8,12},{9,13},{10,... | collective-permute-start | bytes 98312 | tf_op jit(solution)/shard_map/ppermute | solution.py:582
  52.3 7.9 %collective-permute-start.5 = (bf16[128,128]{1,0:T(8,128)(2,1)S(1)}, bf16[128,128]{1,0:T(8,128)(2,1)S(1)}, u32[]{:S(2)}, u32[]{:S(2)}) collective-permute-start(bf16[128,128]{1,0:T(8,128)(2,1)S(1)} %get-tuple-element.49), channel_id=1, source_target_pairs={{0,8},{1,9},{2,10},{3,11},{4,12},{5,13},{6,14},{7,15},{8,0},{9,1},... | collective-permute-start | bytes 98312 | tf_op jit(solution)/shard_map/ppermute | solution.py:582
  53.7 6.5 %collective-permute-start.6 = (bf16[128,128]{1,0:T(8,128)(2,1)S(1)}, bf16[128,128]{1,0:T(8,128)(2,1)S(1)}, u32[]{:S(2)}, u32[]{:S(2)}) collective-permute-start(bf16[128,128]{1,0:T(8,128)(2,1)S(1)} %get-tuple-element.50), channel_id=1, source_target_pairs={{0,12},{1,13},{2,14},{3,15},{4,8},{5,9},{6,10},{7,11},{8,4},{9,5},... | collective-permute-start | bytes 98312 | tf_op jit(solution)/shard_map/ppermute | solution.py:582
  62.0 1.6 %collective-permute-start.7 = (bf16[8,128,128]{2,1,0:T(8,128)(2,1)S(1)}, bf16[8,128,128]{2,1,0:T(8,128)(2,1)S(1)}, u32[]{:S(2)}, u32[]{:S(2)}) collective-permute-start(bf16[8,128,128]{2,1,0:T(8,128)(2,1)S(1)} %get-tuple-element.52), channel_id=1, source_target_pairs={{0,1},{1,0},{2,3},{3,2},{4,5},{5,4},{6,7},{7,6},{8,9},{9,8},{10,11... | collective-permute-start | bytes 786440 | tf_op jit(solution)/shard_map/ppermute | solution.py:582

commit v17 on v15

--- a/solution.py
+++ b/solution.py
@@ -53,7 +53,7 @@
 
 
 def prepare_kernel(
-    slots_dev, hidden_ref, gain_ref, slots_ref, block_ref, holder_ref, pair_ref, wide_scr
+    slots_dev, hidden_ref, gain_ref, slots_ref, block_ref, pair_ref, wide_scr
 ):
     steps, model = hidden_ref.shape
     pieces = model // LANES
@@ -67,10 +67,9 @@
     lane = lax.broadcasted_iota(jnp.int32, (EXTRA, LANES), 1)
     parity = lax.broadcasted_iota(jnp.int32, (EXTRA, LANES), 0)
     table = jnp.zeros((EXTRA, LANES), jnp.int32)
-    for m in range(holder_ref.shape[0]):
+    for m in range(pair_ref.shape[0]):
         slot = slots_ref[0, 2 * m]
         holder = lax.div(slot, slots_dev)
-        holder_ref[m] = holder
         pair_ref[holder] = m
         base = holder * slots_dev
         pair = jnp.where(parity == 0, slot - base, slots_ref[0, 2 * m + 1] - base)
@@ -92,10 +91,9 @@
     return pl.pallas_call(
         functools.partial(prepare_kernel, slots_dev),
         in_specs=[whole(), whole(), whole(SMEM)],
-        out_specs=(whole(), whole(SMEM), whole(SMEM)),
+        out_specs=(whole(), whole(SMEM)),
         out_shape=(
             jax.ShapeDtypeStruct((copies, rows, LANES), BF16),
-            jax.ShapeDtypeStruct((block_slot.shape[1] // 2,), jnp.int32),
             jax.ShapeDtypeStruct((block_slot.shape[1] // 2,), jnp.int32),
         ),
         scratch_shapes=[VMEM((rows, LANES), F32)],
@@ -613,7 +611,7 @@
     pieces = model // LANES
 
     me_word = me.astype(jnp.int32).reshape(1)
-    block, holder, pair = prepare(
+    block, pair = prepare(
         hidden[:, 0], norm_gain.reshape(pieces, LANES), block_slot, slots_dev, PAIRS if fast else 1
     )
     if fast:

time: 76.4 us -> 76.4 us (level)
  no operation moved by 1% of the time
where the time goes in v17:
time: 76.4 us; the launch traced here: 75.8 us
  starting transfers between devices  21.2 us (28%)
  Pallas kernels  18.4 us (24%)
  waiting for transfers between devices  17.6 us (23%)
  blocking collectives  12.5 us (16%)
  local copies, waits for them, and re-layouts  2.99 us (4%)
  other arithmetic  2.32 us (3%)
  between operations  0.88 us (1%)
    all_to_all x3, waiting for transfers between devices, exchange(): lax.all_to_all(blocks, AXIS, split_axis=0, concat_axis=0, tiled=True, axi...  16 us
    all_to_all x3, starting transfers between devices, exchange(): lax.all_to_all(blocks, AXIS, split_axis=0, concat_axis=0, tiled=True, axi...  14.6 us
    all_to_all x1, blocking collectives, exchange(): lax.all_to_all(blocks, AXIS, split_axis=0, concat_axis=0, tiled=True, axi...  12.5 us
    ppermute x8, starting transfers between devices, swap(): return lax.ppermute(block, AXIS, [(i, i ^ bit) for i in range(devices)])  6.54 us
    pallas_call x2, Pallas kernels, fetch(): pl.pallas_call(fetch_kernel, in_specs=[whole(pl.ANY)], out_specs=whole(pl...  5.1 us
    pallas_call x1, Pallas kernels, project(): pl.pallas_call(functools.partial(project_kernel, order, fast), in_specs=[...  5.08 us
    unnamed x9, local copies, waits for them, and re-layouts  2.28 us
    pallas_call x1, Pallas kernels, output(): pl.pallas_call(functools.partial(output_kernel, fast, len(lhs)), in_specs...  1.78 us
  transfers between devices with their start and end apart: 11, of which 4 were waited for; matrix products, arithmetic and copies ran while one was open for 4% of the time, Pallas kernels for 18%

profile of v17, /device:TPU:0, one launch (start us, length us, event | category | flops | bytes accessed | tf_op | source)
XLA Modules:
  0.0 75.8 jit_solution(4429568598314228309)
XLA Ops:
  0.0 1.7 %prepare.1 = (bf16[8,144,128]{2,1,0:T(8,128)(2,1)}, s32[16]{0:T(128)}) custom-call(bf16[2,8192]{1,0:T(2,128)(2,1)} %bitcast.11, bf16[64,128]{1,0:T(8,128)(2,1)} %bitcast.12, s32[1,32]{1,0:T(1,128)} %slots_ref.1), custom_call_target="tpu_custom_call" | custom-call | tf_op jit(solution)/shard_map/prepare/pallas_call | solution.py:91
  1.7 7.3 %all-to-all-start = ((bf16[8,144,128]{2,1,0:T(8,128)(2,1)}), bf16[8,144,128]{2,1,0:T(8,128)(2,1)S(1)}, u32[]{:S(2)}, u32[]{:S(2)}) async-start(bf16[8,144,128]{2,1,0:T(8,128)(2,1)} %get-tuple-element.28), calls=%async_computation | async-start | bytes 589824 | tf_op jit(solution)/shard_map/all_to_all | solution.py:584
  9.0 1.2 %copy-done = bf16[32,16,1024]{2,1,0:T(8,128)(2,1)S(1)} copy-done((bf16[32,16,1024]{2,1,0:T(8,128)(2,1)S(1)}, bf16[32,16,1024]{2,1,0:T(8,128)(2,1)}, u32[]{:S(2)}) %copy-start) | copy-done | bytes 1048600
  10.2 1.0 %split_values.1 = (bf16[512,512]{1,0:T(8,128)(2,1)S(1)}, bf16[512,512]{1,0:T(8,128)(2,1)}) custom-call(s32[1]{0:T(128)S(6)} %and.20.x_ref, bf16[32,16,1024]{2,1,0:T(8,128)(2,1)S(1)} %copy-done), custom_call_target="tpu_custom_call" | custom-call | tf_op jit(solution)/shard_map/split_values/pallas_call | solution.py:157
  11.2 2.0 %collective-permute-start.1 = (bf16[512,512]{1,0:T(8,128)(2,1)}, bf16[512,512]{1,0:T(8,128)(2,1)S(1)}, u32[]{:S(2)}, u32[]{:S(2)}) collective-permute-start(bf16[512,512]{1,0:T(8,128)(2,1)} %get-tuple-element.36), channel_id=1, source_target_pairs={{0,2},{1,3},{2,0},{3,1},{4,6},{5,7},{6,4},{7,5},{8,10},{9,11},{10,... | collective-permute-start | bytes 1572872 | tf_op jit(solution)/shard_map/ppermute | solution.py:580
  14.5 1.0 %copy.13 = bf16[1,512,160]{2,1,0:T(8,128)(2,1)S(1)} copy(bf16[1,512,160]{1,2,0:T(8,128)(2,1)} %param.16) | data formatting | bytes 327680 | tf_op args[5]
  15.8 2.9 %all-to-all-done.first_ref = bf16[8,144,128]{2,1,0:T(8,128)(2,1)S(1)} async-done(((bf16[8,144,128]{2,1,0:T(8,128)(2,1)}), bf16[8,144,128]{2,1,0:T(8,128)(2,1)S(1)}, u32[]{:S(2)}, u32[]{:S(2)}) %all-to-all-start) | async-done | bytes 294944 | tf_op jit(solution)/shard_map/all_to_all | solution.py:584
  18.8 1.6 %fetch_weight.2.wk_ref = bf16[8192,128]{1,0:T(8,128)(2,1)S(1)} custom-call(bf16[8192,128]{1,0:T(8,128)(2,1)} %source_ref), custom_call_target="tpu_custom_call" | custom-call | bytes 2097152 | tf_op jit(solution)/shard_map/fetch_weight/pallas_call | solution.py:275
  20.5 5.1 %norm_project.1 = (bf16[16,16,128]{2,1,0:T(8,128)(2,1)}, s32[128]{0:T(128)S(1)}) custom-call(s32[1]{0:T(128)} %bitcast.me_ref, bf16[8,144,128]{2,1,0:T(8,128)(2,1)S(1)} %all-to-all-done.first_ref, bf16[8,144,128]{2,1,0:T(8,128)(2,1)S(1)} %collective-permute-done.second_ref, bf16[8192,512]{1,0:T(8,128)(2,1)} %wq_ref.1, bf16[8192,128]{1,0:T(8,128)(2,1)S(1)} %fetch_weight.2.wk_ref), custom_call_target="tpu_custom_call" | custom-call | flops 335544320 | bytes 10485760 | tf_op jit(solution)/shard_map/norm_project/pallas_call | solution.py:378
  25.6 3.8 %all-to-all-start.1 = ((bf16[16,16,128]{2,1,0:T(8,128)(2,1)}), bf16[16,16,128]{2,1,0:T(8,128)(2,1)S(1)}, u32[]{:S(2)}, u32[]{:S(2)}) async-start(bf16[16,16,128]{2,1,0:T(8,128)(2,1)} %get-tuple-element.34), calls=%async_computation.1 | async-start | bytes 131072 | tf_op jit(solution)/shard_map/all_to_all | solution.py:584
  29.4 1.0 %fusion = (f32[512,64]{1,0:T(8,128)S(1)}, f32[512,64]{1,0:T(8,128)S(1)}, f32[512,64]{1,0:T(8,128)S(1)}) fusion(f32[64]{0:T(128)S(1)} %multiply_exponential_fusion, f32[512]{0:T(512)S(1)} %get-tuple-element.55), kind=kLoop, calls=%fused_computation.5 | loop fusion | flops 65536 | bytes 395520 | tf_op jit(solution)/shard_map/neg | solution.py:41
  30.6 1.3 %turned_keys.1.keys_ref = bf16[512,1024]{1,0:T(8,128)(2,1)S(1)} custom-call(s32[16]{0:T(128)S(1)} %copy-done.2, bf16[512,160]{1,0:T(8,128)(2,1)S(1)} %bitcast.9, bf16[160,1024]{1,0:T(8,128)(2,1)S(1)} %bitcast.10, f32[512,128]{1,0:T(8,128)S(1)} %get-tuple-element.59.cos_ref, f32[512,128]{1,0:T(8,128)S(1)} %get-tuple-element.60.sin_ref), custom_call_target="tpu_custom_call" | custom-call | flops 167772160 | bytes 2097152 | tf_op jit(solution)/shard_map/turned_keys/pallas_call | solution.py:239
  32.1 4.2 %all-to-all-done.1.columns_ref = bf16[16,16,128]{2,1,0:T(8,128)(2,1)S(1)} async-done(((bf16[16,16,128]{2,1,0:T(8,128)(2,1)}), bf16[16,16,128]{2,1,0:T(8,128)(2,1)S(1)}, u32[]{:S(2)}, u32[]{:S(2)}) %all-to-all-start.1) | async-done | bytes 65568 | tf_op jit(solution)/shard_map/all_to_all | solution.py:584
  36.3 1.3 %attend.1 = bf16[16,48,128]{2,1,0:T(8,128)(2,1)} custom-call(bf16[16,16,128]{2,1,0:T(8,128)(2,1)S(1)} %all-to-all-done.1.columns_ref, bf16[512,1024]{1,0:T(8,128)(2,1)S(1)} %turned_keys.1.keys_ref, f32[2,512]{1,0:T(2,128)S(1)} %and_select_fusion.bias_ref, f32[2,128]{1,0:T(2,128)S(1)} %get-tuple-element.61.cos_ref, f32[2,128]{1,0:T(2,128)S(1)} %get-tuple-element.62.sin_ref), custom_call_target="tpu_custom_call" | custom-call | flops 33554432 | bytes 2097152 | tf_op jit(solution)/shard_map/attend/pallas_call | solution.py:502
  37.6 3.5 %all-to-all-start.2 = ((bf16[16,48,128]{2,1,0:T(8,128)(2,1)}), bf16[16,48,128]{2,1,0:T(8,128)(2,1)S(1)}, u32[]{:S(2)}, u32[]{:S(2)}) async-start(bf16[16,48,128]{2,1,0:T(8,128)(2,1)} %attend.1), calls=%async_computation.2 | async-start | bytes 393216 | tf_op jit(solution)/shard_map/all_to_all | solution.py:584
  41.1 9.0 %all-to-all-done.2.weights_ref = bf16[16,48,128]{2,1,0:T(8,128)(2,1)S(1)} async-done(((bf16[16,48,128]{2,1,0:T(8,128)(2,1)}), bf16[16,48,128]{2,1,0:T(8,128)(2,1)S(1)}, u32[]{:S(2)}, u32[]{:S(2)}) %all-to-all-start.2) | async-done | bytes 196640 | tf_op jit(solution)/shard_map/all_to_all | solution.py:584
  50.1 1.1 %mix_values.1 = (bf16[128,128]{1,0:T(8,128)(2,1)S(1)}, bf16[128,128]{1,0:T(8,128)(2,1)S(1)}, bf16[128,128]{1,0:T(8,128)(2,1)S(1)}, bf16[128,128]{1,0:T(8,128)(2,1)S(1)}) custom-call(s32[1]{0:T(128)} %bitcast.me_ref, s32[128]{0:T(128)S(1)} %get-tuple-element.31.rows_ref, bf16[16,48,128]{2,1,0:T(8,128)(2,1)S(1)} %all-to-all-done.2.weights_ref, ...), custom_call_target="tpu_custom_call" | custom-call | flops 67108864 | bytes 4194304 | tf_op jit(solution)/shard_map/mix_values/pallas_call | solution.py:203
  51.3 1.4 %collective-permute-start.5 = (bf16[128,128]{1,0:T(8,128)(2,1)S(1)}, bf16[128,128]{1,0:T(8,128)(2,1)S(1)}, u32[]{:S(2)}, u32[]{:S(2)}) collective-permute-start(bf16[128,128]{1,0:T(8,128)(2,1)S(1)} %get-tuple-element.47), channel_id=1, source_target_pairs={{0,8},{1,9},{2,10},{3,11},{4,12},{5,13},{6,14},{7,15},{8,0},{9,1},... | collective-permute-start | bytes 98312 | tf_op jit(solution)/shard_map/ppermute | solution.py:580
  52.6 3.0 %collective-permute-start.6 = (bf16[128,128]{1,0:T(8,128)(2,1)S(1)}, bf16[128,128]{1,0:T(8,128)(2,1)S(1)}, u32[]{:S(2)}, u32[]{:S(2)}) collective-permute-start(bf16[128,128]{1,0:T(8,128)(2,1)S(1)} %get-tuple-element.48), channel_id=1, source_target_pairs={{0,12},{1,13},{2,14},{3,15},{4,8},{5,9},{6,10},{7,11},{8,4},{9,5},... | collective-permute-start | bytes 98312 | tf_op jit(solution)/shard_map/ppermute | solution.py:580
  55.6 3.5 %fetch_weight.3.weight_ref = bf16[512,8192]{1,0:T(8,128)(2,1)S(1)} custom-call(bf16[512,8192]{1,0:T(8,128)(2,1)} %source_ref.1), custom_call_target="tpu_custom_call" | custom-call | bytes 8388608 | tf_op jit(solution)/shard_map/fetch_weight/pallas_call | solution.py:275
  59.2 1.8 %output_project.1 = (bf16[8,128,128]{2,1,0:T(8,128)(2,1)S(1)}, bf16[8,128,128]{2,1,0:T(8,128)(2,1)S(1)}) custom-call(s32[1]{0:T(128)} %bitcast.me_ref, bf16[512,8192]{1,0:T(8,128)(2,1)S(1)} %fetch_weight.3.weight_ref, bf16[128,128]{1,0:T(8,128)(2,1)S(1)} %get-tuple-element.45.rest_0_, bf16[128,128]{1,0:T(8,128)(2,1)S(1)} %collective-permute-done.4.rest_1_, ...), custom_call_target="tpu_custom_call" | custom-call | flops 268435456 | bytes 8388608 | tf_op jit(solution)/shard_map/output_project/pallas_call | solution.py:562
  61.1 1.5 %collective-permute-done.7 = bf16[8,128,128]{2,1,0:T(8,128)(2,1)S(1)} collective-permute-done((bf16[8,128,128]{2,1,0:T(8,128)(2,1)S(1)}, bf16[8,128,128]{2,1,0:T(8,128)(2,1)S(1)}, u32[]{:S(2)}, u32[]{:S(2)}) %collective-permute-start.7) | collective-permute-done | bytes 262176 | tf_op jit(solution)/shard_map/ppermute | solution.py:580
  62.7 12.5 %all_to_all.20 = bf16[8,128,128]{2,1,0:T(8,128)(2,1)S(1)} all-to-all(bf16[8,128,128]{2,1,0:T(8,128)(2,1)S(1)} %add_convert_fusion), channel_id=1, replica_groups={{0,2,4,6,8,10,12,14},{1,3,5,7,9,11,13,15},{16,18,20,22,24,26,28,30},{17..., dimensions={0} | all-to-all | bytes 524288 | tf_op jit(solution)/shard_map/all_to_all | solution.py:584
  75.2 0.6 reshape.32
  (33 shorter events, 1.6 us)
Async XLA Ops:
  1.7 16.9 %all-to-all-start = ((bf16[8,144,128]{2,1,0:T(8,128)(2,1)}), bf16[8,144,128]{2,1,0:T(8,128)(2,1)S(1)}, u32[]{:S(2)}, u32[]{:S(2)}) async-start(bf16[8,144,128]{2,1,0:T(8,128)(2,1)} %get-tuple-element.28), calls=%async_computation | async-start | bytes 589824 | tf_op jit(solution)/shard_map/all_to_all | solution.py:584
  9.0 1.2 %copy-start = (bf16[32,16,1024]{2,1,0:T(8,128)(2,1)S(1)}, bf16[32,16,1024]{2,1,0:T(8,128)(2,1)}, u32[]{:S(2)}) copy-start(bf16[32,16,1024]{2,1,0:T(8,128)(2,1)} %store_ref.1) | copy-start | bytes 3145732
  11.2 26.4 %collective-permute-start.1 = (bf16[512,512]{1,0:T(8,128)(2,1)}, bf16[512,512]{1,0:T(8,128)(2,1)S(1)}, u32[]{:S(2)}, u32[]{:S(2)}) collective-permute-start(bf16[512,512]{1,0:T(8,128)(2,1)} %get-tuple-element.36), channel_id=1, source_target_pairs={{0,2},{1,3},{2,0},{3,1},{4,6},{5,7},{6,4},{7,5},{8,10},{9,11},{10,... | collective-permute-start | bytes 1572872 | tf_op jit(solution)/shard_map/ppermute | solution.py:580
  13.3 27.9 %collective-permute-start.2 = (bf16[512,512]{1,0:T(8,128)(2,1)S(1)}, bf16[512,512]{1,0:T(8,128)(2,1)S(1)}, u32[]{:S(2)}, u32[]{:S(2)}) collective-permute-start(bf16[512,512]{1,0:T(8,128)(2,1)S(1)} %get-tuple-element.38.rest_0_), channel_id=1, source_target_pairs={{0,1},{1,0},{2,3},{3,2},{4,5},{5,4},{6,7},{7,6},{8,9},{9,8},{10,11... | collective-permute-start | bytes 1572872 | tf_op jit(solution)/shard_map/ppermute | solution.py:580
  18.6 1.8 %collective-permute-start = (bf16[8,144,128]{2,1,0:T(8,128)(2,1)S(1)}, bf16[8,144,128]{2,1,0:T(8,128)(2,1)S(1)}, u32[]{:S(2)}, u32[]{:S(2)}) collective-permute-start(bf16[8,144,128]{2,1,0:T(8,128)(2,1)S(1)} %all-to-all-done.first_ref), channel_id=1, source_target_pairs={{0,1},{1,0},{2,3},{3,2},{4,5},{5,4},{6,7},{7,6},{8,9},{9,8},{10,11... | collective-permute-start | bytes 884744 | tf_op jit(solution)/shard_map/ppermute | solution.py:580
  18.8 11.8 %copy-start.1 = (bf16[1,160,1024]{2,1,0:T(8,128)(2,1)S(1)}, bf16[1,160,1024]{2,1,0:T(8,128)(2,1)}, u32[]{:S(2)}) copy-start(bf16[1,160,1024]{2,1,0:T(8,128)(2,1)} %param.17) | copy-start | bytes 983044
  18.8 11.8 %copy-start.2 = (s32[16]{0:T(128)S(1)}, s32[16]{0:T(128)}, u32[]{:S(2)}) copy-start(s32[16]{0:T(128)} %get-tuple-element.33.pair_ref) | copy-start | bytes 196
  20.4 11.5 %copy-start.3 = (s32[2,1,16]{2,1,0:T(1,128)S(1)}, s32[2,1,16]{2,1,0:T(1,128)}, u32[]{:S(2)}) copy-start(s32[2,1,16]{2,1,0:T(1,128)} %param.21) | copy-start | bytes 388
  25.6 10.7 %all-to-all-start.1 = ((bf16[16,16,128]{2,1,0:T(8,128)(2,1)}), bf16[16,16,128]{2,1,0:T(8,128)(2,1)S(1)}, u32[]{:S(2)}, u32[]{:S(2)}) async-start(bf16[16,16,128]{2,1,0:T(8,128)(2,1)} %get-tuple-element.34), calls=%async_computation.1 | async-start | bytes 131072 | tf_op jit(solution)/shard_map/all_to_all | solution.py:584
  37.6 12.5 %collective-permute-start.3 = (bf16[512,512]{1,0:T(8,128)(2,1)S(1)}, bf16[512,512]{1,0:T(8,128)(2,1)S(1)}, u32[]{:S(2)}, u32[]{:S(2)}) collective-permute-start(bf16[512,512]{1,0:T(8,128)(2,1)S(1)} %collective-permute-done.1.rest_2_), channel_id=1, source_target_pairs={{0,1},{1,0},{2,3},{3,2},{4,5},{5,4},{6,7},{7,6},{8,9},{9,8},{10,11... | collective-permute-start | bytes 1572872 | tf_op jit(solution)/shard_map/ppermute | solution.py:580
  37.6 12.5 %all-to-all-start.2 = ((bf16[16,48,128]{2,1,0:T(8,128)(2,1)}), bf16[16,48,128]{2,1,0:T(8,128)(2,1)S(1)}, u32[]{:S(2)}, u32[]{:S(2)}) async-start(bf16[16,48,128]{2,1,0:T(8,128)(2,1)} %attend.1), calls=%async_computation.2 | async-start | bytes 393216 | tf_op jit(solution)/shard_map/all_to_all | solution.py:584
  51.2 8.0 %collective-permute-start.4 = (bf16[128,128]{1,0:T(8,128)(2,1)S(1)}, bf16[128,128]{1,0:T(8,128)(2,1)S(1)}, u32[]{:S(2)}, u32[]{:S(2)}) collective-permute-start(bf16[128,128]{1,0:T(8,128)(2,1)S(1)} %get-tuple-element.46), channel_id=1, source_target_pairs={{0,4},{1,5},{2,6},{3,7},{4,0},{5,1},{6,2},{7,3},{8,12},{9,13},{10,... | collective-permute-start | bytes 98312 | tf_op jit(solution)/shard_map/ppermute | solution.py:580
  51.3 7.9 %collective-permute-start.5 = (bf16[128,128]{1,0:T(8,128)(2,1)S(1)}, bf16[128,128]{1,0:T(8,128)(2,1)S(1)}, u32[]{:S(2)}, u32[]{:S(2)}) collective-permute-start(bf16[128,128]{1,0:T(8,128)(2,1)S(1)} %get-tuple-element.47), channel_id=1, source_target_pairs={{0,8},{1,9},{2,10},{3,11},{4,12},{5,13},{6,14},{7,15},{8,0},{9,1},... | collective-permute-start | bytes 98312 | tf_op jit(solution)/shard_map/ppermute | solution.py:580
  52.6 6.5 %collective-permute-start.6 = (bf16[128,128]{1,0:T(8,128)(2,1)S(1)}, bf16[128,128]{1,0:T(8,128)(2,1)S(1)}, u32[]{:S(2)}, u32[]{:S(2)}) collective-permute-start(bf16[128,128]{1,0:T(8,128)(2,1)S(1)} %get-tuple-element.48), channel_id=1, source_target_pairs={{0,12},{1,13},{2,14},{3,15},{4,8},{5,9},{6,10},{7,11},{8,4},{9,5},... | collective-permute-start | bytes 98312 | tf_op jit(solution)/shard_map/ppermute | solution.py:580
  61.0 1.6 %collective-permute-start.7 = (bf16[8,128,128]{2,1,0:T(8,128)(2,1)S(1)}, bf16[8,128,128]{2,1,0:T(8,128)(2,1)S(1)}, u32[]{:S(2)}, u32[]{:S(2)}) collective-permute-start(bf16[8,128,128]{2,1,0:T(8,128)(2,1)S(1)} %get-tuple-element.50), channel_id=1, source_target_pairs={{0,1},{1,0},{2,3},{3,2},{4,5},{5,4},{6,7},{7,6},{8,9},{9,8},{10,11... | collective-permute-start | bytes 786440 | tf_op jit(solution)/shard_map/ppermute | solution.py:580

commit v18 on v15

--- a/solution.py
+++ b/solution.py
@@ -279,7 +279,7 @@
         in_specs=[whole(pl.ANY)],
         out_specs=whole(pl.ANY),
         out_shape=jax.ShapeDtypeStruct(weight.shape, weight.dtype),
-        scratch_shapes=[pltpu.SemaphoreType.DMA((4,))],
+        scratch_shapes=[pltpu.SemaphoreType.DMA((16,))],
         compiler_params=pltpu.CompilerParams(vmem_limit_bytes=limit * 2**20),
         cost_estimate=pl.CostEstimate(
             flops=0, bytes_accessed=2 * weight.size, transcendentals=0

time: 76.4 us -> 76.5 us (level)
  no operation moved by 1% of the time
where the time goes in v18:
time: 76.5 us; the launch traced here: 76 us
  starting transfers between devices  21.1 us (28%)
  Pallas kernels  18.6 us (24%)
  waiting for transfers between devices  17.6 us (23%)
  blocking collectives  12.5 us (16%)
  local copies, waits for them, and re-layouts  2.99 us (4%)
  other arithmetic  2.32 us (3%)
  between operations  0.88 us (1%)
    all_to_all x3, waiting for transfers between devices, exchange(): lax.all_to_all(blocks, AXIS, split_axis=0, concat_axis=0, tiled=True, axi...  16 us
    all_to_all x3, starting transfers between devices, exchange(): lax.all_to_all(blocks, AXIS, split_axis=0, concat_axis=0, tiled=True, axi...  14.6 us
    all_to_all x1, blocking collectives, exchange(): lax.all_to_all(blocks, AXIS, split_axis=0, concat_axis=0, tiled=True, axi...  12.5 us
    ppermute x8, starting transfers between devices, swap(): return lax.ppermute(block, AXIS, [(i, i ^ bit) for i in range(devices)])  6.54 us
    pallas_call x2, Pallas kernels, fetch(): pl.pallas_call(fetch_kernel, in_specs=[whole(pl.ANY)], out_specs=whole(pl...  5.29 us
    pallas_call x1, Pallas kernels, project(): pl.pallas_call(functools.partial(project_kernel, order, fast), in_specs=[...  5.08 us
    unnamed x9, local copies, waits for them, and re-layouts  2.28 us
    pallas_call x1, Pallas kernels, output(): pl.pallas_call(functools.partial(output_kernel, fast, len(lhs)), in_specs...  1.78 us
  transfers between devices with their start and end apart: 11, of which 4 were waited for; matrix products, arithmetic and copies ran while one was open for 4% of the time, Pallas kernels for 18%

profile of v18, /device:TPU:0, one launch (start us, length us, event | category | flops | bytes accessed | tf_op | source)
XLA Modules:
  0.0 76.0 jit_solution(12850240691887587582)
XLA Ops:
  0.0 1.7 %prepare.1 = (bf16[8,144,128]{2,1,0:T(8,128)(2,1)}, s32[16]{0:T(128)}, s32[16]{0:T(128)}) custom-call(bf16[2,8192]{1,0:T(2,128)(2,1)} %bitcast.11, bf16[64,128]{1,0:T(8,128)(2,1)} %bitcast.12, s32[1,32]{1,0:T(1,128)} %slots_ref.1), custom_call_target="tpu_custom_call" | custom-call | tf_op jit(solution)/shard_map/prepare/pallas_call | solution.py:92
  1.8 7.3 %all-to-all-start = ((bf16[8,144,128]{2,1,0:T(8,128)(2,1)}), bf16[8,144,128]{2,1,0:T(8,128)(2,1)S(1)}, u32[]{:S(2)}, u32[]{:S(2)}) async-start(bf16[8,144,128]{2,1,0:T(8,128)(2,1)} %get-tuple-element.28), calls=%async_computation | async-start | bytes 589824 | tf_op jit(solution)/shard_map/all_to_all | solution.py:586
  9.0 1.2 %copy-done = bf16[32,16,1024]{2,1,0:T(8,128)(2,1)S(1)} copy-done((bf16[32,16,1024]{2,1,0:T(8,128)(2,1)S(1)}, bf16[32,16,1024]{2,1,0:T(8,128)(2,1)}, u32[]{:S(2)}) %copy-start) | copy-done | bytes 1048600
  10.2 1.0 %split_values.1 = (bf16[512,512]{1,0:T(8,128)(2,1)S(1)}, bf16[512,512]{1,0:T(8,128)(2,1)}) custom-call(s32[1]{0:T(128)S(6)} %and.20.x_ref, bf16[32,16,1024]{2,1,0:T(8,128)(2,1)S(1)} %copy-done), custom_call_target="tpu_custom_call" | custom-call | tf_op jit(solution)/shard_map/split_values/pallas_call | solution.py:159
  11.2 2.0 %collective-permute-start.1 = (bf16[512,512]{1,0:T(8,128)(2,1)}, bf16[512,512]{1,0:T(8,128)(2,1)S(1)}, u32[]{:S(2)}, u32[]{:S(2)}) collective-permute-start(bf16[512,512]{1,0:T(8,128)(2,1)} %get-tuple-element.36), channel_id=1, source_target_pairs={{0,2},{1,3},{2,0},{3,1},{4,6},{5,7},{6,4},{7,5},{8,10},{9,11},{10,... | collective-permute-start | bytes 1572872 | tf_op jit(solution)/shard_map/ppermute | solution.py:582
  14.5 1.0 %copy.13 = bf16[1,512,160]{2,1,0:T(8,128)(2,1)S(1)} copy(bf16[1,512,160]{1,2,0:T(8,128)(2,1)} %param.16) | data formatting | bytes 327680 | tf_op args[5]
  15.8 2.9 %all-to-all-done.first_ref = bf16[8,144,128]{2,1,0:T(8,128)(2,1)S(1)} async-done(((bf16[8,144,128]{2,1,0:T(8,128)(2,1)}), bf16[8,144,128]{2,1,0:T(8,128)(2,1)S(1)}, u32[]{:S(2)}, u32[]{:S(2)}) %all-to-all-start) | async-done | bytes 294944 | tf_op jit(solution)/shard_map/all_to_all | solution.py:586
  18.8 1.8 %fetch_weight.2.wk_ref = bf16[8192,128]{1,0:T(8,128)(2,1)S(1)} custom-call(bf16[8192,128]{1,0:T(8,128)(2,1)} %source_ref), custom_call_target="tpu_custom_call" | custom-call | bytes 2097152 | tf_op jit(solution)/shard_map/fetch_weight/pallas_call | solution.py:277
  20.6 5.1 %norm_project.1 = (bf16[16,16,128]{2,1,0:T(8,128)(2,1)}, s32[128]{0:T(128)S(1)}) custom-call(s32[1]{0:T(128)} %bitcast.me_ref, bf16[8,144,128]{2,1,0:T(8,128)(2,1)S(1)} %all-to-all-done.first_ref, bf16[8,144,128]{2,1,0:T(8,128)(2,1)S(1)} %collective-permute-done.second_ref, bf16[8192,512]{1,0:T(8,128)(2,1)} %wq_ref.1, bf16[8192,128]{1,0:T(8,128)(2,1)S(1)} %fetch_weight.2.wk_ref), custom_call_target="tpu_custom_call" | custom-call | flops 335544320 | bytes 10485760 | tf_op jit(solution)/shard_map/norm_project/pallas_call | solution.py:380
  25.7 3.8 %all-to-all-start.1 = ((bf16[16,16,128]{2,1,0:T(8,128)(2,1)}), bf16[16,16,128]{2,1,0:T(8,128)(2,1)S(1)}, u32[]{:S(2)}, u32[]{:S(2)}) async-start(bf16[16,16,128]{2,1,0:T(8,128)(2,1)} %get-tuple-element.34), calls=%async_computation.1 | async-start | bytes 131072 | tf_op jit(solution)/shard_map/all_to_all | solution.py:586
  29.6 1.0 %fusion = (f32[512,64]{1,0:T(8,128)S(1)}, f32[512,64]{1,0:T(8,128)S(1)}, f32[512,64]{1,0:T(8,128)S(1)}) fusion(f32[64]{0:T(128)S(1)} %multiply_exponential_fusion, f32[512]{0:T(512)S(1)} %get-tuple-element.55), kind=kLoop, calls=%fused_computation.5 | loop fusion | flops 65536 | bytes 395520 | tf_op jit(solution)/shard_map/neg | solution.py:41
  30.8 1.3 %turned_keys.1.keys_ref = bf16[512,1024]{1,0:T(8,128)(2,1)S(1)} custom-call(s32[16]{0:T(128)S(1)} %copy-done.2, bf16[512,160]{1,0:T(8,128)(2,1)S(1)} %bitcast.9, bf16[160,1024]{1,0:T(8,128)(2,1)S(1)} %bitcast.10, f32[512,128]{1,0:T(8,128)S(1)} %get-tuple-element.59.cos_ref, f32[512,128]{1,0:T(8,128)S(1)} %get-tuple-element.60.sin_ref), custom_call_target="tpu_custom_call" | custom-call | flops 167772160 | bytes 2097152 | tf_op jit(solution)/shard_map/turned_keys/pallas_call | solution.py:241
  32.3 4.2 %all-to-all-done.1.columns_ref = bf16[16,16,128]{2,1,0:T(8,128)(2,1)S(1)} async-done(((bf16[16,16,128]{2,1,0:T(8,128)(2,1)}), bf16[16,16,128]{2,1,0:T(8,128)(2,1)S(1)}, u32[]{:S(2)}, u32[]{:S(2)}) %all-to-all-start.1) | async-done | bytes 65568 | tf_op jit(solution)/shard_map/all_to_all | solution.py:586
  36.5 1.3 %attend.1 = bf16[16,48,128]{2,1,0:T(8,128)(2,1)} custom-call(bf16[16,16,128]{2,1,0:T(8,128)(2,1)S(1)} %all-to-all-done.1.columns_ref, bf16[512,1024]{1,0:T(8,128)(2,1)S(1)} %turned_keys.1.keys_ref, f32[2,512]{1,0:T(2,128)S(1)} %and_select_fusion.bias_ref, f32[2,128]{1,0:T(2,128)S(1)} %get-tuple-element.61.cos_ref, f32[2,128]{1,0:T(2,128)S(1)} %get-tuple-element.62.sin_ref), custom_call_target="tpu_custom_call" | custom-call | flops 33554432 | bytes 2097152 | tf_op jit(solution)/shard_map/attend/pallas_call | solution.py:504
  37.8 3.5 %all-to-all-start.2 = ((bf16[16,48,128]{2,1,0:T(8,128)(2,1)}), bf16[16,48,128]{2,1,0:T(8,128)(2,1)S(1)}, u32[]{:S(2)}, u32[]{:S(2)}) async-start(bf16[16,48,128]{2,1,0:T(8,128)(2,1)} %attend.1), calls=%async_computation.2 | async-start | bytes 393216 | tf_op jit(solution)/shard_map/all_to_all | solution.py:586
  41.3 9.0 %all-to-all-done.2.weights_ref = bf16[16,48,128]{2,1,0:T(8,128)(2,1)S(1)} async-done(((bf16[16,48,128]{2,1,0:T(8,128)(2,1)}), bf16[16,48,128]{2,1,0:T(8,128)(2,1)S(1)}, u32[]{:S(2)}, u32[]{:S(2)}) %all-to-all-start.2) | async-done | bytes 196640 | tf_op jit(solution)/shard_map/all_to_all | solution.py:586
  50.3 1.1 %mix_values.1 = (bf16[128,128]{1,0:T(8,128)(2,1)S(1)}, bf16[128,128]{1,0:T(8,128)(2,1)S(1)}, bf16[128,128]{1,0:T(8,128)(2,1)S(1)}, bf16[128,128]{1,0:T(8,128)(2,1)S(1)}) custom-call(s32[1]{0:T(128)} %bitcast.me_ref, s32[128]{0:T(128)S(1)} %get-tuple-element.31.rows_ref, bf16[16,48,128]{2,1,0:T(8,128)(2,1)S(1)} %all-to-all-done.2.weights_ref, ...), custom_call_target="tpu_custom_call" | custom-call | flops 67108864 | bytes 4194304 | tf_op jit(solution)/shard_map/mix_values/pallas_call | solution.py:205
  51.4 1.4 %collective-permute-start.5 = (bf16[128,128]{1,0:T(8,128)(2,1)S(1)}, bf16[128,128]{1,0:T(8,128)(2,1)S(1)}, u32[]{:S(2)}, u32[]{:S(2)}) collective-permute-start(bf16[128,128]{1,0:T(8,128)(2,1)S(1)} %get-tuple-element.47), channel_id=1, source_target_pairs={{0,8},{1,9},{2,10},{3,11},{4,12},{5,13},{6,14},{7,15},{8,0},{9,1},... | collective-permute-start | bytes 98312 | tf_op jit(solution)/shard_map/ppermute | solution.py:582
  52.8 3.0 %collective-permute-start.6 = (bf16[128,128]{1,0:T(8,128)(2,1)S(1)}, bf16[128,128]{1,0:T(8,128)(2,1)S(1)}, u32[]{:S(2)}, u32[]{:S(2)}) collective-permute-start(bf16[128,128]{1,0:T(8,128)(2,1)S(1)} %get-tuple-element.48), channel_id=1, source_target_pairs={{0,12},{1,13},{2,14},{3,15},{4,8},{5,9},{6,10},{7,11},{8,4},{9,5},... | collective-permute-start | bytes 98312 | tf_op jit(solution)/shard_map/ppermute | solution.py:582
  55.8 3.5 %fetch_weight.3.weight_ref = bf16[512,8192]{1,0:T(8,128)(2,1)S(1)} custom-call(bf16[512,8192]{1,0:T(8,128)(2,1)} %source_ref.1), custom_call_target="tpu_custom_call" | custom-call | bytes 8388608 | tf_op jit(solution)/shard_map/fetch_weight/pallas_call | solution.py:277
  59.4 1.8 %output_project.1 = (bf16[8,128,128]{2,1,0:T(8,128)(2,1)S(1)}, bf16[8,128,128]{2,1,0:T(8,128)(2,1)S(1)}) custom-call(s32[1]{0:T(128)} %bitcast.me_ref, bf16[512,8192]{1,0:T(8,128)(2,1)S(1)} %fetch_weight.3.weight_ref, bf16[128,128]{1,0:T(8,128)(2,1)S(1)} %get-tuple-element.45.rest_0_, bf16[128,128]{1,0:T(8,128)(2,1)S(1)} %collective-permute-done.4.rest_1_, ...), custom_call_target="tpu_custom_call" | custom-call | flops 268435456 | bytes 8388608 | tf_op jit(solution)/shard_map/output_project/pallas_call | solution.py:564
  61.2 1.5 %collective-permute-done.7 = bf16[8,128,128]{2,1,0:T(8,128)(2,1)S(1)} collective-permute-done((bf16[8,128,128]{2,1,0:T(8,128)(2,1)S(1)}, bf16[8,128,128]{2,1,0:T(8,128)(2,1)S(1)}, u32[]{:S(2)}, u32[]{:S(2)}) %collective-permute-start.7) | collective-permute-done | bytes 262176 | tf_op jit(solution)/shard_map/ppermute | solution.py:582
  62.8 12.5 %all_to_all.20 = bf16[8,128,128]{2,1,0:T(8,128)(2,1)S(1)} all-to-all(bf16[8,128,128]{2,1,0:T(8,128)(2,1)S(1)} %add_convert_fusion), channel_id=1, replica_groups={{0,2,4,6,8,10,12,14},{1,3,5,7,9,11,13,15},{16,18,20,22,24,26,28,30},{17..., dimensions={0} | all-to-all | bytes 524288 | tf_op jit(solution)/shard_map/all_to_all | solution.py:586
  75.3 0.6 reshape.32
  (33 shorter events, 1.6 us)
Async XLA Ops:
  1.8 16.9 %all-to-all-start = ((bf16[8,144,128]{2,1,0:T(8,128)(2,1)}), bf16[8,144,128]{2,1,0:T(8,128)(2,1)S(1)}, u32[]{:S(2)}, u32[]{:S(2)}) async-start(bf16[8,144,128]{2,1,0:T(8,128)(2,1)} %get-tuple-element.28), calls=%async_computation | async-start | bytes 589824 | tf_op jit(solution)/shard_map/all_to_all | solution.py:586
  9.0 1.2 %copy-start = (bf16[32,16,1024]{2,1,0:T(8,128)(2,1)S(1)}, bf16[32,16,1024]{2,1,0:T(8,128)(2,1)}, u32[]{:S(2)}) copy-start(bf16[32,16,1024]{2,1,0:T(8,128)(2,1)} %store_ref.1) | copy-start | bytes 3145732
  11.2 26.5 %collective-permute-start.1 = (bf16[512,512]{1,0:T(8,128)(2,1)}, bf16[512,512]{1,0:T(8,128)(2,1)S(1)}, u32[]{:S(2)}, u32[]{:S(2)}) collective-permute-start(bf16[512,512]{1,0:T(8,128)(2,1)} %get-tuple-element.36), channel_id=1, source_target_pairs={{0,2},{1,3},{2,0},{3,1},{4,6},{5,7},{6,4},{7,5},{8,10},{9,11},{10,... | collective-permute-start | bytes 1572872 | tf_op jit(solution)/shard_map/ppermute | solution.py:582
  13.3 28.1 %collective-permute-start.2 = (bf16[512,512]{1,0:T(8,128)(2,1)S(1)}, bf16[512,512]{1,0:T(8,128)(2,1)S(1)}, u32[]{:S(2)}, u32[]{:S(2)}) collective-permute-start(bf16[512,512]{1,0:T(8,128)(2,1)S(1)} %get-tuple-element.38.rest_0_), channel_id=1, source_target_pairs={{0,1},{1,0},{2,3},{3,2},{4,5},{5,4},{6,7},{7,6},{8,9},{9,8},{10,11... | collective-permute-start | bytes 1572872 | tf_op jit(solution)/shard_map/ppermute | solution.py:582
  18.6 2.0 %collective-permute-start = (bf16[8,144,128]{2,1,0:T(8,128)(2,1)S(1)}, bf16[8,144,128]{2,1,0:T(8,128)(2,1)S(1)}, u32[]{:S(2)}, u32[]{:S(2)}) collective-permute-start(bf16[8,144,128]{2,1,0:T(8,128)(2,1)S(1)} %all-to-all-done.first_ref), channel_id=1, source_target_pairs={{0,1},{1,0},{2,3},{3,2},{4,5},{5,4},{6,7},{7,6},{8,9},{9,8},{10,11... | collective-permute-start | bytes 884744 | tf_op jit(solution)/shard_map/ppermute | solution.py:582
  18.8 12.0 %copy-start.1 = (bf16[1,160,1024]{2,1,0:T(8,128)(2,1)S(1)}, bf16[1,160,1024]{2,1,0:T(8,128)(2,1)}, u32[]{:S(2)}) copy-start(bf16[1,160,1024]{2,1,0:T(8,128)(2,1)} %param.17) | copy-start | bytes 983044
  18.8 12.0 %copy-start.2 = (s32[16]{0:T(128)S(1)}, s32[16]{0:T(128)}, u32[]{:S(2)}) copy-start(s32[16]{0:T(128)} %get-tuple-element.33.pair_ref) | copy-start | bytes 196
  20.6 11.5 %copy-start.3 = (s32[2,1,16]{2,1,0:T(1,128)S(1)}, s32[2,1,16]{2,1,0:T(1,128)}, u32[]{:S(2)}) copy-start(s32[2,1,16]{2,1,0:T(1,128)} %param.21) | copy-start | bytes 388
  25.7 10.7 %all-to-all-start.1 = ((bf16[16,16,128]{2,1,0:T(8,128)(2,1)}), bf16[16,16,128]{2,1,0:T(8,128)(2,1)S(1)}, u32[]{:S(2)}, u32[]{:S(2)}) async-start(bf16[16,16,128]{2,1,0:T(8,128)(2,1)} %get-tuple-element.34), calls=%async_computation.1 | async-start | bytes 131072 | tf_op jit(solution)/shard_map/all_to_all | solution.py:586
  37.8 12.5 %collective-permute-start.3 = (bf16[512,512]{1,0:T(8,128)(2,1)S(1)}, bf16[512,512]{1,0:T(8,128)(2,1)S(1)}, u32[]{:S(2)}, u32[]{:S(2)}) collective-permute-start(bf16[512,512]{1,0:T(8,128)(2,1)S(1)} %collective-permute-done.1.rest_2_), channel_id=1, source_target_pairs={{0,1},{1,0},{2,3},{3,2},{4,5},{5,4},{6,7},{7,6},{8,9},{9,8},{10,11... | collective-permute-start | bytes 1572872 | tf_op jit(solution)/shard_map/ppermute | solution.py:582
  37.8 12.5 %all-to-all-start.2 = ((bf16[16,48,128]{2,1,0:T(8,128)(2,1)}), bf16[16,48,128]{2,1,0:T(8,128)(2,1)S(1)}, u32[]{:S(2)}, u32[]{:S(2)}) async-start(bf16[16,48,128]{2,1,0:T(8,128)(2,1)} %attend.1), calls=%async_computation.2 | async-start | bytes 393216 | tf_op jit(solution)/shard_map/all_to_all | solution.py:586
  51.4 8.0 %collective-permute-start.4 = (bf16[128,128]{1,0:T(8,128)(2,1)S(1)}, bf16[128,128]{1,0:T(8,128)(2,1)S(1)}, u32[]{:S(2)}, u32[]{:S(2)}) collective-permute-start(bf16[128,128]{1,0:T(8,128)(2,1)S(1)} %get-tuple-element.46), channel_id=1, source_target_pairs={{0,4},{1,5},{2,6},{3,7},{4,0},{5,1},{6,2},{7,3},{8,12},{9,13},{10,... | collective-permute-start | bytes 98312 | tf_op jit(solution)/shard_map/ppermute | solution.py:582
  51.4 7.9 %collective-permute-start.5 = (bf16[128,128]{1,0:T(8,128)(2,1)S(1)}, bf16[128,128]{1,0:T(8,128)(2,1)S(1)}, u32[]{:S(2)}, u32[]{:S(2)}) collective-permute-start(bf16[128,128]{1,0:T(8,128)(2,1)S(1)} %get-tuple-element.47), channel_id=1, source_target_pairs={{0,8},{1,9},{2,10},{3,11},{4,12},{5,13},{6,14},{7,15},{8,0},{9,1},... | collective-permute-start | bytes 98312 | tf_op jit(solution)/shard_map/ppermute | solution.py:582
  52.8 6.5 %collective-permute-start.6 = (bf16[128,128]{1,0:T(8,128)(2,1)S(1)}, bf16[128,128]{1,0:T(8,128)(2,1)S(1)}, u32[]{:S(2)}, u32[]{:S(2)}) collective-permute-start(bf16[128,128]{1,0:T(8,128)(2,1)S(1)} %get-tuple-element.48), channel_id=1, source_target_pairs={{0,12},{1,13},{2,14},{3,15},{4,8},{5,9},{6,10},{7,11},{8,4},{9,5},... | collective-permute-start | bytes 98312 | tf_op jit(solution)/shard_map/ppermute | solution.py:582
  61.2 1.6 %collective-permute-start.7 = (bf16[8,128,128]{2,1,0:T(8,128)(2,1)S(1)}, bf16[8,128,128]{2,1,0:T(8,128)(2,1)S(1)}, u32[]{:S(2)}, u32[]{:S(2)}) collective-permute-start(bf16[8,128,128]{2,1,0:T(8,128)(2,1)S(1)} %get-tuple-element.50), channel_id=1, source_target_pairs={{0,1},{1,0},{2,3},{3,2},{4,5},{5,4},{6,7},{7,6},{8,9},{9,8},{10,11... | collective-permute-start | bytes 786440 | tf_op jit(solution)/shard_map/ppermute | solution.py:582
